TPU v7x, 32 devices: a whole 2x2x4 slice. The times are simulated.
32 devices in a mesh: pipe: 4 (over x, core), ctx: 2 (over y), tp: 4 (over z).
Axes of the slice: x: 2, y: 2, z: 4, core: 2. Of those that a mesh axis runs over, the one named last changes fastest.
Arguments:
- segment_inputs: bfloat16 [4, 2, 256, 4096], P('pipe', None, ('ctx', 'tp')), may hold values from -128 to 128
- keys: bfloat16 [4, 2, 256, 512], P('pipe', None, 'ctx', 'tp'), may hold values from -64 to 64
- values: bfloat16 [4, 2, 256, 512], P('pipe', None, 'ctx', 'tp'), may hold values from -6 to 6
- norm_gain: float32 [4, 4096], P('pipe'), may hold values from 0.1 to 1.9
- waiting_grads: bfloat16 [4, 256, 4096], P('pipe', ('ctx', 'tp')), may hold values from -32 to 32
- output_grads: bfloat16 [1, 256, 4096], P(None, ('ctx', 'tp')), may hold values from -32 to 32
- doc_lengths: int32 [5, 8], replicated, may hold values from 1 to 128, as said below
Outputs:
- input_grads: bfloat16 [4, 2, 256, 4096], P('pipe', None, ('ctx', 'tp'))
- key_grads: float32 [4, 2, 256, 512], P('pipe', None, 'ctx', 'tp')
- value_grads: float32 [4, 2, 256, 512], P('pipe', None, 'ctx', 'tp')
- gain_grads: float32 [4, 4096], P('pipe')
Inputs may be any that keep to these rules, and one draw needn't show every extreme that they name: `doc_lengths`: row m lists in order of position the lengths of the 8 documents packed into microbatch m's sequence; each row sums to 256; the last document is exactly 128 long.
All inputs are finite; a program needn't handle non-finite values.
Results may differ from a plain program's by a relative error of at most 0.009.
The roundings to bfloat16 on the way count: a program that leaves them out, or rounds other values in their place, can miss the bound.
Values may be sent and summed in bfloat16 or wider, within the bound.
No kernel may reach another device: no remote copies, remote signals or barrier semaphores. Data moves between devices by JAX's collectives and lax.ppermute only.
A program may use at most 64 MiB of HBM per device.

v0:
```python
import jax
import jax.numpy as jnp
from jax import lax
from jax.sharding import PartitionSpec as P

HD = 128
S_DEV = 128
TICKS = 2


epsilon = 1e-05
masked_fill = -1e30


def passed_along(value, axis, by):
    count = lax.axis_size(axis)
    return lax.ppermute(value, axis, [(i, (i + by) % count) for i in range(count)])


def from_behind(value, axis, steps):
    count = lax.axis_size(axis)
    first, last = (max(0, -steps), min(count, count - steps))
    return lax.ppermute(value, axis, [(source, source + steps) for source in range(first, last)])


def row_positions(rows, half_rows, cycle_count):
    section = rows // half_rows
    offset = rows % half_rows
    owner = section // 2
    placed = jnp.where(section % 2 == 0, owner, 2 * cycle_count - 1 - owner)
    return placed * half_rows + offset


def document_starts(lengths_row, positions):
    closing = jnp.cumsum(lengths_row)
    passed = closing[None, :] <= positions[:, None]
    return jnp.sum(jnp.where(passed, lengths_row[None, :], 0), axis=1)


def keep_same(current):
    return current


def key_positions(key_first, key_count, cycle_count):
    rows = key_first + jnp.arange(key_count, dtype=jnp.int32)
    return row_positions(rows, S_DEV // 2, cycle_count)


def block_active(key_first, key_count, query_pos, query_start, cycle_count):
    key_pos = key_positions(key_first, key_count, cycle_count)
    return (jnp.min(key_pos) <= jnp.max(query_pos)) & (jnp.max(key_pos) >= jnp.min(query_start))


def score_block(query_block, key_block, query_pos, query_start, key_first, cycle_count):
    key_count = key_block.shape[0]
    key_pos = key_positions(key_first, key_count, cycle_count)
    scores = HD ** (-0.5) * jnp.einsum(
        "rkgd,skd->kgrs", query_block, key_block, preferred_element_type=jnp.float32
    )
    visible = (key_pos[None, :] <= query_pos[:, None]) & (key_pos[None, :] >= query_start[:, None])
    return (scores, visible[None, None])


def forward_update(carry, key_flat, value_flat, key_first, context):
    query_block, grad_block, query_pos, query_start, cycle_count = context
    key_count = key_flat.shape[0]

    def apply_block(current):
        row_peak, row_total, weighted = current
        key_block = key_flat.reshape(key_count, -1, HD)
        value_block = value_flat.reshape(key_count, -1, HD)
        scores, visible = score_block(
            query_block, key_block, query_pos, query_start, key_first, cycle_count
        )
        block_peak = jnp.max(jnp.where(visible, scores, masked_fill), axis=-1)
        new_peak = jnp.maximum(row_peak, block_peak)
        weights = jnp.where(visible, jnp.exp(scores - new_peak[..., None]), 0.0)
        prob_grad = jnp.einsum(
            "rkgd,skd->kgrs", grad_block, value_block, preferred_element_type=jnp.float32
        )
        return (new_peak, jnp.sum(weights, axis=-1), jnp.sum(weights * prob_grad, axis=-1))

    return lax.cond(
        block_active(key_first, key_count, query_pos, query_start, cycle_count),
        apply_block,
        keep_same,
        carry,
    )


def backward_terms(key_flat, value_flat, key_first, context, row_stats):
    query_block, grad_block, query_pos, query_start, cycle_count = context
    logsum, row_term = row_stats
    key_count = key_flat.shape[0]
    key_block = key_flat.reshape(key_count, -1, HD)
    value_block = value_flat.reshape(key_count, -1, HD)
    scale_factor = HD ** (-0.5)
    scores, visible = score_block(
        query_block, key_block, query_pos, query_start, key_first, cycle_count
    )
    prob_weights = jnp.where(visible, jnp.exp(scores - logsum[..., None]), 0.0)
    prob_grad = jnp.einsum(
        "rkgd,skd->kgrs", grad_block, value_block, preferred_element_type=jnp.float32
    )
    dscore = (prob_weights * (prob_grad - row_term[..., None])).astype(jnp.bfloat16)
    probs_low = prob_weights.astype(jnp.bfloat16)
    query_add = scale_factor * jnp.einsum(
        "kgrs,skd->rkgd", dscore, key_block, preferred_element_type=jnp.float32
    )
    key_add = scale_factor * jnp.einsum(
        "kgrs,rkgd->skd", dscore, query_block, preferred_element_type=jnp.float32
    )
    value_add = jnp.einsum(
        "kgrs,rkgd->skd", probs_low, grad_block, preferred_element_type=jnp.float32
    )
    return (query_add, key_add.reshape(key_count, -1), value_add.reshape(key_count, -1))


def segment_tick(inputs, key_local, value_local, gain_row, arriving, lengths_row):
    widened = inputs.astype(jnp.float32)
    inverse = lax.rsqrt(jnp.mean(widened * widened, axis=-1, keepdims=True) + epsilon)
    normed = widened * inverse
    queries = (normed * gain_row[None, :]).astype(jnp.bfloat16)
    query_heads, grad_heads = (
        lax.all_to_all(queries, "tp", split_axis=1, concat_axis=0, tiled=True),
        lax.all_to_all(arriving, "tp", split_axis=1, concat_axis=0, tiled=True),
    )
    row_count = key_local.shape[0]
    kv_local = key_local.shape[1] // HD
    group_size = query_heads.shape[1] // (HD * kv_local)
    query_block = query_heads.reshape(row_count, kv_local, group_size, HD)
    grad_block = grad_heads.reshape(row_count, kv_local, group_size, HD)
    cycle_count = lax.axis_size("ctx")
    cycle_place = lax.axis_index("ctx")
    query_pos = key_positions(cycle_place * row_count, row_count, cycle_count)
    query_start = document_starts(lengths_row, query_pos)
    context = (query_block, grad_block, query_pos, query_start, cycle_count)
    empty_peak = jnp.full((kv_local, group_size, row_count), masked_fill, jnp.float32)
    zero_rows = jnp.zeros((kv_local, group_size, row_count), jnp.float32)
    initial = (empty_peak, zero_rows, zero_rows)
    row_peak, row_total, weighted = forward_update(
        initial,
        lax.all_gather(key_local, "ctx", axis=0, tiled=True),
        lax.all_gather(value_local, "ctx", axis=0, tiled=True),
        jnp.int32(0),
        context,
    )
    row_stats = (row_peak + jnp.log(row_total), weighted / row_total)
    query_zero = jnp.zeros((row_count, kv_local, group_size, HD), jnp.float32)

    def cycle_turn(cycle_step, carry):
        key_block, value_block, key_grad, value_grad, query_grad = carry
        owner_index = (cycle_place - cycle_step) % cycle_count
        block_first = owner_index * row_count

        def apply_terms(current):
            added_terms = backward_terms(key_block, value_block, block_first, context, row_stats)
            return (
                current[0] + added_terms[1],
                current[1] + added_terms[2],
                current[2] + added_terms[0],
            )

        key_grad, value_grad, query_grad = lax.cond(
            block_active(block_first, row_count, query_pos, query_start, cycle_count),
            apply_terms,
            keep_same,
            (key_grad, value_grad, query_grad),
        )
        key_block, value_block = passed_along((key_block, value_block), "ctx", 1)
        key_grad, value_grad = passed_along((key_grad, value_grad), "ctx", 1)
        return (key_block, value_block, key_grad, value_grad, query_grad)

    zero_kv = jnp.zeros(key_local.shape, jnp.float32)
    finished = lax.fori_loop(
        0, cycle_count, cycle_turn, (key_local, value_local, zero_kv, zero_kv, query_zero)
    )
    key_grad, value_grad, query_grad = (finished[2], finished[3], finished[4])
    query_low = query_grad.reshape(row_count, -1).astype(jnp.bfloat16)
    grad_rows = lax.all_to_all(query_low, "tp", split_axis=0, concat_axis=1, tiled=True)
    rounded = grad_rows.astype(jnp.float32)
    scaled = rounded * gain_row[None, :]
    coupling = jnp.mean(scaled * normed, axis=-1, keepdims=True)
    input_grad = (arriving.astype(jnp.float32) + inverse * (scaled - normed * coupling)).astype(
        jnp.bfloat16
    )
    gain_part = jnp.sum(rounded * normed, axis=0)
    return (input_grad, key_grad, value_grad, gain_part)


def on_device(segment_inputs, keys, values, norm_gain, waiting_grads, output_grads, doc_lengths):
    segment_index = lax.axis_index("pipe")
    last_segment = lax.axis_size("pipe") - 1
    gain_row = norm_gain[0]
    arriving = waiting_grads[0]
    input_list = []
    key_list = []
    value_list = []
    gain_running = jnp.zeros(gain_row.shape, jnp.float32)
    for tick_index in range(TICKS):
        micro_index = segment_index + tick_index
        lengths_row = lax.dynamic_index_in_dim(doc_lengths, micro_index, 0, keepdims=False)
        input_grad, key_grad, value_grad, gain_part = segment_tick(
            segment_inputs[0, tick_index],
            keys[0, tick_index],
            values[0, tick_index],
            gain_row,
            arriving,
            lengths_row,
        )
        input_list.append(input_grad)
        key_list.append(key_grad)
        value_list.append(value_grad)
        gain_running = gain_running + gain_part
        if tick_index + 1 < TICKS:
            arrived = from_behind(input_grad, "pipe", -1)
            arriving = jnp.where(segment_index == last_segment, output_grads[tick_index], arrived)
    gain_grads = lax.psum(gain_running, ("ctx", "tp"))
    return (
        jnp.stack(input_list)[None],
        jnp.stack(key_list)[None],
        jnp.stack(value_list)[None],
        gain_grads[None],
    )


def solution(mesh):
    in_specs = (
        P("pipe", None, ("ctx", "tp"), None),
        P("pipe", None, "ctx", "tp"),
        P("pipe", None, "ctx", "tp"),
        P("pipe", None),
        P("pipe", ("ctx", "tp"), None),
        P(None, ("ctx", "tp"), None),
        P(),
    )
    out_specs = (
        P("pipe", None, ("ctx", "tp"), None),
        P("pipe", None, "ctx", "tp"),
        P("pipe", None, "ctx", "tp"),
        P("pipe", None),
    )
    return jax.shard_map(
        on_device, mesh=mesh, in_specs=in_specs, out_specs=out_specs, check_vma=False
    )
```

profile of v0, /device:TPU:0, one launch (start us, length us, event | category | flops | bytes accessed | tf_op | source)
XLA Modules:
  0.0 192.2 jit_solution(4643874019224985885)
XLA Ops:
  0.6 1.3 fusion.107
  1.9 0.9 slice_convert_fusion.1
  3.7 0.7 reduce.19
  4.4 1.0 multiply_convert_fusion.1
  5.4 6.4 %all-to-all-start = ((bf16[32,4,1024]{2,0,1:T(8,128)(2,1)}), bf16[32,4,1024]{2,0,1:T(8,128)(2,1)S(1)}, u32[]{:S(2)}, u32[]{:S(2)}) async-start(bf16[32,4,1024]{2,0,1:T(8,128)(2,1)} %multiply_convert_fusion.1), calls=%async_computation | async-start | bytes 524288 | tf_op jit(solution)/shard_map/all_to_all | solution.py:125
  12.1 0.8 copy.84
  12.8 0.8 fusion.121
  13.6 7.2 %all-to-all-done = bf16[32,4,1024]{2,0,1:T(8,128)(2,1)S(1)} async-done(((bf16[32,4,1024]{2,0,1:T(8,128)(2,1)}), bf16[32,4,1024]{2,0,1:T(8,128)(2,1)S(1)}, u32[]{:S(2)}, u32[]{:S(2)}) %all-to-all-start) | async-done | bytes 262176 | tf_op jit(solution)/shard_map/all_to_all | solution.py:125
  20.8 3.5 %all-to-all-start.1 = ((bf16[32,4,1024]{2,0,1:T(8,128)(2,1)}), bf16[32,4,1024]{2,0,1:T(8,128)(2,1)S(1)}, u32[]{:S(2)}, u32[]{:S(2)}) async-start(bf16[32,4,1024]{2,0,1:T(8,128)(2,1)} %copy.84), calls=%async_computation.1 | async-start | bytes 524288 | tf_op jit(solution)/shard_map/all_to_all | solution.py:126
  24.7 0.7 select_reduce_fusion.3
  26.1 0.7 fusion.116
  30.5 4.6 %all-gather = bf16[1,1,256,128]{3,2,1,0:T(8,128)(2,1)S(1)} all-gather(bf16[1,1,128,128]{3,2,1,0:T(8,128)(2,1)S(1)} %get-tuple-element.1500), channel_id=2, replica_groups=mesh['pipe'=4,'ctx'=2,'tp'=4] {'ctx'}, dimensions={2}, use_global_device_ids=true | all-gather | bytes 98304 | tf_op jit(solution)/shard_map/all_gather | solution.py:143
  35.1 4.6 %all-gather.1 = bf16[1,1,256,128]{3,2,1,0:T(8,128)(2,1)S(1)} all-gather(bf16[1,1,128,128]{3,2,1,0:T(8,128)(2,1)S(1)} %get-tuple-element.1487), channel_id=3, replica_groups=mesh['pipe'=4,'ctx'=2,'tp'=4] {'ctx'}, dimensions={2}, use_global_device_ids=true | all-gather | bytes 98304 | tf_op jit(solution)/shard_map/all_gather | solution.py:144
  39.9 1.1 conditional.4
  41.0 23.6 %while.50 = (s32[]{:T(128)}, bf16[128,128]{1,0:T(8,128)(2,1)S(1)}, bf16[128,128]{1,0:T(8,128)(2,1)S(1)}, f32[128,128]{1,0:T(8,128)S(1)}, f32[128,128]{1,0:T(8,12...) while((s32[]{:T(128)}, bf16[128,128]{1,0:T(8,128)(2,1)S(1)}, ...), condition=%wide.region_17.18_spmd.clone, body=%wide.region_12.17_spmd.clone.sunk | while | flops 169071120 | bytes 6050592 | solution.py:175
  41.1 0.7 fusion.131
  44.4 1.4 conditional.10
  45.8 1.6 collective-permute-start.2
  47.9 1.5 collective-permute-start
  50.1 1.5 collective-permute-done.3
  52.0 1.3 collective-permute-done.1
  53.4 0.7 fusion.131
  56.7 1.4 conditional.10
  58.7 1.5 collective-permute-start.3
  60.7 1.5 collective-permute-start.1
  62.5 0.7 collective-permute-done.3
  63.2 1.0 collective-permute-done
  64.9 0.8 convert_element_type.172
  65.7 5.1 %all-to-all-start.2 = ((bf16[4,32,1024]{2,1,0:T(8,128)(2,1)}), bf16[4,32,1024]{2,1,0:T(8,128)(2,1)S(1)}, u32[]{:S(2)}, u32[]{:S(2)}) async-start(bf16[4,32,1024]{2,1,0:T(8,128)(2,1)} %convert_element_type.172), calls=%async_computation.2 | async-start | bytes 524288 | tf_op jit(solution)/shard_map/all_to_all | solution.py:180
  71.1 6.4 %all-to-all-done.2 = bf16[4,32,1024]{2,1,0:T(8,128)(2,1)S(1)} async-done(((bf16[4,32,1024]{2,1,0:T(8,128)(2,1)}), bf16[4,32,1024]{2,1,0:T(8,128)(2,1)S(1)}, u32[]{:S(2)}, u32[]{:S(2)}) %all-to-all-start.2) | async-done | bytes 262176 | tf_op jit(solution)/shard_map/all_to_all | solution.py:180
  78.3 1.5 multiply_reduce_fusion
  80.6 1.3 collective-permute-start.8
  81.9 3.6 %all-to-all-start.3 = ((bf16[32,4,1024]{2,0,1:T(8,128)(2,1)}), bf16[32,4,1024]{2,0,1:T(8,128)(2,1)S(1)}, u32[]{:S(2)}, u32[]{:S(2)}) async-start(bf16[32,4,1024]{2,0,1:T(8,128)(2,1)} %get-tuple-element.1492), calls=%async_computation.3 | async-start | bytes 524288 | tf_op jit(solution)/shard_map/all_to_all | solution.py:125
  85.5 0.7 copy.145
  86.2 9.4 %all-to-all-done.3 = bf16[32,4,1024]{2,0,1:T(8,128)(2,1)S(1)} async-done(((bf16[32,4,1024]{2,0,1:T(8,128)(2,1)}), bf16[32,4,1024]{2,0,1:T(8,128)(2,1)S(1)}, u32[]{:S(2)}, u32[]{:S(2)}) %all-to-all-start.3) | async-done | bytes 262176 | tf_op jit(solution)/shard_map/all_to_all | solution.py:125
  95.7 3.4 %all-to-all-start.4 = ((bf16[32,4,1024]{2,0,1:T(8,128)(2,1)}), bf16[32,4,1024]{2,0,1:T(8,128)(2,1)S(1)}, u32[]{:S(2)}, u32[]{:S(2)}) async-start(bf16[32,4,1024]{2,0,1:T(8,128)(2,1)} %bitcast.378), calls=%async_computation.4 | async-start | bytes 524288 | tf_op jit(solution)/shard_map/all_to_all | solution.py:126
  99.1 0.7 copy-done.9
  101.7 4.6 %all-gather.2 = bf16[1,1,256,128]{3,2,1,0:T(8,128)(2,1)S(1)} all-gather(bf16[1,1,128,128]{3,2,1,0:T(8,128)(2,1)S(1)} %get-tuple-element.1497), channel_id=4, replica_groups=mesh['pipe'=4,'ctx'=2,'tp'=4] {'ctx'}, dimensions={2}, use_global_device_ids=true | all-gather | bytes 98304 | tf_op jit(solution)/shard_map/all_gather | solution.py:143
  106.2 4.7 %all-gather.3 = bf16[1,1,256,128]{3,2,1,0:T(8,128)(2,1)} all-gather(bf16[1,1,128,128]{3,2,1,0:T(8,128)(2,1)S(1)} %get-tuple-element.1484), channel_id=5, replica_groups=mesh['pipe'=4,'ctx'=2,'tp'=4] {'ctx'}, dimensions={2}, use_global_device_ids=true | all-gather | bytes 98304 | tf_op jit(solution)/shard_map/all_gather | solution.py:144
  111.3 1.2 reshape.1040
  112.7 0.8 copy-done.6
  113.4 1.0 conditional.5
  114.6 26.2 %while.51 = (s32[]{:T(128)}, bf16[128,128]{1,0:T(8,128)(2,1)S(1)}, bf16[128,128]{1,0:T(8,128)(2,1)S(1)}, f32[128,128]{1,0:T(8,128)S(1)}, f32[128,128]{1,0:T(8,12...) while((s32[]{:T(128)}, bf16[128,128]{1,0:T(8,128)(2,1)S(1)}, ...), condition=%wide.region_33.34_spmd.clone, body=%wide.region_28.33_spmd.clone.sunk | while | flops 169071120 | bytes 6054752 | solution.py:175
  114.7 0.7 fusion.132
  117.9 2.1 %conditional.11 = ((f32[128,128]{1,0:T(8,128)S(1)}, f32[128,128]{1,0:T(8,128)S(1)}, f32[128,1,8,128]{3,0,2,1:T(8,128)S(1)})) conditional(s32[]{:T(128)} %convert_element_type.279, (f32[128,128]{1,0:T(8,128)S(1)}, f32[128,128]{1,0:T(8,128)S(1)}, f32[128,1,8,128]{3,0,2,1:T(8,128)S(1)}) %tuple.213, (s32[]{:T(128)}, s32[128]{0:T(128)S(1)}, ...), branch_computations={%region_31.31_spmd, %region_32.32_spmd.clone} | conditional | flops 169057408 | bytes 4868416 | solution.py:164
  118.0 0.7 copy-done.11
  120.0 1.6 collective-permute-start.6
  122.1 1.5 collective-permute-start.4
  124.5 1.3 collective-permute-done.7
  126.2 1.3 collective-permute-done.5
  127.5 0.7 copy-done.10
  128.3 0.7 fusion.132
  131.5 2.1 %conditional.11 = ((f32[128,128]{1,0:T(8,128)S(1)}, f32[128,128]{1,0:T(8,128)S(1)}, f32[128,1,8,128]{3,0,2,1:T(8,128)S(1)})) conditional(s32[]{:T(128)} %convert_element_type.279, (f32[128,128]{1,0:T(8,128)S(1)}, f32[128,128]{1,0:T(8,128)S(1)}, f32[128,1,8,128]{3,0,2,1:T(8,128)S(1)}) %tuple.213, (s32[]{:T(128)}, s32[128]{0:T(128)S(1)}, ...), branch_computations={%region_31.31_spmd, %region_32.32_spmd.clone} | conditional | flops 169057408 | bytes 4868416 | solution.py:164
  131.6 0.7 copy-done.11
  134.2 1.5 collective-permute-start.7
  136.2 1.5 collective-permute-start.5
  137.9 0.7 collective-permute-done.7
  138.6 1.0 collective-permute-done.4
  140.1 0.7 copy-done.10
  141.0 0.8 convert_element_type.193
  141.8 5.2 %all-to-all-start.5 = ((bf16[4,32,1024]{2,1,0:T(8,128)(2,1)}), bf16[4,32,1024]{2,1,0:T(8,128)(2,1)S(1)}, u32[]{:S(2)}, u32[]{:S(2)}) async-start(bf16[4,32,1024]{2,1,0:T(8,128)(2,1)} %convert_element_type.193), calls=%async_computation.5 | async-start | bytes 524288 | tf_op jit(solution)/shard_map/all_to_all | solution.py:180
  148.5 5.3 %all-to-all-done.5 = bf16[4,32,1024]{2,1,0:T(8,128)(2,1)S(1)} async-done(((bf16[4,32,1024]{2,1,0:T(8,128)(2,1)}), bf16[4,32,1024]{2,1,0:T(8,128)(2,1)S(1)}, u32[]{:S(2)}, u32[]{:S(2)}) %all-to-all-start.5) | async-done | bytes 262176 | tf_op jit(solution)/shard_map/all_to_all | solution.py:180
  154.3 36.7 %psum.7 = f32[1,4096]{1,0:T(1,128)} all-reduce(f32[1,4096]{1,0:T(1,128)S(1)} %bitcast.409), channel_id=1, replica_groups=mesh['pipe'=4,'ctx'=2,'tp'=4] {'ctx','tp'}, use_global_device_ids=true, to_apply=%region_37.38 | all-reduce | flops 4096 | bytes 32768 | tf_op jit(solution)/shard_map/psum | solution.py:218
  191.4 0.8 maximum_bitcast_fusion
  (196 shorter events, 24.1 us)
Async XLA Ops:
  0.6 1.3 copy-start
  2.8 1.6 copy-start.12
  2.8 0.9 copy-start.4
  5.4 6.5 %copy-start.1 = (bf16[1,32,4096]{2,1,0:T(8,128)(2,1)S(1)}, bf16[1,32,4096]{2,1,0:T(8,128)(2,1)}, u32[]{:S(2)}) copy-start(bf16[1,32,4096]{2,1,0:T(8,128)(2,1)} %param.23) | copy-start | bytes 786436
  5.4 15.4 %all-to-all-start = ((bf16[32,4,1024]{2,0,1:T(8,128)(2,1)}), bf16[32,4,1024]{2,0,1:T(8,128)(2,1)S(1)}, u32[]{:S(2)}, u32[]{:S(2)}) async-start(bf16[32,4,1024]{2,0,1:T(8,128)(2,1)} %multiply_convert_fusion.1), calls=%async_computation | async-start | bytes 524288 | tf_op jit(solution)/shard_map/all_to_all | solution.py:125
  20.8 9.6 %copy-start.7 = (bf16[1,2,128,128]{3,2,1,0:T(8,128)(2,1)S(1)}, bf16[1,2,128,128]{3,2,1,0:T(8,128)(2,1)}, u32[]{:S(2)}) copy-start(bf16[1,2,128,128]{3,2,1,0:T(8,128)(2,1)} %param.21) | copy-start | bytes 196612
  20.8 9.6 %copy-start.8 = (bf16[1,2,128,128]{3,2,1,0:T(8,128)(2,1)S(1)}, bf16[1,2,128,128]{3,2,1,0:T(8,128)(2,1)}, u32[]{:S(2)}) copy-start(bf16[1,2,128,128]{3,2,1,0:T(8,128)(2,1)} %param.20) | copy-start | bytes 196612
  20.8 18.9 %all-to-all-start.1 = ((bf16[32,4,1024]{2,0,1:T(8,128)(2,1)}), bf16[32,4,1024]{2,0,1:T(8,128)(2,1)S(1)}, u32[]{:S(2)}, u32[]{:S(2)}) async-start(bf16[32,4,1024]{2,0,1:T(8,128)(2,1)} %copy.84), calls=%async_computation.1 | async-start | bytes 524288 | tf_op jit(solution)/shard_map/all_to_all | solution.py:126
  24.4 15.5 %copy-start.17 = (s32[128]{0:T(128)}, s32[128]{0:T(128)S(1)}, u32[]{:S(2)}) copy-start(s32[128]{0:T(128)S(1)} %fusion.115) | copy-start | bytes 1540
  45.8 4.3 %collective-permute-start.2 = (f32[128,128]{1,0:T(8,128)S(1)}, f32[128,128]{1,0:T(8,128)S(1)}, u32[]{:S(2)}, u32[]{:S(2)}) collective-permute-start(f32[128,128]{1,0:T(8,128)S(1)} %get-tuple-element.1692), channel_id=1, source_target_pairs={{0,4},{4,0},{1,5},{5,1},{2,6},{6,2},{3,7},{7,3},{8,12},{12,8},{9,1... | collective-permute-start | bytes 196616 | tf_op jit(solution)/shard_map/while/body/eval_jaxpr/ppermute | solution.py:17
  47.4 4.3 %collective-permute-start.3 = (f32[128,128]{1,0:T(8,128)S(1)}, f32[128,128]{1,0:T(8,128)S(1)}, u32[]{:S(2)}, u32[]{:S(2)}) collective-permute-start(f32[128,128]{1,0:T(8,128)S(1)} %get-tuple-element.1693), channel_id=1, source_target_pairs={{0,4},{4,0},{1,5},{5,1},{2,6},{6,2},{3,7},{7,3},{8,12},{12,8},{9,1... | collective-permute-start | bytes 196616 | tf_op jit(solution)/shard_map/while/body/eval_jaxpr/ppermute | solution.py:17
  47.9 4.1 %collective-permute-start = (bf16[128,128]{1,0:T(8,128)(2,1)S(1)}, bf16[128,128]{1,0:T(8,128)(2,1)S(1)}, u32[]{:S(2)}, u32[]{:S(2)}) collective-permute-start(bf16[128,128]{1,0:T(8,128)(2,1)S(1)} %copy.171), channel_id=1, source_target_pairs={{0,4},{4,0},{1,5},{5,1},{2,6},{6,2},{3,7},{7,3},{8,12},{12,8},{9,1... | collective-permute-start | bytes 98312 | tf_op jit(solution)/shard_map/while/body/eval_jaxpr/ppermute | solution.py:17
  49.4 3.9 %collective-permute-start.1 = (bf16[128,128]{1,0:T(8,128)(2,1)S(1)}, bf16[128,128]{1,0:T(8,128)(2,1)S(1)}, u32[]{:S(2)}, u32[]{:S(2)}) collective-permute-start(bf16[128,128]{1,0:T(8,128)(2,1)S(1)} %copy.172), channel_id=1, source_target_pairs={{0,4},{4,0},{1,5},{5,1},{2,6},{6,2},{3,7},{7,3},{8,12},{12,8},{9,1... | collective-permute-start | bytes 98312 | tf_op jit(solution)/shard_map/while/body/eval_jaxpr/ppermute | solution.py:17
  58.1 4.3 %collective-permute-start.2 = (f32[128,128]{1,0:T(8,128)S(1)}, f32[128,128]{1,0:T(8,128)S(1)}, u32[]{:S(2)}, u32[]{:S(2)}) collective-permute-start(f32[128,128]{1,0:T(8,128)S(1)} %get-tuple-element.1692), channel_id=1, source_target_pairs={{0,4},{4,0},{1,5},{5,1},{2,6},{6,2},{3,7},{7,3},{8,12},{12,8},{9,1... | collective-permute-start | bytes 196616 | tf_op jit(solution)/shard_map/while/body/eval_jaxpr/ppermute | solution.py:17
  58.7 4.5 %collective-permute-start.3 = (f32[128,128]{1,0:T(8,128)S(1)}, f32[128,128]{1,0:T(8,128)S(1)}, u32[]{:S(2)}, u32[]{:S(2)}) collective-permute-start(f32[128,128]{1,0:T(8,128)S(1)} %get-tuple-element.1693), channel_id=1, source_target_pairs={{0,4},{4,0},{1,5},{5,1},{2,6},{6,2},{3,7},{7,3},{8,12},{12,8},{9,1... | collective-permute-start | bytes 196616 | tf_op jit(solution)/shard_map/while/body/eval_jaxpr/ppermute | solution.py:17
  60.2 3.9 %collective-permute-start = (bf16[128,128]{1,0:T(8,128)(2,1)S(1)}, bf16[128,128]{1,0:T(8,128)(2,1)S(1)}, u32[]{:S(2)}, u32[]{:S(2)}) collective-permute-start(bf16[128,128]{1,0:T(8,128)(2,1)S(1)} %copy.171), channel_id=1, source_target_pairs={{0,4},{4,0},{1,5},{5,1},{2,6},{6,2},{3,7},{7,3},{8,12},{12,8},{9,1... | collective-permute-start | bytes 98312 | tf_op jit(solution)/shard_map/while/body/eval_jaxpr/ppermute | solution.py:17
  60.7 3.9 %collective-permute-start.1 = (bf16[128,128]{1,0:T(8,128)(2,1)S(1)}, bf16[128,128]{1,0:T(8,128)(2,1)S(1)}, u32[]{:S(2)}, u32[]{:S(2)}) collective-permute-start(bf16[128,128]{1,0:T(8,128)(2,1)S(1)} %copy.172), channel_id=1, source_target_pairs={{0,4},{4,0},{1,5},{5,1},{2,6},{6,2},{3,7},{7,3},{8,12},{12,8},{9,1... | collective-permute-start | bytes 98312 | tf_op jit(solution)/shard_map/while/body/eval_jaxpr/ppermute | solution.py:17
  64.9 5.9 %copy-start.2 = (f32[1,1,32,4096]{3,2,1,0:T(8,128)S(1)}, f32[1,1,32,4096]{3,2,1,0:T(8,128)}, u32[]{:S(2)}) copy-start(f32[1,1,32,4096]{3,2,1,0:T(8,128)} %get-tuple-element.1481) | copy-start | bytes 1572868
  65.7 11.8 %all-to-all-start.2 = ((bf16[4,32,1024]{2,1,0:T(8,128)(2,1)}), bf16[4,32,1024]{2,1,0:T(8,128)(2,1)S(1)}, u32[]{:S(2)}, u32[]{:S(2)}) async-start(bf16[4,32,1024]{2,1,0:T(8,128)(2,1)} %convert_element_type.172), calls=%async_computation.2 | async-start | bytes 524288 | tf_op jit(solution)/shard_map/all_to_all | solution.py:180
  71.1 6.5 %copy-start.15 = (f32[32]{0:T(128)}, f32[32]{0:T(128)S(1)}, u32[]{:S(2)}) copy-start(f32[32]{0:T(128)S(1)} %add_rsqrt_fusion) | copy-start | bytes 388
  77.6 0.7 copy-start.13
  79.8 0.6 copy-start.19
  80.6 4.9 %collective-permute-start.8 = (bf16[32,4096]{1,0:T(8,128)(2,1)S(1)}, bf16[32,4096]{1,0:T(8,128)(2,1)S(1)}, u32[]{:S(2)}, u32[]{:S(2)}) collective-permute-start(bf16[32,4096]{1,0:T(8,128)(2,1)S(1)} %fusion.94), channel_id=1, source_target_pairs={{8,0},{16,8},{24,16},{9,1},{17,9},{25,17},{10,2},{18,10},{26,18},{... | collective-permute-start | bytes 786440 | tf_op jit(solution)/shard_map/ppermute | solution.py:23
  81.9 3.6 %copy-start.5 = (bf16[1,32,4096]{2,1,0:T(8,128)(2,1)S(1)}, bf16[1,32,4096]{2,1,0:T(8,128)(2,1)}, u32[]{:S(2)}) copy-start(bf16[1,32,4096]{2,1,0:T(8,128)(2,1)} %param.24) | copy-start | bytes 786436
  81.9 13.8 %all-to-all-start.3 = ((bf16[32,4,1024]{2,0,1:T(8,128)(2,1)}), bf16[32,4,1024]{2,0,1:T(8,128)(2,1)S(1)}, u32[]{:S(2)}, u32[]{:S(2)}) async-start(bf16[32,4,1024]{2,0,1:T(8,128)(2,1)} %get-tuple-element.1492), calls=%async_computation.3 | async-start | bytes 524288 | tf_op jit(solution)/shard_map/all_to_all | solution.py:125
  95.7 16.9 %all-to-all-start.4 = ((bf16[32,4,1024]{2,0,1:T(8,128)(2,1)}), bf16[32,4,1024]{2,0,1:T(8,128)(2,1)S(1)}, u32[]{:S(2)}, u32[]{:S(2)}) async-start(bf16[32,4,1024]{2,0,1:T(8,128)(2,1)} %bitcast.378), calls=%async_computation.4 | async-start | bytes 524288 | tf_op jit(solution)/shard_map/all_to_all | solution.py:126
  99.1 0.7 copy-start.9
  112.6 0.8 copy-start.6
  112.6 0.8 copy-start.18
  118.0 0.7 copy-start.11
  120.0 4.5 %collective-permute-start.6 = (f32[128,128]{1,0:T(8,128)S(1)}, f32[128,128]{1,0:T(8,128)S(1)}, u32[]{:S(2)}, u32[]{:S(2)}) collective-permute-start(f32[128,128]{1,0:T(8,128)S(1)} %get-tuple-element.1716), channel_id=1, source_target_pairs={{0,4},{4,0},{1,5},{5,1},{2,6},{6,2},{3,7},{7,3},{8,12},{12,8},{9,1... | collective-permute-start | bytes 196616 | tf_op jit(solution)/shard_map/while/body/eval_jaxpr/ppermute | solution.py:17
  121.6 4.3 %collective-permute-start.7 = (f32[128,128]{1,0:T(8,128)S(1)}, f32[128,128]{1,0:T(8,128)S(1)}, u32[]{:S(2)}, u32[]{:S(2)}) collective-permute-start(f32[128,128]{1,0:T(8,128)S(1)} %get-tuple-element.1717), channel_id=1, source_target_pairs={{0,4},{4,0},{1,5},{5,1},{2,6},{6,2},{3,7},{7,3},{8,12},{12,8},{9,1... | collective-permute-start | bytes 196616 | tf_op jit(solution)/shard_map/while/body/eval_jaxpr/ppermute | solution.py:17
  122.1 4.1 %collective-permute-start.4 = (bf16[128,128]{1,0:T(8,128)(2,1)S(1)}, bf16[128,128]{1,0:T(8,128)(2,1)S(1)}, u32[]{:S(2)}, u32[]{:S(2)}) collective-permute-start(bf16[128,128]{1,0:T(8,128)(2,1)S(1)} %copy.195), channel_id=1, source_target_pairs={{0,4},{4,0},{1,5},{5,1},{2,6},{6,2},{3,7},{7,3},{8,12},{12,8},{9,1... | collective-permute-start | bytes 98312 | tf_op jit(solution)/shard_map/while/body/eval_jaxpr/ppermute | solution.py:17
  123.6 3.9 %collective-permute-start.5 = (bf16[128,128]{1,0:T(8,128)(2,1)S(1)}, bf16[128,128]{1,0:T(8,128)(2,1)S(1)}, u32[]{:S(2)}, u32[]{:S(2)}) collective-permute-start(bf16[128,128]{1,0:T(8,128)(2,1)S(1)} %copy.196), channel_id=1, source_target_pairs={{0,4},{4,0},{1,5},{5,1},{2,6},{6,2},{3,7},{7,3},{8,12},{12,8},{9,1... | collective-permute-start | bytes 98312 | tf_op jit(solution)/shard_map/while/body/eval_jaxpr/ppermute | solution.py:17
  127.5 0.7 copy-start.10
  131.6 0.7 copy-start.11
  133.6 4.3 %collective-permute-start.6 = (f32[128,128]{1,0:T(8,128)S(1)}, f32[128,128]{1,0:T(8,128)S(1)}, u32[]{:S(2)}, u32[]{:S(2)}) collective-permute-start(f32[128,128]{1,0:T(8,128)S(1)} %get-tuple-element.1716), channel_id=1, source_target_pairs={{0,4},{4,0},{1,5},{5,1},{2,6},{6,2},{3,7},{7,3},{8,12},{12,8},{9,1... | collective-permute-start | bytes 196616 | tf_op jit(solution)/shard_map/while/body/eval_jaxpr/ppermute | solution.py:17
  134.2 4.5 %collective-permute-start.7 = (f32[128,128]{1,0:T(8,128)S(1)}, f32[128,128]{1,0:T(8,128)S(1)}, u32[]{:S(2)}, u32[]{:S(2)}) collective-permute-start(f32[128,128]{1,0:T(8,128)S(1)} %get-tuple-element.1717), channel_id=1, source_target_pairs={{0,4},{4,0},{1,5},{5,1},{2,6},{6,2},{3,7},{7,3},{8,12},{12,8},{9,1... | collective-permute-start | bytes 196616 | tf_op jit(solution)/shard_map/while/body/eval_jaxpr/ppermute | solution.py:17
  135.7 3.9 %collective-permute-start.4 = (bf16[128,128]{1,0:T(8,128)(2,1)S(1)}, bf16[128,128]{1,0:T(8,128)(2,1)S(1)}, u32[]{:S(2)}, u32[]{:S(2)}) collective-permute-start(bf16[128,128]{1,0:T(8,128)(2,1)S(1)} %copy.195), channel_id=1, source_target_pairs={{0,4},{4,0},{1,5},{5,1},{2,6},{6,2},{3,7},{7,3},{8,12},{12,8},{9,1... | collective-permute-start | bytes 98312 | tf_op jit(solution)/shard_map/while/body/eval_jaxpr/ppermute | solution.py:17
  136.2 3.9 %collective-permute-start.5 = (bf16[128,128]{1,0:T(8,128)(2,1)S(1)}, bf16[128,128]{1,0:T(8,128)(2,1)S(1)}, u32[]{:S(2)}, u32[]{:S(2)}) collective-permute-start(bf16[128,128]{1,0:T(8,128)(2,1)S(1)} %copy.196), channel_id=1, source_target_pairs={{0,4},{4,0},{1,5},{5,1},{2,6},{6,2},{3,7},{7,3},{8,12},{12,8},{9,1... | collective-permute-start | bytes 98312 | tf_op jit(solution)/shard_map/while/body/eval_jaxpr/ppermute | solution.py:17
  140.1 0.7 copy-start.10
  141.0 6.0 %copy-start.3 = (f32[1,32,4096]{2,1,0:T(8,128)S(1)}, f32[1,32,4096]{2,1,0:T(8,128)}, u32[]{:S(2)}) copy-start(f32[1,32,4096]{2,1,0:T(8,128)} %reshape.1040) | copy-start | bytes 1572868
  141.8 5.2 %copy-start.14 = (f32[32]{0:T(128)S(1)}, f32[32]{0:T(128)}, u32[]{:S(2)}) copy-start(f32[32]{0:T(128)} %copy-done.12) | copy-start | bytes 388
  141.8 5.2 %copy-start.20 = (f32[32]{0:T(128)S(1)}, f32[32]{0:T(128)}, u32[]{:S(2)}) copy-start(f32[32]{0:T(128)} %copy-done.19) | copy-start | bytes 388
  141.8 12.0 %all-to-all-start.5 = ((bf16[4,32,1024]{2,1,0:T(8,128)(2,1)}), bf16[4,32,1024]{2,1,0:T(8,128)(2,1)S(1)}, u32[]{:S(2)}, u32[]{:S(2)}) async-start(bf16[4,32,1024]{2,1,0:T(8,128)(2,1)} %convert_element_type.193), calls=%async_computation.5 | async-start | bytes 524288 | tf_op jit(solution)/shard_map/all_to_all | solution.py:180
  147.9 5.9 %copy-start.16 = (f32[32]{0:T(128)S(1)}, f32[32]{0:T(128)}, u32[]{:S(2)}) copy-start(f32[32]{0:T(128)} %copy-done.15) | copy-start | bytes 388
where the time goes:
time: 193 us; the launch traced here: 192 us
  blocking collectives  55.2 us (29%)
  starting transfers between devices  45 us (23%)
  waiting for transfers between devices  39.8 us (21%)
  other arithmetic  17.4 us (9%)
  local copies, waits for them, and re-layouts  13.2 us (7%)
  loops' own time  10.7 us (6%)
  matrix products  6.2 us (3%)
  between operations  4.75 us (2%)
    psum x1, blocking collectives, on_device(): gain_grads = lax.psum(gain_running, ('ctx', 'tp'))  36.7 us
    all_to_all x2, waiting for transfers between devices, segment_tick(): lax.all_to_all(queries, 'tp', split_axis=1, concat_axis=0, tiled=True)  16.6 us
    ppermute x16, starting transfers between devices, passed_along(): lax.ppermute(value, axis, [(i, (i + by) % count) for i in range(count)])  16.5 us
    all_to_all x2, waiting for transfers between devices, segment_tick(): lax.all_to_all(query_low, 'tp', split_axis=0, concat_axis=1, tiled=True)  11.7 us
    ppermute x16, waiting for transfers between devices, passed_along(): lax.ppermute(value, axis, [(i, (i + by) % count) for i in range(count)])  11.6 us
    another operation x2, loops' own time, segment_tick(): lax.fori_loop(0, cycle_count, cycle_turn, (key_local, value_local, zero_k...  10.3 us
    all_to_all x2, starting transfers between devices, segment_tick(): lax.all_to_all(query_low, 'tp', split_axis=0, concat_axis=1, tiled=True)  10.2 us
    all_to_all x2, starting transfers between devices, segment_tick(): lax.all_to_all(queries, 'tp', split_axis=1, concat_axis=0, tiled=True)  10 us
  transfers between devices with their start and end apart: 23, of which 20 were waited for; matrix products, arithmetic and copies ran while one was open for 5% of the time, Pallas kernels for 0%

commit v1 on v0

v1 whole, which is shorter than its diff:
```python
import functools

import jax
import jax.numpy as jnp
from jax import lax
from jax.experimental import pallas as pl
from jax.experimental.pallas import tpu as pltpu
from jax.sharding import PartitionSpec as P

HD = 128
EPSILON = 1e-05
FILL = -1e30
SCALE = HD ** (-0.5)
F32 = jnp.float32
BF16 = jnp.bfloat16

NT = (((1,), (1,)), ((), ()))
NN = (((1,), (0,)), ((), ()))
TN = (((0,), (0,)), ((), ()))


def dot(a, b, dims):
    return lax.dot_general(a, b, dims, preferred_element_type=F32)


def split_two(value):
    high = value.astype(BF16)
    low = (value - high.astype(F32)).astype(BF16)
    return high, low


def joined(high, low):
    return high.astype(F32) + low.astype(F32)


def in_order(values, owners):
    total = None
    for owner in range(len(values)):
        term = jnp.where(owners[0] == owner, values[0], 0.0)
        for value, whose in zip(values[1:], owners[1:]):
            term = jnp.where(whose == owner, value, term)
        total = term if total is None else total + term
    return total


def pack_kernel(tp_count, half, keys_ref, values_ref, own_ref, other_ref):
    parity = lax.axis_index("tp") // (tp_count // 2)
    for tick in range(keys_ref.shape[1]):
        for kind, ref in enumerate((keys_ref, values_ref)):
            own_ref[tick, kind] = ref[0, tick, pl.ds(parity * half, half), :]
            other_ref[tick, kind] = ref[0, tick, pl.ds((1 - parity) * half, half), :]


def attention_kernel(sizes, tick, n_arrive, *refs):
    rows, half, cycle, tp_count, group, columns = sizes
    refs = list(refs)
    doc_ref, x_ref, gain_ref = refs[:3]
    arrive_refs = refs[3 : 3 + n_arrive]
    kv_refs = refs[3 + n_arrive : 3 + n_arrive + cycle]
    rest = refs[3 + n_arrive + cycle :]
    if tick:
        before_gain_ref, before_ref = rest[:2]
        rest = rest[2:]
    input_grad_ref = rest[0]
    gain_part_ref, own_ref = rest[1:3]
    send_refs = rest[3 : 3 + cycle - 1]
    query_grad_ref, gain_rows_ref = rest[3 + cycle - 1 :]

    pipe_place = lax.axis_index("pipe")
    cycle_place = lax.axis_index("ctx")
    tp_place = lax.axis_index("tp")
    parity = tp_place // (tp_count // 2)
    key_count = cycle * half
    stacked = group * rows
    width = group * HD

    def section_first(owner):
        return half * jnp.where(parity == 0, owner, 2 * cycle - 1 - owner)

    row_first = section_first(cycle_place) + (tp_place % (tp_count // 2)) * rows
    query_pos = row_first + (lax.broadcasted_iota(jnp.int32, (1, stacked), 1) & (rows - 1))
    key_place = lax.broadcasted_iota(jnp.int32, (key_count, 1), 0)
    key_pos = key_place + section_first(cycle_place)
    for turn in range(1, cycle):
        owner = (cycle_place - turn + cycle) % cycle
        key_pos = jnp.where(
            key_place >= turn * half, key_place - turn * half + section_first(owner), key_pos
        )
    micro = pipe_place + tick
    closing = jnp.int32(0)
    query_start = jnp.zeros((1, stacked), jnp.int32)
    for doc in range(doc_ref.shape[1]):
        length = doc_ref[micro, doc]
        closing = closing + length
        query_start = query_start + jnp.where(closing <= query_pos, length, 0)
    visible = (key_pos <= query_pos) & (key_pos >= query_start)

    squares = jnp.zeros((rows, HD), F32)
    for first in range(0, columns, HD):
        part = x_ref[0, tick, :, first : first + HD].astype(F32)
        squares = squares + part * part
    mean = jnp.sum(squares, axis=1, keepdims=True) * (1.0 / columns)
    inverse = lax.rsqrt(mean + EPSILON)

    def arriving(first, count):
        where = pl.ds(first, count)
        if n_arrive == 1:
            return arrive_refs[0][:, where]
        last = pipe_place == lax.axis_size("pipe") - 1
        return jnp.where(last, arrive_refs[1][:, where], arrive_refs[0][:, where])

    def one_group(turn, coupled):
        head_group = tp_place ^ turn
        first = pl.multiple_of(head_group * width, width)
        normed, gains, queries, grads = [], [], [], []
        for head in range(group):
            begin = first + head * HD
            normed.append(x_ref[0, tick, :, pl.ds(begin, HD)].astype(F32) * inverse)
            gains.append(gain_ref[:, pl.ds(begin, HD)])
            queries.append((normed[-1] * gains[-1]).astype(BF16))
            grads.append(arriving(begin, HD))
        query = jnp.concatenate(queries, axis=0)
        grad = jnp.concatenate(grads, axis=0)
        key = jnp.concatenate([ref[turn, 0] for ref in kv_refs], axis=0)
        value = jnp.concatenate([ref[turn, 1] for ref in kv_refs], axis=0)

        scores = jnp.where(visible, SCALE * dot(key, query, NT), FILL)
        weights = jnp.exp(scores - jnp.max(scores, axis=0, keepdims=True))
        probs = weights * (1.0 / jnp.sum(weights, axis=0, keepdims=True))
        prob_grad = dot(value, grad, NT)
        row_term = jnp.sum(probs * prob_grad, axis=0, keepdims=True)
        dscore = (probs * (prob_grad - row_term)).astype(BF16)
        probs_low = probs.astype(BF16)
        query_grad = (SCALE * dot(dscore, key, TN)).astype(BF16)
        key_grad = SCALE * dot(dscore, query, NN)
        value_grad = dot(probs_low, grad, NN)

        for kind, part in enumerate((key_grad, value_grad)):
            begin = pl.multiple_of((turn * 2 + kind) * half, half)
            own_ref[pl.ds(begin, half), :] = part[:half]
            for step, ref in enumerate(send_refs, 1):
                ref[pl.ds(begin, half), :] = part[step * half : (step + 1) * half].astype(BF16)

        gain_rows = []
        for head in range(group):
            low = query_grad[head * rows : (head + 1) * rows]
            query_grad_ref[:, pl.ds(first + head * HD, HD)] = low
            term = low.astype(F32) * normed[head]
            coupled = coupled + term * gains[head]
            gain_rows.append(jnp.sum(term, axis=0, keepdims=True))
        gain_rows_ref[pl.ds(pl.multiple_of(head_group * group, group), group), :] = (
            jnp.concatenate(gain_rows, axis=0)
        )
        return coupled

    coupled = jnp.zeros((rows, HD), F32)
    if key_count * stacked <= 65536:
        for turn in range(tp_count):
            coupled = one_group(turn, coupled)
    else:
        coupled = lax.fori_loop(0, tp_count, one_group, coupled)
    coupling = jnp.sum(coupled, axis=1, keepdims=True) * (1.0 / columns)

    for first in range(0, columns, HD):
        here = slice(first, first + HD)
        scaled = query_grad_ref[:, here].astype(F32) * gain_ref[:, here]
        normed_part = x_ref[0, tick, :, here].astype(F32) * inverse
        result = arriving(first, HD).astype(F32) + inverse * (scaled - normed_part * coupling)
        if tick:
            input_grad_ref[0, tick, :, here] = result.astype(BF16)
            input_grad_ref[0, 0, :, here] = before_ref[:, here]
        else:
            input_grad_ref[:, here] = result.astype(BF16)

    gain_rows = gain_rows_ref[...]
    if tick:
        gain_rows = gain_rows + before_gain_ref[...]
    gain_part_ref[...] = gain_rows
    if tick and send_refs:
        high, low = split_two(gain_rows)
        count = high.shape[0]
        begin = tp_count * 2 * half
        for ref in send_refs:
            ref[begin : begin + count, :] = high
            ref[begin + count : begin + 2 * count, :] = low


def cycle_sum_kernel(sizes, ticks, *refs):
    rows, half, cycle, tp_count, group, columns = sizes
    gain_ref = refs[0]
    per_tick = [refs[1 + tick * cycle : 1 + (tick + 1) * cycle] for tick in range(ticks)]
    keep_ref, gain_sum_ref = refs[1 + ticks * cycle :][:2]
    send_refs = refs[1 + ticks * cycle :][2:]
    block = 2 * half
    for tick in range(ticks):
        for turn in range(tp_count):
            here = slice(turn * block, (turn + 1) * block)
            total = per_tick[tick][0][here, :]
            for ref in per_tick[tick][1:]:
                total = total + ref[here, :].astype(F32)
            if turn == 0:
                keep_ref[tick * block : (tick + 1) * block, :] = total
            else:
                send_refs[turn - 1][tick * block : (tick + 1) * block, :] = total.astype(BF16)
    count = gain_ref.shape[0]
    begin = tp_count * block
    cycle_place = lax.axis_index("ctx")
    values = [joined(*split_two(gain_ref[...]))]
    owners = [cycle_place]
    for step, ref in enumerate(per_tick[ticks - 1][1:], 1):
        values.append(
            joined(ref[begin : begin + count, :], ref[begin + count : begin + 2 * count, :])
        )
        owners.append((cycle_place + step) % cycle)
    gain = in_order(values, owners)
    gain_sum_ref[...] = gain
    high, low = split_two(gain)
    for ref in send_refs:
        ref[ticks * block : ticks * block + count, :] = high
        ref[ticks * block + count : ticks * block + 2 * count, :] = low


def finish_kernel(sizes, ticks, *refs):
    rows, half, cycle, tp_count, group, columns = sizes
    keep_ref, gain_ref = refs[:2]
    receive_refs = refs[2 : 2 + tp_count - 1]
    key_ref, value_ref, gain_out_ref = refs[2 + tp_count - 1 :]
    block = 2 * half
    tp_place = lax.axis_index("tp")
    parity = tp_place // (tp_count // 2)
    for tick in range(ticks):
        for kind, out in enumerate((key_ref, value_ref)):
            begin = tick * block + kind * half
            own = keep_ref[begin : begin + half, :]
            other = None
            for turn in range(1, tp_count):
                part = receive_refs[turn - 1][begin : begin + half, :].astype(F32)
                if turn < tp_count // 2:
                    own = own + part
                else:
                    other = part if other is None else other + part
            out[0, tick, pl.ds(pl.multiple_of(parity * half, half), half), :] = own
            out[0, tick, pl.ds(pl.multiple_of((1 - parity) * half, half), half), :] = other
    count = gain_ref.shape[0]
    begin = ticks * block
    values = [joined(*split_two(gain_ref[...]))]
    owners = [tp_place]
    for turn, ref in enumerate(receive_refs, 1):
        values.append(
            joined(ref[begin : begin + count, :], ref[begin + count : begin + 2 * count, :])
        )
        owners.append(tp_place ^ turn)
    gain_out_ref[...] = in_order(values, owners)


def whole(ref_count):
    return [pl.BlockSpec(memory_space=pltpu.VMEM)] * ref_count


def shape(dims, dtype):
    return jax.ShapeDtypeStruct(dims, dtype)


def on_device(segment_inputs, keys, values, norm_gain, waiting_grads, output_grads, doc_lengths):
    cycle = lax.axis_size("ctx")
    tp_count = lax.axis_size("tp")
    pipe_count = lax.axis_size("pipe")
    _, ticks, rows, columns = segment_inputs.shape
    half = keys.shape[2] // 2
    group = columns // (tp_count * HD)
    gain_count = columns // HD
    sizes = (rows, half, cycle, tp_count, group, columns)
    block = 2 * half
    score_bytes = cycle * half * group * rows * 4
    params = pltpu.CompilerParams(vmem_limit_bytes=min(56 << 20, (12 << 20) + 14 * score_bytes))

    def to_partner(value, turn):
        return lax.ppermute(value, "tp", [(i, i ^ turn) for i in range(tp_count)])

    def to_block(value, step):
        return lax.ppermute(value, "ctx", [(i, (i + step) % cycle) for i in range(cycle)])

    packed = shape((ticks, 2, half, HD), BF16)
    own_kv, other_kv = pl.pallas_call(
        functools.partial(pack_kernel, tp_count, half),
        out_shape=(packed, packed),
        in_specs=whole(2),
        out_specs=whole(2),
        compiler_params=params,
        name="pack_kv",
    )(keys, values)

    def gathered(tick):
        parts = [own_kv[tick]]
        for turn in range(1, tp_count):
            parts.append(to_partner((own_kv if turn < tp_count // 2 else other_kv)[tick], turn))
        near = jnp.stack(parts)
        return [near] + [to_block(near, step) for step in range(1, cycle)]

    def attention(tick, arrive, kv, before):
        n_arrive = len(arrive)
        in_specs = [pl.BlockSpec(memory_space=pltpu.SMEM)]
        in_specs += whole(2 + n_arrive + cycle + len(before))
        extra = 2 * gain_count if tick else 0
        out_shape = [
            shape((1, ticks, rows, columns) if tick else (rows, columns), BF16),
            shape((gain_count, HD), F32),
            shape((tp_count * block, HD), F32),
        ]
        out_shape += [shape((tp_count * block + extra, HD), BF16)] * (cycle - 1)
        return pl.pallas_call(
            functools.partial(attention_kernel, sizes, tick, n_arrive),
            out_shape=out_shape,
            in_specs=in_specs,
            out_specs=whole(len(out_shape)),
            scratch_shapes=[
                pltpu.VMEM((rows, columns), BF16),
                pltpu.VMEM((gain_count, HD), F32),
            ],
            compiler_params=params,
            name=f"attention_{tick}",
        )(doc_lengths, segment_inputs, norm_gain, *arrive, *kv, *before)

    kv_first = gathered(0)
    kv_second = gathered(1)
    first = attention(0, [waiting_grads[0]], kv_first, [])
    input_grad_first, gain_first = first[:2]
    arrived = lax.ppermute(
        input_grad_first, "pipe", [(i, (i - 1) % pipe_count) for i in range(pipe_count)]
    )

    def turned(own, sends):
        return [own] + [to_block(value, -step) for step, value in enumerate(sends, 1)]

    sums_first = turned(first[2], first[3:])
    second = attention(
        1, [arrived, output_grads[0]], kv_second, [gain_first, input_grad_first]
    )
    input_grads, gain_rows = second[:2]
    sums_second = turned(second[2], second[3:])

    message = shape((ticks * block + 2 * gain_count, HD), BF16)
    keep, gain_sum, *sends = pl.pallas_call(
        functools.partial(cycle_sum_kernel, sizes, ticks),
        out_shape=[shape((ticks * block, HD), F32), shape((gain_count, HD), F32)]
        + [message] * (tp_count - 1),
        in_specs=whole(1 + ticks * cycle),
        out_specs=whole(2 + tp_count - 1),
        compiler_params=params,
        name="cycle_sum",
    )(gain_rows, *sums_first, *sums_second)
    received = [to_partner(value, turn) for turn, value in enumerate(sends, 1)]
    grads_shape = shape((1, ticks, block, HD), F32)
    key_grads, value_grads, gain_grads = pl.pallas_call(
        functools.partial(finish_kernel, sizes, ticks),
        out_shape=[grads_shape, grads_shape, shape((gain_count, HD), F32)],
        in_specs=whole(2 + tp_count - 1),
        out_specs=whole(3),
        compiler_params=params,
        name="finish",
    )(keep, gain_sum, *received)
    return input_grads, key_grads, value_grads, gain_grads.reshape(1, columns)


def solution(mesh):
    in_specs = (
        P("pipe", None, ("ctx", "tp"), None),
        P("pipe", None, "ctx", "tp"),
        P("pipe", None, "ctx", "tp"),
        P("pipe", None),
        P("pipe", ("ctx", "tp"), None),
        P(None, ("ctx", "tp"), None),
        P(),
    )
    out_specs = (
        P("pipe", None, ("ctx", "tp"), None),
        P("pipe", None, "ctx", "tp"),
        P("pipe", None, "ctx", "tp"),
        P("pipe", None),
    )
    return jax.shard_map(
        on_device, mesh=mesh, in_specs=in_specs, out_specs=out_specs, check_vma=False
    )
```

time: 193 us -> 50 us (0.26)
  blocking collectives: 55.2 us -> 0 us
  starting transfers between devices: 45 us -> 18.9 us
  waiting for transfers between devices: 39.8 us -> 21.3 us
  other arithmetic: 17.4 us -> 0.04 us
  loops' own time: 10.7 us -> 0 us
  local copies, waits for them, and re-layouts: 13.2 us -> 2.72 us
  matrix products: 6.2 us -> 0 us
  Pallas kernels: 0 us -> 6.17 us
  between operations: 4.75 us -> 0.76 us
    psum x1 -> x0, blocking collectives: 36.7 us -> none  [on_device(): gain_grads = lax.psum(gain_running, ('ctx', 'tp'))]
    all_to_all x6 -> x0, waiting for transfers between devices: 28.3 us -> none  [the longest x2 16.6 us: segment_tick(): lax.all_to_all(queries, 'tp', split_axis=1, concat_axis=0, tiled=True)]
    all_to_all x6 -> x0, starting transfers between devices: 27.2 us -> none  [the longest x2 10.2 us: segment_tick(): lax.all_to_all(query_low, 'tp', split_axis=0, concat_axis=1, tiled=True)]
    all_gather x4 -> x0, blocking collectives: 18.4 us -> none  [the longest x2 9.26 us: segment_tick(): lax.all_gather(value_local, 'ctx', axis=0, tiled=True)]
    another operation x8 -> x0, loops' own time: 10.7 us -> none  [the longest x2 10.3 us: segment_tick(): lax.fori_loop(0, cycle_count, cycle_turn, (key_local, value_local, zero_k...]
    ppermute x17 -> x14, waiting for transfers between devices: 11.6 us -> 21.3 us  [the longest x4 10.9 us: to_block(): lax.ppermute(value, 'ctx', [(i, (i + step) % cycle) for i in range(cycle)])]
    dot_general x24 -> x0, matrix products: 6.2 us -> none  [the longest x6 1.66 us: score_block(): jnp.einsum('rkgd,skd->kgrs', query_block, key_block, preferred_element_ty...]
    pallas_call x0 -> x5, Pallas kernels: none -> 6.17 us  [the longest x2 5.36 us: attention(): pl.pallas_call(functools.partial(attention_kernel, sizes, tick, n_arrive)...]
  transfers between devices with their start and end apart: 23 -> 14, of which waited for: 20 -> 6; matrix products, arithmetic and copies ran while one was open for 5% -> 0% of each run, Pallas kernels for 0% -> 5%
where the time goes in v1:
time: 50 us; the launch traced here: 49.8 us
  waiting for transfers between devices  21.3 us (43%)
  starting transfers between devices  18.9 us (38%)
  Pallas kernels  6.17 us (12%)
  local copies, waits for them, and re-layouts  2.72 us (5%)
  between operations  0.76 us (2%)
    ppermute x9, starting transfers between devices, to_partner(): return lax.ppermute(value, 'tp', [(i, i ^ turn) for i in range(tp_count)])  13.7 us
    ppermute x4, waiting for transfers between devices, to_block(): lax.ppermute(value, 'ctx', [(i, (i + step) % cycle) for i in range(cycle)])  10.9 us
    ppermute x9, waiting for transfers between devices, to_partner(): return lax.ppermute(value, 'tp', [(i, i ^ turn) for i in range(tp_count)])  10.4 us
    pallas_call x2, Pallas kernels, attention(): pl.pallas_call(functools.partial(attention_kernel, sizes, tick, n_arrive)...  5.36 us
    ppermute x4, starting transfers between devices, to_block(): lax.ppermute(value, 'ctx', [(i, (i + step) % cycle) for i in range(cycle)])  5.14 us
    unnamed x14, local copies, waits for them, and re-layouts  2.69 us
  transfers between devices with their start and end apart: 14, of which 6 were waited for; matrix products, arithmetic and copies ran while one was open for 0% of the time, Pallas kernels for 5%

profile of v1, /device:TPU:0, one launch (start us, length us, event | category | flops | bytes accessed | tf_op | source)
XLA Modules:
  0.0 49.8 jit_solution(12327228886924936758)
XLA Ops:
  0.6 0.0 copy-start
  0.6 0.0 copy-start.4
  0.7 0.9 %copy-done.4 = bf16[1,2,128,128]{3,2,1,0:T(8,128)(2,1)S(1)} copy-done((bf16[1,2,128,128]{3,2,1,0:T(8,128)(2,1)S(1)}, bf16[1,2,128,128]{3,2,1,0:T(8,128)(2,1)}, u32[]{:S(2)}) %copy-start.4) | copy-done | bytes 65560
  1.5 0.0 copy-start.5
  1.5 0.8 %copy-done.5 = bf16[1,2,128,128]{3,2,1,0:T(8,128)(2,1)S(1)} copy-done((bf16[1,2,128,128]{3,2,1,0:T(8,128)(2,1)S(1)}, bf16[1,2,128,128]{3,2,1,0:T(8,128)(2,1)}, u32[]{:S(2)}) %copy-start.5) | copy-done | bytes 65560
  2.4 3.1 %collective-permute-start = (bf16[2,64,128]{2,1,0:T(8,128)(2,1)S(1)}, bf16[2,64,128]{2,1,0:T(8,128)(2,1)S(1)}, u32[]{:S(2)}, u32[]{:S(2)}) collective-permute-start(bf16[2,64,128]{2,1,0:T(8,128)(2,1)S(1)} %get-tuple-element.41), channel_id=1, source_target_pairs={{0,1},{1,0},{2,3},{3,2},{4,5},{5,4},{6,7},{7,6},{8,9},{9,8},{10,11... | collective-permute-start | bytes 98312 | tf_op jit(solution)/shard_map/ppermute | solution.py:278
  5.5 2.5 %collective-permute-start.2 = (bf16[2,64,128]{2,1,0:T(8,128)(2,1)S(1)}, bf16[2,64,128]{2,1,0:T(8,128)(2,1)S(1)}, u32[]{:S(2)}, u32[]{:S(2)}) collective-permute-start(bf16[2,64,128]{2,1,0:T(8,128)(2,1)S(1)} %get-tuple-element.45), channel_id=1, source_target_pairs={{0,3},{1,2},{2,1},{3,0},{4,7},{5,6},{6,5},{7,4},{8,11},{9,10},{10,... | collective-permute-start | bytes 98312 | tf_op jit(solution)/shard_map/ppermute | solution.py:278
  8.0 0.2 collective-permute-start.1
  8.2 0.0 collective-permute-done
  8.2 3.5 %collective-permute-done.2 = bf16[2,64,128]{2,1,0:T(8,128)(2,1)S(1)} collective-permute-done((bf16[2,64,128]{2,1,0:T(8,128)(2,1)S(1)}, bf16[2,64,128]{2,1,0:T(8,128)(2,1)S(1)}, u32[]{:S(2)}, u32[]{:S(2)}) %collective-permute-start.2) | collective-permute-done | bytes 32800 | tf_op jit(solution)/shard_map/ppermute | solution.py:278
  11.7 1.5 %collective-permute-done.1 = bf16[2,64,128]{2,1,0:T(8,128)(2,1)S(1)} collective-permute-done((bf16[2,64,128]{2,1,0:T(8,128)(2,1)S(1)}, bf16[2,64,128]{2,1,0:T(8,128)(2,1)S(1)}, u32[]{:S(2)}, u32[]{:S(2)}) %collective-permute-start.1) | collective-permute-done | bytes 32800 | tf_op jit(solution)/shard_map/ppermute | solution.py:278
  13.2 0.0 copy-start.3
  13.2 0.0 copy-start.6
  13.2 1.6 %collective-permute-start.3 = (bf16[4,2,64,128]{3,2,1,0:T(8,128)(2,1)S(1)}, bf16[4,2,64,128]{3,2,1,0:T(8,128)(2,1)S(1)}, u32[]{:S(2)}, u32[]{:S(2)}) collective-permute-start(bf16[4,2,64,128]{3,2,1,0:T(8,128)(2,1)S(1)} %pad_maximum_fusion.refs_4_), channel_id=1, source_target_pairs={{0,4},{4,0},{1,5},{5,1},{2,6},{6,2},{3,7},{7,3},{8,12},{12,8},{9,1... | collective-permute-start | bytes 393224 | tf_op jit(solution)/shard_map/ppermute | solution.py:281
  14.8 0.4 collective-permute-start.5
  15.2 1.1 %collective-permute-start.7 = (bf16[2,64,128]{2,1,0:T(8,128)(2,1)S(1)}, bf16[2,64,128]{2,1,0:T(8,128)(2,1)S(1)}, u32[]{:S(2)}, u32[]{:S(2)}) collective-permute-start(bf16[2,64,128]{2,1,0:T(8,128)(2,1)S(1)} %get-tuple-element.44), channel_id=1, source_target_pairs={{0,3},{1,2},{2,1},{3,0},{4,7},{5,6},{6,5},{7,4},{8,11},{9,10},{10,... | collective-permute-start | bytes 98312 | tf_op jit(solution)/shard_map/ppermute | solution.py:278
  16.3 2.0 %collective-permute-start.6 = (bf16[2,64,128]{2,1,0:T(8,128)(2,1)S(1)}, bf16[2,64,128]{2,1,0:T(8,128)(2,1)S(1)}, u32[]{:S(2)}, u32[]{:S(2)}) collective-permute-start(bf16[2,64,128]{2,1,0:T(8,128)(2,1)S(1)} %get-tuple-element.44), channel_id=1, source_target_pairs={{0,2},{1,3},{2,0},{3,1},{4,6},{5,7},{6,4},{7,5},{8,10},{9,11},{10,... | collective-permute-start | bytes 98312 | tf_op jit(solution)/shard_map/ppermute | solution.py:278
  18.3 0.0 collective-permute-done.3.refs_5_
  18.3 0.0 copy-done
  18.3 0.0 copy-done.3
  18.3 0.0 copy-done.6
  18.3 0.0 copy-start.2
  18.3 0.9 %copy-done.2 = bf16[1,32,4096]{2,1,0:T(8,128)(2,1)S(1)} copy-done((bf16[1,32,4096]{2,1,0:T(8,128)(2,1)S(1)}, bf16[1,32,4096]{2,1,0:T(8,128)(2,1)}, u32[]{:S(2)}) %copy-start.2) | copy-done | bytes 262168
  19.2 2.3 %attention_0.1 = (bf16[32,4096]{1,0:T(8,128)(2,1)S(1)}, f32[32,128]{1,0:T(8,128)S(1)}, f32[512,128]{1,0:T(8,128)S(1)}, bf16[512,128]{1,0:T(8,128)(2,1)S(1)}) custom-call(s32[5,8]{1,0:T(8,128)S(1)} %copy-done.6, bf16[1,2,32,4096]{3,2,1,0:T(8,128)(2,1)S(1)} %copy-done, f32[1,4096]{1,0:T(1,128)S(1)} %copy-done.3, bf16[32,4096]{1,0:T(8,128)(2,1)S(1)} %bitcast.18, ...), custom_call_target="tpu_custom_call" | custom-call | tf_op jit(solution)/shard_map/attention_0/pallas_call | solution.py:311
  21.5 0.0 copy-start.1
  21.5 0.1 collective-permute-start.4
  21.6 0.0 collective-permute-done.5
  21.6 0.0 collective-permute-done.7
  21.6 0.0 collective-permute-done.6
  21.6 1.5 %collective-permute-start.8 = (bf16[4,2,64,128]{3,2,1,0:T(8,128)(2,1)S(1)}, bf16[4,2,64,128]{3,2,1,0:T(8,128)(2,1)S(1)}, u32[]{:S(2)}, u32[]{:S(2)}) collective-permute-start(bf16[4,2,64,128]{3,2,1,0:T(8,128)(2,1)S(1)} %pad_maximum_fusion.1.refs_5_), channel_id=1, source_target_pairs={{0,4},{4,0},{1,5},{5,1},{2,6},{6,2},{3,7},{7,3},{8,12},{12,8},{9,1... | collective-permute-start | bytes 393224 | tf_op jit(solution)/shard_map/ppermute | solution.py:281
  23.2 4.4 %collective-permute-done.8.refs_6_ = bf16[4,2,64,128]{3,2,1,0:T(8,128)(2,1)S(1)} collective-permute-done((bf16[4,2,64,128]{3,2,1,0:T(8,128)(2,1)S(1)}, bf16[4,2,64,128]{3,2,1,0:T(8,128)(2,1)S(1)}, u32[]{:S(2)}, u32[]{:S(2)}) %collective-permute-start.8) | collective-permute-done | bytes 131104 | tf_op jit(solution)/shard_map/ppermute | solution.py:281
  27.6 0.0 collective-permute-done.4.refs_3_
  27.6 0.0 copy-done.1
  27.6 3.1 %attention_1.1 = (bf16[1,2,32,4096]{3,2,1,0:T(8,128)(2,1)}, f32[32,128]{1,0:T(8,128)S(1)}, f32[512,128]{1,0:T(8,128)S(1)}, bf16[576,128]{1,0:T(8,128)(2,1)S(1)}) custom-call(s32[5,8]{1,0:T(8,128)S(1)} %copy-done.6, bf16[1,2,32,4096]{3,2,1,0:T(8,128)(2,1)S(1)} %copy-done, f32[1,4096]{1,0:T(1,128)S(1)} %copy-done.3, ...), custom_call_target="tpu_custom_call" | custom-call | tf_op jit(solution)/shard_map/attention_1/pallas_call | solution.py:311
  30.7 1.5 %collective-permute-start.10 = (bf16[576,128]{1,0:T(8,128)(2,1)S(1)}, bf16[576,128]{1,0:T(8,128)(2,1)S(1)}, u32[]{:S(2)}, u32[]{:S(2)}) collective-permute-start(bf16[576,128]{1,0:T(8,128)(2,1)S(1)} %get-tuple-element.31), channel_id=1, source_target_pairs={{0,4},{4,0},{1,5},{5,1},{2,6},{6,2},{3,7},{7,3},{8,12},{12,8},{9,1... | collective-permute-start | bytes 442376 | tf_op jit(solution)/shard_map/ppermute | solution.py:281
  32.2 0.6 %collective-permute-start.9 = (bf16[512,128]{1,0:T(8,128)(2,1)S(1)}, bf16[512,128]{1,0:T(8,128)(2,1)S(1)}, u32[]{:S(2)}, u32[]{:S(2)}) collective-permute-start(bf16[512,128]{1,0:T(8,128)(2,1)S(1)} %get-tuple-element.29), channel_id=1, source_target_pairs={{0,4},{4,0},{1,5},{5,1},{2,6},{6,2},{3,7},{7,3},{8,12},{12,8},{9,1... | collective-permute-start | bytes 393224 | tf_op jit(solution)/shard_map/ppermute | solution.py:281
  32.7 6.5 %collective-permute-done.9.refs_2_ = bf16[512,128]{1,0:T(8,128)(2,1)S(1)} collective-permute-done((bf16[512,128]{1,0:T(8,128)(2,1)S(1)}, bf16[512,128]{1,0:T(8,128)(2,1)S(1)}, u32[]{:S(2)}, u32[]{:S(2)}) %collective-permute-start.9) | collective-permute-done | bytes 131104 | tf_op jit(solution)/shard_map/ppermute | solution.py:281
  39.2 0.0 collective-permute-done.10.refs_4_
  39.2 0.1 cycle_sum.1
  39.3 1.4 %collective-permute-start.11 = (bf16[320,128]{1,0:T(8,128)(2,1)S(1)}, bf16[320,128]{1,0:T(8,128)(2,1)S(1)}, u32[]{:S(2)}, u32[]{:S(2)}) collective-permute-start(bf16[320,128]{1,0:T(8,128)(2,1)S(1)} %get-tuple-element.34), channel_id=1, source_target_pairs={{0,1},{1,0},{2,3},{3,2},{4,5},{5,4},{6,7},{7,6},{8,9},{9,8},{10,11... | collective-permute-start | bytes 245768 | tf_op jit(solution)/shard_map/ppermute | solution.py:278
  40.7 0.5 collective-permute-start.12
  41.2 2.6 %collective-permute-start.13 = (bf16[320,128]{1,0:T(8,128)(2,1)S(1)}, bf16[320,128]{1,0:T(8,128)(2,1)S(1)}, u32[]{:S(2)}, u32[]{:S(2)}) collective-permute-start(bf16[320,128]{1,0:T(8,128)(2,1)S(1)} %get-tuple-element.36), channel_id=1, source_target_pairs={{0,3},{1,2},{2,1},{3,0},{4,7},{5,6},{6,5},{7,4},{8,11},{9,10},{10,... | collective-permute-start | bytes 245768 | tf_op jit(solution)/shard_map/ppermute | solution.py:278
  43.7 0.8 %collective-permute-done.11.refs_2_ = bf16[320,128]{1,0:T(8,128)(2,1)S(1)} collective-permute-done((bf16[320,128]{1,0:T(8,128)(2,1)S(1)}, bf16[320,128]{1,0:T(8,128)(2,1)S(1)}, u32[]{:S(2)}, u32[]{:S(2)}) %collective-permute-start.11) | collective-permute-done | bytes 81952 | tf_op jit(solution)/shard_map/ppermute | solution.py:278
  44.6 4.5 %collective-permute-done.12.refs_3_ = bf16[320,128]{1,0:T(8,128)(2,1)S(1)} collective-permute-done((bf16[320,128]{1,0:T(8,128)(2,1)S(1)}, bf16[320,128]{1,0:T(8,128)(2,1)S(1)}, u32[]{:S(2)}, u32[]{:S(2)}) %collective-permute-start.12) | collective-permute-done | bytes 81952 | tf_op jit(solution)/shard_map/ppermute | solution.py:278
  49.1 0.0 collective-permute-done.13.refs_4_
  49.1 0.7 %finish.1 = (f32[1,2,128,128]{3,2,1,0:T(8,128)}, f32[1,2,128,128]{3,2,1,0:T(8,128)}, f32[32,128]{1,0:T(8,128)}) custom-call(f32[256,128]{1,0:T(8,128)S(1)} %get-tuple-element.32.refs_0_, f32[32,128]{1,0:T(8,128)S(1)} %get-tuple-element.33.refs_1_, bf16[320,128]{1,0:T(8,128)(2,1)S(1)} %collective-permute-done.11.refs_2_, ...), custom_call_target="tpu_custom_call" | custom-call | tf_op jit(solution)/shard_map/finish/pallas_call | solution.py:354
  (5 shorter events, 0.1 us)
Async XLA Ops:
  0.6 17.6 %copy-start = (bf16[1,2,32,4096]{3,2,1,0:T(8,128)(2,1)S(1)}, bf16[1,2,32,4096]{3,2,1,0:T(8,128)(2,1)}, u32[]{:S(2)}) copy-start(bf16[1,2,32,4096]{3,2,1,0:T(8,128)(2,1)} %refs_1_.3) | copy-start | bytes 1572868
  0.6 0.9 %copy-start.4 = (bf16[1,2,128,128]{3,2,1,0:T(8,128)(2,1)S(1)}, bf16[1,2,128,128]{3,2,1,0:T(8,128)(2,1)}, u32[]{:S(2)}) copy-start(bf16[1,2,128,128]{3,2,1,0:T(8,128)(2,1)} %keys_ref.1) | copy-start | bytes 196612
  1.5 0.8 %copy-start.5 = (bf16[1,2,128,128]{3,2,1,0:T(8,128)(2,1)S(1)}, bf16[1,2,128,128]{3,2,1,0:T(8,128)(2,1)}, u32[]{:S(2)}) copy-start(bf16[1,2,128,128]{3,2,1,0:T(8,128)(2,1)} %values_ref.1) | copy-start | bytes 196612
  2.4 5.8 %collective-permute-start = (bf16[2,64,128]{2,1,0:T(8,128)(2,1)S(1)}, bf16[2,64,128]{2,1,0:T(8,128)(2,1)S(1)}, u32[]{:S(2)}, u32[]{:S(2)}) collective-permute-start(bf16[2,64,128]{2,1,0:T(8,128)(2,1)S(1)} %get-tuple-element.41), channel_id=1, source_target_pairs={{0,1},{1,0},{2,3},{3,2},{4,5},{5,4},{6,7},{7,6},{8,9},{9,8},{10,11... | collective-permute-start | bytes 98312 | tf_op jit(solution)/shard_map/ppermute | solution.py:278
  5.5 6.2 %collective-permute-start.2 = (bf16[2,64,128]{2,1,0:T(8,128)(2,1)S(1)}, bf16[2,64,128]{2,1,0:T(8,128)(2,1)S(1)}, u32[]{:S(2)}, u32[]{:S(2)}) collective-permute-start(bf16[2,64,128]{2,1,0:T(8,128)(2,1)S(1)} %get-tuple-element.45), channel_id=1, source_target_pairs={{0,3},{1,2},{2,1},{3,0},{4,7},{5,6},{6,5},{7,4},{8,11},{9,10},{10,... | collective-permute-start | bytes 98312 | tf_op jit(solution)/shard_map/ppermute | solution.py:278
  8.0 5.2 %collective-permute-start.1 = (bf16[2,64,128]{2,1,0:T(8,128)(2,1)S(1)}, bf16[2,64,128]{2,1,0:T(8,128)(2,1)S(1)}, u32[]{:S(2)}, u32[]{:S(2)}) collective-permute-start(bf16[2,64,128]{2,1,0:T(8,128)(2,1)S(1)} %get-tuple-element.45), channel_id=1, source_target_pairs={{0,2},{1,3},{2,0},{3,1},{4,6},{5,7},{6,4},{7,5},{8,10},{9,11},{10,... | collective-permute-start | bytes 98312 | tf_op jit(solution)/shard_map/ppermute | solution.py:278
  13.2 5.1 %copy-start.3 = (f32[1,4096]{1,0:T(1,128)S(1)}, f32[1,4096]{1,0:T(1,128)}, u32[]{:S(2)}) copy-start(f32[1,4096]{1,0:T(1,128)} %refs_2_.3) | copy-start | bytes 49156
  13.2 5.1 %copy-start.6 = (s32[5,8]{1,0:T(8,128)S(1)}, s32[5,8]{1,0:T(8,128)}, u32[]{:S(2)}) copy-start(s32[5,8]{1,0:T(8,128)} %refs_0_.3) | copy-start | bytes 484
  13.2 5.1 %collective-permute-start.3 = (bf16[4,2,64,128]{3,2,1,0:T(8,128)(2,1)S(1)}, bf16[4,2,64,128]{3,2,1,0:T(8,128)(2,1)S(1)}, u32[]{:S(2)}, u32[]{:S(2)}) collective-permute-start(bf16[4,2,64,128]{3,2,1,0:T(8,128)(2,1)S(1)} %pad_maximum_fusion.refs_4_), channel_id=1, source_target_pairs={{0,4},{4,0},{1,5},{5,1},{2,6},{6,2},{3,7},{7,3},{8,12},{12,8},{9,1... | collective-permute-start | bytes 393224 | tf_op jit(solution)/shard_map/ppermute | solution.py:281
  14.8 6.8 %collective-permute-start.5 = (bf16[2,64,128]{2,1,0:T(8,128)(2,1)S(1)}, bf16[2,64,128]{2,1,0:T(8,128)(2,1)S(1)}, u32[]{:S(2)}, u32[]{:S(2)}) collective-permute-start(bf16[2,64,128]{2,1,0:T(8,128)(2,1)S(1)} %get-tuple-element.42), channel_id=1, source_target_pairs={{0,1},{1,0},{2,3},{3,2},{4,5},{5,4},{6,7},{7,6},{8,9},{9,8},{10,11... | collective-permute-start | bytes 98312 | tf_op jit(solution)/shard_map/ppermute | solution.py:278
  15.2 6.4 %collective-permute-start.7 = (bf16[2,64,128]{2,1,0:T(8,128)(2,1)S(1)}, bf16[2,64,128]{2,1,0:T(8,128)(2,1)S(1)}, u32[]{:S(2)}, u32[]{:S(2)}) collective-permute-start(bf16[2,64,128]{2,1,0:T(8,128)(2,1)S(1)} %get-tuple-element.44), channel_id=1, source_target_pairs={{0,3},{1,2},{2,1},{3,0},{4,7},{5,6},{6,5},{7,4},{8,11},{9,10},{10,... | collective-permute-start | bytes 98312 | tf_op jit(solution)/shard_map/ppermute | solution.py:278
  16.3 5.4 %collective-permute-start.6 = (bf16[2,64,128]{2,1,0:T(8,128)(2,1)S(1)}, bf16[2,64,128]{2,1,0:T(8,128)(2,1)S(1)}, u32[]{:S(2)}, u32[]{:S(2)}) collective-permute-start(bf16[2,64,128]{2,1,0:T(8,128)(2,1)S(1)} %get-tuple-element.44), channel_id=1, source_target_pairs={{0,2},{1,3},{2,0},{3,1},{4,6},{5,7},{6,4},{7,5},{8,10},{9,11},{10,... | collective-permute-start | bytes 98312 | tf_op jit(solution)/shard_map/ppermute | solution.py:278
  18.3 1.0 %copy-start.2 = (bf16[1,32,4096]{2,1,0:T(8,128)(2,1)S(1)}, bf16[1,32,4096]{2,1,0:T(8,128)(2,1)}, u32[]{:S(2)}) copy-start(bf16[1,32,4096]{2,1,0:T(8,128)(2,1)} %param.11) | copy-start | bytes 786436
  21.5 6.1 %copy-start.1 = (bf16[1,32,4096]{2,1,0:T(8,128)(2,1)S(1)}, bf16[1,32,4096]{2,1,0:T(8,128)(2,1)}, u32[]{:S(2)}) copy-start(bf16[1,32,4096]{2,1,0:T(8,128)(2,1)} %param.12) | copy-start | bytes 786436
  21.5 6.1 %collective-permute-start.4 = (bf16[32,4096]{1,0:T(8,128)(2,1)S(1)}, bf16[32,4096]{1,0:T(8,128)(2,1)S(1)}, u32[]{:S(2)}, u32[]{:S(2)}) collective-permute-start(bf16[32,4096]{1,0:T(8,128)(2,1)S(1)} %get-tuple-element.24.refs_8_), channel_id=1, source_target_pairs={{0,24},{8,0},{16,8},{24,16},{1,25},{9,1},{17,9},{25,17},{2,26},{10... | collective-permute-start | bytes 786440 | tf_op jit(solution)/shard_map/ppermute | solution.py:328
  21.6 5.9 %collective-permute-start.8 = (bf16[4,2,64,128]{3,2,1,0:T(8,128)(2,1)S(1)}, bf16[4,2,64,128]{3,2,1,0:T(8,128)(2,1)S(1)}, u32[]{:S(2)}, u32[]{:S(2)}) collective-permute-start(bf16[4,2,64,128]{3,2,1,0:T(8,128)(2,1)S(1)} %pad_maximum_fusion.1.refs_5_), channel_id=1, source_target_pairs={{0,4},{4,0},{1,5},{5,1},{2,6},{6,2},{3,7},{7,3},{8,12},{12,8},{9,1... | collective-permute-start | bytes 393224 | tf_op jit(solution)/shard_map/ppermute | solution.py:281
  30.7 8.5 %collective-permute-start.10 = (bf16[576,128]{1,0:T(8,128)(2,1)S(1)}, bf16[576,128]{1,0:T(8,128)(2,1)S(1)}, u32[]{:S(2)}, u32[]{:S(2)}) collective-permute-start(bf16[576,128]{1,0:T(8,128)(2,1)S(1)} %get-tuple-element.31), channel_id=1, source_target_pairs={{0,4},{4,0},{1,5},{5,1},{2,6},{6,2},{3,7},{7,3},{8,12},{12,8},{9,1... | collective-permute-start | bytes 442376 | tf_op jit(solution)/shard_map/ppermute | solution.py:281
  32.2 7.0 %collective-permute-start.9 = (bf16[512,128]{1,0:T(8,128)(2,1)S(1)}, bf16[512,128]{1,0:T(8,128)(2,1)S(1)}, u32[]{:S(2)}, u32[]{:S(2)}) collective-permute-start(bf16[512,128]{1,0:T(8,128)(2,1)S(1)} %get-tuple-element.29), channel_id=1, source_target_pairs={{0,4},{4,0},{1,5},{5,1},{2,6},{6,2},{3,7},{7,3},{8,12},{12,8},{9,1... | collective-permute-start | bytes 393224 | tf_op jit(solution)/shard_map/ppermute | solution.py:281
  39.3 5.3 %collective-permute-start.11 = (bf16[320,128]{1,0:T(8,128)(2,1)S(1)}, bf16[320,128]{1,0:T(8,128)(2,1)S(1)}, u32[]{:S(2)}, u32[]{:S(2)}) collective-permute-start(bf16[320,128]{1,0:T(8,128)(2,1)S(1)} %get-tuple-element.34), channel_id=1, source_target_pairs={{0,1},{1,0},{2,3},{3,2},{4,5},{5,4},{6,7},{7,6},{8,9},{9,8},{10,11... | collective-permute-start | bytes 245768 | tf_op jit(solution)/shard_map/ppermute | solution.py:278
  40.7 8.4 %collective-permute-start.12 = (bf16[320,128]{1,0:T(8,128)(2,1)S(1)}, bf16[320,128]{1,0:T(8,128)(2,1)S(1)}, u32[]{:S(2)}, u32[]{:S(2)}) collective-permute-start(bf16[320,128]{1,0:T(8,128)(2,1)S(1)} %get-tuple-element.35), channel_id=1, source_target_pairs={{0,2},{1,3},{2,0},{3,1},{4,6},{5,7},{6,4},{7,5},{8,10},{9,11},{10,... | collective-permute-start | bytes 245768 | tf_op jit(solution)/shard_map/ppermute | solution.py:278
  41.2 7.9 %collective-permute-start.13 = (bf16[320,128]{1,0:T(8,128)(2,1)S(1)}, bf16[320,128]{1,0:T(8,128)(2,1)S(1)}, u32[]{:S(2)}, u32[]{:S(2)}) collective-permute-start(bf16[320,128]{1,0:T(8,128)(2,1)S(1)} %get-tuple-element.36), channel_id=1, source_target_pairs={{0,3},{1,2},{2,1},{3,0},{4,7},{5,6},{6,5},{7,4},{8,11},{9,10},{10,... | collective-permute-start | bytes 245768 | tf_op jit(solution)/shard_map/ppermute | solution.py:278

commit v2 on v1

v2 whole, which is shorter than its diff:
```python
import functools

import jax
import jax.numpy as jnp
from jax import lax
from jax.experimental import pallas as pl
from jax.experimental.pallas import tpu as pltpu
from jax.sharding import PartitionSpec as P

HD = 128
EPSILON = 1e-05
FILL = -1e30
SCALE = HD ** (-0.5)
F32 = jnp.float32
BF16 = jnp.bfloat16

NT = (((1,), (1,)), ((), ()))
NN = (((1,), (0,)), ((), ()))
TN = (((0,), (0,)), ((), ()))


def dot(a, b, dims):
    return lax.dot_general(a, b, dims, preferred_element_type=F32)


def split_two(value):
    high = value.astype(BF16)
    low = (value - high.astype(F32)).astype(BF16)
    return high, low


def joined(high, low):
    return high.astype(F32) + low.astype(F32)


def in_order(values, owners):
    total = None
    for owner in range(len(values)):
        term = jnp.where(owners[0] == owner, values[0], 0.0)
        for value, whose in zip(values[1:], owners[1:]):
            term = jnp.where(whose == owner, value, term)
        total = term if total is None else total + term
    return total


def pack_kernel(tp_count, half, keys_ref, values_ref, own_ref, other_ref, later_ref, sems):
    parity = lax.axis_index("tp") // (tp_count // 2)
    own_first = pl.multiple_of(parity * half, half)
    other_first = pl.multiple_of((1 - parity) * half, half)
    copies = []
    for kind, ref in enumerate((keys_ref, values_ref)):
        moves = (
            (ref.at[0, 0, pl.ds(own_first, half), :], own_ref.at[kind]),
            (ref.at[0, 0, pl.ds(other_first, half), :], other_ref.at[kind]),
            (ref.at[0, 1], later_ref.at[kind]),
        )
        for place, (source, target) in enumerate(moves):
            copies.append(pltpu.make_async_copy(source, target, sems.at[kind, place]))
    for copy in copies:
        copy.start()
    for copy in copies:
        copy.wait()


def section_kernel(tp_count, half, cycle, *refs):
    blocks, (own_ref, other_ref) = refs[:cycle], refs[cycle:]
    parity = lax.axis_index("tp") // (tp_count // 2)
    for turn, ref in enumerate(blocks):
        own_ref[turn] = ref[:, pl.ds(pl.multiple_of(parity * half, half), half), :]
        other_ref[turn] = ref[:, pl.ds(pl.multiple_of((1 - parity) * half, half), half), :]


def norm_kernel(x_ref, gain_ref, query_ref, inverse_ref):
    _, ticks, rows, columns = x_ref.shape
    for tick in range(ticks):
        squares = jnp.zeros((rows, HD), F32)
        for first in range(0, columns, HD):
            part = x_ref[0, tick, :, first : first + HD].astype(F32)
            squares = squares + part * part
        mean = jnp.sum(squares, axis=1, keepdims=True) * (1.0 / columns)
        inverse = jnp.broadcast_to(lax.rsqrt(mean + EPSILON), (rows, HD))
        inverse_ref[tick] = inverse
        for first in range(0, columns, HD):
            here = slice(first, first + HD)
            normed = x_ref[0, tick, :, here].astype(F32) * inverse
            query_ref[tick, :, here] = (normed * gain_ref[:, here]).astype(BF16)


class Group:
    def __init__(self, sizes, turn):
        self.rows, self.group = sizes[0], sizes[4]
        width = self.group * HD
        self.head_group = lax.axis_index("tp") ^ turn
        self.first = pl.multiple_of(self.head_group * width, width)

    def head(self, index):
        return pl.ds(self.first + index * HD, HD)

    def stacked(self, load):
        return jnp.concatenate([load(self.head(index)) for index in range(self.group)], axis=0)

    def unstacked(self, value):
        return [value[index * self.rows : (index + 1) * self.rows] for index in range(self.group)]


def arriving_from(refs):
    if len(refs) == 1:
        return lambda where: refs[0][0, :, where]
    last = lax.axis_index("pipe") == lax.axis_size("pipe") - 1
    return lambda where: jnp.where(last, refs[1][0, :, where], refs[0][:, where])


def visible_keys(sizes, tick, doc_ref):
    rows, half, cycle, tp_count, group, columns = sizes
    cycle_place = lax.axis_index("ctx")
    tp_place = lax.axis_index("tp")
    parity = tp_place // (tp_count // 2)
    stacked = group * rows

    def section_first(owner):
        return half * jnp.where(parity == 0, owner, 2 * cycle - 1 - owner)

    row_first = section_first(cycle_place) + (tp_place % (tp_count // 2)) * rows
    query_pos = row_first + (lax.broadcasted_iota(jnp.int32, (1, stacked), 1) & (rows - 1))
    key_place = lax.broadcasted_iota(jnp.int32, (cycle * half, 1), 0)
    key_pos = key_place + section_first(cycle_place)
    for turn in range(1, cycle):
        first = section_first((cycle_place - turn + cycle) % cycle)
        key_pos = jnp.where(key_place >= turn * half, key_place - turn * half + first, key_pos)
    micro = lax.axis_index("pipe") + tick
    closing = jnp.int32(0)
    query_start = jnp.zeros((1, stacked), jnp.int32)
    for doc in range(doc_ref.shape[1]):
        length = doc_ref[micro, doc]
        closing = closing + length
        query_start = query_start + jnp.where(closing <= query_pos, length, 0)
    return (key_pos <= query_pos) & (key_pos >= query_start)


def probabilities(visible, key, query):
    scores = jnp.where(visible, SCALE * dot(key, query, NT), FILL)
    weights = jnp.exp(scores - jnp.max(scores, axis=0, keepdims=True))
    return weights * (1.0 / jnp.sum(weights, axis=0, keepdims=True))


def score_grads(probs, value, grad):
    prob_grad = dot(value, grad, NT)
    row_term = jnp.sum(probs * prob_grad, axis=0, keepdims=True)
    return (probs * (prob_grad - row_term)).astype(BF16)


def by_block(refs, turn, kind):
    return jnp.concatenate([ref[turn, kind] for ref in refs], axis=0)


def by_head(refs, turn, kind):
    parts = refs[turn]
    return jnp.concatenate([parts[block, kind] for block in range(parts.shape[0])], axis=0)


def put_key_grads(sizes, turn, key_grad, value_grad, own_ref, send_refs):
    half = sizes[1]
    for kind, part in enumerate((key_grad, value_grad)):
        here = slice((turn * 2 + kind) * half, (turn * 2 + kind + 1) * half)
        own_ref[here, :] = part[:half]
        for step, ref in enumerate(send_refs, 1):
            ref[here, :] = part[step * half : (step + 1) * half].astype(BF16)


def gain_terms(columns_of, low_parts, normed_of, gain_rows_ref):
    rows = []
    for index, low in enumerate(low_parts):
        term = low.astype(F32) * normed_of(columns_of.head(index))
        rows.append(jnp.sum(term, axis=0, keepdims=True))
    group = columns_of.group
    place = pl.ds(pl.multiple_of(columns_of.head_group * group, group), group)
    gain_rows_ref[place, :] = jnp.concatenate(rows, axis=0)


def write_input_grads(sizes, tick, x_ref, gain_ref, inverse, query_grad_ref, arriving, write):
    rows, columns = sizes[0], sizes[5]
    coupled = jnp.zeros((rows, HD), F32)
    for first in range(0, columns, HD):
        here = slice(first, first + HD)
        scaled = query_grad_ref[:, here].astype(F32) * gain_ref[:, here]
        coupled = coupled + scaled * (x_ref[0, tick, :, here].astype(F32) * inverse)
    coupling = jnp.sum(coupled, axis=1, keepdims=True) * (1.0 / columns)
    for first in range(0, columns, HD):
        here = slice(first, first + HD)
        scaled = query_grad_ref[:, here].astype(F32) * gain_ref[:, here]
        normed = x_ref[0, tick, :, here].astype(F32) * inverse
        result = arriving(here).astype(F32) + inverse * (scaled - normed * coupling)
        write(here, result.astype(BF16))


def first_rows_kernel(sizes, *refs):
    cycle, tp_count = sizes[2:4]
    doc_ref, x_ref, gain_ref, query_ref, inverse_ref, waiting_ref = refs[:6]
    kv_refs = refs[6 : 6 + cycle]
    input_grad_ref, query_grad_ref, dscore_ref, probs_ref = refs[6 + cycle :]
    visible = visible_keys(sizes, 0, doc_ref)
    arriving = arriving_from([waiting_ref])
    for turn in range(tp_count):
        columns_of = Group(sizes, turn)
        query = columns_of.stacked(lambda where: query_ref[0, :, where])
        grad = columns_of.stacked(arriving)
        key, value = by_block(kv_refs, turn, 0), by_block(kv_refs, turn, 1)
        probs = probabilities(visible, key, query)
        dscore = score_grads(probs, value, grad)
        dscore_ref[turn] = dscore
        probs_ref[turn] = probs.astype(BF16)
        query_grad = (SCALE * dot(dscore, key, TN)).astype(BF16)
        for index, low in enumerate(columns_of.unstacked(query_grad)):
            query_grad_ref[:, columns_of.head(index)] = low

    def write(here, result):
        input_grad_ref[:, here] = result

    write_input_grads(
        sizes, 0, x_ref, gain_ref, inverse_ref[0], query_grad_ref, arriving, write
    )


def first_keys_kernel(sizes, *refs):
    tp_count = sizes[3]
    x_ref, query_ref, inverse_ref, waiting_ref, query_grad_ref, dscore_ref, probs_ref = refs[:7]
    gain_rows_ref, own_ref = refs[7:9]
    send_refs = refs[9:]
    arriving = arriving_from([waiting_ref])
    inverse = inverse_ref[0]
    for turn in range(tp_count):
        columns_of = Group(sizes, turn)
        query = columns_of.stacked(lambda where: query_ref[0, :, where])
        grad = columns_of.stacked(arriving)
        key_grad = SCALE * dot(dscore_ref[turn], query, NN)
        value_grad = dot(probs_ref[turn], grad, NN)
        put_key_grads(sizes, turn, key_grad, value_grad, own_ref, send_refs)
        gain_terms(
            columns_of,
            [query_grad_ref[:, columns_of.head(index)] for index in range(columns_of.group)],
            lambda where: x_ref[0, 0, :, where].astype(F32) * inverse,
            gain_rows_ref,
        )


def second_probs_kernel(sizes, *refs):
    tp_count = sizes[3]
    doc_ref, query_ref = refs[:2]
    kv_refs, probs_ref = refs[2 : 2 + tp_count], refs[2 + tp_count]
    visible = visible_keys(sizes, 1, doc_ref)
    for turn in range(tp_count):
        query = Group(sizes, turn).stacked(lambda where: query_ref[1, :, where])
        probs_ref[turn] = probabilities(visible, by_head(kv_refs, turn, 0), query)


def second_keys_kernel(sizes, *refs):
    tp_count = sizes[3]
    x_ref, query_ref, inverse_ref, arrived_ref, output_ref, probs_ref, before_ref = refs[:7]
    kv_refs = refs[7 : 7 + tp_count]
    query_grad_ref, gain_rows_ref, own_ref = refs[7 + tp_count :][:3]
    send_refs, (gain_scratch,) = refs[7 + tp_count :][3:-1], refs[-1:]
    arriving = arriving_from([arrived_ref, output_ref])
    inverse = inverse_ref[1]
    for turn in range(tp_count):
        columns_of = Group(sizes, turn)
        query = columns_of.stacked(lambda where: query_ref[1, :, where])
        grad = columns_of.stacked(arriving)
        key, value = by_head(kv_refs, turn, 0), by_head(kv_refs, turn, 1)
        probs = probs_ref[turn]
        dscore = score_grads(probs, value, grad)
        key_grad = SCALE * dot(dscore, query, NN)
        value_grad = dot(probs.astype(BF16), grad, NN)
        put_key_grads(sizes, turn, key_grad, value_grad, own_ref, send_refs)
        query_grad = (SCALE * dot(dscore, key, TN)).astype(BF16)
        low_parts = columns_of.unstacked(query_grad)
        for index, low in enumerate(low_parts):
            query_grad_ref[:, columns_of.head(index)] = low
        gain_terms(
            columns_of,
            low_parts,
            lambda where: x_ref[0, 1, :, where].astype(F32) * inverse,
            gain_scratch,
        )
    gain_rows = gain_scratch[...] + before_ref[...]
    gain_rows_ref[...] = gain_rows
    high, low = split_two(gain_rows)
    count = high.shape[0]
    begin = own_ref.shape[0]
    for ref in send_refs:
        ref[begin : begin + count, :] = high
        ref[begin + count : begin + 2 * count, :] = low


def second_rows_kernel(sizes, *refs):
    x_ref, gain_ref, inverse_ref, arrived_ref, output_ref, query_grad_ref, first_ref = refs[:7]
    input_grads_ref = refs[7]
    input_grads_ref[0, 0] = first_ref[...]

    def write(here, result):
        input_grads_ref[0, 1, :, here] = result

    arriving = arriving_from([arrived_ref, output_ref])
    write_input_grads(
        sizes, 1, x_ref, gain_ref, inverse_ref[1], query_grad_ref, arriving, write
    )


def cycle_sum_kernel(sizes, with_gain, *refs):
    rows, half, cycle, tp_count, group, columns = sizes
    parts, refs = refs[:cycle], refs[cycle:]
    if with_gain:
        gain_ref, refs = refs[0], refs[1:]
        gain_sum_ref, refs = refs[0], refs[1:]
    keep_ref, send_refs = refs[0], refs[1:]
    block = 2 * half
    for turn in range(tp_count):
        here = slice(turn * block, (turn + 1) * block)
        total = parts[0][here, :]
        for ref in parts[1:]:
            total = total + ref[here, :].astype(F32)
        if turn == 0:
            keep_ref[...] = total
        else:
            send_refs[turn - 1][:block, :] = total.astype(BF16)
    if not with_gain:
        return
    count = gain_ref.shape[0]
    begin = tp_count * block
    cycle_place = lax.axis_index("ctx")
    values = [joined(*split_two(gain_ref[...]))]
    owners = [cycle_place]
    for step, ref in enumerate(parts[1:], 1):
        values.append(
            joined(ref[begin : begin + count, :], ref[begin + count : begin + 2 * count, :])
        )
        owners.append((cycle_place + step) % cycle)
    gain = in_order(values, owners)
    gain_sum_ref[...] = gain
    high, low = split_two(gain)
    for ref in send_refs:
        ref[block : block + count, :] = high
        ref[block + count : block + 2 * count, :] = low


def finish_kernel(sizes, ticks, *refs):
    rows, half, cycle, tp_count, group, columns = sizes
    gain_ref, refs = refs[0], refs[1:]
    per_tick = [refs[tick * tp_count : (tick + 1) * tp_count] for tick in range(ticks)]
    key_ref, value_ref, gain_out_ref = refs[ticks * tp_count :]
    block = 2 * half
    tp_place = lax.axis_index("tp")
    parity = tp_place // (tp_count // 2)
    for tick in range(ticks):
        keep_ref, receive_refs = per_tick[tick][0], per_tick[tick][1:]
        for kind, out in enumerate((key_ref, value_ref)):
            here = slice(kind * half, (kind + 1) * half)
            own = keep_ref[here, :]
            other = None
            for turn, ref in enumerate(receive_refs, 1):
                part = ref[here, :].astype(F32)
                if turn < tp_count // 2:
                    own = own + part
                else:
                    other = part if other is None else other + part
            out[0, tick, pl.ds(pl.multiple_of(parity * half, half), half), :] = own
            out[0, tick, pl.ds(pl.multiple_of((1 - parity) * half, half), half), :] = other
    count = gain_ref.shape[0]
    values = [joined(*split_two(gain_ref[...]))]
    owners = [tp_place]
    for turn, ref in enumerate(per_tick[ticks - 1][1:], 1):
        values.append(
            joined(ref[block : block + count, :], ref[block + count : block + 2 * count, :])
        )
        owners.append(tp_place ^ turn)
    gain_out_ref[...] = in_order(values, owners)


def shape(dims, dtype):
    return jax.ShapeDtypeStruct(dims, dtype)


def on_device(segment_inputs, keys, values, norm_gain, waiting_grads, output_grads, doc_lengths):
    cycle = lax.axis_size("ctx")
    tp_count = lax.axis_size("tp")
    pipe_count = lax.axis_size("pipe")
    _, ticks, rows, columns = segment_inputs.shape
    half = keys.shape[2] // 2
    group = columns // (tp_count * HD)
    gain_count = columns // HD
    sizes = (rows, half, cycle, tp_count, group, columns)
    block = 2 * half
    key_count = cycle * half
    stacked = group * rows
    score_bytes = key_count * stacked * 4
    params = pltpu.CompilerParams(vmem_limit_bytes=min(56 << 20, (12 << 20) + 16 * score_bytes))

    def call(kernel, name, operands, out_shape, memory=pltpu.VMEM, scratch=(), scalars=0):
        in_specs = [pl.BlockSpec(memory_space=pltpu.SMEM)] * scalars
        in_specs += [pl.BlockSpec(memory_space=memory)] * (len(operands) - scalars)
        return pl.pallas_call(
            kernel,
            out_shape=out_shape,
            in_specs=in_specs,
            out_specs=[pl.BlockSpec(memory_space=pltpu.VMEM)] * len(out_shape),
            scratch_shapes=scratch,
            compiler_params=params,
            name=name,
        )(*operands)

    def to_partner(value, turn):
        return lax.ppermute(value, "tp", [(i, i ^ turn) for i in range(tp_count)])

    def to_block(value, step):
        return lax.ppermute(value, "ctx", [(i, (i + step) % cycle) for i in range(cycle)])

    def from_partners(own, other):
        return [to_partner(own if d < tp_count // 2 else other, d) for d in range(1, tp_count)]

    section = shape((2, half, HD), BF16)
    own_kv, other_kv, later_kv = call(
        functools.partial(pack_kernel, tp_count, half),
        "pack_kv",
        (keys, values),
        [section, section, shape((2, block, HD), BF16)],
        memory=pl.ANY,
        scratch=[pltpu.SemaphoreType.DMA((2, 3))],
    )
    heads_first = from_partners(own_kv, other_kv)
    blocks_second = [to_block(later_kv, step) for step in range(1, cycle)]
    queries, inverse = call(
        norm_kernel,
        "norm",
        (segment_inputs, norm_gain),
        [shape((ticks, rows, columns), BF16), shape((ticks, rows, HD), F32)],
    )
    near = jnp.stack([own_kv] + heads_first)
    kv_first = [near] + [to_block(near, step) for step in range(1, cycle)]
    sections = shape((cycle, 2, half, HD), BF16)
    own_second, other_second = call(
        functools.partial(section_kernel, tp_count, half, cycle),
        "sections",
        (later_kv, *blocks_second),
        [sections, sections],
    )
    kv_second = [own_second] + from_partners(own_second, other_second)

    low_rows = shape((rows, columns), BF16)
    low_scores = shape((tp_count, key_count, stacked), BF16)
    input_grad_first, query_grad_first, dscore_first, probs_first = call(
        functools.partial(first_rows_kernel, sizes),
        "first_rows",
        (doc_lengths, segment_inputs, norm_gain, queries, inverse, waiting_grads, *kv_first),
        [low_rows, low_rows, low_scores, low_scores],
        scalars=1,
    )
    arrived = lax.ppermute(
        input_grad_first, "pipe", [(i, (i - 1) % pipe_count) for i in range(pipe_count)]
    )
    gain_shape = shape((gain_count, HD), F32)
    own_shape = shape((tp_count * block, HD), F32)

    def send_shapes(extra):
        return [shape((tp_count * block + extra, HD), BF16)] * (cycle - 1)

    def turned(sends):
        return [to_block(value, -step) for step, value in enumerate(sends, 1)]

    gain_first, own_first, *sends_first = call(
        functools.partial(first_keys_kernel, sizes),
        "first_keys",
        (
            segment_inputs,
            queries,
            inverse,
            waiting_grads,
            query_grad_first,
            dscore_first,
            probs_first,
        ),
        [gain_shape, own_shape] + send_shapes(0),
    )
    turned_first = turned(sends_first)
    (probs_second,) = call(
        functools.partial(second_probs_kernel, sizes),
        "second_probs",
        (doc_lengths, queries, *kv_second),
        [shape((tp_count, key_count, stacked), F32)],
        scalars=1,
    )
    query_grad_second, gain_rows, own_second_sum, *sends_second = call(
        functools.partial(second_keys_kernel, sizes),
        "second_keys",
        (
            segment_inputs,
            queries,
            inverse,
            arrived,
            output_grads,
            probs_second,
            gain_first,
            *kv_second,
        ),
        [low_rows, gain_shape, own_shape] + send_shapes(2 * gain_count),
        scratch=[pltpu.VMEM((gain_count, HD), F32)],
    )
    turned_second = turned(sends_second)
    (input_grads,) = call(
        functools.partial(second_rows_kernel, sizes),
        "second_rows",
        (
            segment_inputs,
            norm_gain,
            inverse,
            arrived,
            output_grads,
            query_grad_second,
            input_grad_first,
        ),
        [shape((1, ticks, rows, columns), BF16)],
    )
    keep_shape = shape((block, HD), F32)
    keep_first, *heads_sums_first = call(
        functools.partial(cycle_sum_kernel, sizes, False),
        "first_sum",
        (own_first, *turned_first),
        [keep_shape] + [shape((block, HD), BF16)] * (tp_count - 1),
    )
    received_first = [to_partner(value, d) for d, value in enumerate(heads_sums_first, 1)]
    gain_sum, keep_second, *heads_sums_second = call(
        functools.partial(cycle_sum_kernel, sizes, True),
        "second_sum",
        (own_second_sum, *turned_second, gain_rows),
        [gain_shape, keep_shape]
        + [shape((block + 2 * gain_count, HD), BF16)] * (tp_count - 1),
    )
    received_second = [to_partner(value, d) for d, value in enumerate(heads_sums_second, 1)]
    grads_shape = shape((1, ticks, block, HD), F32)
    key_grads, value_grads, gain_grads = call(
        functools.partial(finish_kernel, sizes, ticks),
        "finish",
        (gain_sum, keep_first, *received_first, keep_second, *received_second),
        [grads_shape, grads_shape, gain_shape],
    )
    return input_grads, key_grads, value_grads, gain_grads.reshape(1, columns)


def solution(mesh):
    in_specs = (
        P("pipe", None, ("ctx", "tp"), None),
        P("pipe", None, "ctx", "tp"),
        P("pipe", None, "ctx", "tp"),
        P("pipe", None),
        P("pipe", ("ctx", "tp"), None),
        P(None, ("ctx", "tp"), None),
        P(),
    )
    out_specs = (
        P("pipe", None, ("ctx", "tp"), None),
        P("pipe", None, "ctx", "tp"),
        P("pipe", None, "ctx", "tp"),
        P("pipe", None),
    )
    return jax.shard_map(
        on_device, mesh=mesh, in_specs=in_specs, out_specs=out_specs, check_vma=False
    )
```

time: 50 us -> 56.7 us (1.13)
  starting transfers between devices: 18.9 us -> 23.4 us
  waiting for transfers between devices: 21.3 us -> 22.2 us
  Pallas kernels: 6.17 us -> 6.78 us
    ppermute x9 -> x12, starting transfers between devices: 13.7 us -> 18.1 us  [to_partner(): return lax.ppermute(value, 'tp', [(i, i ^ turn) for i in range(tp_count)])]
    ppermute x9 -> x12, waiting for transfers between devices: 10.4 us -> 12.6 us  [to_partner(): return lax.ppermute(value, 'tp', [(i, i ^ turn) for i in range(tp_count)])]
    ppermute x4, waiting for transfers between devices: 10.9 us -> 9.58 us  [to_block(): lax.ppermute(value, 'ctx', [(i, (i + step) % cycle) for i in range(cycle)])]
    pallas_call x5 -> x11, Pallas kernels: 6.17 us -> 6.78 us  [call(): pl.pallas_call(kernel, out_shape=out_shape, in_specs=in_specs, out_specs=...]
    unnamed x14 -> x16, local copies, waits for them, and re-layouts: 2.69 us -> 3.18 us
  transfers between devices with their start and end apart: 14 -> 17, of which waited for: 6 -> 9; matrix products, arithmetic and copies ran while one was open for 0% -> 0% of each run, Pallas kernels for 5% -> 5%
where the time goes in v2:
time: 56.7 us; the launch traced here: 56.4 us
  starting transfers between devices  23.4 us (41%)
  waiting for transfers between devices  22.2 us (39%)
  Pallas kernels  6.78 us (12%)
  local copies, waits for them, and re-layouts  3.18 us (6%)
  between operations  0.77 us (1%)
    ppermute x12, starting transfers between devices, to_partner(): return lax.ppermute(value, 'tp', [(i, i ^ turn) for i in range(tp_count)])  18.1 us
    ppermute x12, waiting for transfers between devices, to_partner(): return lax.ppermute(value, 'tp', [(i, i ^ turn) for i in range(tp_count)])  12.6 us
    ppermute x4, waiting for transfers between devices, to_block(): lax.ppermute(value, 'ctx', [(i, (i + step) % cycle) for i in range(cycle)])  9.58 us
    pallas_call x11, Pallas kernels, call(): pl.pallas_call(kernel, out_shape=out_shape, in_specs=in_specs, out_specs=...  6.78 us
    ppermute x4, starting transfers between devices, to_block(): lax.ppermute(value, 'ctx', [(i, (i + step) % cycle) for i in range(cycle)])  5.26 us
    unnamed x16, local copies, waits for them, and re-layouts  3.18 us
  transfers between devices with their start and end apart: 17, of which 9 were waited for; matrix products, arithmetic and copies ran while one was open for 0% of the time, Pallas kernels for 5%

profile of v2, /device:TPU:0, one launch (start us, length us, event | category | flops | bytes accessed | tf_op | source)
XLA Modules:
  0.0 56.4 jit_solution(14589312677785333386)
XLA Ops:
  0.6 0.0 copy-start.5
  0.6 0.8 %copy-done.5 = bf16[1,2,128,128]{3,2,1,0:T(8,128)(2,1)S(1)} copy-done((bf16[1,2,128,128]{3,2,1,0:T(8,128)(2,1)S(1)}, bf16[1,2,128,128]{3,2,1,0:T(8,128)(2,1)}, u32[]{:S(2)}) %copy-start.5) | copy-done | bytes 65560
  1.5 0.0 copy-start.6
  1.5 0.8 %copy-done.6 = bf16[1,2,128,128]{3,2,1,0:T(8,128)(2,1)S(1)} copy-done((bf16[1,2,128,128]{3,2,1,0:T(8,128)(2,1)S(1)}, bf16[1,2,128,128]{3,2,1,0:T(8,128)(2,1)}, u32[]{:S(2)}) %copy-start.6) | copy-done | bytes 65560
  2.3 0.2 pack_kv.1
  2.5 3.1 %collective-permute-start = (bf16[2,64,128]{2,1,0:T(8,128)(2,1)S(1)}, bf16[2,64,128]{2,1,0:T(8,128)(2,1)S(1)}, u32[]{:S(2)}, u32[]{:S(2)}) collective-permute-start(bf16[2,64,128]{2,1,0:T(8,128)(2,1)S(1)} %get-tuple-element.36), channel_id=1, source_target_pairs={{0,1},{1,0},{2,3},{3,2},{4,5},{5,4},{6,7},{7,6},{8,9},{9,8},{10,11... | collective-permute-start | bytes 98312 | tf_op jit(solution)/shard_map/ppermute | solution.py:411
  5.6 2.6 %collective-permute-start.1 = (bf16[2,64,128]{2,1,0:T(8,128)(2,1)S(1)}, bf16[2,64,128]{2,1,0:T(8,128)(2,1)S(1)}, u32[]{:S(2)}, u32[]{:S(2)}) collective-permute-start(bf16[2,64,128]{2,1,0:T(8,128)(2,1)S(1)} %get-tuple-element.37), channel_id=1, source_target_pairs={{0,2},{1,3},{2,0},{3,1},{4,6},{5,7},{6,4},{7,5},{8,10},{9,11},{10,... | collective-permute-start | bytes 98312 | tf_op jit(solution)/shard_map/ppermute | solution.py:411
  8.2 0.0 collective-permute-start.2
  8.2 0.0 collective-permute-done
  8.2 2.8 %collective-permute-done.1 = bf16[2,64,128]{2,1,0:T(8,128)(2,1)S(1)} collective-permute-done((bf16[2,64,128]{2,1,0:T(8,128)(2,1)S(1)}, bf16[2,64,128]{2,1,0:T(8,128)(2,1)S(1)}, u32[]{:S(2)}, u32[]{:S(2)}) %collective-permute-start.1) | collective-permute-done | bytes 32800 | tf_op jit(solution)/shard_map/ppermute | solution.py:411
  11.0 2.9 %collective-permute-done.2 = bf16[2,64,128]{2,1,0:T(8,128)(2,1)S(1)} collective-permute-done((bf16[2,64,128]{2,1,0:T(8,128)(2,1)S(1)}, bf16[2,64,128]{2,1,0:T(8,128)(2,1)S(1)}, u32[]{:S(2)}, u32[]{:S(2)}) %collective-permute-start.2) | collective-permute-done | bytes 32800 | tf_op jit(solution)/shard_map/ppermute | solution.py:411
  13.9 0.0 copy-start.4
  13.9 1.6 %collective-permute-start.3 = (bf16[4,2,64,128]{3,2,1,0:T(8,128)(2,1)S(1)}, bf16[4,2,64,128]{3,2,1,0:T(8,128)(2,1)S(1)}, u32[]{:S(2)}, u32[]{:S(2)}) collective-permute-start(bf16[4,2,64,128]{3,2,1,0:T(8,128)(2,1)S(1)} %pad_maximum_fusion.refs_6_), channel_id=1, source_target_pairs={{0,4},{4,0},{1,5},{5,1},{2,6},{6,2},{3,7},{7,3},{8,12},{12,8},{9,1... | collective-permute-start | bytes 393224 | tf_op jit(solution)/shard_map/ppermute | solution.py:414
  15.5 0.0 copy-done.4
  15.5 0.0 copy-start
  15.5 1.0 %copy-done = bf16[1,2,32,4096]{3,2,1,0:T(8,128)(2,1)S(1)} copy-done((bf16[1,2,32,4096]{3,2,1,0:T(8,128)(2,1)S(1)}, bf16[1,2,32,4096]{3,2,1,0:T(8,128)(2,1)}, u32[]{:S(2)}) %copy-start) | copy-done | bytes 524312
  16.6 0.0 copy-start.2
  16.6 0.0 copy-start.7
  16.6 0.3 norm.1
  16.8 2.1 %collective-permute-done.3.refs_7_ = bf16[4,2,64,128]{3,2,1,0:T(8,128)(2,1)S(1)} collective-permute-done((bf16[4,2,64,128]{3,2,1,0:T(8,128)(2,1)S(1)}, bf16[4,2,64,128]{3,2,1,0:T(8,128)(2,1)S(1)}, u32[]{:S(2)}, u32[]{:S(2)}) %collective-permute-start.3) | collective-permute-done | bytes 131104 | tf_op jit(solution)/shard_map/ppermute | solution.py:414
  19.0 0.0 copy-done.2
  19.0 0.0 copy-done.7
  19.0 2.1 %first_rows.1 = (bf16[32,4096]{1,0:T(8,128)(2,1)S(1)}, bf16[32,4096]{1,0:T(8,128)(2,1)S(1)}, bf16[4,128,256]{2,1,0:T(8,128)(2,1)S(1)}, bf16[4,128,256]{2,1,0:T(8,128)(2,1)S(1)}) custom-call(s32[5,8]{1,0:T(8,128)S(1)} %copy-done.7, bf16[1,2,32,4096]{3,2,1,0:T(8,128)(2,1)S(1)} %copy-done, f32[1,4096]{1,0:T(1,128)S(1)} %copy-done.4, ...), custom_call_target="tpu_custom_call" | custom-call | tf_op jit(solution)/shard_map/first_rows/pallas_call | solution.py:400
  21.1 0.1 collective-permute-start.4
  21.2 1.6 %collective-permute-start.5 = (bf16[2,128,128]{2,1,0:T(8,128)(2,1)S(1)}, bf16[2,128,128]{2,1,0:T(8,128)(2,1)S(1)}, u32[]{:S(2)}, u32[]{:S(2)}) collective-permute-start(bf16[2,128,128]{2,1,0:T(8,128)(2,1)S(1)} %get-tuple-element.39.refs_0_), channel_id=1, source_target_pairs={{0,4},{4,0},{1,5},{5,1},{2,6},{6,2},{3,7},{7,3},{8,12},{12,8},{9,1... | collective-permute-start | bytes 196616 | tf_op jit(solution)/shard_map/ppermute | solution.py:414
  22.8 2.9 %collective-permute-done.5.refs_1_ = bf16[2,128,128]{2,1,0:T(8,128)(2,1)S(1)} collective-permute-done((bf16[2,128,128]{2,1,0:T(8,128)(2,1)S(1)}, bf16[2,128,128]{2,1,0:T(8,128)(2,1)S(1)}, u32[]{:S(2)}, u32[]{:S(2)}) %collective-permute-start.5) | collective-permute-done | bytes 65568 | tf_op jit(solution)/shard_map/ppermute | solution.py:414
  25.7 0.1 collective-permute-start.6
  25.8 0.0 copy-start.1
  25.8 0.9 %collective-permute-start.7 = (bf16[2,2,64,128]{3,2,1,0:T(8,128)(2,1)S(1)}, bf16[2,2,64,128]{3,2,1,0:T(8,128)(2,1)S(1)}, u32[]{:S(2)}, u32[]{:S(2)}) collective-permute-start(bf16[2,2,64,128]{3,2,1,0:T(8,128)(2,1)S(1)} %get-tuple-element.41), channel_id=1, source_target_pairs={{0,2},{1,3},{2,0},{3,1},{4,6},{5,7},{6,4},{7,5},{8,10},{9,11},{10,... | collective-permute-start | bytes 196616 | tf_op jit(solution)/shard_map/ppermute | solution.py:411
  26.7 3.5 %collective-permute-start.8 = (bf16[2,2,64,128]{3,2,1,0:T(8,128)(2,1)S(1)}, bf16[2,2,64,128]{3,2,1,0:T(8,128)(2,1)S(1)}, u32[]{:S(2)}, u32[]{:S(2)}) collective-permute-start(bf16[2,2,64,128]{3,2,1,0:T(8,128)(2,1)S(1)} %get-tuple-element.41), channel_id=1, source_target_pairs={{0,3},{1,2},{2,1},{3,0},{4,7},{5,6},{6,5},{7,4},{8,11},{9,10},{10,... | collective-permute-start | bytes 196616 | tf_op jit(solution)/shard_map/ppermute | solution.py:411
  30.2 0.3 collective-permute-done.6.refs_3_.refs_8_
  30.4 3.5 %collective-permute-done.7.refs_4_.refs_9_ = bf16[2,2,64,128]{3,2,1,0:T(8,128)(2,1)S(1)} collective-permute-done((bf16[2,2,64,128]{3,2,1,0:T(8,128)(2,1)S(1)}, bf16[2,2,64,128]{3,2,1,0:T(8,128)(2,1)S(1)}, u32[]{:S(2)}, u32[]{:S(2)}) %collective-permute-start.7) | collective-permute-done | bytes 65568 | tf_op jit(solution)/shard_map/ppermute | solution.py:411
  33.9 0.0 collective-permute-done.8.refs_5_.refs_10_
  33.9 1.0 %second_probs.1.refs_5_ = f32[4,128,256]{2,1,0:T(8,128)S(1)} custom-call(s32[5,8]{1,0:T(8,128)S(1)} %copy-done.7, bf16[2,32,4096]{2,1,0:T(8,128)(2,1)S(1)} %get-tuple-element.35.refs_3_.refs_1_, bf16[2,2,64,128]{3,2,1,0:T(8,128)(2,1)S(1)} %get-tuple-element.40.refs_2_.refs_7_, bf16[2,2,64,128]{3,2,1,0:T(8,128)(2,1)S(1)} %collective-permute-done.6.refs_3_.refs_8_, ...), custom_call_target="tpu_custom_call" | custom-call | tf_op jit(solution)/shard_map/second_probs/pallas_call | solution.py:400
  34.9 0.0 copy-done.1
  34.9 0.0 copy-start.3
  34.9 0.5 first_keys.1
  35.4 0.0 collective-permute-done.4.refs_3_
  35.4 0.4 copy-done.3
  35.9 0.8 %second_keys.1 = (bf16[32,4096]{1,0:T(8,128)(2,1)S(1)}, f32[32,128]{1,0:T(8,128)S(1)}, f32[512,128]{1,0:T(8,128)S(1)}, bf16[576,128]{1,0:T(8,128)(2,1)S(1)}) custom-call(bf16[1,2,32,4096]{3,2,1,0:T(8,128)(2,1)S(1)} %copy-done.1, bf16[2,32,4096]{2,1,0:T(8,128)(2,1)S(1)} %get-tuple-element.35.refs_3_.refs_1_, ...), custom_call_target="tpu_custom_call" | custom-call | tf_op jit(solution)/shard_map/second_keys/pallas_call | solution.py:400
  36.7 1.6 %collective-permute-start.9 = (bf16[576,128]{1,0:T(8,128)(2,1)S(1)}, bf16[576,128]{1,0:T(8,128)(2,1)S(1)}, u32[]{:S(2)}, u32[]{:S(2)}) collective-permute-start(bf16[576,128]{1,0:T(8,128)(2,1)S(1)} %get-tuple-element.48), channel_id=1, source_target_pairs={{0,4},{4,0},{1,5},{5,1},{2,6},{6,2},{3,7},{7,3},{8,12},{12,8},{9,1... | collective-permute-start | bytes 442376 | tf_op jit(solution)/shard_map/ppermute | solution.py:414
  38.3 0.5 collective-permute-start.10
  38.8 4.5 %collective-permute-done.10.refs_1_ = bf16[512,128]{1,0:T(8,128)(2,1)S(1)} collective-permute-done((bf16[512,128]{1,0:T(8,128)(2,1)S(1)}, bf16[512,128]{1,0:T(8,128)(2,1)S(1)}, u32[]{:S(2)}, u32[]{:S(2)}) %collective-permute-start.10) | collective-permute-done | bytes 131104 | tf_op jit(solution)/shard_map/ppermute | solution.py:414
  43.3 1.9 %collective-permute-start.11 = (bf16[128,128]{1,0:T(8,128)(2,1)S(1)}, bf16[128,128]{1,0:T(8,128)(2,1)S(1)}, u32[]{:S(2)}, u32[]{:S(2)}) collective-permute-start(bf16[128,128]{1,0:T(8,128)(2,1)S(1)} %get-tuple-element.54), channel_id=1, source_target_pairs={{0,1},{1,0},{2,3},{3,2},{4,5},{5,4},{6,7},{7,6},{8,9},{9,8},{10,11... | collective-permute-start | bytes 98312 | tf_op jit(solution)/shard_map/ppermute | solution.py:411
  45.3 0.0 collective-permute-done.9.refs_1_
  45.3 0.2 collective-permute-start.14
  45.5 1.6 %collective-permute-start.15 = (bf16[192,128]{1,0:T(8,128)(2,1)S(1)}, bf16[192,128]{1,0:T(8,128)(2,1)S(1)}, u32[]{:S(2)}, u32[]{:S(2)}) collective-permute-start(bf16[192,128]{1,0:T(8,128)(2,1)S(1)} %get-tuple-element.59), channel_id=1, source_target_pairs={{0,2},{1,3},{2,0},{3,1},{4,6},{5,7},{6,4},{7,5},{8,10},{9,11},{10,... | collective-permute-start | bytes 147464 | tf_op jit(solution)/shard_map/ppermute | solution.py:411
  47.1 2.7 %collective-permute-start.16 = (bf16[192,128]{1,0:T(8,128)(2,1)S(1)}, bf16[192,128]{1,0:T(8,128)(2,1)S(1)}, u32[]{:S(2)}, u32[]{:S(2)}) collective-permute-start(bf16[192,128]{1,0:T(8,128)(2,1)S(1)} %get-tuple-element.60), channel_id=1, source_target_pairs={{0,3},{1,2},{2,1},{3,0},{4,7},{5,6},{6,5},{7,4},{8,11},{9,10},{10,... | collective-permute-start | bytes 147464 | tf_op jit(solution)/shard_map/ppermute | solution.py:411
  49.8 0.2 collective-permute-start.12
  49.9 0.0 collective-permute-done.11.refs_2_
  49.9 1.5 %collective-permute-start.13 = (bf16[128,128]{1,0:T(8,128)(2,1)S(1)}, bf16[128,128]{1,0:T(8,128)(2,1)S(1)}, u32[]{:S(2)}, u32[]{:S(2)}) collective-permute-start(bf16[128,128]{1,0:T(8,128)(2,1)S(1)} %get-tuple-element.56), channel_id=1, source_target_pairs={{0,3},{1,2},{2,1},{3,0},{4,7},{5,6},{6,5},{7,4},{8,11},{9,10},{10,... | collective-permute-start | bytes 98312 | tf_op jit(solution)/shard_map/ppermute | solution.py:411
  51.4 1.1 %second_rows.1 = bf16[1,2,32,4096]{3,2,1,0:T(8,128)(2,1)} custom-call(bf16[1,2,32,4096]{3,2,1,0:T(8,128)(2,1)S(1)} %copy-done.1, f32[1,4096]{1,0:T(1,128)S(1)} %copy-done.4, f32[2,32,128]{2,1,0:T(8,128)S(1)} %get-tuple-element.34.refs_4_.refs_2_, bf16[32,4096]{1,0:T(8,128)(2,1)S(1)} %collective-permute-done.4.refs_3_, bf16[1,32,4096]{2,1,0:T(8,128)(2,1)S(1)} %copy-done.3, ...), custom_call_target="tpu_custom_call" | custom-call | tf_op jit(solution)/shard_map/second_rows/pallas_call | solution.py:400
  52.5 2.1 %collective-permute-done.12.refs_3_ = bf16[128,128]{1,0:T(8,128)(2,1)S(1)} collective-permute-done((bf16[128,128]{1,0:T(8,128)(2,1)S(1)}, bf16[128,128]{1,0:T(8,128)(2,1)S(1)}, u32[]{:S(2)}, u32[]{:S(2)}) %collective-permute-start.12) | collective-permute-done | bytes 32800 | tf_op jit(solution)/shard_map/ppermute | solution.py:411
  54.6 1.1 %collective-permute-done.13.refs_4_ = bf16[128,128]{1,0:T(8,128)(2,1)S(1)} collective-permute-done((bf16[128,128]{1,0:T(8,128)(2,1)S(1)}, bf16[128,128]{1,0:T(8,128)(2,1)S(1)}, u32[]{:S(2)}, u32[]{:S(2)}) %collective-permute-start.13) | collective-permute-done | bytes 32800 | tf_op jit(solution)/shard_map/ppermute | solution.py:411
  55.6 0.0 collective-permute-done.14.refs_6_
  55.6 0.0 collective-permute-done.15.refs_7_
  55.6 0.0 collective-permute-done.16.refs_8_
  55.6 0.7 %finish.1 = (f32[1,2,128,128]{3,2,1,0:T(8,128)}, f32[1,2,128,128]{3,2,1,0:T(8,128)}, f32[32,128]{1,0:T(8,128)}) custom-call(f32[32,128]{1,0:T(8,128)S(1)} %get-tuple-element.50.refs_0_, f32[128,128]{1,0:T(8,128)S(1)} %get-tuple-element.53.refs_1_, bf16[128,128]{1,0:T(8,128)(2,1)S(1)} %collective-permute-done.11.refs_2_, ...), custom_call_target="tpu_custom_call" | custom-call | tf_op jit(solution)/shard_map/finish/pallas_call | solution.py:400
  (4 shorter events, 0.1 us)
Async XLA Ops:
  0.6 0.8 %copy-start.5 = (bf16[1,2,128,128]{3,2,1,0:T(8,128)(2,1)S(1)}, bf16[1,2,128,128]{3,2,1,0:T(8,128)(2,1)}, u32[]{:S(2)}) copy-start(bf16[1,2,128,128]{3,2,1,0:T(8,128)(2,1)} %keys_ref.1) | copy-start | bytes 196612
  1.5 0.8 %copy-start.6 = (bf16[1,2,128,128]{3,2,1,0:T(8,128)(2,1)S(1)}, bf16[1,2,128,128]{3,2,1,0:T(8,128)(2,1)}, u32[]{:S(2)}) copy-start(bf16[1,2,128,128]{3,2,1,0:T(8,128)(2,1)} %values_ref.1) | copy-start | bytes 196612
  2.5 5.7 %collective-permute-start = (bf16[2,64,128]{2,1,0:T(8,128)(2,1)S(1)}, bf16[2,64,128]{2,1,0:T(8,128)(2,1)S(1)}, u32[]{:S(2)}, u32[]{:S(2)}) collective-permute-start(bf16[2,64,128]{2,1,0:T(8,128)(2,1)S(1)} %get-tuple-element.36), channel_id=1, source_target_pairs={{0,1},{1,0},{2,3},{3,2},{4,5},{5,4},{6,7},{7,6},{8,9},{9,8},{10,11... | collective-permute-start | bytes 98312 | tf_op jit(solution)/shard_map/ppermute | solution.py:411
  5.6 5.4 %collective-permute-start.1 = (bf16[2,64,128]{2,1,0:T(8,128)(2,1)S(1)}, bf16[2,64,128]{2,1,0:T(8,128)(2,1)S(1)}, u32[]{:S(2)}, u32[]{:S(2)}) collective-permute-start(bf16[2,64,128]{2,1,0:T(8,128)(2,1)S(1)} %get-tuple-element.37), channel_id=1, source_target_pairs={{0,2},{1,3},{2,0},{3,1},{4,6},{5,7},{6,4},{7,5},{8,10},{9,11},{10,... | collective-permute-start | bytes 98312 | tf_op jit(solution)/shard_map/ppermute | solution.py:411
  8.2 5.7 %collective-permute-start.2 = (bf16[2,64,128]{2,1,0:T(8,128)(2,1)S(1)}, bf16[2,64,128]{2,1,0:T(8,128)(2,1)S(1)}, u32[]{:S(2)}, u32[]{:S(2)}) collective-permute-start(bf16[2,64,128]{2,1,0:T(8,128)(2,1)S(1)} %get-tuple-element.37), channel_id=1, source_target_pairs={{0,3},{1,2},{2,1},{3,0},{4,7},{5,6},{6,5},{7,4},{8,11},{9,10},{10,... | collective-permute-start | bytes 98312 | tf_op jit(solution)/shard_map/ppermute | solution.py:411
  13.9 1.6 %copy-start.4 = (f32[1,4096]{1,0:T(1,128)S(1)}, f32[1,4096]{1,0:T(1,128)}, u32[]{:S(2)}) copy-start(f32[1,4096]{1,0:T(1,128)} %refs_1_.3) | copy-start | bytes 49156
  13.9 5.0 %collective-permute-start.3 = (bf16[4,2,64,128]{3,2,1,0:T(8,128)(2,1)S(1)}, bf16[4,2,64,128]{3,2,1,0:T(8,128)(2,1)S(1)}, u32[]{:S(2)}, u32[]{:S(2)}) collective-permute-start(bf16[4,2,64,128]{3,2,1,0:T(8,128)(2,1)S(1)} %pad_maximum_fusion.refs_6_), channel_id=1, source_target_pairs={{0,4},{4,0},{1,5},{5,1},{2,6},{6,2},{3,7},{7,3},{8,12},{12,8},{9,1... | collective-permute-start | bytes 393224 | tf_op jit(solution)/shard_map/ppermute | solution.py:414
  15.5 1.0 %copy-start = (bf16[1,2,32,4096]{3,2,1,0:T(8,128)(2,1)S(1)}, bf16[1,2,32,4096]{3,2,1,0:T(8,128)(2,1)}, u32[]{:S(2)}) copy-start(bf16[1,2,32,4096]{3,2,1,0:T(8,128)(2,1)} %refs_0_.9) | copy-start | bytes 1572868
  16.6 2.4 %copy-start.2 = (bf16[1,32,4096]{2,1,0:T(8,128)(2,1)S(1)}, bf16[1,32,4096]{2,1,0:T(8,128)(2,1)}, u32[]{:S(2)}) copy-start(bf16[1,32,4096]{2,1,0:T(8,128)(2,1)} %refs_3_.1) | copy-start | bytes 786436
  16.6 2.4 %copy-start.7 = (s32[5,8]{1,0:T(8,128)S(1)}, s32[5,8]{1,0:T(8,128)}, u32[]{:S(2)}) copy-start(s32[5,8]{1,0:T(8,128)} %refs_0_.6) | copy-start | bytes 484
  21.1 14.3 %collective-permute-start.4 = (bf16[32,4096]{1,0:T(8,128)(2,1)S(1)}, bf16[32,4096]{1,0:T(8,128)(2,1)S(1)}, u32[]{:S(2)}, u32[]{:S(2)}) collective-permute-start(bf16[32,4096]{1,0:T(8,128)(2,1)S(1)} %get-tuple-element.38.refs_6_), channel_id=1, source_target_pairs={{0,24},{8,0},{16,8},{24,16},{1,25},{9,1},{17,9},{25,17},{2,26},{10... | collective-permute-start | bytes 786440 | tf_op jit(solution)/shard_map/ppermute | solution.py:456
  21.2 4.5 %collective-permute-start.5 = (bf16[2,128,128]{2,1,0:T(8,128)(2,1)S(1)}, bf16[2,128,128]{2,1,0:T(8,128)(2,1)S(1)}, u32[]{:S(2)}, u32[]{:S(2)}) collective-permute-start(bf16[2,128,128]{2,1,0:T(8,128)(2,1)S(1)} %get-tuple-element.39.refs_0_), channel_id=1, source_target_pairs={{0,4},{4,0},{1,5},{5,1},{2,6},{6,2},{3,7},{7,3},{8,12},{12,8},{9,1... | collective-permute-start | bytes 196616 | tf_op jit(solution)/shard_map/ppermute | solution.py:414
  25.7 4.7 %collective-permute-start.6 = (bf16[2,2,64,128]{3,2,1,0:T(8,128)(2,1)S(1)}, bf16[2,2,64,128]{3,2,1,0:T(8,128)(2,1)S(1)}, u32[]{:S(2)}, u32[]{:S(2)}) collective-permute-start(bf16[2,2,64,128]{3,2,1,0:T(8,128)(2,1)S(1)} %get-tuple-element.40.refs_2_.refs_7_), channel_id=1, source_target_pairs={{0,1},{1,0},{2,3},{3,2},{4,5},{5,4},{6,7},{7,6},{8,9},{9,8},{10,11... | collective-permute-start | bytes 196616 | tf_op jit(solution)/shard_map/ppermute | solution.py:411
  25.8 9.1 %copy-start.1 = (bf16[1,2,32,4096]{3,2,1,0:T(8,128)(2,1)S(1)}, bf16[1,2,32,4096]{3,2,1,0:T(8,128)(2,1)}, u32[]{:S(2)}) copy-start(bf16[1,2,32,4096]{3,2,1,0:T(8,128)(2,1)} %refs_0_.9) | copy-start | bytes 1572868
  25.8 8.1 %collective-permute-start.7 = (bf16[2,2,64,128]{3,2,1,0:T(8,128)(2,1)S(1)}, bf16[2,2,64,128]{3,2,1,0:T(8,128)(2,1)S(1)}, u32[]{:S(2)}, u32[]{:S(2)}) collective-permute-start(bf16[2,2,64,128]{3,2,1,0:T(8,128)(2,1)S(1)} %get-tuple-element.41), channel_id=1, source_target_pairs={{0,2},{1,3},{2,0},{3,1},{4,6},{5,7},{6,4},{7,5},{8,10},{9,11},{10,... | collective-permute-start | bytes 196616 | tf_op jit(solution)/shard_map/ppermute | solution.py:411
  26.7 7.2 %collective-permute-start.8 = (bf16[2,2,64,128]{3,2,1,0:T(8,128)(2,1)S(1)}, bf16[2,2,64,128]{3,2,1,0:T(8,128)(2,1)S(1)}, u32[]{:S(2)}, u32[]{:S(2)}) collective-permute-start(bf16[2,2,64,128]{3,2,1,0:T(8,128)(2,1)S(1)} %get-tuple-element.41), channel_id=1, source_target_pairs={{0,3},{1,2},{2,1},{3,0},{4,7},{5,6},{6,5},{7,4},{8,11},{9,10},{10,... | collective-permute-start | bytes 196616 | tf_op jit(solution)/shard_map/ppermute | solution.py:411
  34.9 1.0 %copy-start.3 = (bf16[1,32,4096]{2,1,0:T(8,128)(2,1)S(1)}, bf16[1,32,4096]{2,1,0:T(8,128)(2,1)}, u32[]{:S(2)}) copy-start(bf16[1,32,4096]{2,1,0:T(8,128)(2,1)} %refs_4_.3) | copy-start | bytes 786436
  36.7 8.6 %collective-permute-start.9 = (bf16[576,128]{1,0:T(8,128)(2,1)S(1)}, bf16[576,128]{1,0:T(8,128)(2,1)S(1)}, u32[]{:S(2)}, u32[]{:S(2)}) collective-permute-start(bf16[576,128]{1,0:T(8,128)(2,1)S(1)} %get-tuple-element.48), channel_id=1, source_target_pairs={{0,4},{4,0},{1,5},{5,1},{2,6},{6,2},{3,7},{7,3},{8,12},{12,8},{9,1... | collective-permute-start | bytes 442376 | tf_op jit(solution)/shard_map/ppermute | solution.py:414
  38.3 5.0 %collective-permute-start.10 = (bf16[512,128]{1,0:T(8,128)(2,1)S(1)}, bf16[512,128]{1,0:T(8,128)(2,1)S(1)}, u32[]{:S(2)}, u32[]{:S(2)}) collective-permute-start(bf16[512,128]{1,0:T(8,128)(2,1)S(1)} %get-tuple-element.52), channel_id=1, source_target_pairs={{0,4},{4,0},{1,5},{5,1},{2,6},{6,2},{3,7},{7,3},{8,12},{12,8},{9,1... | collective-permute-start | bytes 393224 | tf_op jit(solution)/shard_map/ppermute | solution.py:414
  43.3 6.6 %collective-permute-start.11 = (bf16[128,128]{1,0:T(8,128)(2,1)S(1)}, bf16[128,128]{1,0:T(8,128)(2,1)S(1)}, u32[]{:S(2)}, u32[]{:S(2)}) collective-permute-start(bf16[128,128]{1,0:T(8,128)(2,1)S(1)} %get-tuple-element.54), channel_id=1, source_target_pairs={{0,1},{1,0},{2,3},{3,2},{4,5},{5,4},{6,7},{7,6},{8,9},{9,8},{10,11... | collective-permute-start | bytes 98312 | tf_op jit(solution)/shard_map/ppermute | solution.py:411
  45.3 10.3 %collective-permute-start.14 = (bf16[192,128]{1,0:T(8,128)(2,1)S(1)}, bf16[192,128]{1,0:T(8,128)(2,1)S(1)}, u32[]{:S(2)}, u32[]{:S(2)}) collective-permute-start(bf16[192,128]{1,0:T(8,128)(2,1)S(1)} %get-tuple-element.58), channel_id=1, source_target_pairs={{0,1},{1,0},{2,3},{3,2},{4,5},{5,4},{6,7},{7,6},{8,9},{9,8},{10,11... | collective-permute-start | bytes 147464 | tf_op jit(solution)/shard_map/ppermute | solution.py:411
  45.5 10.1 %collective-permute-start.15 = (bf16[192,128]{1,0:T(8,128)(2,1)S(1)}, bf16[192,128]{1,0:T(8,128)(2,1)S(1)}, u32[]{:S(2)}, u32[]{:S(2)}) collective-permute-start(bf16[192,128]{1,0:T(8,128)(2,1)S(1)} %get-tuple-element.59), channel_id=1, source_target_pairs={{0,2},{1,3},{2,0},{3,1},{4,6},{5,7},{6,4},{7,5},{8,10},{9,11},{10,... | collective-permute-start | bytes 147464 | tf_op jit(solution)/shard_map/ppermute | solution.py:411
  47.1 8.5 %collective-permute-start.16 = (bf16[192,128]{1,0:T(8,128)(2,1)S(1)}, bf16[192,128]{1,0:T(8,128)(2,1)S(1)}, u32[]{:S(2)}, u32[]{:S(2)}) collective-permute-start(bf16[192,128]{1,0:T(8,128)(2,1)S(1)} %get-tuple-element.60), channel_id=1, source_target_pairs={{0,3},{1,2},{2,1},{3,0},{4,7},{5,6},{6,5},{7,4},{8,11},{9,10},{10,... | collective-permute-start | bytes 147464 | tf_op jit(solution)/shard_map/ppermute | solution.py:411
  49.8 4.8 %collective-permute-start.12 = (bf16[128,128]{1,0:T(8,128)(2,1)S(1)}, bf16[128,128]{1,0:T(8,128)(2,1)S(1)}, u32[]{:S(2)}, u32[]{:S(2)}) collective-permute-start(bf16[128,128]{1,0:T(8,128)(2,1)S(1)} %get-tuple-element.55), channel_id=1, source_target_pairs={{0,2},{1,3},{2,0},{3,1},{4,6},{5,7},{6,4},{7,5},{8,10},{9,11},{10,... | collective-permute-start | bytes 98312 | tf_op jit(solution)/shard_map/ppermute | solution.py:411
  49.9 5.7 %collective-permute-start.13 = (bf16[128,128]{1,0:T(8,128)(2,1)S(1)}, bf16[128,128]{1,0:T(8,128)(2,1)S(1)}, u32[]{:S(2)}, u32[]{:S(2)}) collective-permute-start(bf16[128,128]{1,0:T(8,128)(2,1)S(1)} %get-tuple-element.56), channel_id=1, source_target_pairs={{0,3},{1,2},{2,1},{3,0},{4,7},{5,6},{6,5},{7,4},{8,11},{9,10},{10,... | collective-permute-start | bytes 98312 | tf_op jit(solution)/shard_map/ppermute | solution.py:411

commit v3 on v2

v3 whole, which is shorter than its diff:
```python
import functools

import jax
import jax.numpy as jnp
from jax import lax
from jax.experimental import pallas as pl
from jax.experimental.pallas import tpu as pltpu
from jax.sharding import PartitionSpec as P

HD = 128
EPSILON = 1e-05
FILL = -1e30
SCALE = HD ** (-0.5)
F32 = jnp.float32
BF16 = jnp.bfloat16

NT = (((1,), (1,)), ((), ()))
NN = (((1,), (0,)), ((), ()))
TN = (((0,), (0,)), ((), ()))


def dot(a, b, dims):
    return lax.dot_general(a, b, dims, preferred_element_type=F32)


def split_two(value):
    high = value.astype(BF16)
    low = (value - high.astype(F32)).astype(BF16)
    return high, low


def joined(high, low):
    return high.astype(F32) + low.astype(F32)


def in_order(values, owners):
    total = None
    for owner in range(len(values)):
        term = jnp.where(owners[0] == owner, values[0], 0.0)
        for value, whose in zip(values[1:], owners[1:]):
            term = jnp.where(whose == owner, value, term)
        total = term if total is None else total + term
    return total


def pack_kernel(tp_count, half, keys_ref, values_ref, own_ref, other_ref, sems):
    parity = lax.axis_index("tp") // (tp_count // 2)
    own_first = pl.multiple_of(parity * half, half)
    other_first = pl.multiple_of((1 - parity) * half, half)
    copies = []
    for kind, ref in enumerate((keys_ref, values_ref)):
        for tick in range(keys_ref.shape[1]):
            for place, (first, target) in enumerate(
                ((own_first, own_ref), (other_first, other_ref))
            ):
                source = ref.at[0, tick, pl.ds(first, half), :]
                copies.append(
                    pltpu.make_async_copy(
                        source, target.at[tick, kind], sems.at[kind, tick, place]
                    )
                )
    for copy in copies:
        copy.start()
    for copy in copies:
        copy.wait()


def norm_kernel(x_ref, gain_ref, query_ref, inverse_ref):
    _, ticks, rows, columns = x_ref.shape
    for tick in range(ticks):
        squares = jnp.zeros((rows, HD), F32)
        for first in range(0, columns, HD):
            part = x_ref[0, tick, :, first : first + HD].astype(F32)
            squares = squares + part * part
        mean = jnp.sum(squares, axis=1, keepdims=True) * (1.0 / columns)
        inverse = jnp.broadcast_to(lax.rsqrt(mean + EPSILON), (rows, HD))
        inverse_ref[tick] = inverse
        for first in range(0, columns, HD):
            here = slice(first, first + HD)
            normed = x_ref[0, tick, :, here].astype(F32) * inverse
            query_ref[tick, :, here] = (normed * gain_ref[:, here]).astype(BF16)


class Group:
    def __init__(self, sizes, turn):
        self.rows, self.group = sizes[0], sizes[4]
        width = self.group * HD
        self.head_group = lax.axis_index("tp") ^ turn
        self.first = pl.multiple_of(self.head_group * width, width)

    def head(self, index):
        return pl.ds(self.first + index * HD, HD)

    def stacked(self, load):
        return jnp.concatenate([load(self.head(index)) for index in range(self.group)], axis=0)

    def unstacked(self, value):
        return [value[index * self.rows : (index + 1) * self.rows] for index in range(self.group)]


def arriving_from(refs):
    if len(refs) == 1:
        return lambda where: refs[0][0, :, where]
    last = lax.axis_index("pipe") == lax.axis_size("pipe") - 1
    return lambda where: jnp.where(last, refs[1][0, :, where], refs[0][:, where])


def visible_keys(sizes, tick, doc_ref):
    rows, half, cycle, tp_count, group, columns = sizes
    cycle_place = lax.axis_index("ctx")
    tp_place = lax.axis_index("tp")
    parity = tp_place // (tp_count // 2)
    stacked = group * rows

    def section_first(owner):
        return half * jnp.where(parity == 0, owner, 2 * cycle - 1 - owner)

    row_first = section_first(cycle_place) + (tp_place % (tp_count // 2)) * rows
    query_pos = row_first + (lax.broadcasted_iota(jnp.int32, (1, stacked), 1) & (rows - 1))
    key_place = lax.broadcasted_iota(jnp.int32, (cycle * half, 1), 0)
    key_pos = key_place + section_first(cycle_place)
    for turn in range(1, cycle):
        first = section_first((cycle_place - turn + cycle) % cycle)
        key_pos = jnp.where(key_place >= turn * half, key_place - turn * half + first, key_pos)
    micro = lax.axis_index("pipe") + tick
    closing = jnp.int32(0)
    query_start = jnp.zeros((1, stacked), jnp.int32)
    for doc in range(doc_ref.shape[1]):
        length = doc_ref[micro, doc]
        closing = closing + length
        query_start = query_start + jnp.where(closing <= query_pos, length, 0)
    return (key_pos <= query_pos) & (key_pos >= query_start)


def probabilities(visible, products):
    scores = jnp.where(visible, SCALE * products, FILL)
    weights = jnp.exp(scores - jnp.max(scores, axis=0, keepdims=True))
    return weights * (1.0 / jnp.sum(weights, axis=0, keepdims=True))


def score_grads(probs, prob_grad):
    row_term = jnp.sum(probs * prob_grad, axis=0, keepdims=True)
    return (probs * (prob_grad - row_term)).astype(BF16)


class Keys:
    def __init__(self, sizes, tick, refs):
        self.near_count = sizes[3] // 2
        self.cycle = sizes[2]
        self.tick = tick
        self.refs = refs

    def __call__(self, turn, kind):
        near, far = turn % self.near_count, turn // self.near_count
        parts = [self.refs[near][self.tick, far, kind]]
        for step in range(1, self.cycle):
            if self.tick:
                parts.append(self.refs[self.near_count + step - 1][near, far, kind])
            else:
                parts.append(self.refs[step * self.near_count + near][far, kind])
        return jnp.concatenate(parts, axis=0)


def place_of(sizes, far, kind):
    half = sizes[1]
    return slice((far * 2 + kind) * half, (far * 2 + kind + 1) * half)


def gain_terms(columns_of, low_parts, normed_of, gain_rows_ref):
    rows = []
    for index, low in enumerate(low_parts):
        term = low.astype(F32) * normed_of(columns_of.head(index))
        rows.append(jnp.sum(term, axis=0, keepdims=True))
    group = columns_of.group
    place = pl.ds(pl.multiple_of(columns_of.head_group * group, group), group)
    gain_rows_ref[place, :] = jnp.concatenate(rows, axis=0)


def write_input_grads(sizes, tick, x_ref, gain_ref, inverse, query_grad_ref, arriving, write):
    rows, columns = sizes[0], sizes[5]
    coupled = jnp.zeros((rows, HD), F32)
    for first in range(0, columns, HD):
        here = slice(first, first + HD)
        scaled = query_grad_ref[:, here].astype(F32) * gain_ref[:, here]
        coupled = coupled + scaled * (x_ref[0, tick, :, here].astype(F32) * inverse)
    coupling = jnp.sum(coupled, axis=1, keepdims=True) * (1.0 / columns)
    for first in range(0, columns, HD):
        here = slice(first, first + HD)
        scaled = query_grad_ref[:, here].astype(F32) * gain_ref[:, here]
        normed = x_ref[0, tick, :, here].astype(F32) * inverse
        result = arriving(here).astype(F32) + inverse * (scaled - normed * coupling)
        write(here, result.astype(BF16))


def first_rows_kernel(sizes, kv_count, *refs):
    tp_count = sizes[3]
    turns = range(tp_count)
    doc_ref, x_ref, gain_ref, query_ref, inverse_ref, waiting_ref = refs[:6]
    keys = Keys(sizes, 0, refs[6 : 6 + kv_count])
    input_grad_ref, query_grad_ref, dscore_ref, probs_ref = refs[6 + kv_count :]
    visible = visible_keys(sizes, 0, doc_ref)
    arriving = arriving_from([waiting_ref])
    columns_of = [Group(sizes, turn) for turn in turns]
    scores, prob_grads = [], []
    for turn in turns:
        query = columns_of[turn].stacked(lambda where: query_ref[0, :, where])
        scores.append(dot(keys(turn, 0), query, NT))
        grad = columns_of[turn].stacked(arriving)
        prob_grads.append(dot(keys(turn, 1), grad, NT))
    dscores = []
    for turn in turns:
        probs = probabilities(visible, scores[turn])
        dscores.append(score_grads(probs, prob_grads[turn]))
        dscore_ref[turn] = dscores[turn]
        probs_ref[turn] = probs.astype(BF16)
    for turn in turns:
        query_grad = (SCALE * dot(dscores[turn], keys(turn, 0), TN)).astype(BF16)
        for index, low in enumerate(columns_of[turn].unstacked(query_grad)):
            query_grad_ref[:, columns_of[turn].head(index)] = low

    def write(here, result):
        input_grad_ref[:, here] = result

    write_input_grads(
        sizes, 0, x_ref, gain_ref, inverse_ref[0], query_grad_ref, arriving, write
    )


def first_keys_kernel(sizes, *refs):
    half, cycle, tp_count = sizes[1:4]
    x_ref, query_ref, inverse_ref, waiting_ref, query_grad_ref, dscore_ref, probs_ref = refs[:7]
    gain_rows_ref, own_ref = refs[7:9]
    send_refs = refs[9:]
    arriving = arriving_from([waiting_ref])
    inverse = inverse_ref[0]
    for turn in range(tp_count):
        columns_of = Group(sizes, turn)
        query = columns_of.stacked(lambda where: query_ref[0, :, where])
        grad = columns_of.stacked(arriving)
        near, far = turn % (tp_count // 2), turn // (tp_count // 2)
        for kind, part in enumerate(
            (SCALE * dot(dscore_ref[turn], query, NN), dot(probs_ref[turn], grad, NN))
        ):
            here = place_of(sizes, far, kind)
            own_ref[near, here, :] = part[:half]
            for step, ref in enumerate(send_refs, 1):
                ref[near, here, :] = part[step * half : (step + 1) * half].astype(BF16)
        gain_terms(
            columns_of,
            [query_grad_ref[:, columns_of.head(index)] for index in range(columns_of.group)],
            lambda where: x_ref[0, 0, :, where].astype(F32) * inverse,
            gain_rows_ref,
        )


def second_probs_kernel(sizes, kv_count, *refs):
    turns = range(sizes[3])
    doc_ref, query_ref = refs[:2]
    keys, probs_ref = Keys(sizes, 1, refs[2 : 2 + kv_count]), refs[2 + kv_count]
    visible = visible_keys(sizes, 1, doc_ref)
    scores = []
    for turn in turns:
        query = Group(sizes, turn).stacked(lambda where: query_ref[1, :, where])
        scores.append(dot(keys(turn, 0), query, NT))
    for turn in turns:
        probs_ref[turn] = probabilities(visible, scores[turn])


def second_keys_kernel(sizes, kv_count, *refs):
    half, cycle, tp_count = sizes[1:4]
    turns = range(tp_count)
    near_count = tp_count // 2
    x_ref, query_ref, inverse_ref, arrived_ref, output_ref, probs_ref, before_ref = refs[:7]
    keys, refs = Keys(sizes, 1, refs[7 : 7 + kv_count]), refs[7 + kv_count :]
    first_refs, refs = refs[:cycle], refs[cycle:]
    query_grad_ref, gain_rows_ref, own_ref, own_first_ref = refs[:4]
    message_refs, gain_scratch = refs[4:-1], refs[-1]
    arriving = arriving_from([arrived_ref, output_ref])
    inverse = inverse_ref[1]
    columns_of = [Group(sizes, turn) for turn in turns]
    grads = [columns_of[turn].stacked(arriving) for turn in turns]
    prob_grads = [dot(keys(turn, 1), grads[turn], NT) for turn in turns]
    value_grads = [dot(probs_ref[turn].astype(BF16), grads[turn], NN) for turn in turns]
    dscores = [score_grads(probs_ref[turn], prob_grads[turn]) for turn in turns]
    query_grads = [
        (SCALE * dot(dscores[turn], keys(turn, 0), TN)).astype(BF16) for turn in turns
    ]
    for turn in turns:
        query = columns_of[turn].stacked(lambda where: query_ref[1, :, where])
        key_grad = SCALE * dot(dscores[turn], query, NN)
        near, far = turn % near_count, turn // near_count
        for kind, part in enumerate((key_grad, value_grads[turn])):
            here = place_of(sizes, far, kind)
            for step in range(cycle):
                piece = part[step * half : (step + 1) * half]
                if step == 0 and near == 0:
                    own_ref[here, :] = piece
                else:
                    message_refs[step * near_count + near - 1][here, :] = piece.astype(BF16)
    for turn in turns:
        low_parts = columns_of[turn].unstacked(query_grads[turn])
        for index, low in enumerate(low_parts):
            query_grad_ref[:, columns_of[turn].head(index)] = low
        gain_terms(
            columns_of[turn],
            low_parts,
            lambda where: x_ref[0, 1, :, where].astype(F32) * inverse,
            gain_scratch,
        )
    gain_rows = gain_scratch[...] + before_ref[...]
    gain_rows_ref[...] = gain_rows
    high, low = split_two(gain_rows)
    count = high.shape[0]
    begin = own_ref.shape[0]
    for ref in message_refs:
        ref[begin : begin + count, :] = high
        ref[begin + count : begin + 2 * count, :] = low
    begin += 2 * count
    for near in range(near_count):
        total = first_refs[0][near]
        for ref in first_refs[1:]:
            total = total + ref[near].astype(F32)
        if near == 0:
            own_first_ref[...] = total
        else:
            message_refs[near - 1][begin : begin + total.shape[0], :] = total.astype(BF16)


def second_rows_kernel(sizes, *refs):
    x_ref, gain_ref, inverse_ref, arrived_ref, output_ref, query_grad_ref, first_ref = refs[:7]
    input_grads_ref = refs[7]
    input_grads_ref[0, 0] = first_ref[...]

    def write(here, result):
        input_grads_ref[0, 1, :, here] = result

    arriving = arriving_from([arrived_ref, output_ref])
    write_input_grads(
        sizes, 1, x_ref, gain_ref, inverse_ref[1], query_grad_ref, arriving, write
    )


def near_sum_kernel(sizes, *refs):
    rows, half, cycle, tp_count, group, columns = sizes
    near_count = tp_count // 2
    members = cycle * near_count
    own_ref, own_first_ref, gain_ref = refs[:3]
    message_refs = refs[3 : 3 + members - 1]
    keep_ref, gain_sum_ref, send_ref = refs[3 + members - 1 :]
    block = 2 * half
    size = 2 * block
    count = gain_ref.shape[0]
    begin = size + 2 * count
    for tick in range(2):
        for far in range(2):
            here = slice(far * block, (far + 1) * block)
            if tick:
                total = own_ref[here, :]
                for ref in message_refs:
                    total = total + ref[here, :].astype(F32)
            else:
                total = own_first_ref[here, :]
                for ref in message_refs[: near_count - 1]:
                    total = total + ref[begin + far * block : begin + (far + 1) * block, :].astype(F32)
            target = slice(tick * block, (tick + 1) * block)
            if far:
                send_ref[target, :] = total.astype(BF16)
            else:
                keep_ref[target, :] = total
    cycle_place = lax.axis_index("ctx")
    near_place = lax.axis_index("tp") % near_count
    values = [joined(*split_two(gain_ref[...]))]
    owners = [cycle_place * near_count + near_place]
    for place, ref in enumerate(message_refs, 1):
        step, near = place // near_count, place % near_count
        values.append(joined(ref[size : size + count, :], ref[size + count : size + 2 * count, :]))
        owners.append(((cycle_place + step) % cycle) * near_count + (near_place ^ near))
    gain = in_order(values, owners)
    gain_sum_ref[...] = gain
    high, low = split_two(gain)
    send_ref[size : size + count, :] = high
    send_ref[size + count : size + 2 * count, :] = low


def finish_kernel(sizes, keep_ref, gain_ref, receive_ref, key_ref, value_ref, gain_out_ref):
    rows, half, cycle, tp_count, group, columns = sizes
    parity = lax.axis_index("tp") // (tp_count // 2)
    block = 2 * half
    for tick in range(2):
        for kind, out in enumerate((key_ref, value_ref)):
            here = slice(tick * block + kind * half, tick * block + (kind + 1) * half)
            own_first = pl.multiple_of(parity * half, half)
            other_first = pl.multiple_of((1 - parity) * half, half)
            out[0, tick, pl.ds(own_first, half), :] = keep_ref[here, :]
            out[0, tick, pl.ds(other_first, half), :] = receive_ref[here, :].astype(F32)
    count = gain_ref.shape[0]
    size = 2 * block
    own = joined(*split_two(gain_ref[...]))
    other = joined(receive_ref[size : size + count, :], receive_ref[size + count :, :])
    gain_out_ref[...] = own + other


def shape(dims, dtype):
    return jax.ShapeDtypeStruct(dims, dtype)


def on_device(segment_inputs, keys, values, norm_gain, waiting_grads, output_grads, doc_lengths):
    cycle = lax.axis_size("ctx")
    tp_count = lax.axis_size("tp")
    pipe_count = lax.axis_size("pipe")
    _, ticks, rows, columns = segment_inputs.shape
    half = keys.shape[2] // 2
    group = columns // (tp_count * HD)
    gain_count = columns // HD
    sizes = (rows, half, cycle, tp_count, group, columns)
    block = 2 * half
    key_count = cycle * half
    stacked = group * rows
    score_bytes = key_count * stacked * 4
    usual_limit = min(56 << 20, (12 << 20) + 20 * score_bytes)

    def call(
        kernel, name, operands, out_shape, memory=pltpu.VMEM, scratch=(), scalars=0, limit=None
    ):
        in_specs = [pl.BlockSpec(memory_space=pltpu.SMEM)] * scalars
        in_specs += [pl.BlockSpec(memory_space=memory)] * (len(operands) - scalars)
        return pl.pallas_call(
            kernel,
            out_shape=out_shape,
            in_specs=in_specs,
            out_specs=[pl.BlockSpec(memory_space=pltpu.VMEM)] * len(out_shape),
            scratch_shapes=scratch,
            compiler_params=pltpu.CompilerParams(vmem_limit_bytes=limit or usual_limit),
            name=name,
        )(*operands)

    near_count = tp_count // 2

    def to_near(value, step, near):
        if step == 0:
            return lax.ppermute(value, "tp", [(i, i ^ near) for i in range(tp_count)])
        if near == 0:
            return lax.ppermute(value, "ctx", [(i, (i + step) % cycle) for i in range(cycle)])
        pairs = [
            (c * tp_count + t, ((c + step) % cycle) * tp_count + (t ^ near))
            for c in range(cycle)
            for t in range(tp_count)
        ]
        return lax.ppermute(value, ("ctx", "tp"), pairs)

    def to_far(value):
        return lax.ppermute(value, "tp", [(i, i ^ near_count) for i in range(tp_count)])

    sections = shape((ticks, 2, half, HD), BF16)
    own_kv, other_kv = call(
        functools.partial(pack_kernel, tp_count, half),
        "pack_kv",
        (keys, values),
        [sections, sections],
        memory=pl.ANY,
        scratch=[pltpu.SemaphoreType.DMA((2, ticks, 2))],
        limit=60 << 20,
    )
    pair = jnp.stack([own_kv, to_far(other_kv)], axis=1)
    near_kv = [pair] + [to_near(pair, 0, near) for near in range(1, near_count)]
    kv_first = near_kv + [
        to_near(pair[0], step, near) for step in range(1, cycle) for near in range(near_count)
    ]
    later = jnp.stack([part[1] for part in near_kv])
    kv_second = near_kv + [to_near(later, step, 0) for step in range(1, cycle)]
    queries, inverse = call(
        norm_kernel,
        "norm",
        (segment_inputs, norm_gain),
        [shape((ticks, rows, columns), BF16), shape((ticks, rows, HD), F32)],
    )

    low_rows = shape((rows, columns), BF16)
    low_scores = shape((tp_count, key_count, stacked), BF16)
    input_grad_first, query_grad_first, dscore_first, probs_first = call(
        functools.partial(first_rows_kernel, sizes, len(kv_first)),
        "first_rows",
        (doc_lengths, segment_inputs, norm_gain, queries, inverse, waiting_grads, *kv_first),
        [low_rows, low_rows, low_scores, low_scores],
        scalars=1,
    )
    arrived = lax.ppermute(
        input_grad_first, "pipe", [(i, (i - 1) % pipe_count) for i in range(pipe_count)]
    )
    gain_shape = shape((gain_count, HD), F32)
    first_sums = (near_count, 2 * block, HD)
    gain_first, *sums_first = call(
        functools.partial(first_keys_kernel, sizes),
        "first_keys",
        (
            segment_inputs,
            queries,
            inverse,
            waiting_grads,
            query_grad_first,
            dscore_first,
            probs_first,
        ),
        [gain_shape, shape(first_sums, F32)] + [shape(first_sums, BF16)] * (cycle - 1),
    )
    sums_first = sums_first[:1] + [
        to_near(value, -step, 0) for step, value in enumerate(sums_first[1:], 1)
    ]
    (probs_second,) = call(
        functools.partial(second_probs_kernel, sizes, len(kv_second)),
        "second_probs",
        (doc_lengths, queries, *kv_second),
        [shape((tp_count, key_count, stacked), F32)],
        scalars=1,
    )
    places = [(step, near) for step in range(cycle) for near in range(near_count)][1:]
    pair_rows = 2 * block
    own_shape = shape((pair_rows, HD), F32)
    messages = [
        shape((pair_rows * (2 if step == 0 else 1) + 2 * gain_count, HD), BF16)
        for step, near in places
    ]
    query_grad_second, gain_rows, own_second, own_first, *sends = call(
        functools.partial(second_keys_kernel, sizes, len(kv_second)),
        "second_keys",
        (
            segment_inputs,
            queries,
            inverse,
            arrived,
            output_grads,
            probs_second,
            gain_first,
            *kv_second,
            *sums_first,
        ),
        [low_rows, gain_shape, own_shape, own_shape] + messages,
        scratch=[pltpu.VMEM((gain_count, HD), F32)],
    )
    received = [to_near(value, -step, near) for value, (step, near) in zip(sends, places)]
    (input_grads,) = call(
        functools.partial(second_rows_kernel, sizes),
        "second_rows",
        (
            segment_inputs,
            norm_gain,
            inverse,
            arrived,
            output_grads,
            query_grad_second,
            input_grad_first,
        ),
        [shape((1, ticks, rows, columns), BF16)],
    )
    keep, gain_sum, send = call(
        functools.partial(near_sum_kernel, sizes),
        "near_sum",
        (own_second, own_first, gain_rows, *received),
        [own_shape, gain_shape, shape((pair_rows + 2 * gain_count, HD), BF16)],
    )
    grads_shape = shape((1, ticks, block, HD), F32)
    key_grads, value_grads, gain_grads = call(
        functools.partial(finish_kernel, sizes),
        "finish",
        (keep, gain_sum, to_far(send)),
        [grads_shape, grads_shape, gain_shape],
    )
    return input_grads, key_grads, value_grads, gain_grads.reshape(1, columns)


def solution(mesh):
    in_specs = (
        P("pipe", None, ("ctx", "tp"), None),
        P("pipe", None, "ctx", "tp"),
        P("pipe", None, "ctx", "tp"),
        P("pipe", None),
        P("pipe", ("ctx", "tp"), None),
        P(None, ("ctx", "tp"), None),
        P(),
    )
    out_specs = (
        P("pipe", None, ("ctx", "tp"), None),
        P("pipe", None, "ctx", "tp"),
        P("pipe", None, "ctx", "tp"),
        P("pipe", None),
    )
    return jax.shard_map(
        on_device, mesh=mesh, in_specs=in_specs, out_specs=out_specs, check_vma=False
    )
```

time: 56.7 us -> 45.3 us (0.80)
  starting transfers between devices: 23.4 us -> 16.1 us
  waiting for transfers between devices: 22.2 us -> 19 us
  local copies, waits for them, and re-layouts: 3.18 us -> 0.03 us
  other arithmetic: 0.02 us -> 1.66 us
  Pallas kernels: 6.78 us -> 7.52 us
    ppermute x16 -> x10, starting transfers between devices: 23.4 us -> 16.1 us  [the longest x2 6.74 us: to_far(): lax.ppermute(value, 'tp', [(i, i ^ near_count) for i in range(tp_count)])]
    ppermute x16 -> x10, waiting for transfers between devices: 22.2 us -> 19 us  [the longest x4 8.43 us: to_near(): lax.ppermute(value, 'ctx', [(i, (i + step) % cycle) for i in range(cycle)])]
    unnamed x16 -> x10, local copies, waits for them, and re-layouts: 3.18 us -> 0.03 us
    another operation x1 -> x3, other arithmetic: 0.02 us -> 1.66 us  [the longest x2 1.64 us: on_device(): pair = jnp.stack([own_kv, to_far(other_kv)], axis=1)]
    pallas_call x11 -> x9, Pallas kernels: 6.78 us -> 7.52 us  [call(): pl.pallas_call(kernel, out_shape=out_shape, in_specs=in_specs, out_specs=...]
  transfers between devices with their start and end apart: 17 -> 11, of which waited for: 9 -> 8; matrix products, arithmetic and copies ran while one was open for 0% -> 2% of each run, Pallas kernels for 5% -> 6%
where the time goes in v3:
time: 45.3 us; the launch traced here: 45.1 us
  waiting for transfers between devices  19 us (42%)
  starting transfers between devices  16.1 us (36%)
  Pallas kernels  7.52 us (17%)
  other arithmetic  1.66 us (4%)
  between operations  0.75 us (2%)
    ppermute x4, waiting for transfers between devices, to_near(): lax.ppermute(value, 'ctx', [(i, (i + step) % cycle) for i in range(cycle)])  8.43 us
    pallas_call x9, Pallas kernels, call(): pl.pallas_call(kernel, out_shape=out_shape, in_specs=in_specs, out_specs=...  7.52 us
    ppermute x2, starting transfers between devices, to_far(): lax.ppermute(value, 'tp', [(i, i ^ near_count) for i in range(tp_count)])  6.74 us
    ppermute x2, waiting for transfers between devices, to_far(): lax.ppermute(value, 'tp', [(i, i ^ near_count) for i in range(tp_count)])  6.38 us
    ppermute x2, starting transfers between devices, to_near(): return lax.ppermute(value, ('ctx', 'tp'), pairs)  4.39 us
    ppermute x2, waiting for transfers between devices, to_near(): return lax.ppermute(value, ('ctx', 'tp'), pairs)  4.15 us
    ppermute x4, starting transfers between devices, to_near(): lax.ppermute(value, 'ctx', [(i, (i + step) % cycle) for i in range(cycle)])  3.67 us
    another operation x2, other arithmetic, on_device(): pair = jnp.stack([own_kv, to_far(other_kv)], axis=1)  1.64 us
  transfers between devices with their start and end apart: 11, of which 8 were waited for; matrix products, arithmetic and copies ran while one was open for 2% of the time, Pallas kernels for 6%

profile of v3, /device:TPU:0, one launch (start us, length us, event | category | flops | bytes accessed | tf_op | source)
XLA Modules:
  0.0 45.1 jit_solution(13066000624580050949)
XLA Ops:
  0.6 0.0 copy-start
  0.6 1.6 %pack_kv.1 = (bf16[2,2,64,128]{3,2,1,0:T(8,128)(2,1)}, bf16[2,2,64,128]{3,2,1,0:T(8,128)(2,1)}) custom-call(bf16[1,2,128,128]{3,2,1,0:T(8,128)(2,1)} %keys_ref.1, bf16[1,2,128,128]{3,2,1,0:T(8,128)(2,1)} %values_ref.1), custom_call_target="tpu_custom_call" | custom-call | tf_op jit(solution)/shard_map/pack_kv/pallas_call | solution.py:427
  2.3 4.1 %collective-permute-start = (bf16[2,2,64,128]{3,2,1,0:T(8,128)(2,1)}, bf16[2,2,64,128]{3,2,1,0:T(8,128)(2,1)S(1)}, u32[]{:S(2)}, u32[]{:S(2)}) collective-permute-start(bf16[2,2,64,128]{3,2,1,0:T(8,128)(2,1)} %get-tuple-element.31), channel_id=1, source_target_pairs={{0,2},{1,3},{2,0},{3,1},{4,6},{5,7},{6,4},{7,5},{8,10},{9,11},{10,... | collective-permute-start | bytes 196616 | tf_op jit(solution)/shard_map/ppermute | solution.py:452
  6.4 3.9 %collective-permute-done = bf16[2,2,64,128]{3,2,1,0:T(8,128)(2,1)S(1)} collective-permute-done((bf16[2,2,64,128]{3,2,1,0:T(8,128)(2,1)}, bf16[2,2,64,128]{3,2,1,0:T(8,128)(2,1)S(1)}, u32[]{:S(2)}, u32[]{:S(2)}) %collective-permute-start) | collective-permute-done | bytes 65568 | tf_op jit(solution)/shard_map/ppermute | solution.py:452
  10.2 0.9 %pad_maximum_fusion.refs_6_.refs_2_.refs_7_ = bf16[2,2,2,64,128]{4,3,2,1,0:T(8,128)(2,1)S(1)} fusion(bf16[2,1,2,64,128]{4,3,2,1,0:T(8,128)(2,1)S(1)} %bitcast.7, bf16[2,1,2,64,128]{4,3,2,1,0:T(8,128)(2,1)} %bitcast.5), kind=kLoop, calls=%fused_computation.2 | loop fusion | flops 65536 | bytes 262144 | tf_op jit(solution)/shard_map/stack | solution.py:464
  11.1 0.0 copy-start.3
  11.1 0.7 %collective-permute-start.1 = (bf16[2,2,2,64,128]{4,3,2,1,0:T(8,128)(2,1)S(1)}, bf16[2,2,2,64,128]{4,3,2,1,0:T(8,128)(2,1)S(1)}, u32[]{:S(2)}, u32[]{:S(2)}) collective-permute-start(bf16[2,2,2,64,128]{4,3,2,1,0:T(8,128)(2,1)S(1)} %pad_maximum_fusion.refs_6_.refs_2_.refs_7_), channel_id=1, source_target_pairs={{0,1},{1,0},{2,3},{3,2},{4,5},{5,4},{6,7},{7,6},{8,9},{9,8},{10,11... | collective-permute-start | bytes 393224 | tf_op jit(solution)/shard_map/ppermute | solution.py:441
  11.8 0.8 %fusion.2 = (bf16[1,2,2,64,128]{4,3,2,1,0:T(8,128)(2,1)S(1)}, bf16[2,2,64,128]{3,2,1,0:T(8,128)(2,1)S(1)}) fusion(bf16[2,1,2,64,128]{4,3,2,1,0:T(8,128)(2,1)} %bitcast.6, bf16[2,1,2,64,128]{4,3,2,1,0:T(8,128)(2,1)S(1)} %bitcast.8), kind=kLoop, calls=%fused_computation.8 | loop fusion | flops 65536 | bytes 262144 | tf_op jit(solution)/shard_map/stack | solution.py:464
  12.6 0.0 copy-start.2
  12.6 2.6 %collective-permute-start.3 = (bf16[2,2,64,128]{3,2,1,0:T(8,128)(2,1)S(1)}, bf16[2,2,64,128]{3,2,1,0:T(8,128)(2,1)S(1)}, u32[]{:S(2)}, u32[]{:S(2)}) collective-permute-start(bf16[2,2,64,128]{3,2,1,0:T(8,128)(2,1)S(1)} %get-tuple-element.53), channel_id=1, source_target_pairs={{0,5},{1,4},{2,7},{3,6},{4,1},{5,0},{6,3},{7,2},{8,13},{9,12},{10,... | collective-permute-start | bytes 196616 | tf_op jit(solution)/shard_map/ppermute | solution.py:449
  15.2 0.3 collective-permute-start.2
  15.5 0.0 copy-done
  15.5 0.0 copy-done.3
  15.5 0.0 copy-start.4
  15.5 0.3 norm.1
  15.8 2.5 %collective-permute-done.3.refs_9_ = bf16[2,2,64,128]{3,2,1,0:T(8,128)(2,1)S(1)} collective-permute-done((bf16[2,2,64,128]{3,2,1,0:T(8,128)(2,1)S(1)}, bf16[2,2,64,128]{3,2,1,0:T(8,128)(2,1)S(1)}, u32[]{:S(2)}, u32[]{:S(2)}) %collective-permute-start.3) | collective-permute-done | bytes 65568 | tf_op jit(solution)/shard_map/ppermute | solution.py:449
  18.3 1.2 %collective-permute-done.2.refs_8_ = bf16[2,2,64,128]{3,2,1,0:T(8,128)(2,1)S(1)} collective-permute-done((bf16[2,2,64,128]{3,2,1,0:T(8,128)(2,1)S(1)}, bf16[2,2,64,128]{3,2,1,0:T(8,128)(2,1)S(1)}, u32[]{:S(2)}, u32[]{:S(2)}) %collective-permute-start.2) | collective-permute-done | bytes 65568 | tf_op jit(solution)/shard_map/ppermute | solution.py:443
  19.5 0.0 collective-permute-done.1.refs_7_.refs_3_.refs_8_
  19.5 0.0 copy-done.2
  19.5 0.0 copy-done.4
  19.5 1.6 %first_rows.1 = (bf16[32,4096]{1,0:T(8,128)(2,1)S(1)}, bf16[32,4096]{1,0:T(8,128)(2,1)S(1)}, bf16[4,128,256]{2,1,0:T(8,128)(2,1)S(1)}, bf16[4,128,256]{2,1,0:T(8,128)(2,1)S(1)}) custom-call(s32[5,8]{1,0:T(8,128)S(1)} %copy-done.4, bf16[1,2,32,4096]{3,2,1,0:T(8,128)(2,1)S(1)} %copy-done, f32[1,4096]{1,0:T(1,128)S(1)} %copy-done.3, ...), custom_call_target="tpu_custom_call" | custom-call | tf_op jit(solution)/shard_map/first_rows/pallas_call | solution.py:427
  21.1 0.1 collective-permute-start.4
  21.2 0.7 %collective-permute-start.5 = (bf16[2,2,2,64,128]{4,3,2,1,0:T(8,128)(2,1)S(1)}, bf16[2,2,2,64,128]{4,3,2,1,0:T(8,128)(2,1)S(1)}, u32[]{:S(2)}, u32[]{:S(2)}) collective-permute-start(bf16[2,2,2,64,128]{4,3,2,1,0:T(8,128)(2,1)S(1)} %pad_maximum_fusion.1), channel_id=1, source_target_pairs={{0,4},{4,0},{1,5},{5,1},{2,6},{6,2},{3,7},{7,3},{8,12},{12,8},{9,1... | collective-permute-start | bytes 393224 | tf_op jit(solution)/shard_map/ppermute | solution.py:443
  21.9 0.5 %first_keys.1 = (f32[32,128]{1,0:T(8,128)S(1)}, f32[2,256,128]{2,1,0:T(8,128)S(1)}, bf16[2,256,128]{2,1,0:T(8,128)(2,1)S(1)}) custom-call(bf16[1,2,32,4096]{3,2,1,0:T(8,128)(2,1)S(1)} %copy-done, bf16[2,32,4096]{2,1,0:T(8,128)(2,1)S(1)} %get-tuple-element.29.refs_3_.refs_1_, f32[2,32,128]{2,1,0:T(8,128)S(1)} %get-tuple-element.28.refs_4_.refs_2_, ...), custom_call_target="tpu_custom_call" | custom-call | tf_op jit(solution)/shard_map/first_keys/pallas_call | solution.py:427
  22.3 0.0 copy-start.1
  22.3 1.5 %collective-permute-start.6 = (bf16[2,256,128]{2,1,0:T(8,128)(2,1)S(1)}, bf16[2,256,128]{2,1,0:T(8,128)(2,1)S(1)}, u32[]{:S(2)}, u32[]{:S(2)}) collective-permute-start(bf16[2,256,128]{2,1,0:T(8,128)(2,1)S(1)} %get-tuple-element.38), channel_id=1, source_target_pairs={{0,4},{4,0},{1,5},{5,1},{2,6},{6,2},{3,7},{7,3},{8,12},{12,8},{9,1... | collective-permute-start | bytes 393224 | tf_op jit(solution)/shard_map/ppermute | solution.py:443
  23.8 3.7 %collective-permute-done.5.refs_4_.refs_9_ = bf16[2,2,2,64,128]{4,3,2,1,0:T(8,128)(2,1)S(1)} collective-permute-done((bf16[2,2,2,64,128]{4,3,2,1,0:T(8,128)(2,1)S(1)}, bf16[2,2,2,64,128]{4,3,2,1,0:T(8,128)(2,1)S(1)}, u32[]{:S(2)}, u32[]{:S(2)}) %collective-permute-start.5) | collective-permute-done | bytes 131104 | tf_op jit(solution)/shard_map/ppermute | solution.py:443
  27.5 1.0 %second_probs.1.refs_5_ = f32[4,128,256]{2,1,0:T(8,128)S(1)} custom-call(s32[5,8]{1,0:T(8,128)S(1)} %copy-done.4, bf16[2,32,4096]{2,1,0:T(8,128)(2,1)S(1)} %get-tuple-element.29.refs_3_.refs_1_, bf16[2,2,2,64,128]{4,3,2,1,0:T(8,128)(2,1)S(1)} %pad_maximum_fusion.refs_6_.refs_2_.refs_7_, ...), custom_call_target="tpu_custom_call" | custom-call | tf_op jit(solution)/shard_map/second_probs/pallas_call | solution.py:427
  28.5 1.4 %collective-permute-done.6.refs_11_ = bf16[2,256,128]{2,1,0:T(8,128)(2,1)S(1)} collective-permute-done((bf16[2,256,128]{2,1,0:T(8,128)(2,1)S(1)}, bf16[2,256,128]{2,1,0:T(8,128)(2,1)S(1)}, u32[]{:S(2)}, u32[]{:S(2)}) %collective-permute-start.6) | collective-permute-done | bytes 131104 | tf_op jit(solution)/shard_map/ppermute | solution.py:443
  29.9 0.0 collective-permute-done.4.refs_3_
  29.9 0.0 copy-done.1
  29.9 0.7 %second_keys.1 = (bf16[32,4096]{1,0:T(8,128)(2,1)S(1)}, f32[32,128]{1,0:T(8,128)S(1)}, f32[256,128]{1,0:T(8,128)S(1)}, f32[256,128]{1,0:T(8,128)S(1)}, bf16[576,...) custom-call(bf16[1,2,32,4096]{3,2,1,0:T(8,128)(2,1)S(1)} %copy-done, ...), custom_call_target="tpu_custom_call" | custom-call | tf_op jit(solution)/shard_map/second_keys/pallas_call | solution.py:427
  30.7 0.5 %collective-permute-start.7 = (bf16[576,128]{1,0:T(8,128)(2,1)S(1)}, bf16[576,128]{1,0:T(8,128)(2,1)S(1)}, u32[]{:S(2)}, u32[]{:S(2)}) collective-permute-start(bf16[576,128]{1,0:T(8,128)(2,1)S(1)} %get-tuple-element.43), channel_id=1, source_target_pairs={{0,1},{1,0},{2,3},{3,2},{4,5},{5,4},{6,7},{7,6},{8,9},{9,8},{10,11... | collective-permute-start | bytes 442376 | tf_op jit(solution)/shard_map/ppermute | solution.py:441
  31.2 1.2 %collective-permute-start.8 = (bf16[320,128]{1,0:T(8,128)(2,1)S(1)}, bf16[320,128]{1,0:T(8,128)(2,1)S(1)}, u32[]{:S(2)}, u32[]{:S(2)}) collective-permute-start(bf16[320,128]{1,0:T(8,128)(2,1)S(1)} %get-tuple-element.44), channel_id=1, source_target_pairs={{0,4},{4,0},{1,5},{5,1},{2,6},{6,2},{3,7},{7,3},{8,12},{12,8},{9,1... | collective-permute-start | bytes 245768 | tf_op jit(solution)/shard_map/ppermute | solution.py:443
  32.4 1.8 %collective-permute-start.9 = (bf16[320,128]{1,0:T(8,128)(2,1)S(1)}, bf16[320,128]{1,0:T(8,128)(2,1)S(1)}, u32[]{:S(2)}, u32[]{:S(2)}) collective-permute-start(bf16[320,128]{1,0:T(8,128)(2,1)S(1)} %get-tuple-element.45), channel_id=1, source_target_pairs={{0,5},{1,4},{2,7},{3,6},{4,1},{5,0},{6,3},{7,2},{8,13},{9,12},{10,... | collective-permute-start | bytes 245768 | tf_op jit(solution)/shard_map/ppermute | solution.py:449
  34.2 2.1 %collective-permute-done.8.refs_4_ = bf16[320,128]{1,0:T(8,128)(2,1)S(1)} collective-permute-done((bf16[320,128]{1,0:T(8,128)(2,1)S(1)}, bf16[320,128]{1,0:T(8,128)(2,1)S(1)}, u32[]{:S(2)}, u32[]{:S(2)}) %collective-permute-start.8) | collective-permute-done | bytes 81952 | tf_op jit(solution)/shard_map/ppermute | solution.py:443
  36.3 1.7 %collective-permute-done.9.refs_5_ = bf16[320,128]{1,0:T(8,128)(2,1)S(1)} collective-permute-done((bf16[320,128]{1,0:T(8,128)(2,1)S(1)}, bf16[320,128]{1,0:T(8,128)(2,1)S(1)}, u32[]{:S(2)}, u32[]{:S(2)}) %collective-permute-start.9) | collective-permute-done | bytes 81952 | tf_op jit(solution)/shard_map/ppermute | solution.py:449
  38.0 0.0 collective-permute-done.7.refs_3_
  38.0 0.1 near_sum.1
  38.0 2.6 %collective-permute-start.10 = (bf16[320,128]{1,0:T(8,128)(2,1)S(1)}, bf16[320,128]{1,0:T(8,128)(2,1)S(1)}, u32[]{:S(2)}, u32[]{:S(2)}) collective-permute-start(bf16[320,128]{1,0:T(8,128)(2,1)S(1)} %get-tuple-element.48), channel_id=1, source_target_pairs={{0,2},{1,3},{2,0},{3,1},{4,6},{5,7},{6,4},{7,5},{8,10},{9,11},{10,... | collective-permute-start | bytes 245768 | tf_op jit(solution)/shard_map/ppermute | solution.py:452
  40.7 1.1 %second_rows.1 = bf16[1,2,32,4096]{3,2,1,0:T(8,128)(2,1)} custom-call(bf16[1,2,32,4096]{3,2,1,0:T(8,128)(2,1)S(1)} %copy-done, f32[1,4096]{1,0:T(1,128)S(1)} %copy-done.3, f32[2,32,128]{2,1,0:T(8,128)S(1)} %get-tuple-element.28.refs_4_.refs_2_, bf16[32,4096]{1,0:T(8,128)(2,1)S(1)} %collective-permute-done.4.refs_3_, bf16[1,32,4096]{2,1,0:T(8,128)(2,1)S(1)} %copy-done.1, ...), custom_call_target="tpu_custom_call" | custom-call | tf_op jit(solution)/shard_map/second_rows/pallas_call | solution.py:427
  41.8 2.5 %collective-permute-done.10.receive_ref = bf16[320,128]{1,0:T(8,128)(2,1)S(1)} collective-permute-done((bf16[320,128]{1,0:T(8,128)(2,1)S(1)}, bf16[320,128]{1,0:T(8,128)(2,1)S(1)}, u32[]{:S(2)}, u32[]{:S(2)}) %collective-permute-start.10) | collective-permute-done | bytes 81952 | tf_op jit(solution)/shard_map/ppermute | solution.py:452
  44.3 0.7 %finish.1 = (f32[1,2,128,128]{3,2,1,0:T(8,128)}, f32[1,2,128,128]{3,2,1,0:T(8,128)}, f32[32,128]{1,0:T(8,128)}) custom-call(f32[256,128]{1,0:T(8,128)S(1)} %get-tuple-element.46.keep_ref, f32[32,128]{1,0:T(8,128)S(1)} %get-tuple-element.47.gain_ref, bf16[320,128]{1,0:T(8,128)(2,1)S(1)} %collective-permute-done.10.receive_ref), custom_call_target="tpu_custom_call" | custom-call | tf_op jit(solution)/shard_map/finish/pallas_call | solution.py:427
  (2 shorter events, 0.0 us)
Async XLA Ops:
  0.6 14.9 %copy-start = (bf16[1,2,32,4096]{3,2,1,0:T(8,128)(2,1)S(1)}, bf16[1,2,32,4096]{3,2,1,0:T(8,128)(2,1)}, u32[]{:S(2)}) copy-start(bf16[1,2,32,4096]{3,2,1,0:T(8,128)(2,1)} %refs_0_.9) | copy-start | bytes 1572868
  2.3 8.0 %collective-permute-start = (bf16[2,2,64,128]{3,2,1,0:T(8,128)(2,1)}, bf16[2,2,64,128]{3,2,1,0:T(8,128)(2,1)S(1)}, u32[]{:S(2)}, u32[]{:S(2)}) collective-permute-start(bf16[2,2,64,128]{3,2,1,0:T(8,128)(2,1)} %get-tuple-element.31), channel_id=1, source_target_pairs={{0,2},{1,3},{2,0},{3,1},{4,6},{5,7},{6,4},{7,5},{8,10},{9,11},{10,... | collective-permute-start | bytes 196616 | tf_op jit(solution)/shard_map/ppermute | solution.py:452
  11.1 4.4 %copy-start.3 = (f32[1,4096]{1,0:T(1,128)S(1)}, f32[1,4096]{1,0:T(1,128)}, u32[]{:S(2)}) copy-start(f32[1,4096]{1,0:T(1,128)} %refs_1_.3) | copy-start | bytes 49156
  11.1 8.4 %collective-permute-start.1 = (bf16[2,2,2,64,128]{4,3,2,1,0:T(8,128)(2,1)S(1)}, bf16[2,2,2,64,128]{4,3,2,1,0:T(8,128)(2,1)S(1)}, u32[]{:S(2)}, u32[]{:S(2)}) collective-permute-start(bf16[2,2,2,64,128]{4,3,2,1,0:T(8,128)(2,1)S(1)} %pad_maximum_fusion.refs_6_.refs_2_.refs_7_), channel_id=1, source_target_pairs={{0,1},{1,0},{2,3},{3,2},{4,5},{5,4},{6,7},{7,6},{8,9},{9,8},{10,11... | collective-permute-start | bytes 393224 | tf_op jit(solution)/shard_map/ppermute | solution.py:441
  12.6 6.9 %copy-start.2 = (bf16[1,32,4096]{2,1,0:T(8,128)(2,1)S(1)}, bf16[1,32,4096]{2,1,0:T(8,128)(2,1)}, u32[]{:S(2)}) copy-start(bf16[1,32,4096]{2,1,0:T(8,128)(2,1)} %refs_3_.1) | copy-start | bytes 786436
  12.6 5.6 %collective-permute-start.3 = (bf16[2,2,64,128]{3,2,1,0:T(8,128)(2,1)S(1)}, bf16[2,2,64,128]{3,2,1,0:T(8,128)(2,1)S(1)}, u32[]{:S(2)}, u32[]{:S(2)}) collective-permute-start(bf16[2,2,64,128]{3,2,1,0:T(8,128)(2,1)S(1)} %get-tuple-element.53), channel_id=1, source_target_pairs={{0,5},{1,4},{2,7},{3,6},{4,1},{5,0},{6,3},{7,2},{8,13},{9,12},{10,... | collective-permute-start | bytes 196616 | tf_op jit(solution)/shard_map/ppermute | solution.py:449
  15.2 4.3 %collective-permute-start.2 = (bf16[2,2,64,128]{3,2,1,0:T(8,128)(2,1)S(1)}, bf16[2,2,64,128]{3,2,1,0:T(8,128)(2,1)S(1)}, u32[]{:S(2)}, u32[]{:S(2)}) collective-permute-start(bf16[2,2,64,128]{3,2,1,0:T(8,128)(2,1)S(1)} %get-tuple-element.53), channel_id=1, source_target_pairs={{0,4},{4,0},{1,5},{5,1},{2,6},{6,2},{3,7},{7,3},{8,12},{12,8},{9,1... | collective-permute-start | bytes 196616 | tf_op jit(solution)/shard_map/ppermute | solution.py:443
  15.5 4.0 %copy-start.4 = (s32[5,8]{1,0:T(8,128)S(1)}, s32[5,8]{1,0:T(8,128)}, u32[]{:S(2)}) copy-start(s32[5,8]{1,0:T(8,128)} %refs_0_.6) | copy-start | bytes 484
  21.1 8.9 %collective-permute-start.4 = (bf16[32,4096]{1,0:T(8,128)(2,1)S(1)}, bf16[32,4096]{1,0:T(8,128)(2,1)S(1)}, u32[]{:S(2)}, u32[]{:S(2)}) collective-permute-start(bf16[32,4096]{1,0:T(8,128)(2,1)S(1)} %get-tuple-element.32.refs_6_), channel_id=1, source_target_pairs={{0,24},{8,0},{16,8},{24,16},{1,25},{9,1},{17,9},{25,17},{2,26},{10... | collective-permute-start | bytes 786440 | tf_op jit(solution)/shard_map/ppermute | solution.py:487
  21.2 6.4 %collective-permute-start.5 = (bf16[2,2,2,64,128]{4,3,2,1,0:T(8,128)(2,1)S(1)}, bf16[2,2,2,64,128]{4,3,2,1,0:T(8,128)(2,1)S(1)}, u32[]{:S(2)}, u32[]{:S(2)}) collective-permute-start(bf16[2,2,2,64,128]{4,3,2,1,0:T(8,128)(2,1)S(1)} %pad_maximum_fusion.1), channel_id=1, source_target_pairs={{0,4},{4,0},{1,5},{5,1},{2,6},{6,2},{3,7},{7,3},{8,12},{12,8},{9,1... | collective-permute-start | bytes 393224 | tf_op jit(solution)/shard_map/ppermute | solution.py:443
  22.3 7.6 %copy-start.1 = (bf16[1,32,4096]{2,1,0:T(8,128)(2,1)S(1)}, bf16[1,32,4096]{2,1,0:T(8,128)(2,1)}, u32[]{:S(2)}) copy-start(bf16[1,32,4096]{2,1,0:T(8,128)(2,1)} %refs_4_.3) | copy-start | bytes 786436
  22.3 7.6 %collective-permute-start.6 = (bf16[2,256,128]{2,1,0:T(8,128)(2,1)S(1)}, bf16[2,256,128]{2,1,0:T(8,128)(2,1)S(1)}, u32[]{:S(2)}, u32[]{:S(2)}) collective-permute-start(bf16[2,256,128]{2,1,0:T(8,128)(2,1)S(1)} %get-tuple-element.38), channel_id=1, source_target_pairs={{0,4},{4,0},{1,5},{5,1},{2,6},{6,2},{3,7},{7,3},{8,12},{12,8},{9,1... | collective-permute-start | bytes 393224 | tf_op jit(solution)/shard_map/ppermute | solution.py:443
  30.7 7.3 %collective-permute-start.7 = (bf16[576,128]{1,0:T(8,128)(2,1)S(1)}, bf16[576,128]{1,0:T(8,128)(2,1)S(1)}, u32[]{:S(2)}, u32[]{:S(2)}) collective-permute-start(bf16[576,128]{1,0:T(8,128)(2,1)S(1)} %get-tuple-element.43), channel_id=1, source_target_pairs={{0,1},{1,0},{2,3},{3,2},{4,5},{5,4},{6,7},{7,6},{8,9},{9,8},{10,11... | collective-permute-start | bytes 442376 | tf_op jit(solution)/shard_map/ppermute | solution.py:441
  31.2 5.1 %collective-permute-start.8 = (bf16[320,128]{1,0:T(8,128)(2,1)S(1)}, bf16[320,128]{1,0:T(8,128)(2,1)S(1)}, u32[]{:S(2)}, u32[]{:S(2)}) collective-permute-start(bf16[320,128]{1,0:T(8,128)(2,1)S(1)} %get-tuple-element.44), channel_id=1, source_target_pairs={{0,4},{4,0},{1,5},{5,1},{2,6},{6,2},{3,7},{7,3},{8,12},{12,8},{9,1... | collective-permute-start | bytes 245768 | tf_op jit(solution)/shard_map/ppermute | solution.py:443
  32.4 5.6 %collective-permute-start.9 = (bf16[320,128]{1,0:T(8,128)(2,1)S(1)}, bf16[320,128]{1,0:T(8,128)(2,1)S(1)}, u32[]{:S(2)}, u32[]{:S(2)}) collective-permute-start(bf16[320,128]{1,0:T(8,128)(2,1)S(1)} %get-tuple-element.45), channel_id=1, source_target_pairs={{0,5},{1,4},{2,7},{3,6},{4,1},{5,0},{6,3},{7,2},{8,13},{9,12},{10,... | collective-permute-start | bytes 245768 | tf_op jit(solution)/shard_map/ppermute | solution.py:449
  38.0 6.3 %collective-permute-start.10 = (bf16[320,128]{1,0:T(8,128)(2,1)S(1)}, bf16[320,128]{1,0:T(8,128)(2,1)S(1)}, u32[]{:S(2)}, u32[]{:S(2)}) collective-permute-start(bf16[320,128]{1,0:T(8,128)(2,1)S(1)} %get-tuple-element.48), channel_id=1, source_target_pairs={{0,2},{1,3},{2,0},{3,1},{4,6},{5,7},{6,4},{7,5},{8,10},{9,11},{10,... | collective-permute-start | bytes 245768 | tf_op jit(solution)/shard_map/ppermute | solution.py:452

commit v4 on v3

--- a/solution.py
+++ b/solution.py
@@ -11,6 +11,7 @@
 EPSILON = 1e-05
 FILL = -1e30
 SCALE = HD ** (-0.5)
+TICKS = 2
 F32 = jnp.float32
 BF16 = jnp.bfloat16
 
@@ -43,26 +44,14 @@
     return total
 
 
-def pack_kernel(tp_count, half, keys_ref, values_ref, own_ref, other_ref, sems):
+def pack_kernel(tp_count, half, both_ref, own_ref, other_ref):
     parity = lax.axis_index("tp") // (tp_count // 2)
     own_first = pl.multiple_of(parity * half, half)
     other_first = pl.multiple_of((1 - parity) * half, half)
-    copies = []
-    for kind, ref in enumerate((keys_ref, values_ref)):
-        for tick in range(keys_ref.shape[1]):
-            for place, (first, target) in enumerate(
-                ((own_first, own_ref), (other_first, other_ref))
-            ):
-                source = ref.at[0, tick, pl.ds(first, half), :]
-                copies.append(
-                    pltpu.make_async_copy(
-                        source, target.at[tick, kind], sems.at[kind, tick, place]
-                    )
-                )
-    for copy in copies:
-        copy.start()
-    for copy in copies:
-        copy.wait()
+    for kind in range(2):
+        for tick in range(TICKS):
+            own_ref[tick, kind] = both_ref[kind, tick, pl.ds(own_first, half), :]
+            other_ref[tick, kind] = both_ref[kind, tick, pl.ds(other_first, half), :]
 
 
 def norm_kernel(x_ref, gain_ref, query_ref, inverse_ref):
@@ -146,24 +135,32 @@
 class Keys:
     def __init__(self, sizes, tick, refs):
         self.near_count = sizes[3] // 2
-        self.cycle = sizes[2]
         self.tick = tick
         self.refs = refs
 
     def __call__(self, turn, kind):
         near, far = turn % self.near_count, turn // self.near_count
-        parts = [self.refs[near][self.tick, far, kind]]
-        for step in range(1, self.cycle):
-            if self.tick:
-                parts.append(self.refs[self.near_count + step - 1][near, far, kind])
-            else:
-                parts.append(self.refs[step * self.near_count + near][far, kind])
+        parts = [ref[self.tick, far, kind] for ref in self.refs[near :: self.near_count]]
         return jnp.concatenate(parts, axis=0)
 
 
 def place_of(sizes, far, kind):
     half = sizes[1]
     return slice((far * 2 + kind) * half, (far * 2 + kind + 1) * half)
+
+
+def put_key_grads(sizes, turn, parts, own_ref, message_refs):
+    half, cycle, tp_count = sizes[1:4]
+    near_count = tp_count // 2
+    near, far = turn % near_count, turn // near_count
+    for kind, part in enumerate(parts):
+        here = place_of(sizes, far, kind)
+        for step in range(cycle):
+            piece = part[step * half : (step + 1) * half]
+            if step == 0 and near == 0:
+                own_ref[here, :] = piece
+            else:
+                message_refs[step * near_count + near - 1][here, :] = piece.astype(BF16)
 
 
 def gain_terms(columns_of, low_parts, normed_of, gain_rows_ref):
@@ -237,10 +234,9 @@
         columns_of = Group(sizes, turn)
         query = columns_of.stacked(lambda where: query_ref[0, :, where])
         grad = columns_of.stacked(arriving)
+        parts = (SCALE * dot(dscore_ref[turn], query, NN), dot(probs_ref[turn], grad, NN))
         near, far = turn % (tp_count // 2), turn // (tp_count // 2)
-        for kind, part in enumerate(
-            (SCALE * dot(dscore_ref[turn], query, NN), dot(probs_ref[turn], grad, NN))
-        ):
+        for kind, part in enumerate(parts):
             here = place_of(sizes, far, kind)
             own_ref[near, here, :] = part[:half]
             for step, ref in enumerate(send_refs, 1):
@@ -266,12 +262,12 @@
         probs_ref[turn] = probabilities(visible, scores[turn])
 
 
-def second_keys_kernel(sizes, kv_count, *refs):
-    half, cycle, tp_count = sizes[1:4]
+def second_keys_kernel(sizes, *refs):
+    cycle, tp_count = sizes[2:4]
     turns = range(tp_count)
-    near_count = tp_count // 2
+    members = cycle * (tp_count // 2)
     x_ref, query_ref, inverse_ref, arrived_ref, output_ref, probs_ref, before_ref = refs[:7]
-    keys, refs = Keys(sizes, 1, refs[7 : 7 + kv_count]), refs[7 + kv_count :]
+    keys, refs = Keys(sizes, 1, refs[7 : 7 + members]), refs[7 + members :]
     first_refs, refs = refs[:cycle], refs[cycle:]
     query_grad_ref, gain_rows_ref, own_ref, own_first_ref = refs[:4]
     message_refs, gain_scratch = refs[4:-1], refs[-1]
@@ -288,15 +284,7 @@
     for turn in turns:
         query = columns_of[turn].stacked(lambda where: query_ref[1, :, where])
         key_grad = SCALE * dot(dscores[turn], query, NN)
-        near, far = turn % near_count, turn // near_count
-        for kind, part in enumerate((key_grad, value_grads[turn])):
-            here = place_of(sizes, far, kind)
-            for step in range(cycle):
-                piece = part[step * half : (step + 1) * half]
-                if step == 0 and near == 0:
-                    own_ref[here, :] = piece
-                else:
-                    message_refs[step * near_count + near - 1][here, :] = piece.astype(BF16)
+        put_key_grads(sizes, turn, (key_grad, value_grads[turn]), own_ref, message_refs)
     for turn in turns:
         low_parts = columns_of[turn].unstacked(query_grads[turn])
         for index, low in enumerate(low_parts):
@@ -316,14 +304,14 @@
         ref[begin : begin + count, :] = high
         ref[begin + count : begin + 2 * count, :] = low
     begin += 2 * count
-    for near in range(near_count):
+    for near in range(tp_count // 2):
         total = first_refs[0][near]
         for ref in first_refs[1:]:
             total = total + ref[near].astype(F32)
         if near == 0:
             own_first_ref[...] = total
         else:
-            message_refs[near - 1][begin : begin + total.shape[0], :] = total.astype(BF16)
+            message_refs[near - 1][begin:, :] = total.astype(BF16)
 
 
 def second_rows_kernel(sizes, *refs):
@@ -344,24 +332,20 @@
     rows, half, cycle, tp_count, group, columns = sizes
     near_count = tp_count // 2
     members = cycle * near_count
-    own_ref, own_first_ref, gain_ref = refs[:3]
-    message_refs = refs[3 : 3 + members - 1]
-    keep_ref, gain_sum_ref, send_ref = refs[3 + members - 1 :]
+    own_refs, gain_ref = refs[:TICKS], refs[TICKS]
+    message_refs = refs[TICKS + 1 : TICKS + members]
+    keep_ref, gain_sum_ref, send_ref = refs[TICKS + members :]
     block = 2 * half
-    size = 2 * block
+    size = TICKS * block
     count = gain_ref.shape[0]
-    begin = size + 2 * count
-    for tick in range(2):
+    after = 2 * block + 2 * count
+    for tick in range(TICKS):
         for far in range(2):
             here = slice(far * block, (far + 1) * block)
-            if tick:
-                total = own_ref[here, :]
-                for ref in message_refs:
-                    total = total + ref[here, :].astype(F32)
-            else:
-                total = own_first_ref[here, :]
-                for ref in message_refs[: near_count - 1]:
-                    total = total + ref[begin + far * block : begin + (far + 1) * block, :].astype(F32)
+            there = here if tick else slice(after + here.start, after + here.stop)
+            total = own_refs[tick][here, :]
+            for ref in message_refs if tick else message_refs[: near_count - 1]:
+                total = total + ref[there, :].astype(F32)
             target = slice(tick * block, (tick + 1) * block)
             if far:
                 send_ref[target, :] = total.astype(BF16)
@@ -373,7 +357,10 @@
     owners = [cycle_place * near_count + near_place]
     for place, ref in enumerate(message_refs, 1):
         step, near = place // near_count, place % near_count
-        values.append(joined(ref[size : size + count, :], ref[size + count : size + 2 * count, :]))
+        begin = 2 * block
+        values.append(
+            joined(ref[begin : begin + count, :], ref[begin + count : begin + 2 * count, :])
+        )
         owners.append(((cycle_place + step) % cycle) * near_count + (near_place ^ near))
     gain = in_order(values, owners)
     gain_sum_ref[...] = gain
@@ -386,7 +373,7 @@
     rows, half, cycle, tp_count, group, columns = sizes
     parity = lax.axis_index("tp") // (tp_count // 2)
     block = 2 * half
-    for tick in range(2):
+    for tick in range(TICKS):
         for kind, out in enumerate((key_ref, value_ref)):
             here = slice(tick * block + kind * half, tick * block + (kind + 1) * half)
             own_first = pl.multiple_of(parity * half, half)
@@ -419,18 +406,16 @@
     score_bytes = key_count * stacked * 4
     usual_limit = min(56 << 20, (12 << 20) + 20 * score_bytes)
 
-    def call(
-        kernel, name, operands, out_shape, memory=pltpu.VMEM, scratch=(), scalars=0, limit=None
-    ):
+    def call(kernel, name, operands, out_shape, scratch=(), scalars=0):
         in_specs = [pl.BlockSpec(memory_space=pltpu.SMEM)] * scalars
-        in_specs += [pl.BlockSpec(memory_space=memory)] * (len(operands) - scalars)
+        in_specs += [pl.BlockSpec(memory_space=pltpu.VMEM)] * (len(operands) - scalars)
         return pl.pallas_call(
             kernel,
             out_shape=out_shape,
             in_specs=in_specs,
             out_specs=[pl.BlockSpec(memory_space=pltpu.VMEM)] * len(out_shape),
             scratch_shapes=scratch,
-            compiler_params=pltpu.CompilerParams(vmem_limit_bytes=limit or usual_limit),
+            compiler_params=pltpu.CompilerParams(vmem_limit_bytes=usual_limit),
             name=name,
         )(*operands)
 
@@ -455,19 +440,12 @@
     own_kv, other_kv = call(
         functools.partial(pack_kernel, tp_count, half),
         "pack_kv",
-        (keys, values),
+        (jnp.stack([keys[0], values[0]]),),
         [sections, sections],
-        memory=pl.ANY,
-        scratch=[pltpu.SemaphoreType.DMA((2, ticks, 2))],
-        limit=60 << 20,
     )
     pair = jnp.stack([own_kv, to_far(other_kv)], axis=1)
-    near_kv = [pair] + [to_near(pair, 0, near) for near in range(1, near_count)]
-    kv_first = near_kv + [
-        to_near(pair[0], step, near) for step in range(1, cycle) for near in range(near_count)
-    ]
-    later = jnp.stack([part[1] for part in near_kv])
-    kv_second = near_kv + [to_near(later, step, 0) for step in range(1, cycle)]
+    places = [(step, near) for step in range(cycle) for near in range(near_count)][1:]
+    kv = [pair] + [to_near(pair, step, near) for step, near in places]
     queries, inverse = call(
         norm_kernel,
         "norm",
@@ -478,9 +456,9 @@
     low_rows = shape((rows, columns), BF16)
     low_scores = shape((tp_count, key_count, stacked), BF16)
     input_grad_first, query_grad_first, dscore_first, probs_first = call(
-        functools.partial(first_rows_kernel, sizes, len(kv_first)),
+        functools.partial(first_rows_kernel, sizes, len(kv)),
         "first_rows",
-        (doc_lengths, segment_inputs, norm_gain, queries, inverse, waiting_grads, *kv_first),
+        (doc_lengths, segment_inputs, norm_gain, queries, inverse, waiting_grads, *kv),
         [low_rows, low_rows, low_scores, low_scores],
         scalars=1,
     )
@@ -488,7 +466,9 @@
         input_grad_first, "pipe", [(i, (i - 1) % pipe_count) for i in range(pipe_count)]
     )
     gain_shape = shape((gain_count, HD), F32)
-    first_sums = (near_count, 2 * block, HD)
+    pair_rows = 2 * block
+    own_shape = shape((pair_rows, HD), F32)
+    first_sums = (near_count, pair_rows, HD)
     gain_first, *sums_first = call(
         functools.partial(first_keys_kernel, sizes),
         "first_keys",
@@ -507,21 +487,18 @@
         to_near(value, -step, 0) for step, value in enumerate(sums_first[1:], 1)
     ]
     (probs_second,) = call(
-        functools.partial(second_probs_kernel, sizes, len(kv_second)),
+        functools.partial(second_probs_kernel, sizes, len(kv)),
         "second_probs",
-        (doc_lengths, queries, *kv_second),
+        (doc_lengths, queries, *kv),
         [shape((tp_count, key_count, stacked), F32)],
         scalars=1,
     )
-    places = [(step, near) for step in range(cycle) for near in range(near_count)][1:]
-    pair_rows = 2 * block
-    own_shape = shape((pair_rows, HD), F32)
     messages = [
         shape((pair_rows * (2 if step == 0 else 1) + 2 * gain_count, HD), BF16)
         for step, near in places
     ]
     query_grad_second, gain_rows, own_second, own_first, *sends = call(
-        functools.partial(second_keys_kernel, sizes, len(kv_second)),
+        functools.partial(second_keys_kernel, sizes),
         "second_keys",
         (
             segment_inputs,
@@ -531,7 +508,7 @@
             output_grads,
             probs_second,
             gain_first,
-            *kv_second,
+            *kv,
             *sums_first,
         ),
         [low_rows, gain_shape, own_shape, own_shape] + messages,
@@ -555,7 +532,7 @@
     keep, gain_sum, send = call(
         functools.partial(near_sum_kernel, sizes),
         "near_sum",
-        (own_second, own_first, gain_rows, *received),
+        (own_first, own_second, gain_rows, *received),
         [own_shape, gain_shape, shape((pair_rows + 2 * gain_count, HD), BF16)],
     )
     grads_shape = shape((1, ticks, block, HD), F32)

time: 45.3 us -> 41.5 us (0.916)
  Pallas kernels: 7.52 us -> 5.9 us
  waiting for transfers between devices: 19 us -> 18 us
  other arithmetic: 1.66 us -> 0.96 us
    ppermute x2, starting transfers between devices: 1.27 us -> 2.98 us  [to_near(): return lax.ppermute(value, 'tp', [(i, i ^ near) for i in range(tp_count)])]
    ppermute x2, starting transfers between devices: 4.39 us -> 2.74 us  [to_near(): return lax.ppermute(value, ('ctx', 'tp'), pairs)]
    another operation x2 -> x1, other arithmetic: 1.64 us -> 0.01 us  [on_device(): pair = jnp.stack([own_kv, to_far(other_kv)], axis=1)]
    pallas_call x9, Pallas kernels: 7.52 us -> 5.9 us  [call(): pl.pallas_call(kernel, out_shape=out_shape, in_specs=in_specs, out_specs=...]
    ppermute x4 -> x3, waiting for transfers between devices: 8.43 us -> 7.17 us  [to_near(): lax.ppermute(value, 'ctx', [(i, (i + step) % cycle) for i in range(cycle)])]
    another operation x1, other arithmetic: 0.02 us -> 0.94 us  [on_device(): jnp.stack([keys[0], values[0]])]
    ppermute x4 -> x3, starting transfers between devices: 3.67 us -> 2.84 us  [to_near(): lax.ppermute(value, 'ctx', [(i, (i + step) % cycle) for i in range(cycle)])]
    ppermute x2, waiting for transfers between devices: 4.15 us -> 4.71 us  [to_near(): return lax.ppermute(value, ('ctx', 'tp'), pairs)]
  transfers between devices with their start and end apart: 11 -> 10, of which waited for: 8 -> 8; matrix products, arithmetic and copies ran while one was open for 2% -> 0% of each run, Pallas kernels for 6% -> 7%
where the time goes in v4:
time: 41.5 us; the launch traced here: 41.4 us
  waiting for transfers between devices  18 us (43%)
  starting transfers between devices  15.8 us (38%)
  Pallas kernels  5.9 us (14%)
  other arithmetic  0.96 us (2%)
  between operations  0.73 us (2%)
    ppermute x3, waiting for transfers between devices, to_near(): lax.ppermute(value, 'ctx', [(i, (i + step) % cycle) for i in range(cycle)])  7.17 us
    ppermute x2, starting transfers between devices, to_far(): lax.ppermute(value, 'tp', [(i, i ^ near_count) for i in range(tp_count)])  7.16 us
    pallas_call x9, Pallas kernels, call(): pl.pallas_call(kernel, out_shape=out_shape, in_specs=in_specs, out_specs=...  5.9 us
    ppermute x2, waiting for transfers between devices, to_far(): lax.ppermute(value, 'tp', [(i, i ^ near_count) for i in range(tp_count)])  5.83 us
    ppermute x2, waiting for transfers between devices, to_near(): return lax.ppermute(value, ('ctx', 'tp'), pairs)  4.71 us
    ppermute x2, starting transfers between devices, to_near(): return lax.ppermute(value, 'tp', [(i, i ^ near) for i in range(tp_count)])  2.98 us
    ppermute x3, starting transfers between devices, to_near(): lax.ppermute(value, 'ctx', [(i, (i + step) % cycle) for i in range(cycle)])  2.84 us
    ppermute x2, starting transfers between devices, to_near(): return lax.ppermute(value, ('ctx', 'tp'), pairs)  2.74 us
  transfers between devices with their start and end apart: 10, of which 8 were waited for; matrix products, arithmetic and copies ran while one was open for 0% of the time, Pallas kernels for 7%

profile of v4, /device:TPU:0, one launch (start us, length us, event | category | flops | bytes accessed | tf_op | source)
XLA Modules:
  0.0 41.4 jit_solution(17936222560775235181)
XLA Ops:
  0.6 0.0 copy-start
  0.6 0.9 %pad_maximum_fusion.both_ref = bf16[2,2,128,128]{3,2,1,0:T(8,128)(2,1)S(1)} fusion(bf16[1,2,128,128]{3,2,1,0:T(8,128)(2,1)} %param.9, bf16[1,2,128,128]{3,2,1,0:T(8,128)(2,1)} %param.8), kind=kLoop, calls=%fused_computation | loop fusion | flops 65536 | bytes 262144 | tf_op jit(solution)/shard_map/stack | solution.py:443
  1.6 4.1 %collective-permute-start = (bf16[2,2,64,128]{3,2,1,0:T(8,128)(2,1)S(1)}, bf16[2,2,64,128]{3,2,1,0:T(8,128)(2,1)S(1)}, u32[]{:S(2)}, u32[]{:S(2)}) collective-permute-start(bf16[2,2,64,128]{3,2,1,0:T(8,128)(2,1)S(1)} %get-tuple-element.31), channel_id=1, source_target_pairs={{0,2},{1,3},{2,0},{3,1},{4,6},{5,7},{6,4},{7,5},{8,10},{9,11},{10,... | collective-permute-start | bytes 196616 | tf_op jit(solution)/shard_map/ppermute | solution.py:437
  5.7 3.6 %collective-permute-done = bf16[2,2,64,128]{3,2,1,0:T(8,128)(2,1)S(1)} collective-permute-done((bf16[2,2,64,128]{3,2,1,0:T(8,128)(2,1)S(1)}, bf16[2,2,64,128]{3,2,1,0:T(8,128)(2,1)S(1)}, u32[]{:S(2)}, u32[]{:S(2)}) %collective-permute-start) | collective-permute-done | bytes 65568 | tf_op jit(solution)/shard_map/ppermute | solution.py:437
  9.4 0.0 copy-start.3
  9.4 0.0 copy-start.1
  9.4 1.6 %collective-permute-start.3 = (bf16[2,2,2,64,128]{4,3,2,1,0:T(8,128)(2,1)S(1)}, bf16[2,2,2,64,128]{4,3,2,1,0:T(8,128)(2,1)S(1)}, u32[]{:S(2)}, u32[]{:S(2)}) collective-permute-start(bf16[2,2,2,64,128]{4,3,2,1,0:T(8,128)(2,1)S(1)} %pad_maximum_fusion.1.refs_6_.refs_2_.refs_7_), channel_id=1, source_target_pairs={{0,5},{1,4},{2,7},{3,6},{4,1},{5,0},{6,3},{7,2},{8,13},{9,12},{10,... | collective-permute-start | bytes 393224 | tf_op jit(solution)/shard_map/ppermute | solution.py:434
  11.0 0.5 %collective-permute-start.2 = (bf16[2,2,2,64,128]{4,3,2,1,0:T(8,128)(2,1)S(1)}, bf16[2,2,2,64,128]{4,3,2,1,0:T(8,128)(2,1)S(1)}, u32[]{:S(2)}, u32[]{:S(2)}) collective-permute-start(bf16[2,2,2,64,128]{4,3,2,1,0:T(8,128)(2,1)S(1)} %pad_maximum_fusion.1.refs_6_.refs_2_.refs_7_), channel_id=1, source_target_pairs={{0,4},{4,0},{1,5},{5,1},{2,6},{6,2},{3,7},{7,3},{8,12},{12,8},{9,1... | collective-permute-start | bytes 393224 | tf_op jit(solution)/shard_map/ppermute | solution.py:428
  11.5 1.5 %collective-permute-start.1 = (bf16[2,2,2,64,128]{4,3,2,1,0:T(8,128)(2,1)S(1)}, bf16[2,2,2,64,128]{4,3,2,1,0:T(8,128)(2,1)S(1)}, u32[]{:S(2)}, u32[]{:S(2)}) collective-permute-start(bf16[2,2,2,64,128]{4,3,2,1,0:T(8,128)(2,1)S(1)} %pad_maximum_fusion.1.refs_6_.refs_2_.refs_7_), channel_id=1, source_target_pairs={{0,1},{1,0},{2,3},{3,2},{4,5},{5,4},{6,7},{7,6},{8,9},{9,8},{10,11... | collective-permute-start | bytes 393224 | tf_op jit(solution)/shard_map/ppermute | solution.py:426
  13.0 0.0 copy-done
  13.0 0.0 copy-done.3
  13.0 0.0 copy-start.4
  13.0 0.3 norm.1
  13.2 3.4 %collective-permute-done.3.refs_9_.refs_5_.refs_10_ = bf16[2,2,2,64,128]{4,3,2,1,0:T(8,128)(2,1)S(1)} collective-permute-done((bf16[2,2,2,64,128]{4,3,2,1,0:T(8,128)(2,1)S(1)}, bf16[2,2,2,64,128]{4,3,2,1,0:T(8,128)(2,1)S(1)}, u32[]{:S(2)}, u32[]{:S(2)}) %collective-permute-start.3) | collective-permute-done | bytes 131104 | tf_op jit(solution)/shard_map/ppermute | solution.py:434
  16.7 0.4 collective-permute-done.2.refs_8_.refs_4_.refs_9_
  17.0 0.3 collective-permute-done.1.refs_7_.refs_3_.refs_8_
  17.3 0.0 copy-done.1
  17.3 0.0 copy-done.4
  17.3 1.6 %first_rows.1 = (bf16[32,4096]{1,0:T(8,128)(2,1)S(1)}, bf16[32,4096]{1,0:T(8,128)(2,1)S(1)}, bf16[4,128,256]{2,1,0:T(8,128)(2,1)S(1)}, bf16[4,128,256]{2,1,0:T(8,128)(2,1)S(1)}) custom-call(s32[5,8]{1,0:T(8,128)S(1)} %copy-done.4, bf16[1,2,32,4096]{3,2,1,0:T(8,128)(2,1)S(1)} %copy-done, f32[1,4096]{1,0:T(1,128)S(1)} %copy-done.3, ...), custom_call_target="tpu_custom_call" | custom-call | tf_op jit(solution)/shard_map/first_rows/pallas_call | solution.py:412
  18.9 0.1 collective-permute-start.4
  18.9 0.5 %first_keys.1 = (f32[32,128]{1,0:T(8,128)S(1)}, f32[2,256,128]{2,1,0:T(8,128)S(1)}, bf16[2,256,128]{2,1,0:T(8,128)(2,1)S(1)}) custom-call(bf16[1,2,32,4096]{3,2,1,0:T(8,128)(2,1)S(1)} %copy-done, bf16[2,32,4096]{2,1,0:T(8,128)(2,1)S(1)} %get-tuple-element.29.refs_3_.refs_1_, f32[2,32,128]{2,1,0:T(8,128)S(1)} %get-tuple-element.28.refs_4_.refs_2_, ...), custom_call_target="tpu_custom_call" | custom-call | tf_op jit(solution)/shard_map/first_keys/pallas_call | solution.py:412
  19.4 0.0 copy-start.2
  19.4 1.5 %collective-permute-start.5 = (bf16[2,256,128]{2,1,0:T(8,128)(2,1)S(1)}, bf16[2,256,128]{2,1,0:T(8,128)(2,1)S(1)}, u32[]{:S(2)}, u32[]{:S(2)}) collective-permute-start(bf16[2,256,128]{2,1,0:T(8,128)(2,1)S(1)} %get-tuple-element.38), channel_id=1, source_target_pairs={{0,4},{4,0},{1,5},{5,1},{2,6},{6,2},{3,7},{7,3},{8,12},{12,8},{9,1... | collective-permute-start | bytes 393224 | tf_op jit(solution)/shard_map/ppermute | solution.py:428
  20.9 1.0 %second_probs.1.refs_5_ = f32[4,128,256]{2,1,0:T(8,128)S(1)} custom-call(s32[5,8]{1,0:T(8,128)S(1)} %copy-done.4, bf16[2,32,4096]{2,1,0:T(8,128)(2,1)S(1)} %get-tuple-element.29.refs_3_.refs_1_, bf16[2,2,2,64,128]{4,3,2,1,0:T(8,128)(2,1)S(1)} %pad_maximum_fusion.1.refs_6_.refs_2_.refs_7_, ...), custom_call_target="tpu_custom_call" | custom-call | tf_op jit(solution)/shard_map/second_probs/pallas_call | solution.py:412
  21.9 3.5 %collective-permute-done.5.refs_12_ = bf16[2,256,128]{2,1,0:T(8,128)(2,1)S(1)} collective-permute-done((bf16[2,256,128]{2,1,0:T(8,128)(2,1)S(1)}, bf16[2,256,128]{2,1,0:T(8,128)(2,1)S(1)}, u32[]{:S(2)}, u32[]{:S(2)}) %collective-permute-start.5) | collective-permute-done | bytes 131104 | tf_op jit(solution)/shard_map/ppermute | solution.py:428
  25.4 0.0 collective-permute-done.4.refs_3_
  25.4 0.0 copy-done.2
  25.4 0.7 %second_keys.1 = (bf16[32,4096]{1,0:T(8,128)(2,1)S(1)}, f32[32,128]{1,0:T(8,128)S(1)}, f32[256,128]{1,0:T(8,128)S(1)}, f32[256,128]{1,0:T(8,128)S(1)}, bf16[576,...) custom-call(bf16[1,2,32,4096]{3,2,1,0:T(8,128)(2,1)S(1)} %copy-done, ...), custom_call_target="tpu_custom_call" | custom-call | tf_op jit(solution)/shard_map/second_keys/pallas_call | solution.py:412
  26.1 1.5 %collective-permute-start.6 = (bf16[576,128]{1,0:T(8,128)(2,1)S(1)}, bf16[576,128]{1,0:T(8,128)(2,1)S(1)}, u32[]{:S(2)}, u32[]{:S(2)}) collective-permute-start(bf16[576,128]{1,0:T(8,128)(2,1)S(1)} %get-tuple-element.43), channel_id=1, source_target_pairs={{0,1},{1,0},{2,3},{3,2},{4,5},{5,4},{6,7},{7,6},{8,9},{9,8},{10,11... | collective-permute-start | bytes 442376 | tf_op jit(solution)/shard_map/ppermute | solution.py:426
  27.6 0.9 %collective-permute-start.7 = (bf16[320,128]{1,0:T(8,128)(2,1)S(1)}, bf16[320,128]{1,0:T(8,128)(2,1)S(1)}, u32[]{:S(2)}, u32[]{:S(2)}) collective-permute-start(bf16[320,128]{1,0:T(8,128)(2,1)S(1)} %get-tuple-element.44), channel_id=1, source_target_pairs={{0,4},{4,0},{1,5},{5,1},{2,6},{6,2},{3,7},{7,3},{8,12},{12,8},{9,1... | collective-permute-start | bytes 245768 | tf_op jit(solution)/shard_map/ppermute | solution.py:428
  28.5 1.1 %collective-permute-start.8 = (bf16[320,128]{1,0:T(8,128)(2,1)S(1)}, bf16[320,128]{1,0:T(8,128)(2,1)S(1)}, u32[]{:S(2)}, u32[]{:S(2)}) collective-permute-start(bf16[320,128]{1,0:T(8,128)(2,1)S(1)} %get-tuple-element.45), channel_id=1, source_target_pairs={{0,5},{1,4},{2,7},{3,6},{4,1},{5,0},{6,3},{7,2},{8,13},{9,12},{10,... | collective-permute-start | bytes 245768 | tf_op jit(solution)/shard_map/ppermute | solution.py:434
  29.7 3.3 %collective-permute-done.7.refs_4_ = bf16[320,128]{1,0:T(8,128)(2,1)S(1)} collective-permute-done((bf16[320,128]{1,0:T(8,128)(2,1)S(1)}, bf16[320,128]{1,0:T(8,128)(2,1)S(1)}, u32[]{:S(2)}, u32[]{:S(2)}) %collective-permute-start.7) | collective-permute-done | bytes 81952 | tf_op jit(solution)/shard_map/ppermute | solution.py:428
  32.9 1.3 %collective-permute-done.8.refs_5_ = bf16[320,128]{1,0:T(8,128)(2,1)S(1)} collective-permute-done((bf16[320,128]{1,0:T(8,128)(2,1)S(1)}, bf16[320,128]{1,0:T(8,128)(2,1)S(1)}, u32[]{:S(2)}, u32[]{:S(2)}) %collective-permute-start.8) | collective-permute-done | bytes 81952 | tf_op jit(solution)/shard_map/ppermute | solution.py:434
  34.2 0.0 collective-permute-done.6.refs_3_
  34.2 0.1 near_sum.1
  34.3 3.1 %collective-permute-start.9 = (bf16[320,128]{1,0:T(8,128)(2,1)S(1)}, bf16[320,128]{1,0:T(8,128)(2,1)S(1)}, u32[]{:S(2)}, u32[]{:S(2)}) collective-permute-start(bf16[320,128]{1,0:T(8,128)(2,1)S(1)} %get-tuple-element.48), channel_id=1, source_target_pairs={{0,2},{1,3},{2,0},{3,1},{4,6},{5,7},{6,4},{7,5},{8,10},{9,11},{10,... | collective-permute-start | bytes 245768 | tf_op jit(solution)/shard_map/ppermute | solution.py:437
  37.4 1.1 %second_rows.1 = bf16[1,2,32,4096]{3,2,1,0:T(8,128)(2,1)} custom-call(bf16[1,2,32,4096]{3,2,1,0:T(8,128)(2,1)S(1)} %copy-done, f32[1,4096]{1,0:T(1,128)S(1)} %copy-done.3, f32[2,32,128]{2,1,0:T(8,128)S(1)} %get-tuple-element.28.refs_4_.refs_2_, bf16[32,4096]{1,0:T(8,128)(2,1)S(1)} %collective-permute-done.4.refs_3_, bf16[1,32,4096]{2,1,0:T(8,128)(2,1)S(1)} %copy-done.2, ...), custom_call_target="tpu_custom_call" | custom-call | tf_op jit(solution)/shard_map/second_rows/pallas_call | solution.py:412
  38.5 2.2 %collective-permute-done.9.receive_ref = bf16[320,128]{1,0:T(8,128)(2,1)S(1)} collective-permute-done((bf16[320,128]{1,0:T(8,128)(2,1)S(1)}, bf16[320,128]{1,0:T(8,128)(2,1)S(1)}, u32[]{:S(2)}, u32[]{:S(2)}) %collective-permute-start.9) | collective-permute-done | bytes 81952 | tf_op jit(solution)/shard_map/ppermute | solution.py:437
  40.6 0.7 %finish.1 = (f32[1,2,128,128]{3,2,1,0:T(8,128)}, f32[1,2,128,128]{3,2,1,0:T(8,128)}, f32[32,128]{1,0:T(8,128)}) custom-call(f32[256,128]{1,0:T(8,128)S(1)} %get-tuple-element.46.keep_ref, f32[32,128]{1,0:T(8,128)S(1)} %get-tuple-element.47.gain_ref, bf16[320,128]{1,0:T(8,128)(2,1)S(1)} %collective-permute-done.9.receive_ref), custom_call_target="tpu_custom_call" | custom-call | tf_op jit(solution)/shard_map/finish/pallas_call | solution.py:412
  (2 shorter events, 0.0 us)
Async XLA Ops:
  0.6 12.3 %copy-start = (bf16[1,2,32,4096]{3,2,1,0:T(8,128)(2,1)S(1)}, bf16[1,2,32,4096]{3,2,1,0:T(8,128)(2,1)}, u32[]{:S(2)}) copy-start(bf16[1,2,32,4096]{3,2,1,0:T(8,128)(2,1)} %refs_0_.9) | copy-start | bytes 1572868
  1.6 7.8 %collective-permute-start = (bf16[2,2,64,128]{3,2,1,0:T(8,128)(2,1)S(1)}, bf16[2,2,64,128]{3,2,1,0:T(8,128)(2,1)S(1)}, u32[]{:S(2)}, u32[]{:S(2)}) collective-permute-start(bf16[2,2,64,128]{3,2,1,0:T(8,128)(2,1)S(1)} %get-tuple-element.31), channel_id=1, source_target_pairs={{0,2},{1,3},{2,0},{3,1},{4,6},{5,7},{6,4},{7,5},{8,10},{9,11},{10,... | collective-permute-start | bytes 196616 | tf_op jit(solution)/shard_map/ppermute | solution.py:437
  9.4 3.6 %copy-start.3 = (f32[1,4096]{1,0:T(1,128)S(1)}, f32[1,4096]{1,0:T(1,128)}, u32[]{:S(2)}) copy-start(f32[1,4096]{1,0:T(1,128)} %refs_1_.3) | copy-start | bytes 49156
  9.4 7.9 %copy-start.1 = (bf16[1,32,4096]{2,1,0:T(8,128)(2,1)S(1)}, bf16[1,32,4096]{2,1,0:T(8,128)(2,1)}, u32[]{:S(2)}) copy-start(bf16[1,32,4096]{2,1,0:T(8,128)(2,1)} %refs_3_.1) | copy-start | bytes 786436
  9.4 7.3 %collective-permute-start.3 = (bf16[2,2,2,64,128]{4,3,2,1,0:T(8,128)(2,1)S(1)}, bf16[2,2,2,64,128]{4,3,2,1,0:T(8,128)(2,1)S(1)}, u32[]{:S(2)}, u32[]{:S(2)}) collective-permute-start(bf16[2,2,2,64,128]{4,3,2,1,0:T(8,128)(2,1)S(1)} %pad_maximum_fusion.1.refs_6_.refs_2_.refs_7_), channel_id=1, source_target_pairs={{0,5},{1,4},{2,7},{3,6},{4,1},{5,0},{6,3},{7,2},{8,13},{9,12},{10,... | collective-permute-start | bytes 393224 | tf_op jit(solution)/shard_map/ppermute | solution.py:434
  11.0 6.1 %collective-permute-start.2 = (bf16[2,2,2,64,128]{4,3,2,1,0:T(8,128)(2,1)S(1)}, bf16[2,2,2,64,128]{4,3,2,1,0:T(8,128)(2,1)S(1)}, u32[]{:S(2)}, u32[]{:S(2)}) collective-permute-start(bf16[2,2,2,64,128]{4,3,2,1,0:T(8,128)(2,1)S(1)} %pad_maximum_fusion.1.refs_6_.refs_2_.refs_7_), channel_id=1, source_target_pairs={{0,4},{4,0},{1,5},{5,1},{2,6},{6,2},{3,7},{7,3},{8,12},{12,8},{9,1... | collective-permute-start | bytes 393224 | tf_op jit(solution)/shard_map/ppermute | solution.py:428
  11.5 5.8 %collective-permute-start.1 = (bf16[2,2,2,64,128]{4,3,2,1,0:T(8,128)(2,1)S(1)}, bf16[2,2,2,64,128]{4,3,2,1,0:T(8,128)(2,1)S(1)}, u32[]{:S(2)}, u32[]{:S(2)}) collective-permute-start(bf16[2,2,2,64,128]{4,3,2,1,0:T(8,128)(2,1)S(1)} %pad_maximum_fusion.1.refs_6_.refs_2_.refs_7_), channel_id=1, source_target_pairs={{0,1},{1,0},{2,3},{3,2},{4,5},{5,4},{6,7},{7,6},{8,9},{9,8},{10,11... | collective-permute-start | bytes 393224 | tf_op jit(solution)/shard_map/ppermute | solution.py:426
  13.0 4.4 %copy-start.4 = (s32[5,8]{1,0:T(8,128)S(1)}, s32[5,8]{1,0:T(8,128)}, u32[]{:S(2)}) copy-start(s32[5,8]{1,0:T(8,128)} %refs_0_.6) | copy-start | bytes 484
  18.9 6.5 %collective-permute-start.4 = (bf16[32,4096]{1,0:T(8,128)(2,1)S(1)}, bf16[32,4096]{1,0:T(8,128)(2,1)S(1)}, u32[]{:S(2)}, u32[]{:S(2)}) collective-permute-start(bf16[32,4096]{1,0:T(8,128)(2,1)S(1)} %get-tuple-element.32.refs_6_), channel_id=1, source_target_pairs={{0,24},{8,0},{16,8},{24,16},{1,25},{9,1},{17,9},{25,17},{2,26},{10... | collective-permute-start | bytes 786440 | tf_op jit(solution)/shard_map/ppermute | solution.py:465
  19.4 6.0 %copy-start.2 = (bf16[1,32,4096]{2,1,0:T(8,128)(2,1)S(1)}, bf16[1,32,4096]{2,1,0:T(8,128)(2,1)}, u32[]{:S(2)}) copy-start(bf16[1,32,4096]{2,1,0:T(8,128)(2,1)} %refs_4_.3) | copy-start | bytes 786436
  19.4 6.0 %collective-permute-start.5 = (bf16[2,256,128]{2,1,0:T(8,128)(2,1)S(1)}, bf16[2,256,128]{2,1,0:T(8,128)(2,1)S(1)}, u32[]{:S(2)}, u32[]{:S(2)}) collective-permute-start(bf16[2,256,128]{2,1,0:T(8,128)(2,1)S(1)} %get-tuple-element.38), channel_id=1, source_target_pairs={{0,4},{4,0},{1,5},{5,1},{2,6},{6,2},{3,7},{7,3},{8,12},{12,8},{9,1... | collective-permute-start | bytes 393224 | tf_op jit(solution)/shard_map/ppermute | solution.py:428
  26.1 8.1 %collective-permute-start.6 = (bf16[576,128]{1,0:T(8,128)(2,1)S(1)}, bf16[576,128]{1,0:T(8,128)(2,1)S(1)}, u32[]{:S(2)}, u32[]{:S(2)}) collective-permute-start(bf16[576,128]{1,0:T(8,128)(2,1)S(1)} %get-tuple-element.43), channel_id=1, source_target_pairs={{0,1},{1,0},{2,3},{3,2},{4,5},{5,4},{6,7},{7,6},{8,9},{9,8},{10,11... | collective-permute-start | bytes 442376 | tf_op jit(solution)/shard_map/ppermute | solution.py:426
  27.6 5.3 %collective-permute-start.7 = (bf16[320,128]{1,0:T(8,128)(2,1)S(1)}, bf16[320,128]{1,0:T(8,128)(2,1)S(1)}, u32[]{:S(2)}, u32[]{:S(2)}) collective-permute-start(bf16[320,128]{1,0:T(8,128)(2,1)S(1)} %get-tuple-element.44), channel_id=1, source_target_pairs={{0,4},{4,0},{1,5},{5,1},{2,6},{6,2},{3,7},{7,3},{8,12},{12,8},{9,1... | collective-permute-start | bytes 245768 | tf_op jit(solution)/shard_map/ppermute | solution.py:428
  28.5 5.7 %collective-permute-start.8 = (bf16[320,128]{1,0:T(8,128)(2,1)S(1)}, bf16[320,128]{1,0:T(8,128)(2,1)S(1)}, u32[]{:S(2)}, u32[]{:S(2)}) collective-permute-start(bf16[320,128]{1,0:T(8,128)(2,1)S(1)} %get-tuple-element.45), channel_id=1, source_target_pairs={{0,5},{1,4},{2,7},{3,6},{4,1},{5,0},{6,3},{7,2},{8,13},{9,12},{10,... | collective-permute-start | bytes 245768 | tf_op jit(solution)/shard_map/ppermute | solution.py:434
  34.3 6.4 %collective-permute-start.9 = (bf16[320,128]{1,0:T(8,128)(2,1)S(1)}, bf16[320,128]{1,0:T(8,128)(2,1)S(1)}, u32[]{:S(2)}, u32[]{:S(2)}) collective-permute-start(bf16[320,128]{1,0:T(8,128)(2,1)S(1)} %get-tuple-element.48), channel_id=1, source_target_pairs={{0,2},{1,3},{2,0},{3,1},{4,6},{5,7},{6,4},{7,5},{8,10},{9,11},{10,... | collective-permute-start | bytes 245768 | tf_op jit(solution)/shard_map/ppermute | solution.py:437

commit v5 on v4

--- a/solution.py
+++ b/solution.py
@@ -140,7 +140,9 @@
 
     def __call__(self, turn, kind):
         near, far = turn % self.near_count, turn // self.near_count
-        parts = [ref[self.tick, far, kind] for ref in self.refs[near :: self.near_count]]
+        count = len(self.refs) // 2
+        refs = self.refs[far * count : (far + 1) * count]
+        parts = [ref[self.tick, kind] for ref in refs[near :: self.near_count]]
         return jnp.concatenate(parts, axis=0)
 
 
@@ -267,10 +269,9 @@
     turns = range(tp_count)
     members = cycle * (tp_count // 2)
     x_ref, query_ref, inverse_ref, arrived_ref, output_ref, probs_ref, before_ref = refs[:7]
-    keys, refs = Keys(sizes, 1, refs[7 : 7 + members]), refs[7 + members :]
-    first_refs, refs = refs[:cycle], refs[cycle:]
-    query_grad_ref, gain_rows_ref, own_ref, own_first_ref = refs[:4]
-    message_refs, gain_scratch = refs[4:-1], refs[-1]
+    keys, refs = Keys(sizes, 1, refs[7 : 7 + 2 * members]), refs[7 + 2 * members :]
+    query_grad_ref, gain_rows_ref, own_ref = refs[:3]
+    message_refs, gain_scratch = refs[3:-1], refs[-1]
     arriving = arriving_from([arrived_ref, output_ref])
     inverse = inverse_ref[1]
     columns_of = [Group(sizes, turn) for turn in turns]
@@ -303,15 +304,19 @@
     for ref in message_refs:
         ref[begin : begin + count, :] = high
         ref[begin + count : begin + 2 * count, :] = low
-    begin += 2 * count
-    for near in range(tp_count // 2):
-        total = first_refs[0][near]
-        for ref in first_refs[1:]:
+
+
+def first_sum_kernel(sizes, *refs):
+    cycle = sizes[2]
+    parts, own_ref, message_refs = refs[:cycle], refs[cycle], refs[cycle + 1 :]
+    for near in range(sizes[3] // 2):
+        total = parts[0][near]
+        for ref in parts[1:]:
             total = total + ref[near].astype(F32)
         if near == 0:
-            own_first_ref[...] = total
+            own_ref[...] = total
         else:
-            message_refs[near - 1][begin:, :] = total.astype(BF16)
+            message_refs[near - 1][...] = total.astype(BF16)
 
 
 def second_rows_kernel(sizes, *refs):
@@ -328,36 +333,37 @@
     )
 
 
-def near_sum_kernel(sizes, *refs):
+def first_near_kernel(sizes, own_ref, *refs):
+    block = 2 * sizes[1]
+    keep_ref, send_ref = refs[-2:]
+    total = own_ref[...]
+    for ref in refs[:-2]:
+        total = total + ref[...].astype(F32)
+    keep_ref[...] = total[:block]
+    send_ref[...] = total[block:].astype(BF16)
+
+
+def second_near_kernel(sizes, *refs):
     rows, half, cycle, tp_count, group, columns = sizes
     near_count = tp_count // 2
     members = cycle * near_count
-    own_refs, gain_ref = refs[:TICKS], refs[TICKS]
-    message_refs = refs[TICKS + 1 : TICKS + members]
-    keep_ref, gain_sum_ref, send_ref = refs[TICKS + members :]
+    own_ref, gain_ref = refs[:2]
+    message_refs = refs[2 : 1 + members]
+    keep_ref, gain_sum_ref, send_ref = refs[1 + members :]
     block = 2 * half
-    size = TICKS * block
     count = gain_ref.shape[0]
-    after = 2 * block + 2 * count
-    for tick in range(TICKS):
-        for far in range(2):
-            here = slice(far * block, (far + 1) * block)
-            there = here if tick else slice(after + here.start, after + here.stop)
-            total = own_refs[tick][here, :]
-            for ref in message_refs if tick else message_refs[: near_count - 1]:
-                total = total + ref[there, :].astype(F32)
-            target = slice(tick * block, (tick + 1) * block)
-            if far:
-                send_ref[target, :] = total.astype(BF16)
-            else:
-                keep_ref[target, :] = total
+    total = own_ref[...]
+    for ref in message_refs:
+        total = total + ref[: 2 * block, :].astype(F32)
+    keep_ref[...] = total[:block]
+    send_ref[:block, :] = total[block:].astype(BF16)
     cycle_place = lax.axis_index("ctx")
     near_place = lax.axis_index("tp") % near_count
     values = [joined(*split_two(gain_ref[...]))]
     owners = [cycle_place * near_count + near_place]
+    begin = 2 * block
     for place, ref in enumerate(message_refs, 1):
         step, near = place // near_count, place % near_count
-        begin = 2 * block
         values.append(
             joined(ref[begin : begin + count, :], ref[begin + count : begin + 2 * count, :])
         )
@@ -365,26 +371,27 @@
     gain = in_order(values, owners)
     gain_sum_ref[...] = gain
     high, low = split_two(gain)
-    send_ref[size : size + count, :] = high
-    send_ref[size + count : size + 2 * count, :] = low
-
-
-def finish_kernel(sizes, keep_ref, gain_ref, receive_ref, key_ref, value_ref, gain_out_ref):
-    rows, half, cycle, tp_count, group, columns = sizes
-    parity = lax.axis_index("tp") // (tp_count // 2)
+    send_ref[block : block + count, :] = high
+    send_ref[block + count : block + 2 * count, :] = low
+
+
+def finish_kernel(sizes, *refs):
+    half = sizes[1]
+    keep_refs, receive_refs, gain_ref = refs[:TICKS], refs[TICKS : 2 * TICKS], refs[2 * TICKS]
+    key_ref, value_ref, gain_out_ref = refs[2 * TICKS + 1 :]
+    parity = lax.axis_index("tp") // (sizes[3] // 2)
     block = 2 * half
+    own_first = pl.multiple_of(parity * half, half)
+    other_first = pl.multiple_of((1 - parity) * half, half)
     for tick in range(TICKS):
         for kind, out in enumerate((key_ref, value_ref)):
-            here = slice(tick * block + kind * half, tick * block + (kind + 1) * half)
-            own_first = pl.multiple_of(parity * half, half)
-            other_first = pl.multiple_of((1 - parity) * half, half)
-            out[0, tick, pl.ds(own_first, half), :] = keep_ref[here, :]
-            out[0, tick, pl.ds(other_first, half), :] = receive_ref[here, :].astype(F32)
+            here = slice(kind * half, (kind + 1) * half)
+            out[0, tick, pl.ds(own_first, half), :] = keep_refs[tick][here, :]
+            out[0, tick, pl.ds(other_first, half), :] = receive_refs[tick][here, :].astype(F32)
     count = gain_ref.shape[0]
-    size = 2 * block
+    last = receive_refs[TICKS - 1]
     own = joined(*split_two(gain_ref[...]))
-    other = joined(receive_ref[size : size + count, :], receive_ref[size + count :, :])
-    gain_out_ref[...] = own + other
+    gain_out_ref[...] = own + joined(last[block : block + count, :], last[block + count :, :])
 
 
 def shape(dims, dtype):
@@ -443,9 +450,13 @@
         (jnp.stack([keys[0], values[0]]),),
         [sections, sections],
     )
-    pair = jnp.stack([own_kv, to_far(other_kv)], axis=1)
+    far_kv = to_far(other_kv)
     places = [(step, near) for step in range(cycle) for near in range(near_count)][1:]
-    kv = [pair] + [to_near(pair, step, near) for step, near in places]
+    kv = [
+        block if place == (0, 0) else to_near(block, *place)
+        for block in (own_kv, far_kv)
+        for place in [(0, 0)] + places
+    ]
     queries, inverse = call(
         norm_kernel,
         "norm",
@@ -493,11 +504,8 @@
         [shape((tp_count, key_count, stacked), F32)],
         scalars=1,
     )
-    messages = [
-        shape((pair_rows * (2 if step == 0 else 1) + 2 * gain_count, HD), BF16)
-        for step, near in places
-    ]
-    query_grad_second, gain_rows, own_second, own_first, *sends = call(
+    message = shape((pair_rows + 2 * gain_count, HD), BF16)
+    query_grad_second, gain_rows, own_second, *sends = call(
         functools.partial(second_keys_kernel, sizes),
         "second_keys",
         (
@@ -509,12 +517,18 @@
             probs_second,
             gain_first,
             *kv,
-            *sums_first,
         ),
-        [low_rows, gain_shape, own_shape, own_shape] + messages,
+        [low_rows, gain_shape, own_shape] + [message] * len(places),
         scratch=[pltpu.VMEM((gain_count, HD), F32)],
     )
     received = [to_near(value, -step, near) for value, (step, near) in zip(sends, places)]
+    own_first, *sends_first = call(
+        functools.partial(first_sum_kernel, sizes),
+        "first_sum",
+        sums_first,
+        [own_shape] + [shape((pair_rows, HD), BF16)] * (near_count - 1),
+    )
+    received_first = [to_near(value, 0, near) for near, value in enumerate(sends_first, 1)]
     (input_grads,) = call(
         functools.partial(second_rows_kernel, sizes),
         "second_rows",
@@ -529,17 +543,24 @@
         ),
         [shape((1, ticks, rows, columns), BF16)],
     )
-    keep, gain_sum, send = call(
-        functools.partial(near_sum_kernel, sizes),
-        "near_sum",
-        (own_first, own_second, gain_rows, *received),
-        [own_shape, gain_shape, shape((pair_rows + 2 * gain_count, HD), BF16)],
+    keep_shape = shape((block, HD), F32)
+    keep_first, send_first = call(
+        functools.partial(first_near_kernel, sizes),
+        "first_near",
+        (own_first, *received_first),
+        [keep_shape, shape((block, HD), BF16)],
+    )
+    keep_second, gain_sum, send_second = call(
+        functools.partial(second_near_kernel, sizes),
+        "second_near",
+        (own_second, gain_rows, *received),
+        [keep_shape, gain_shape, shape((block + 2 * gain_count, HD), BF16)],
     )
     grads_shape = shape((1, ticks, block, HD), F32)
     key_grads, value_grads, gain_grads = call(
         functools.partial(finish_kernel, sizes),
         "finish",
-        (keep, gain_sum, to_far(send)),
+        (keep_first, keep_second, to_far(send_first), to_far(send_second), gain_sum),
         [grads_shape, grads_shape, gain_shape],
     )
     return input_grads, key_grads, value_grads, gain_grads.reshape(1, columns)

time: 41.5 us -> 39.1 us (0.942)
  waiting for transfers between devices: 18 us -> 9.2 us
  starting transfers between devices: 15.8 us -> 21.1 us
  local copies, waits for them, and re-layouts: 0.02 us -> 1.07 us
    ppermute x3 -> x4, waiting for transfers between devices: 7.17 us -> 1.52 us  [to_near(): lax.ppermute(value, 'ctx', [(i, (i + step) % cycle) for i in range(cycle)])]
    ppermute x2 -> x3, starting transfers between devices: 2.74 us -> 6.58 us  [to_near(): return lax.ppermute(value, ('ctx', 'tp'), pairs)]
    ppermute x2 -> x3, waiting for transfers between devices: 5.83 us -> 3 us  [to_far(): lax.ppermute(value, 'tp', [(i, i ^ near_count) for i in range(tp_count)])]
    ppermute x2 -> x3, waiting for transfers between devices: 4.71 us -> 3.41 us  [to_near(): return lax.ppermute(value, ('ctx', 'tp'), pairs)]
    unnamed x10 -> x12, local copies, waits for them, and re-layouts: 0.02 us -> 1.07 us
    ppermute x3 -> x4, starting transfers between devices: 2.84 us -> 3.67 us  [to_near(): lax.ppermute(value, 'ctx', [(i, (i + step) % cycle) for i in range(cycle)])]
    ppermute x1, waiting for transfers between devices: 0.01 us -> 0.81 us  [on_device(): lax.ppermute(input_grad_first, 'pipe', [(i, (i - 1) % pipe_count) for i i...]
    ppermute x2 -> x4, starting transfers between devices: 2.98 us -> 3.29 us  [to_near(): return lax.ppermute(value, 'tp', [(i, i ^ near) for i in range(tp_count)])]
  transfers between devices with their start and end apart: 10 -> 15, of which waited for: 8 -> 7; matrix products, arithmetic and copies ran while one was open for 0% -> 0% of each run, Pallas kernels for 7% -> 9%
where the time goes in v5:
time: 39.1 us; the launch traced here: 38.9 us
  starting transfers between devices  21.1 us (54%)
  waiting for transfers between devices  9.2 us (24%)
  Pallas kernels  5.94 us (15%)
  local copies, waits for them, and re-layouts  1.07 us (3%)
  other arithmetic  0.93 us (2%)
  between operations  0.76 us (2%)
    ppermute x3, starting transfers between devices, to_far(): lax.ppermute(value, 'tp', [(i, i ^ near_count) for i in range(tp_count)])  7.46 us
    ppermute x3, starting transfers between devices, to_near(): return lax.ppermute(value, ('ctx', 'tp'), pairs)  6.58 us
    pallas_call x11, Pallas kernels, call(): pl.pallas_call(kernel, out_shape=out_shape, in_specs=in_specs, out_specs=...  5.94 us
    ppermute x4, starting transfers between devices, to_near(): lax.ppermute(value, 'ctx', [(i, (i + step) % cycle) for i in range(cycle)])  3.67 us
    ppermute x3, waiting for transfers between devices, to_near(): return lax.ppermute(value, ('ctx', 'tp'), pairs)  3.41 us
    ppermute x4, starting transfers between devices, to_near(): return lax.ppermute(value, 'tp', [(i, i ^ near) for i in range(tp_count)])  3.29 us
    ppermute x3, waiting for transfers between devices, to_far(): lax.ppermute(value, 'tp', [(i, i ^ near_count) for i in range(tp_count)])  3 us
    ppermute x4, waiting for transfers between devices, to_near(): lax.ppermute(value, 'ctx', [(i, (i + step) % cycle) for i in range(cycle)])  1.52 us
  transfers between devices with their start and end apart: 15, of which 7 were waited for; matrix products, arithmetic and copies ran while one was open for 0% of the time, Pallas kernels for 9%

profile of v5, /device:TPU:0, one launch (start us, length us, event | category | flops | bytes accessed | tf_op | source)
XLA Modules:
  0.0 38.9 jit_solution(1703516996790909671)
XLA Ops:
  0.6 0.0 copy-start.2
  0.6 0.9 %pad_maximum_fusion.both_ref = bf16[2,2,128,128]{3,2,1,0:T(8,128)(2,1)S(1)} fusion(bf16[1,2,128,128]{3,2,1,0:T(8,128)(2,1)} %param.9, bf16[1,2,128,128]{3,2,1,0:T(8,128)(2,1)} %param.8), kind=kLoop, calls=%fused_computation | loop fusion | flops 65536 | bytes 262144 | tf_op jit(solution)/shard_map/stack | solution.py:450
  1.6 0.0 copy-start.4
  1.6 4.1 %collective-permute-start.3 = (bf16[2,2,64,128]{3,2,1,0:T(8,128)(2,1)S(1)}, bf16[2,2,64,128]{3,2,1,0:T(8,128)(2,1)S(1)}, u32[]{:S(2)}, u32[]{:S(2)}) collective-permute-start(bf16[2,2,64,128]{3,2,1,0:T(8,128)(2,1)S(1)} %get-tuple-element.34), channel_id=1, source_target_pairs={{0,2},{1,3},{2,0},{3,1},{4,6},{5,7},{6,4},{7,5},{8,10},{9,11},{10,... | collective-permute-start | bytes 196616 | tf_op jit(solution)/shard_map/ppermute | solution.py:444
  5.7 2.5 %collective-permute-start.2 = (bf16[2,2,64,128]{3,2,1,0:T(8,128)(2,1)S(1)}, bf16[2,2,64,128]{3,2,1,0:T(8,128)(2,1)S(1)}, u32[]{:S(2)}, u32[]{:S(2)}) collective-permute-start(bf16[2,2,64,128]{3,2,1,0:T(8,128)(2,1)S(1)} %get-tuple-element.33.refs_6_.refs_2_.refs_7_), channel_id=1, source_target_pairs={{0,5},{1,4},{2,7},{3,6},{4,1},{5,0},{6,3},{7,2},{8,13},{9,12},{10,... | collective-permute-start | bytes 196616 | tf_op jit(solution)/shard_map/ppermute | solution.py:441
  8.3 0.5 %collective-permute-start.1 = (bf16[2,2,64,128]{3,2,1,0:T(8,128)(2,1)S(1)}, bf16[2,2,64,128]{3,2,1,0:T(8,128)(2,1)S(1)}, u32[]{:S(2)}, u32[]{:S(2)}) collective-permute-start(bf16[2,2,64,128]{3,2,1,0:T(8,128)(2,1)S(1)} %get-tuple-element.33.refs_6_.refs_2_.refs_7_), channel_id=1, source_target_pairs={{0,4},{4,0},{1,5},{5,1},{2,6},{6,2},{3,7},{7,3},{8,12},{12,8},{9,1... | collective-permute-start | bytes 196616 | tf_op jit(solution)/shard_map/ppermute | solution.py:435
  8.8 0.4 %collective-permute-start = (bf16[2,2,64,128]{3,2,1,0:T(8,128)(2,1)S(1)}, bf16[2,2,64,128]{3,2,1,0:T(8,128)(2,1)S(1)}, u32[]{:S(2)}, u32[]{:S(2)}) collective-permute-start(bf16[2,2,64,128]{3,2,1,0:T(8,128)(2,1)S(1)} %get-tuple-element.33.refs_6_.refs_2_.refs_7_), channel_id=1, source_target_pairs={{0,1},{1,0},{2,3},{3,2},{4,5},{5,4},{6,7},{7,6},{8,9},{9,8},{10,11... | collective-permute-start | bytes 196616 | tf_op jit(solution)/shard_map/ppermute | solution.py:433
  9.2 0.0 collective-permute-done.3.refs_10_.refs_6_.refs_11_
  9.2 2.5 %collective-permute-start.6 = (bf16[2,2,64,128]{3,2,1,0:T(8,128)(2,1)S(1)}, bf16[2,2,64,128]{3,2,1,0:T(8,128)(2,1)S(1)}, u32[]{:S(2)}, u32[]{:S(2)}) collective-permute-start(bf16[2,2,64,128]{3,2,1,0:T(8,128)(2,1)S(1)} %collective-permute-done.3.refs_10_.refs_6_.refs_11_), channel_id=1, source_target_pairs={{0,5},{1,4},{2,7},{3,6},{4,1},{5,0},{6,3},{7,2},{8,13},{9,12},{10,... | collective-permute-start | bytes 196616 | tf_op jit(solution)/shard_map/ppermute | solution.py:441
  11.7 0.5 %collective-permute-start.5 = (bf16[2,2,64,128]{3,2,1,0:T(8,128)(2,1)S(1)}, bf16[2,2,64,128]{3,2,1,0:T(8,128)(2,1)S(1)}, u32[]{:S(2)}, u32[]{:S(2)}) collective-permute-start(bf16[2,2,64,128]{3,2,1,0:T(8,128)(2,1)S(1)} %collective-permute-done.3.refs_10_.refs_6_.refs_11_), channel_id=1, source_target_pairs={{0,4},{4,0},{1,5},{5,1},{2,6},{6,2},{3,7},{7,3},{8,12},{12,8},{9,1... | collective-permute-start | bytes 196616 | tf_op jit(solution)/shard_map/ppermute | solution.py:435
  12.3 0.0 collective-permute-done.2.refs_9_.refs_5_.refs_10_
  12.3 0.9 %collective-permute-start.4 = (bf16[2,2,64,128]{3,2,1,0:T(8,128)(2,1)S(1)}, bf16[2,2,64,128]{3,2,1,0:T(8,128)(2,1)S(1)}, u32[]{:S(2)}, u32[]{:S(2)}) collective-permute-start(bf16[2,2,64,128]{3,2,1,0:T(8,128)(2,1)S(1)} %collective-permute-done.3.refs_10_.refs_6_.refs_11_), channel_id=1, source_target_pairs={{0,1},{1,0},{2,3},{3,2},{4,5},{5,4},{6,7},{7,6},{8,9},{9,8},{10,11... | collective-permute-start | bytes 196616 | tf_op jit(solution)/shard_map/ppermute | solution.py:433
  13.2 0.0 copy-done.4
  13.2 0.0 copy-start
  13.2 1.0 %copy-done = bf16[1,2,32,4096]{3,2,1,0:T(8,128)(2,1)S(1)} copy-done((bf16[1,2,32,4096]{3,2,1,0:T(8,128)(2,1)S(1)}, bf16[1,2,32,4096]{3,2,1,0:T(8,128)(2,1)}, u32[]{:S(2)}) %copy-start) | copy-done | bytes 524312
  14.2 0.0 copy-start.5
  14.2 0.3 norm.1
  14.5 0.0 collective-permute-done.1.refs_8_.refs_4_.refs_9_
  14.5 0.0 collective-permute-done.refs_7_.refs_3_.refs_8_
  14.5 1.0 %collective-permute-done.6.refs_13_.refs_9_.refs_14_ = bf16[2,2,64,128]{3,2,1,0:T(8,128)(2,1)S(1)} collective-permute-done((bf16[2,2,64,128]{3,2,1,0:T(8,128)(2,1)S(1)}, bf16[2,2,64,128]{3,2,1,0:T(8,128)(2,1)S(1)}, u32[]{:S(2)}, u32[]{:S(2)}) %collective-permute-start.6) | collective-permute-done | bytes 65568 | tf_op jit(solution)/shard_map/ppermute | solution.py:441
  15.5 0.6 %collective-permute-done.5.refs_12_.refs_8_.refs_13_ = bf16[2,2,64,128]{3,2,1,0:T(8,128)(2,1)S(1)} collective-permute-done((bf16[2,2,64,128]{3,2,1,0:T(8,128)(2,1)S(1)}, bf16[2,2,64,128]{3,2,1,0:T(8,128)(2,1)S(1)}, u32[]{:S(2)}, u32[]{:S(2)}) %collective-permute-start.5) | collective-permute-done | bytes 65568 | tf_op jit(solution)/shard_map/ppermute | solution.py:435
  16.1 0.4 %collective-permute-done.4.refs_11_.refs_7_.refs_12_ = bf16[2,2,64,128]{3,2,1,0:T(8,128)(2,1)S(1)} collective-permute-done((bf16[2,2,64,128]{3,2,1,0:T(8,128)(2,1)S(1)}, bf16[2,2,64,128]{3,2,1,0:T(8,128)(2,1)S(1)}, u32[]{:S(2)}, u32[]{:S(2)}) %collective-permute-start.4) | collective-permute-done | bytes 65568 | tf_op jit(solution)/shard_map/ppermute | solution.py:433
  16.5 0.0 copy-done.2
  16.5 0.0 copy-done.5
  16.5 1.6 %first_rows.1 = (bf16[32,4096]{1,0:T(8,128)(2,1)S(1)}, bf16[32,4096]{1,0:T(8,128)(2,1)S(1)}, bf16[4,128,256]{2,1,0:T(8,128)(2,1)S(1)}, bf16[4,128,256]{2,1,0:T(8,128)(2,1)S(1)}) custom-call(s32[5,8]{1,0:T(8,128)S(1)} %copy-done.5, bf16[1,2,32,4096]{3,2,1,0:T(8,128)(2,1)S(1)} %copy-done, f32[1,4096]{1,0:T(1,128)S(1)} %copy-done.4, ...), custom_call_target="tpu_custom_call" | custom-call | tf_op jit(solution)/shard_map/first_rows/pallas_call | solution.py:419
  18.1 0.1 collective-permute-start.7
  18.2 0.5 %first_keys.1 = (f32[32,128]{1,0:T(8,128)S(1)}, f32[2,256,128]{2,1,0:T(8,128)S(1)}, bf16[2,256,128]{2,1,0:T(8,128)(2,1)S(1)}) custom-call(bf16[1,2,32,4096]{3,2,1,0:T(8,128)(2,1)S(1)} %copy-done, bf16[2,32,4096]{2,1,0:T(8,128)(2,1)S(1)} %get-tuple-element.32.refs_3_.refs_1_, f32[2,32,128]{2,1,0:T(8,128)S(1)} %get-tuple-element.31.refs_4_.refs_2_, ...), custom_call_target="tpu_custom_call" | custom-call | tf_op jit(solution)/shard_map/first_keys/pallas_call | solution.py:419
  18.6 0.0 copy-start.1
  18.6 0.0 copy-start.3
  18.7 1.6 %collective-permute-start.8 = (bf16[2,256,128]{2,1,0:T(8,128)(2,1)S(1)}, bf16[2,256,128]{2,1,0:T(8,128)(2,1)S(1)}, u32[]{:S(2)}, u32[]{:S(2)}) collective-permute-start(bf16[2,256,128]{2,1,0:T(8,128)(2,1)S(1)} %get-tuple-element.42), channel_id=1, source_target_pairs={{0,4},{4,0},{1,5},{5,1},{2,6},{6,2},{3,7},{7,3},{8,12},{12,8},{9,1... | collective-permute-start | bytes 393224 | tf_op jit(solution)/shard_map/ppermute | solution.py:435
  20.2 1.0 %second_probs.1.refs_5_ = f32[4,128,256]{2,1,0:T(8,128)S(1)} custom-call(s32[5,8]{1,0:T(8,128)S(1)} %copy-done.5, bf16[2,32,4096]{2,1,0:T(8,128)(2,1)S(1)} %get-tuple-element.32.refs_3_.refs_1_, bf16[2,2,64,128]{3,2,1,0:T(8,128)(2,1)S(1)} %get-tuple-element.33.refs_6_.refs_2_.refs_7_, ...), custom_call_target="tpu_custom_call" | custom-call | tf_op jit(solution)/shard_map/second_probs/pallas_call | solution.py:419
  21.2 0.8 %collective-permute-done.7.refs_3_ = bf16[32,4096]{1,0:T(8,128)(2,1)S(1)} collective-permute-done((bf16[32,4096]{1,0:T(8,128)(2,1)S(1)}, bf16[32,4096]{1,0:T(8,128)(2,1)S(1)}, u32[]{:S(2)}, u32[]{:S(2)}) %collective-permute-start.7) | collective-permute-done | bytes 262176 | tf_op jit(solution)/shard_map/ppermute | solution.py:476
  22.0 0.0 copy-done.1
  22.0 0.0 copy-done.3
  22.0 0.7 %second_keys.1 = (bf16[32,4096]{1,0:T(8,128)(2,1)S(1)}, f32[32,128]{1,0:T(8,128)S(1)}, f32[256,128]{1,0:T(8,128)S(1)}, bf16[320,128]{1,0:T(8,128)(2,1)S(1)}, bf1...) custom-call(bf16[1,2,32,4096]{3,2,1,0:T(8,128)(2,1)S(1)} %copy-done.1, ...), custom_call_target="tpu_custom_call" | custom-call | tf_op jit(solution)/shard_map/second_keys/pallas_call | solution.py:419
  22.7 1.0 %collective-permute-start.10 = (bf16[320,128]{1,0:T(8,128)(2,1)S(1)}, bf16[320,128]{1,0:T(8,128)(2,1)S(1)}, u32[]{:S(2)}, u32[]{:S(2)}) collective-permute-start(bf16[320,128]{1,0:T(8,128)(2,1)S(1)} %get-tuple-element.48), channel_id=1, source_target_pairs={{0,1},{1,0},{2,3},{3,2},{4,5},{5,4},{6,7},{7,6},{8,9},{9,8},{10,11... | collective-permute-start | bytes 245768 | tf_op jit(solution)/shard_map/ppermute | solution.py:433
  23.7 1.1 %collective-permute-start.11 = (bf16[320,128]{1,0:T(8,128)(2,1)S(1)}, bf16[320,128]{1,0:T(8,128)(2,1)S(1)}, u32[]{:S(2)}, u32[]{:S(2)}) collective-permute-start(bf16[320,128]{1,0:T(8,128)(2,1)S(1)} %get-tuple-element.49), channel_id=1, source_target_pairs={{0,4},{4,0},{1,5},{5,1},{2,6},{6,2},{3,7},{7,3},{8,12},{12,8},{9,1... | collective-permute-start | bytes 245768 | tf_op jit(solution)/shard_map/ppermute | solution.py:435
  24.8 1.5 %collective-permute-start.12 = (bf16[320,128]{1,0:T(8,128)(2,1)S(1)}, bf16[320,128]{1,0:T(8,128)(2,1)S(1)}, u32[]{:S(2)}, u32[]{:S(2)}) collective-permute-start(bf16[320,128]{1,0:T(8,128)(2,1)S(1)} %get-tuple-element.50), channel_id=1, source_target_pairs={{0,5},{1,4},{2,7},{3,6},{4,1},{5,0},{6,3},{7,2},{8,13},{9,12},{10,... | collective-permute-start | bytes 245768 | tf_op jit(solution)/shard_map/ppermute | solution.py:441
  26.3 0.0 collective-permute-done.8.refs_1_
  26.3 1.0 %collective-permute-start.9 = (bf16[256,128]{1,0:T(8,128)(2,1)S(1)}, bf16[256,128]{1,0:T(8,128)(2,1)S(1)}, u32[]{:S(2)}, u32[]{:S(2)}) collective-permute-start(bf16[256,128]{1,0:T(8,128)(2,1)S(1)} %get-tuple-element.44), channel_id=1, source_target_pairs={{0,1},{1,0},{2,3},{3,2},{4,5},{5,4},{6,7},{7,6},{8,9},{9,8},{10,11... | collective-permute-start | bytes 196616 | tf_op jit(solution)/shard_map/ppermute | solution.py:433
  27.3 0.0 collective-permute-done.10.refs_2_
  27.3 0.9 %collective-permute-done.11.refs_3_ = bf16[320,128]{1,0:T(8,128)(2,1)S(1)} collective-permute-done((bf16[320,128]{1,0:T(8,128)(2,1)S(1)}, bf16[320,128]{1,0:T(8,128)(2,1)S(1)}, u32[]{:S(2)}, u32[]{:S(2)}) %collective-permute-start.11) | collective-permute-done | bytes 81952 | tf_op jit(solution)/shard_map/ppermute | solution.py:435
  28.2 2.4 %collective-permute-done.12.refs_4_ = bf16[320,128]{1,0:T(8,128)(2,1)S(1)} collective-permute-done((bf16[320,128]{1,0:T(8,128)(2,1)S(1)}, bf16[320,128]{1,0:T(8,128)(2,1)S(1)}, u32[]{:S(2)}, u32[]{:S(2)}) %collective-permute-start.12) | collective-permute-done | bytes 81952 | tf_op jit(solution)/shard_map/ppermute | solution.py:441
  30.6 0.1 second_near.1
  30.7 2.6 %collective-permute-start.14 = (bf16[192,128]{1,0:T(8,128)(2,1)S(1)}, bf16[192,128]{1,0:T(8,128)(2,1)S(1)}, u32[]{:S(2)}, u32[]{:S(2)}) collective-permute-start(bf16[192,128]{1,0:T(8,128)(2,1)S(1)} %get-tuple-element.53), channel_id=1, source_target_pairs={{0,2},{1,3},{2,0},{3,1},{4,6},{5,7},{6,4},{7,5},{8,10},{9,11},{10,... | collective-permute-start | bytes 147464 | tf_op jit(solution)/shard_map/ppermute | solution.py:444
  33.3 0.0 collective-permute-done.9.refs_0_
  33.3 0.8 %collective-permute-start.13 = (bf16[128,128]{1,0:T(8,128)(2,1)S(1)}, bf16[128,128]{1,0:T(8,128)(2,1)S(1)}, u32[]{:S(2)}, u32[]{:S(2)}) collective-permute-start(bf16[128,128]{1,0:T(8,128)(2,1)S(1)} %get-tuple-element.52), channel_id=1, source_target_pairs={{0,2},{1,3},{2,0},{3,1},{4,6},{5,7},{6,4},{7,5},{8,10},{9,11},{10,... | collective-permute-start | bytes 98312 | tf_op jit(solution)/shard_map/ppermute | solution.py:444
  34.1 1.1 %second_rows.1 = bf16[1,2,32,4096]{3,2,1,0:T(8,128)(2,1)} custom-call(bf16[1,2,32,4096]{3,2,1,0:T(8,128)(2,1)S(1)} %copy-done.1, f32[1,4096]{1,0:T(1,128)S(1)} %copy-done.4, f32[2,32,128]{2,1,0:T(8,128)S(1)} %get-tuple-element.31.refs_4_.refs_2_, bf16[32,4096]{1,0:T(8,128)(2,1)S(1)} %collective-permute-done.7.refs_3_, bf16[1,32,4096]{2,1,0:T(8,128)(2,1)S(1)} %copy-done.3, ...), custom_call_target="tpu_custom_call" | custom-call | tf_op jit(solution)/shard_map/second_rows/pallas_call | solution.py:419
  35.2 3.0 %collective-permute-done.13.refs_2_ = bf16[128,128]{1,0:T(8,128)(2,1)S(1)} collective-permute-done((bf16[128,128]{1,0:T(8,128)(2,1)S(1)}, bf16[128,128]{1,0:T(8,128)(2,1)S(1)}, u32[]{:S(2)}, u32[]{:S(2)}) %collective-permute-start.13) | collective-permute-done | bytes 32800 | tf_op jit(solution)/shard_map/ppermute | solution.py:444
  38.2 0.0 collective-permute-done.14.refs_3_
  38.2 0.7 %finish.1 = (f32[1,2,128,128]{3,2,1,0:T(8,128)}, f32[1,2,128,128]{3,2,1,0:T(8,128)}, f32[32,128]{1,0:T(8,128)}) custom-call(f32[128,128]{1,0:T(8,128)S(1)} %get-tuple-element.45.refs_0_, f32[128,128]{1,0:T(8,128)S(1)} %get-tuple-element.51.refs_1_, bf16[128,128]{1,0:T(8,128)(2,1)S(1)} %collective-permute-done.13.refs_2_, ...), custom_call_target="tpu_custom_call" | custom-call | tf_op jit(solution)/shard_map/finish/pallas_call | solution.py:419
  (3 shorter events, 0.1 us)
Async XLA Ops:
  0.6 15.9 %copy-start.2 = (bf16[1,32,4096]{2,1,0:T(8,128)(2,1)S(1)}, bf16[1,32,4096]{2,1,0:T(8,128)(2,1)}, u32[]{:S(2)}) copy-start(bf16[1,32,4096]{2,1,0:T(8,128)(2,1)} %refs_3_.1) | copy-start | bytes 786436
  1.6 11.6 %copy-start.4 = (f32[1,4096]{1,0:T(1,128)S(1)}, f32[1,4096]{1,0:T(1,128)}, u32[]{:S(2)}) copy-start(f32[1,4096]{1,0:T(1,128)} %refs_1_.3) | copy-start | bytes 49156
  1.6 7.6 %collective-permute-start.3 = (bf16[2,2,64,128]{3,2,1,0:T(8,128)(2,1)S(1)}, bf16[2,2,64,128]{3,2,1,0:T(8,128)(2,1)S(1)}, u32[]{:S(2)}, u32[]{:S(2)}) collective-permute-start(bf16[2,2,64,128]{3,2,1,0:T(8,128)(2,1)S(1)} %get-tuple-element.34), channel_id=1, source_target_pairs={{0,2},{1,3},{2,0},{3,1},{4,6},{5,7},{6,4},{7,5},{8,10},{9,11},{10,... | collective-permute-start | bytes 196616 | tf_op jit(solution)/shard_map/ppermute | solution.py:444
  5.7 6.5 %collective-permute-start.2 = (bf16[2,2,64,128]{3,2,1,0:T(8,128)(2,1)S(1)}, bf16[2,2,64,128]{3,2,1,0:T(8,128)(2,1)S(1)}, u32[]{:S(2)}, u32[]{:S(2)}) collective-permute-start(bf16[2,2,64,128]{3,2,1,0:T(8,128)(2,1)S(1)} %get-tuple-element.33.refs_6_.refs_2_.refs_7_), channel_id=1, source_target_pairs={{0,5},{1,4},{2,7},{3,6},{4,1},{5,0},{6,3},{7,2},{8,13},{9,12},{10,... | collective-permute-start | bytes 196616 | tf_op jit(solution)/shard_map/ppermute | solution.py:441
  8.3 6.2 %collective-permute-start.1 = (bf16[2,2,64,128]{3,2,1,0:T(8,128)(2,1)S(1)}, bf16[2,2,64,128]{3,2,1,0:T(8,128)(2,1)S(1)}, u32[]{:S(2)}, u32[]{:S(2)}) collective-permute-start(bf16[2,2,64,128]{3,2,1,0:T(8,128)(2,1)S(1)} %get-tuple-element.33.refs_6_.refs_2_.refs_7_), channel_id=1, source_target_pairs={{0,4},{4,0},{1,5},{5,1},{2,6},{6,2},{3,7},{7,3},{8,12},{12,8},{9,1... | collective-permute-start | bytes 196616 | tf_op jit(solution)/shard_map/ppermute | solution.py:435
  8.8 5.7 %collective-permute-start = (bf16[2,2,64,128]{3,2,1,0:T(8,128)(2,1)S(1)}, bf16[2,2,64,128]{3,2,1,0:T(8,128)(2,1)S(1)}, u32[]{:S(2)}, u32[]{:S(2)}) collective-permute-start(bf16[2,2,64,128]{3,2,1,0:T(8,128)(2,1)S(1)} %get-tuple-element.33.refs_6_.refs_2_.refs_7_), channel_id=1, source_target_pairs={{0,1},{1,0},{2,3},{3,2},{4,5},{5,4},{6,7},{7,6},{8,9},{9,8},{10,11... | collective-permute-start | bytes 196616 | tf_op jit(solution)/shard_map/ppermute | solution.py:433
  9.2 6.3 %collective-permute-start.6 = (bf16[2,2,64,128]{3,2,1,0:T(8,128)(2,1)S(1)}, bf16[2,2,64,128]{3,2,1,0:T(8,128)(2,1)S(1)}, u32[]{:S(2)}, u32[]{:S(2)}) collective-permute-start(bf16[2,2,64,128]{3,2,1,0:T(8,128)(2,1)S(1)} %collective-permute-done.3.refs_10_.refs_6_.refs_11_), channel_id=1, source_target_pairs={{0,5},{1,4},{2,7},{3,6},{4,1},{5,0},{6,3},{7,2},{8,13},{9,12},{10,... | collective-permute-start | bytes 196616 | tf_op jit(solution)/shard_map/ppermute | solution.py:441
  11.7 4.3 %collective-permute-start.5 = (bf16[2,2,64,128]{3,2,1,0:T(8,128)(2,1)S(1)}, bf16[2,2,64,128]{3,2,1,0:T(8,128)(2,1)S(1)}, u32[]{:S(2)}, u32[]{:S(2)}) collective-permute-start(bf16[2,2,64,128]{3,2,1,0:T(8,128)(2,1)S(1)} %collective-permute-done.3.refs_10_.refs_6_.refs_11_), channel_id=1, source_target_pairs={{0,4},{4,0},{1,5},{5,1},{2,6},{6,2},{3,7},{7,3},{8,12},{12,8},{9,1... | collective-permute-start | bytes 196616 | tf_op jit(solution)/shard_map/ppermute | solution.py:435
  12.3 4.3 %collective-permute-start.4 = (bf16[2,2,64,128]{3,2,1,0:T(8,128)(2,1)S(1)}, bf16[2,2,64,128]{3,2,1,0:T(8,128)(2,1)S(1)}, u32[]{:S(2)}, u32[]{:S(2)}) collective-permute-start(bf16[2,2,64,128]{3,2,1,0:T(8,128)(2,1)S(1)} %collective-permute-done.3.refs_10_.refs_6_.refs_11_), channel_id=1, source_target_pairs={{0,1},{1,0},{2,3},{3,2},{4,5},{5,4},{6,7},{7,6},{8,9},{9,8},{10,11... | collective-permute-start | bytes 196616 | tf_op jit(solution)/shard_map/ppermute | solution.py:433
  13.2 1.0 %copy-start = (bf16[1,2,32,4096]{3,2,1,0:T(8,128)(2,1)S(1)}, bf16[1,2,32,4096]{3,2,1,0:T(8,128)(2,1)}, u32[]{:S(2)}) copy-start(bf16[1,2,32,4096]{3,2,1,0:T(8,128)(2,1)} %refs_0_.9) | copy-start | bytes 1572868
  14.2 2.3 %copy-start.5 = (s32[5,8]{1,0:T(8,128)S(1)}, s32[5,8]{1,0:T(8,128)}, u32[]{:S(2)}) copy-start(s32[5,8]{1,0:T(8,128)} %refs_0_.6) | copy-start | bytes 484
  18.1 3.9 %collective-permute-start.7 = (bf16[32,4096]{1,0:T(8,128)(2,1)S(1)}, bf16[32,4096]{1,0:T(8,128)(2,1)S(1)}, u32[]{:S(2)}, u32[]{:S(2)}) collective-permute-start(bf16[32,4096]{1,0:T(8,128)(2,1)S(1)} %get-tuple-element.35.refs_6_), channel_id=1, source_target_pairs={{0,24},{8,0},{16,8},{24,16},{1,25},{9,1},{17,9},{25,17},{2,26},{10... | collective-permute-start | bytes 786440 | tf_op jit(solution)/shard_map/ppermute | solution.py:476
  18.6 3.4 %copy-start.1 = (bf16[1,2,32,4096]{3,2,1,0:T(8,128)(2,1)S(1)}, bf16[1,2,32,4096]{3,2,1,0:T(8,128)(2,1)}, u32[]{:S(2)}) copy-start(bf16[1,2,32,4096]{3,2,1,0:T(8,128)(2,1)} %refs_0_.9) | copy-start | bytes 1572868
  18.6 3.4 %copy-start.3 = (bf16[1,32,4096]{2,1,0:T(8,128)(2,1)S(1)}, bf16[1,32,4096]{2,1,0:T(8,128)(2,1)}, u32[]{:S(2)}) copy-start(bf16[1,32,4096]{2,1,0:T(8,128)(2,1)} %refs_4_.3) | copy-start | bytes 786436
  18.7 7.6 %collective-permute-start.8 = (bf16[2,256,128]{2,1,0:T(8,128)(2,1)S(1)}, bf16[2,256,128]{2,1,0:T(8,128)(2,1)S(1)}, u32[]{:S(2)}, u32[]{:S(2)}) collective-permute-start(bf16[2,256,128]{2,1,0:T(8,128)(2,1)S(1)} %get-tuple-element.42), channel_id=1, source_target_pairs={{0,4},{4,0},{1,5},{5,1},{2,6},{6,2},{3,7},{7,3},{8,12},{12,8},{9,1... | collective-permute-start | bytes 393224 | tf_op jit(solution)/shard_map/ppermute | solution.py:435
  22.7 4.6 %collective-permute-start.10 = (bf16[320,128]{1,0:T(8,128)(2,1)S(1)}, bf16[320,128]{1,0:T(8,128)(2,1)S(1)}, u32[]{:S(2)}, u32[]{:S(2)}) collective-permute-start(bf16[320,128]{1,0:T(8,128)(2,1)S(1)} %get-tuple-element.48), channel_id=1, source_target_pairs={{0,1},{1,0},{2,3},{3,2},{4,5},{5,4},{6,7},{7,6},{8,9},{9,8},{10,11... | collective-permute-start | bytes 245768 | tf_op jit(solution)/shard_map/ppermute | solution.py:433
  23.7 4.5 %collective-permute-start.11 = (bf16[320,128]{1,0:T(8,128)(2,1)S(1)}, bf16[320,128]{1,0:T(8,128)(2,1)S(1)}, u32[]{:S(2)}, u32[]{:S(2)}) collective-permute-start(bf16[320,128]{1,0:T(8,128)(2,1)S(1)} %get-tuple-element.49), channel_id=1, source_target_pairs={{0,4},{4,0},{1,5},{5,1},{2,6},{6,2},{3,7},{7,3},{8,12},{12,8},{9,1... | collective-permute-start | bytes 245768 | tf_op jit(solution)/shard_map/ppermute | solution.py:435
  24.8 5.9 %collective-permute-start.12 = (bf16[320,128]{1,0:T(8,128)(2,1)S(1)}, bf16[320,128]{1,0:T(8,128)(2,1)S(1)}, u32[]{:S(2)}, u32[]{:S(2)}) collective-permute-start(bf16[320,128]{1,0:T(8,128)(2,1)S(1)} %get-tuple-element.50), channel_id=1, source_target_pairs={{0,5},{1,4},{2,7},{3,6},{4,1},{5,0},{6,3},{7,2},{8,13},{9,12},{10,... | collective-permute-start | bytes 245768 | tf_op jit(solution)/shard_map/ppermute | solution.py:441
  26.3 7.0 %collective-permute-start.9 = (bf16[256,128]{1,0:T(8,128)(2,1)S(1)}, bf16[256,128]{1,0:T(8,128)(2,1)S(1)}, u32[]{:S(2)}, u32[]{:S(2)}) collective-permute-start(bf16[256,128]{1,0:T(8,128)(2,1)S(1)} %get-tuple-element.44), channel_id=1, source_target_pairs={{0,1},{1,0},{2,3},{3,2},{4,5},{5,4},{6,7},{7,6},{8,9},{9,8},{10,11... | collective-permute-start | bytes 196616 | tf_op jit(solution)/shard_map/ppermute | solution.py:433
  30.7 7.5 %collective-permute-start.14 = (bf16[192,128]{1,0:T(8,128)(2,1)S(1)}, bf16[192,128]{1,0:T(8,128)(2,1)S(1)}, u32[]{:S(2)}, u32[]{:S(2)}) collective-permute-start(bf16[192,128]{1,0:T(8,128)(2,1)S(1)} %get-tuple-element.53), channel_id=1, source_target_pairs={{0,2},{1,3},{2,0},{3,1},{4,6},{5,7},{6,4},{7,5},{8,10},{9,11},{10,... | collective-permute-start | bytes 147464 | tf_op jit(solution)/shard_map/ppermute | solution.py:444
  33.3 4.9 %collective-permute-start.13 = (bf16[128,128]{1,0:T(8,128)(2,1)S(1)}, bf16[128,128]{1,0:T(8,128)(2,1)S(1)}, u32[]{:S(2)}, u32[]{:S(2)}) collective-permute-start(bf16[128,128]{1,0:T(8,128)(2,1)S(1)} %get-tuple-element.52), channel_id=1, source_target_pairs={{0,2},{1,3},{2,0},{3,1},{4,6},{5,7},{6,4},{7,5},{8,10},{9,11},{10,... | collective-permute-start | bytes 98312 | tf_op jit(solution)/shard_map/ppermute | solution.py:444

commit v6 on v5

--- a/solution.py
+++ b/solution.py
@@ -22,16 +22,6 @@
 
 def dot(a, b, dims):
     return lax.dot_general(a, b, dims, preferred_element_type=F32)
-
-
-def split_two(value):
-    high = value.astype(BF16)
-    low = (value - high.astype(F32)).astype(BF16)
-    return high, low
-
-
-def joined(high, low):
-    return high.astype(F32) + low.astype(F32)
 
 
 def in_order(values, owners):
@@ -298,12 +288,9 @@
         )
     gain_rows = gain_scratch[...] + before_ref[...]
     gain_rows_ref[...] = gain_rows
-    high, low = split_two(gain_rows)
-    count = high.shape[0]
-    begin = own_ref.shape[0]
+    gain_low = gain_rows.astype(BF16)
     for ref in message_refs:
-        ref[begin : begin + count, :] = high
-        ref[begin + count : begin + 2 * count, :] = low
+        ref[own_ref.shape[0] :, :] = gain_low
 
 
 def first_sum_kernel(sizes, *refs):
@@ -351,7 +338,6 @@
     message_refs = refs[2 : 1 + members]
     keep_ref, gain_sum_ref, send_ref = refs[1 + members :]
     block = 2 * half
-    count = gain_ref.shape[0]
     total = own_ref[...]
     for ref in message_refs:
         total = total + ref[: 2 * block, :].astype(F32)
@@ -359,20 +345,15 @@
     send_ref[:block, :] = total[block:].astype(BF16)
     cycle_place = lax.axis_index("ctx")
     near_place = lax.axis_index("tp") % near_count
-    values = [joined(*split_two(gain_ref[...]))]
+    values = [gain_ref[...].astype(BF16).astype(F32)]
     owners = [cycle_place * near_count + near_place]
-    begin = 2 * block
     for place, ref in enumerate(message_refs, 1):
         step, near = place // near_count, place % near_count
-        values.append(
-            joined(ref[begin : begin + count, :], ref[begin + count : begin + 2 * count, :])
-        )
+        values.append(ref[2 * block :, :].astype(F32))
         owners.append(((cycle_place + step) % cycle) * near_count + (near_place ^ near))
     gain = in_order(values, owners)
     gain_sum_ref[...] = gain
-    high, low = split_two(gain)
-    send_ref[block : block + count, :] = high
-    send_ref[block + count : block + 2 * count, :] = low
+    send_ref[block:, :] = gain.astype(BF16)
 
 
 def finish_kernel(sizes, *refs):
@@ -388,10 +369,8 @@
             here = slice(kind * half, (kind + 1) * half)
             out[0, tick, pl.ds(own_first, half), :] = keep_refs[tick][here, :]
             out[0, tick, pl.ds(other_first, half), :] = receive_refs[tick][here, :].astype(F32)
-    count = gain_ref.shape[0]
-    last = receive_refs[TICKS - 1]
-    own = joined(*split_two(gain_ref[...]))
-    gain_out_ref[...] = own + joined(last[block : block + count, :], last[block + count :, :])
+    own = gain_ref[...].astype(BF16).astype(F32)
+    gain_out_ref[...] = own + receive_refs[TICKS - 1][block:, :].astype(F32)
 
 
 def shape(dims, dtype):
@@ -504,7 +483,7 @@
         [shape((tp_count, key_count, stacked), F32)],
         scalars=1,
     )
-    message = shape((pair_rows + 2 * gain_count, HD), BF16)
+    message = shape((pair_rows + gain_count, HD), BF16)
     query_grad_second, gain_rows, own_second, *sends = call(
         functools.partial(second_keys_kernel, sizes),
         "second_keys",
@@ -554,7 +533,7 @@
         functools.partial(second_near_kernel, sizes),
         "second_near",
         (own_second, gain_rows, *received),
-        [keep_shape, gain_shape, shape((block + 2 * gain_count, HD), BF16)],
+        [keep_shape, gain_shape, shape((block + gain_count, HD), BF16)],
     )
     grads_shape = shape((1, ticks, block, HD), F32)
     key_grads, value_grads, gain_grads = call(

time: 39.1 us -> 38.8 us (level)
  no operation moved by 1% of the time
where the time goes in v6:
time: 38.8 us; the launch traced here: 38.6 us
  starting transfers between devices  21.1 us (54%)
  waiting for transfers between devices  8.83 us (23%)
  Pallas kernels  5.93 us (15%)
  local copies, waits for them, and re-layouts  1.07 us (3%)
  other arithmetic  0.93 us (2%)
  between operations  0.76 us (2%)
    ppermute x3, starting transfers between devices, to_far(): lax.ppermute(value, 'tp', [(i, i ^ near_count) for i in range(tp_count)])  7.51 us
    ppermute x3, starting transfers between devices, to_near(): return lax.ppermute(value, ('ctx', 'tp'), pairs)  6.58 us
    pallas_call x11, Pallas kernels, call(): pl.pallas_call(kernel, out_shape=out_shape, in_specs=in_specs, out_specs=...  5.93 us
    ppermute x4, starting transfers between devices, to_near(): lax.ppermute(value, 'ctx', [(i, (i + step) % cycle) for i in range(cycle)])  3.65 us
    ppermute x4, starting transfers between devices, to_near(): return lax.ppermute(value, 'tp', [(i, i ^ near) for i in range(tp_count)])  3.31 us
    ppermute x3, waiting for transfers between devices, to_near(): return lax.ppermute(value, ('ctx', 'tp'), pairs)  3.26 us
    ppermute x3, waiting for transfers between devices, to_far(): lax.ppermute(value, 'tp', [(i, i ^ near_count) for i in range(tp_count)])  2.96 us
    ppermute x4, waiting for transfers between devices, to_near(): lax.ppermute(value, 'ctx', [(i, (i + step) % cycle) for i in range(cycle)])  1.36 us
  transfers between devices with their start and end apart: 15, of which 7 were waited for; matrix products, arithmetic and copies ran while one was open for 0% of the time, Pallas kernels for 9%

profile of v6, /device:TPU:0, one launch (start us, length us, event | category | flops | bytes accessed | tf_op | source)
XLA Modules:
  0.0 38.6 jit_solution(2704538755027537188)
XLA Ops:
  0.6 0.0 copy-start.2
  0.6 0.9 %pad_maximum_fusion.both_ref = bf16[2,2,128,128]{3,2,1,0:T(8,128)(2,1)S(1)} fusion(bf16[1,2,128,128]{3,2,1,0:T(8,128)(2,1)} %param.9, bf16[1,2,128,128]{3,2,1,0:T(8,128)(2,1)} %param.8), kind=kLoop, calls=%fused_computation | loop fusion | flops 65536 | bytes 262144 | tf_op jit(solution)/shard_map/stack | solution.py:429
  1.6 0.0 copy-start.4
  1.6 4.1 %collective-permute-start.3 = (bf16[2,2,64,128]{3,2,1,0:T(8,128)(2,1)S(1)}, bf16[2,2,64,128]{3,2,1,0:T(8,128)(2,1)S(1)}, u32[]{:S(2)}, u32[]{:S(2)}) collective-permute-start(bf16[2,2,64,128]{3,2,1,0:T(8,128)(2,1)S(1)} %get-tuple-element.34), channel_id=1, source_target_pairs={{0,2},{1,3},{2,0},{3,1},{4,6},{5,7},{6,4},{7,5},{8,10},{9,11},{10,... | collective-permute-start | bytes 196616 | tf_op jit(solution)/shard_map/ppermute | solution.py:423
  5.7 2.5 %collective-permute-start.2 = (bf16[2,2,64,128]{3,2,1,0:T(8,128)(2,1)S(1)}, bf16[2,2,64,128]{3,2,1,0:T(8,128)(2,1)S(1)}, u32[]{:S(2)}, u32[]{:S(2)}) collective-permute-start(bf16[2,2,64,128]{3,2,1,0:T(8,128)(2,1)S(1)} %get-tuple-element.33.refs_6_.refs_2_.refs_7_), channel_id=1, source_target_pairs={{0,5},{1,4},{2,7},{3,6},{4,1},{5,0},{6,3},{7,2},{8,13},{9,12},{10,... | collective-permute-start | bytes 196616 | tf_op jit(solution)/shard_map/ppermute | solution.py:420
  8.3 0.5 %collective-permute-start.1 = (bf16[2,2,64,128]{3,2,1,0:T(8,128)(2,1)S(1)}, bf16[2,2,64,128]{3,2,1,0:T(8,128)(2,1)S(1)}, u32[]{:S(2)}, u32[]{:S(2)}) collective-permute-start(bf16[2,2,64,128]{3,2,1,0:T(8,128)(2,1)S(1)} %get-tuple-element.33.refs_6_.refs_2_.refs_7_), channel_id=1, source_target_pairs={{0,4},{4,0},{1,5},{5,1},{2,6},{6,2},{3,7},{7,3},{8,12},{12,8},{9,1... | collective-permute-start | bytes 196616 | tf_op jit(solution)/shard_map/ppermute | solution.py:414
  8.8 0.4 %collective-permute-start = (bf16[2,2,64,128]{3,2,1,0:T(8,128)(2,1)S(1)}, bf16[2,2,64,128]{3,2,1,0:T(8,128)(2,1)S(1)}, u32[]{:S(2)}, u32[]{:S(2)}) collective-permute-start(bf16[2,2,64,128]{3,2,1,0:T(8,128)(2,1)S(1)} %get-tuple-element.33.refs_6_.refs_2_.refs_7_), channel_id=1, source_target_pairs={{0,1},{1,0},{2,3},{3,2},{4,5},{5,4},{6,7},{7,6},{8,9},{9,8},{10,11... | collective-permute-start | bytes 196616 | tf_op jit(solution)/shard_map/ppermute | solution.py:412
  9.2 0.0 collective-permute-done.3.refs_10_.refs_6_.refs_11_
  9.2 2.5 %collective-permute-start.6 = (bf16[2,2,64,128]{3,2,1,0:T(8,128)(2,1)S(1)}, bf16[2,2,64,128]{3,2,1,0:T(8,128)(2,1)S(1)}, u32[]{:S(2)}, u32[]{:S(2)}) collective-permute-start(bf16[2,2,64,128]{3,2,1,0:T(8,128)(2,1)S(1)} %collective-permute-done.3.refs_10_.refs_6_.refs_11_), channel_id=1, source_target_pairs={{0,5},{1,4},{2,7},{3,6},{4,1},{5,0},{6,3},{7,2},{8,13},{9,12},{10,... | collective-permute-start | bytes 196616 | tf_op jit(solution)/shard_map/ppermute | solution.py:420
  11.7 0.5 %collective-permute-start.5 = (bf16[2,2,64,128]{3,2,1,0:T(8,128)(2,1)S(1)}, bf16[2,2,64,128]{3,2,1,0:T(8,128)(2,1)S(1)}, u32[]{:S(2)}, u32[]{:S(2)}) collective-permute-start(bf16[2,2,64,128]{3,2,1,0:T(8,128)(2,1)S(1)} %collective-permute-done.3.refs_10_.refs_6_.refs_11_), channel_id=1, source_target_pairs={{0,4},{4,0},{1,5},{5,1},{2,6},{6,2},{3,7},{7,3},{8,12},{12,8},{9,1... | collective-permute-start | bytes 196616 | tf_op jit(solution)/shard_map/ppermute | solution.py:414
  12.3 0.0 collective-permute-done.2.refs_9_.refs_5_.refs_10_
  12.3 0.9 %collective-permute-start.4 = (bf16[2,2,64,128]{3,2,1,0:T(8,128)(2,1)S(1)}, bf16[2,2,64,128]{3,2,1,0:T(8,128)(2,1)S(1)}, u32[]{:S(2)}, u32[]{:S(2)}) collective-permute-start(bf16[2,2,64,128]{3,2,1,0:T(8,128)(2,1)S(1)} %collective-permute-done.3.refs_10_.refs_6_.refs_11_), channel_id=1, source_target_pairs={{0,1},{1,0},{2,3},{3,2},{4,5},{5,4},{6,7},{7,6},{8,9},{9,8},{10,11... | collective-permute-start | bytes 196616 | tf_op jit(solution)/shard_map/ppermute | solution.py:412
  13.2 0.0 copy-done.4
  13.2 0.0 copy-start
  13.2 1.0 %copy-done = bf16[1,2,32,4096]{3,2,1,0:T(8,128)(2,1)S(1)} copy-done((bf16[1,2,32,4096]{3,2,1,0:T(8,128)(2,1)S(1)}, bf16[1,2,32,4096]{3,2,1,0:T(8,128)(2,1)}, u32[]{:S(2)}) %copy-start) | copy-done | bytes 524312
  14.2 0.0 copy-start.5
  14.2 0.3 norm.1
  14.5 0.0 collective-permute-done.1.refs_8_.refs_4_.refs_9_
  14.5 0.0 collective-permute-done.refs_7_.refs_3_.refs_8_
  14.5 1.0 %collective-permute-done.6.refs_13_.refs_9_.refs_14_ = bf16[2,2,64,128]{3,2,1,0:T(8,128)(2,1)S(1)} collective-permute-done((bf16[2,2,64,128]{3,2,1,0:T(8,128)(2,1)S(1)}, bf16[2,2,64,128]{3,2,1,0:T(8,128)(2,1)S(1)}, u32[]{:S(2)}, u32[]{:S(2)}) %collective-permute-start.6) | collective-permute-done | bytes 65568 | tf_op jit(solution)/shard_map/ppermute | solution.py:420
  15.5 0.6 %collective-permute-done.5.refs_12_.refs_8_.refs_13_ = bf16[2,2,64,128]{3,2,1,0:T(8,128)(2,1)S(1)} collective-permute-done((bf16[2,2,64,128]{3,2,1,0:T(8,128)(2,1)S(1)}, bf16[2,2,64,128]{3,2,1,0:T(8,128)(2,1)S(1)}, u32[]{:S(2)}, u32[]{:S(2)}) %collective-permute-start.5) | collective-permute-done | bytes 65568 | tf_op jit(solution)/shard_map/ppermute | solution.py:414
  16.1 0.4 %collective-permute-done.4.refs_11_.refs_7_.refs_12_ = bf16[2,2,64,128]{3,2,1,0:T(8,128)(2,1)S(1)} collective-permute-done((bf16[2,2,64,128]{3,2,1,0:T(8,128)(2,1)S(1)}, bf16[2,2,64,128]{3,2,1,0:T(8,128)(2,1)S(1)}, u32[]{:S(2)}, u32[]{:S(2)}) %collective-permute-start.4) | collective-permute-done | bytes 65568 | tf_op jit(solution)/shard_map/ppermute | solution.py:412
  16.5 0.0 copy-done.2
  16.5 0.0 copy-done.5
  16.5 1.6 %first_rows.1 = (bf16[32,4096]{1,0:T(8,128)(2,1)S(1)}, bf16[32,4096]{1,0:T(8,128)(2,1)S(1)}, bf16[4,128,256]{2,1,0:T(8,128)(2,1)S(1)}, bf16[4,128,256]{2,1,0:T(8,128)(2,1)S(1)}) custom-call(s32[5,8]{1,0:T(8,128)S(1)} %copy-done.5, bf16[1,2,32,4096]{3,2,1,0:T(8,128)(2,1)S(1)} %copy-done, f32[1,4096]{1,0:T(1,128)S(1)} %copy-done.4, ...), custom_call_target="tpu_custom_call" | custom-call | tf_op jit(solution)/shard_map/first_rows/pallas_call | solution.py:398
  18.1 0.1 collective-permute-start.7
  18.2 0.5 %first_keys.1 = (f32[32,128]{1,0:T(8,128)S(1)}, f32[2,256,128]{2,1,0:T(8,128)S(1)}, bf16[2,256,128]{2,1,0:T(8,128)(2,1)S(1)}) custom-call(bf16[1,2,32,4096]{3,2,1,0:T(8,128)(2,1)S(1)} %copy-done, bf16[2,32,4096]{2,1,0:T(8,128)(2,1)S(1)} %get-tuple-element.32.refs_3_.refs_1_, f32[2,32,128]{2,1,0:T(8,128)S(1)} %get-tuple-element.31.refs_4_.refs_2_, ...), custom_call_target="tpu_custom_call" | custom-call | tf_op jit(solution)/shard_map/first_keys/pallas_call | solution.py:398
  18.6 0.0 copy-start.1
  18.6 0.0 copy-start.3
  18.7 1.6 %collective-permute-start.8 = (bf16[2,256,128]{2,1,0:T(8,128)(2,1)S(1)}, bf16[2,256,128]{2,1,0:T(8,128)(2,1)S(1)}, u32[]{:S(2)}, u32[]{:S(2)}) collective-permute-start(bf16[2,256,128]{2,1,0:T(8,128)(2,1)S(1)} %get-tuple-element.42), channel_id=1, source_target_pairs={{0,4},{4,0},{1,5},{5,1},{2,6},{6,2},{3,7},{7,3},{8,12},{12,8},{9,1... | collective-permute-start | bytes 393224 | tf_op jit(solution)/shard_map/ppermute | solution.py:414
  20.2 1.0 %second_probs.1.refs_5_ = f32[4,128,256]{2,1,0:T(8,128)S(1)} custom-call(s32[5,8]{1,0:T(8,128)S(1)} %copy-done.5, bf16[2,32,4096]{2,1,0:T(8,128)(2,1)S(1)} %get-tuple-element.32.refs_3_.refs_1_, bf16[2,2,64,128]{3,2,1,0:T(8,128)(2,1)S(1)} %get-tuple-element.33.refs_6_.refs_2_.refs_7_, ...), custom_call_target="tpu_custom_call" | custom-call | tf_op jit(solution)/shard_map/second_probs/pallas_call | solution.py:398
  21.2 0.8 %collective-permute-done.7.refs_3_ = bf16[32,4096]{1,0:T(8,128)(2,1)S(1)} collective-permute-done((bf16[32,4096]{1,0:T(8,128)(2,1)S(1)}, bf16[32,4096]{1,0:T(8,128)(2,1)S(1)}, u32[]{:S(2)}, u32[]{:S(2)}) %collective-permute-start.7) | collective-permute-done | bytes 262176 | tf_op jit(solution)/shard_map/ppermute | solution.py:455
  22.0 0.0 copy-done.1
  22.0 0.0 copy-done.3
  22.0 0.7 %second_keys.1 = (bf16[32,4096]{1,0:T(8,128)(2,1)S(1)}, f32[32,128]{1,0:T(8,128)S(1)}, f32[256,128]{1,0:T(8,128)S(1)}, bf16[288,128]{1,0:T(8,128)(2,1)S(1)}, bf1...) custom-call(bf16[1,2,32,4096]{3,2,1,0:T(8,128)(2,1)S(1)} %copy-done.1, ...), custom_call_target="tpu_custom_call" | custom-call | tf_op jit(solution)/shard_map/second_keys/pallas_call | solution.py:398
  22.7 1.0 %collective-permute-start.10 = (bf16[288,128]{1,0:T(8,128)(2,1)S(1)}, bf16[288,128]{1,0:T(8,128)(2,1)S(1)}, u32[]{:S(2)}, u32[]{:S(2)}) collective-permute-start(bf16[288,128]{1,0:T(8,128)(2,1)S(1)} %get-tuple-element.48), channel_id=1, source_target_pairs={{0,1},{1,0},{2,3},{3,2},{4,5},{5,4},{6,7},{7,6},{8,9},{9,8},{10,11... | collective-permute-start | bytes 221192 | tf_op jit(solution)/shard_map/ppermute | solution.py:412
  23.7 1.1 %collective-permute-start.11 = (bf16[288,128]{1,0:T(8,128)(2,1)S(1)}, bf16[288,128]{1,0:T(8,128)(2,1)S(1)}, u32[]{:S(2)}, u32[]{:S(2)}) collective-permute-start(bf16[288,128]{1,0:T(8,128)(2,1)S(1)} %get-tuple-element.49), channel_id=1, source_target_pairs={{0,4},{4,0},{1,5},{5,1},{2,6},{6,2},{3,7},{7,3},{8,12},{12,8},{9,1... | collective-permute-start | bytes 221192 | tf_op jit(solution)/shard_map/ppermute | solution.py:414
  24.8 1.5 %collective-permute-start.12 = (bf16[288,128]{1,0:T(8,128)(2,1)S(1)}, bf16[288,128]{1,0:T(8,128)(2,1)S(1)}, u32[]{:S(2)}, u32[]{:S(2)}) collective-permute-start(bf16[288,128]{1,0:T(8,128)(2,1)S(1)} %get-tuple-element.50), channel_id=1, source_target_pairs={{0,5},{1,4},{2,7},{3,6},{4,1},{5,0},{6,3},{7,2},{8,13},{9,12},{10,... | collective-permute-start | bytes 221192 | tf_op jit(solution)/shard_map/ppermute | solution.py:420
  26.3 0.0 collective-permute-done.8.refs_1_
  26.3 1.0 %collective-permute-start.9 = (bf16[256,128]{1,0:T(8,128)(2,1)S(1)}, bf16[256,128]{1,0:T(8,128)(2,1)S(1)}, u32[]{:S(2)}, u32[]{:S(2)}) collective-permute-start(bf16[256,128]{1,0:T(8,128)(2,1)S(1)} %get-tuple-element.44), channel_id=1, source_target_pairs={{0,1},{1,0},{2,3},{3,2},{4,5},{5,4},{6,7},{7,6},{8,9},{9,8},{10,11... | collective-permute-start | bytes 196616 | tf_op jit(solution)/shard_map/ppermute | solution.py:412
  27.3 0.0 collective-permute-done.10.refs_2_
  27.3 0.8 %collective-permute-done.11.refs_3_ = bf16[288,128]{1,0:T(8,128)(2,1)S(1)} collective-permute-done((bf16[288,128]{1,0:T(8,128)(2,1)S(1)}, bf16[288,128]{1,0:T(8,128)(2,1)S(1)}, u32[]{:S(2)}, u32[]{:S(2)}) %collective-permute-start.11) | collective-permute-done | bytes 73760 | tf_op jit(solution)/shard_map/ppermute | solution.py:414
  28.1 2.3 %collective-permute-done.12.refs_4_ = bf16[288,128]{1,0:T(8,128)(2,1)S(1)} collective-permute-done((bf16[288,128]{1,0:T(8,128)(2,1)S(1)}, bf16[288,128]{1,0:T(8,128)(2,1)S(1)}, u32[]{:S(2)}, u32[]{:S(2)}) %collective-permute-start.12) | collective-permute-done | bytes 73760 | tf_op jit(solution)/shard_map/ppermute | solution.py:420
  30.3 0.1 second_near.1
  30.4 2.6 %collective-permute-start.14 = (bf16[160,128]{1,0:T(8,128)(2,1)S(1)}, bf16[160,128]{1,0:T(8,128)(2,1)S(1)}, u32[]{:S(2)}, u32[]{:S(2)}) collective-permute-start(bf16[160,128]{1,0:T(8,128)(2,1)S(1)} %get-tuple-element.53), channel_id=1, source_target_pairs={{0,2},{1,3},{2,0},{3,1},{4,6},{5,7},{6,4},{7,5},{8,10},{9,11},{10,... | collective-permute-start | bytes 122888 | tf_op jit(solution)/shard_map/ppermute | solution.py:423
  33.0 0.0 collective-permute-done.9.refs_0_
  33.0 0.8 %collective-permute-start.13 = (bf16[128,128]{1,0:T(8,128)(2,1)S(1)}, bf16[128,128]{1,0:T(8,128)(2,1)S(1)}, u32[]{:S(2)}, u32[]{:S(2)}) collective-permute-start(bf16[128,128]{1,0:T(8,128)(2,1)S(1)} %get-tuple-element.52), channel_id=1, source_target_pairs={{0,2},{1,3},{2,0},{3,1},{4,6},{5,7},{6,4},{7,5},{8,10},{9,11},{10,... | collective-permute-start | bytes 98312 | tf_op jit(solution)/shard_map/ppermute | solution.py:423
  33.8 1.1 %second_rows.1 = bf16[1,2,32,4096]{3,2,1,0:T(8,128)(2,1)} custom-call(bf16[1,2,32,4096]{3,2,1,0:T(8,128)(2,1)S(1)} %copy-done.1, f32[1,4096]{1,0:T(1,128)S(1)} %copy-done.4, f32[2,32,128]{2,1,0:T(8,128)S(1)} %get-tuple-element.31.refs_4_.refs_2_, bf16[32,4096]{1,0:T(8,128)(2,1)S(1)} %collective-permute-done.7.refs_3_, bf16[1,32,4096]{2,1,0:T(8,128)(2,1)S(1)} %copy-done.3, ...), custom_call_target="tpu_custom_call" | custom-call | tf_op jit(solution)/shard_map/second_rows/pallas_call | solution.py:398
  34.9 3.0 %collective-permute-done.13.refs_2_ = bf16[128,128]{1,0:T(8,128)(2,1)S(1)} collective-permute-done((bf16[128,128]{1,0:T(8,128)(2,1)S(1)}, bf16[128,128]{1,0:T(8,128)(2,1)S(1)}, u32[]{:S(2)}, u32[]{:S(2)}) %collective-permute-start.13) | collective-permute-done | bytes 32800 | tf_op jit(solution)/shard_map/ppermute | solution.py:423
  37.9 0.0 collective-permute-done.14.refs_3_
  37.9 0.7 %finish.1 = (f32[1,2,128,128]{3,2,1,0:T(8,128)}, f32[1,2,128,128]{3,2,1,0:T(8,128)}, f32[32,128]{1,0:T(8,128)}) custom-call(f32[128,128]{1,0:T(8,128)S(1)} %get-tuple-element.45.refs_0_, f32[128,128]{1,0:T(8,128)S(1)} %get-tuple-element.51.refs_1_, bf16[128,128]{1,0:T(8,128)(2,1)S(1)} %collective-permute-done.13.refs_2_, ...), custom_call_target="tpu_custom_call" | custom-call | tf_op jit(solution)/shard_map/finish/pallas_call | solution.py:398
  (3 shorter events, 0.1 us)
Async XLA Ops:
  0.6 15.9 %copy-start.2 = (bf16[1,32,4096]{2,1,0:T(8,128)(2,1)S(1)}, bf16[1,32,4096]{2,1,0:T(8,128)(2,1)}, u32[]{:S(2)}) copy-start(bf16[1,32,4096]{2,1,0:T(8,128)(2,1)} %refs_3_.1) | copy-start | bytes 786436
  1.6 11.6 %copy-start.4 = (f32[1,4096]{1,0:T(1,128)S(1)}, f32[1,4096]{1,0:T(1,128)}, u32[]{:S(2)}) copy-start(f32[1,4096]{1,0:T(1,128)} %refs_1_.3) | copy-start | bytes 49156
  1.6 7.6 %collective-permute-start.3 = (bf16[2,2,64,128]{3,2,1,0:T(8,128)(2,1)S(1)}, bf16[2,2,64,128]{3,2,1,0:T(8,128)(2,1)S(1)}, u32[]{:S(2)}, u32[]{:S(2)}) collective-permute-start(bf16[2,2,64,128]{3,2,1,0:T(8,128)(2,1)S(1)} %get-tuple-element.34), channel_id=1, source_target_pairs={{0,2},{1,3},{2,0},{3,1},{4,6},{5,7},{6,4},{7,5},{8,10},{9,11},{10,... | collective-permute-start | bytes 196616 | tf_op jit(solution)/shard_map/ppermute | solution.py:423
  5.7 6.5 %collective-permute-start.2 = (bf16[2,2,64,128]{3,2,1,0:T(8,128)(2,1)S(1)}, bf16[2,2,64,128]{3,2,1,0:T(8,128)(2,1)S(1)}, u32[]{:S(2)}, u32[]{:S(2)}) collective-permute-start(bf16[2,2,64,128]{3,2,1,0:T(8,128)(2,1)S(1)} %get-tuple-element.33.refs_6_.refs_2_.refs_7_), channel_id=1, source_target_pairs={{0,5},{1,4},{2,7},{3,6},{4,1},{5,0},{6,3},{7,2},{8,13},{9,12},{10,... | collective-permute-start | bytes 196616 | tf_op jit(solution)/shard_map/ppermute | solution.py:420
  8.3 6.2 %collective-permute-start.1 = (bf16[2,2,64,128]{3,2,1,0:T(8,128)(2,1)S(1)}, bf16[2,2,64,128]{3,2,1,0:T(8,128)(2,1)S(1)}, u32[]{:S(2)}, u32[]{:S(2)}) collective-permute-start(bf16[2,2,64,128]{3,2,1,0:T(8,128)(2,1)S(1)} %get-tuple-element.33.refs_6_.refs_2_.refs_7_), channel_id=1, source_target_pairs={{0,4},{4,0},{1,5},{5,1},{2,6},{6,2},{3,7},{7,3},{8,12},{12,8},{9,1... | collective-permute-start | bytes 196616 | tf_op jit(solution)/shard_map/ppermute | solution.py:414
  8.8 5.7 %collective-permute-start = (bf16[2,2,64,128]{3,2,1,0:T(8,128)(2,1)S(1)}, bf16[2,2,64,128]{3,2,1,0:T(8,128)(2,1)S(1)}, u32[]{:S(2)}, u32[]{:S(2)}) collective-permute-start(bf16[2,2,64,128]{3,2,1,0:T(8,128)(2,1)S(1)} %get-tuple-element.33.refs_6_.refs_2_.refs_7_), channel_id=1, source_target_pairs={{0,1},{1,0},{2,3},{3,2},{4,5},{5,4},{6,7},{7,6},{8,9},{9,8},{10,11... | collective-permute-start | bytes 196616 | tf_op jit(solution)/shard_map/ppermute | solution.py:412
  9.2 6.3 %collective-permute-start.6 = (bf16[2,2,64,128]{3,2,1,0:T(8,128)(2,1)S(1)}, bf16[2,2,64,128]{3,2,1,0:T(8,128)(2,1)S(1)}, u32[]{:S(2)}, u32[]{:S(2)}) collective-permute-start(bf16[2,2,64,128]{3,2,1,0:T(8,128)(2,1)S(1)} %collective-permute-done.3.refs_10_.refs_6_.refs_11_), channel_id=1, source_target_pairs={{0,5},{1,4},{2,7},{3,6},{4,1},{5,0},{6,3},{7,2},{8,13},{9,12},{10,... | collective-permute-start | bytes 196616 | tf_op jit(solution)/shard_map/ppermute | solution.py:420
  11.7 4.3 %collective-permute-start.5 = (bf16[2,2,64,128]{3,2,1,0:T(8,128)(2,1)S(1)}, bf16[2,2,64,128]{3,2,1,0:T(8,128)(2,1)S(1)}, u32[]{:S(2)}, u32[]{:S(2)}) collective-permute-start(bf16[2,2,64,128]{3,2,1,0:T(8,128)(2,1)S(1)} %collective-permute-done.3.refs_10_.refs_6_.refs_11_), channel_id=1, source_target_pairs={{0,4},{4,0},{1,5},{5,1},{2,6},{6,2},{3,7},{7,3},{8,12},{12,8},{9,1... | collective-permute-start | bytes 196616 | tf_op jit(solution)/shard_map/ppermute | solution.py:414
  12.3 4.3 %collective-permute-start.4 = (bf16[2,2,64,128]{3,2,1,0:T(8,128)(2,1)S(1)}, bf16[2,2,64,128]{3,2,1,0:T(8,128)(2,1)S(1)}, u32[]{:S(2)}, u32[]{:S(2)}) collective-permute-start(bf16[2,2,64,128]{3,2,1,0:T(8,128)(2,1)S(1)} %collective-permute-done.3.refs_10_.refs_6_.refs_11_), channel_id=1, source_target_pairs={{0,1},{1,0},{2,3},{3,2},{4,5},{5,4},{6,7},{7,6},{8,9},{9,8},{10,11... | collective-permute-start | bytes 196616 | tf_op jit(solution)/shard_map/ppermute | solution.py:412
  13.2 1.0 %copy-start = (bf16[1,2,32,4096]{3,2,1,0:T(8,128)(2,1)S(1)}, bf16[1,2,32,4096]{3,2,1,0:T(8,128)(2,1)}, u32[]{:S(2)}) copy-start(bf16[1,2,32,4096]{3,2,1,0:T(8,128)(2,1)} %refs_0_.9) | copy-start | bytes 1572868
  14.2 2.3 %copy-start.5 = (s32[5,8]{1,0:T(8,128)S(1)}, s32[5,8]{1,0:T(8,128)}, u32[]{:S(2)}) copy-start(s32[5,8]{1,0:T(8,128)} %refs_0_.6) | copy-start | bytes 484
  18.1 3.9 %collective-permute-start.7 = (bf16[32,4096]{1,0:T(8,128)(2,1)S(1)}, bf16[32,4096]{1,0:T(8,128)(2,1)S(1)}, u32[]{:S(2)}, u32[]{:S(2)}) collective-permute-start(bf16[32,4096]{1,0:T(8,128)(2,1)S(1)} %get-tuple-element.35.refs_6_), channel_id=1, source_target_pairs={{0,24},{8,0},{16,8},{24,16},{1,25},{9,1},{17,9},{25,17},{2,26},{10... | collective-permute-start | bytes 786440 | tf_op jit(solution)/shard_map/ppermute | solution.py:455
  18.6 3.4 %copy-start.1 = (bf16[1,2,32,4096]{3,2,1,0:T(8,128)(2,1)S(1)}, bf16[1,2,32,4096]{3,2,1,0:T(8,128)(2,1)}, u32[]{:S(2)}) copy-start(bf16[1,2,32,4096]{3,2,1,0:T(8,128)(2,1)} %refs_0_.9) | copy-start | bytes 1572868
  18.6 3.4 %copy-start.3 = (bf16[1,32,4096]{2,1,0:T(8,128)(2,1)S(1)}, bf16[1,32,4096]{2,1,0:T(8,128)(2,1)}, u32[]{:S(2)}) copy-start(bf16[1,32,4096]{2,1,0:T(8,128)(2,1)} %refs_4_.3) | copy-start | bytes 786436
  18.7 7.6 %collective-permute-start.8 = (bf16[2,256,128]{2,1,0:T(8,128)(2,1)S(1)}, bf16[2,256,128]{2,1,0:T(8,128)(2,1)S(1)}, u32[]{:S(2)}, u32[]{:S(2)}) collective-permute-start(bf16[2,256,128]{2,1,0:T(8,128)(2,1)S(1)} %get-tuple-element.42), channel_id=1, source_target_pairs={{0,4},{4,0},{1,5},{5,1},{2,6},{6,2},{3,7},{7,3},{8,12},{12,8},{9,1... | collective-permute-start | bytes 393224 | tf_op jit(solution)/shard_map/ppermute | solution.py:414
  22.7 4.6 %collective-permute-start.10 = (bf16[288,128]{1,0:T(8,128)(2,1)S(1)}, bf16[288,128]{1,0:T(8,128)(2,1)S(1)}, u32[]{:S(2)}, u32[]{:S(2)}) collective-permute-start(bf16[288,128]{1,0:T(8,128)(2,1)S(1)} %get-tuple-element.48), channel_id=1, source_target_pairs={{0,1},{1,0},{2,3},{3,2},{4,5},{5,4},{6,7},{7,6},{8,9},{9,8},{10,11... | collective-permute-start | bytes 221192 | tf_op jit(solution)/shard_map/ppermute | solution.py:412
  23.7 4.4 %collective-permute-start.11 = (bf16[288,128]{1,0:T(8,128)(2,1)S(1)}, bf16[288,128]{1,0:T(8,128)(2,1)S(1)}, u32[]{:S(2)}, u32[]{:S(2)}) collective-permute-start(bf16[288,128]{1,0:T(8,128)(2,1)S(1)} %get-tuple-element.49), channel_id=1, source_target_pairs={{0,4},{4,0},{1,5},{5,1},{2,6},{6,2},{3,7},{7,3},{8,12},{12,8},{9,1... | collective-permute-start | bytes 221192 | tf_op jit(solution)/shard_map/ppermute | solution.py:414
  24.8 5.6 %collective-permute-start.12 = (bf16[288,128]{1,0:T(8,128)(2,1)S(1)}, bf16[288,128]{1,0:T(8,128)(2,1)S(1)}, u32[]{:S(2)}, u32[]{:S(2)}) collective-permute-start(bf16[288,128]{1,0:T(8,128)(2,1)S(1)} %get-tuple-element.50), channel_id=1, source_target_pairs={{0,5},{1,4},{2,7},{3,6},{4,1},{5,0},{6,3},{7,2},{8,13},{9,12},{10,... | collective-permute-start | bytes 221192 | tf_op jit(solution)/shard_map/ppermute | solution.py:420
  26.3 6.7 %collective-permute-start.9 = (bf16[256,128]{1,0:T(8,128)(2,1)S(1)}, bf16[256,128]{1,0:T(8,128)(2,1)S(1)}, u32[]{:S(2)}, u32[]{:S(2)}) collective-permute-start(bf16[256,128]{1,0:T(8,128)(2,1)S(1)} %get-tuple-element.44), channel_id=1, source_target_pairs={{0,1},{1,0},{2,3},{3,2},{4,5},{5,4},{6,7},{7,6},{8,9},{9,8},{10,11... | collective-permute-start | bytes 196616 | tf_op jit(solution)/shard_map/ppermute | solution.py:412
  30.4 7.5 %collective-permute-start.14 = (bf16[160,128]{1,0:T(8,128)(2,1)S(1)}, bf16[160,128]{1,0:T(8,128)(2,1)S(1)}, u32[]{:S(2)}, u32[]{:S(2)}) collective-permute-start(bf16[160,128]{1,0:T(8,128)(2,1)S(1)} %get-tuple-element.53), channel_id=1, source_target_pairs={{0,2},{1,3},{2,0},{3,1},{4,6},{5,7},{6,4},{7,5},{8,10},{9,11},{10,... | collective-permute-start | bytes 122888 | tf_op jit(solution)/shard_map/ppermute | solution.py:423
  33.0 4.9 %collective-permute-start.13 = (bf16[128,128]{1,0:T(8,128)(2,1)S(1)}, bf16[128,128]{1,0:T(8,128)(2,1)S(1)}, u32[]{:S(2)}, u32[]{:S(2)}) collective-permute-start(bf16[128,128]{1,0:T(8,128)(2,1)S(1)} %get-tuple-element.52), channel_id=1, source_target_pairs={{0,2},{1,3},{2,0},{3,1},{4,6},{5,7},{6,4},{7,5},{8,10},{9,11},{10,... | collective-permute-start | bytes 98312 | tf_op jit(solution)/shard_map/ppermute | solution.py:423

commit v7 on v6

--- a/solution.py
+++ b/solution.py
@@ -44,9 +44,9 @@
             other_ref[tick, kind] = both_ref[kind, tick, pl.ds(other_first, half), :]
 
 
-def norm_kernel(x_ref, gain_ref, query_ref, inverse_ref):
-    _, ticks, rows, columns = x_ref.shape
-    for tick in range(ticks):
+def norm_kernel(sizes, doc_ref, x_ref, gain_ref, query_ref, inverse_ref, mask_ref):
+    rows, columns = sizes[0], sizes[5]
+    for tick in range(TICKS):
         squares = jnp.zeros((rows, HD), F32)
         for first in range(0, columns, HD):
             part = x_ref[0, tick, :, first : first + HD].astype(F32)
@@ -58,6 +58,7 @@
             here = slice(first, first + HD)
             normed = x_ref[0, tick, :, here].astype(F32) * inverse
             query_ref[tick, :, here] = (normed * gain_ref[:, here]).astype(BF16)
+        mask_ref[tick] = jnp.where(visible_keys(sizes, tick, doc_ref), 0.0, FILL)
 
 
 class Group:
@@ -111,8 +112,8 @@
     return (key_pos <= query_pos) & (key_pos >= query_start)
 
 
-def probabilities(visible, products):
-    scores = jnp.where(visible, SCALE * products, FILL)
+def probabilities(mask, products):
+    scores = SCALE * products + mask
     weights = jnp.exp(scores - jnp.max(scores, axis=0, keepdims=True))
     return weights * (1.0 / jnp.sum(weights, axis=0, keepdims=True))
 
@@ -128,11 +129,8 @@
         self.tick = tick
         self.refs = refs
 
-    def __call__(self, turn, kind):
-        near, far = turn % self.near_count, turn // self.near_count
-        count = len(self.refs) // 2
-        refs = self.refs[far * count : (far + 1) * count]
-        parts = [ref[self.tick, kind] for ref in refs[near :: self.near_count]]
+    def __call__(self, near, kind):
+        parts = [ref[self.tick, kind] for ref in self.refs[near :: self.near_count]]
         return jnp.concatenate(parts, axis=0)
 
 
@@ -155,9 +153,9 @@
                 message_refs[step * near_count + near - 1][here, :] = piece.astype(BF16)
 
 
-def gain_terms(columns_of, low_parts, normed_of, gain_rows_ref):
+def gain_terms(columns_of, query_grad, normed_of, gain_rows_ref):
     rows = []
-    for index, low in enumerate(low_parts):
+    for index, low in enumerate(columns_of.unstacked(query_grad)):
         term = low.astype(F32) * normed_of(columns_of.head(index))
         rows.append(jnp.sum(term, axis=0, keepdims=True))
     group = columns_of.group
@@ -165,105 +163,155 @@
     gain_rows_ref[place, :] = jnp.concatenate(rows, axis=0)
 
 
-def write_input_grads(sizes, tick, x_ref, gain_ref, inverse, query_grad_ref, arriving, write):
-    rows, columns = sizes[0], sizes[5]
-    coupled = jnp.zeros((rows, HD), F32)
-    for first in range(0, columns, HD):
-        here = slice(first, first + HD)
-        scaled = query_grad_ref[:, here].astype(F32) * gain_ref[:, here]
-        coupled = coupled + scaled * (x_ref[0, tick, :, here].astype(F32) * inverse)
-    coupling = jnp.sum(coupled, axis=1, keepdims=True) * (1.0 / columns)
-    for first in range(0, columns, HD):
-        here = slice(first, first + HD)
-        scaled = query_grad_ref[:, here].astype(F32) * gain_ref[:, here]
-        normed = x_ref[0, tick, :, here].astype(F32) * inverse
-        result = arriving(here).astype(F32) + inverse * (scaled - normed * coupling)
-        write(here, result.astype(BF16))
-
-
-def first_rows_kernel(sizes, kv_count, *refs):
-    tp_count = sizes[3]
-    turns = range(tp_count)
-    doc_ref, x_ref, gain_ref, query_ref, inverse_ref, waiting_ref = refs[:6]
-    keys = Keys(sizes, 0, refs[6 : 6 + kv_count])
-    input_grad_ref, query_grad_ref, dscore_ref, probs_ref = refs[6 + kv_count :]
-    visible = visible_keys(sizes, 0, doc_ref)
+def coupled_terms(columns_of, query_grad, normed_of, gain_ref, coupled):
+    for index, low in enumerate(columns_of.unstacked(query_grad)):
+        where = columns_of.head(index)
+        coupled = coupled + low.astype(F32) * gain_ref[:, where] * normed_of(where)
+    return coupled
+
+
+def write_input_grads(sizes, coupled, query_grad_of, normed_of, gain_ref, inverse, arriving, write):
+    coupling = jnp.sum(coupled, axis=1, keepdims=True) * (1.0 / sizes[5])
+    for turn in range(sizes[3]):
+        columns_of = Group(sizes, turn)
+        for index, low in enumerate(columns_of.unstacked(query_grad_of(turn))):
+            where = columns_of.head(index)
+            scaled = low.astype(F32) * gain_ref[:, where]
+            result = arriving(where).astype(F32) + inverse * (scaled - normed_of(where) * coupling)
+            write(where, result.astype(BF16))
+
+
+def normed_from(x_ref, tick, inverse):
+    return lambda where: x_ref[0, tick, :, where].astype(F32) * inverse
+
+
+def first_half(sizes, far, keys, mask, query_ref, arriving, dscore_ref, probs_ref):
+    near_count = sizes[3] // 2
+    nears = range(near_count)
+    columns_of = [Group(sizes, far * near_count + near) for near in nears]
+    scores, prob_grads = [], []
+    for near in nears:
+        query = columns_of[near].stacked(lambda where: query_ref[0, :, where])
+        scores.append(dot(keys(near, 0), query, NT))
+        prob_grads.append(dot(keys(near, 1), columns_of[near].stacked(arriving), NT))
+    dscores = []
+    for near in nears:
+        probs = probabilities(mask, scores[near])
+        dscores.append(score_grads(probs, prob_grads[near]))
+        dscore_ref[near] = dscores[near]
+        probs_ref[near] = probs.astype(BF16)
+    return [(SCALE * dot(dscores[near], keys(near, 0), TN)).astype(BF16) for near in nears]
+
+
+def first_near_rows_kernel(sizes, *refs):
+    members = sizes[2] * sizes[3] // 2
+    x_ref, gain_ref, query_ref, inverse_ref, mask_ref, waiting_ref = refs[:6]
+    keys = Keys(sizes, 0, refs[6 : 6 + members])
+    query_grad_ref, dscore_ref, probs_ref, coupled_ref = refs[6 + members :]
+    query_grads = first_half(
+        sizes,
+        0,
+        keys,
+        mask_ref[0],
+        query_ref,
+        arriving_from([waiting_ref]),
+        dscore_ref,
+        probs_ref,
+    )
+    normed_of = normed_from(x_ref, 0, inverse_ref[0])
+    coupled = jnp.zeros((sizes[0], HD), F32)
+    for near, query_grad in enumerate(query_grads):
+        query_grad_ref[near] = query_grad
+        coupled = coupled_terms(Group(sizes, near), query_grad, normed_of, gain_ref, coupled)
+    coupled_ref[...] = coupled
+
+
+def first_far_rows_kernel(sizes, *refs):
+    near_count = sizes[3] // 2
+    members = sizes[2] * near_count
+    x_ref, gain_ref, query_ref, inverse_ref, mask_ref, waiting_ref = refs[:6]
+    keys = Keys(sizes, 0, refs[6 : 6 + members])
+    near_grad_ref, coupled_ref = refs[6 + members : 8 + members]
+    input_grad_ref, query_grad_ref, dscore_ref, probs_ref = refs[8 + members :]
     arriving = arriving_from([waiting_ref])
-    columns_of = [Group(sizes, turn) for turn in turns]
-    scores, prob_grads = [], []
-    for turn in turns:
-        query = columns_of[turn].stacked(lambda where: query_ref[0, :, where])
-        scores.append(dot(keys(turn, 0), query, NT))
-        grad = columns_of[turn].stacked(arriving)
-        prob_grads.append(dot(keys(turn, 1), grad, NT))
-    dscores = []
-    for turn in turns:
-        probs = probabilities(visible, scores[turn])
-        dscores.append(score_grads(probs, prob_grads[turn]))
-        dscore_ref[turn] = dscores[turn]
-        probs_ref[turn] = probs.astype(BF16)
-    for turn in turns:
-        query_grad = (SCALE * dot(dscores[turn], keys(turn, 0), TN)).astype(BF16)
-        for index, low in enumerate(columns_of[turn].unstacked(query_grad)):
-            query_grad_ref[:, columns_of[turn].head(index)] = low
-
-    def write(here, result):
-        input_grad_ref[:, here] = result
+    query_grads = first_half(
+        sizes, 1, keys, mask_ref[0], query_ref, arriving, dscore_ref, probs_ref
+    )
+    normed_of = normed_from(x_ref, 0, inverse_ref[0])
+    coupled = coupled_ref[...]
+    for near, query_grad in enumerate(query_grads):
+        query_grad_ref[near] = query_grad
+        coupled = coupled_terms(
+            Group(sizes, near_count + near), query_grad, normed_of, gain_ref, coupled
+        )
+
+    def query_grad_of(turn):
+        return near_grad_ref[turn] if turn < near_count else query_grads[turn - near_count]
+
+    def write(where, result):
+        input_grad_ref[:, where] = result
 
     write_input_grads(
-        sizes, 0, x_ref, gain_ref, inverse_ref[0], query_grad_ref, arriving, write
+        sizes, coupled, query_grad_of, normed_of, gain_ref, inverse_ref[0], arriving, write
     )
 
 
 def first_keys_kernel(sizes, *refs):
     half, cycle, tp_count = sizes[1:4]
-    x_ref, query_ref, inverse_ref, waiting_ref, query_grad_ref, dscore_ref, probs_ref = refs[:7]
-    gain_rows_ref, own_ref = refs[7:9]
-    send_refs = refs[9:]
+    near_count = tp_count // 2
+    x_ref, query_ref, inverse_ref, waiting_ref = refs[:4]
+    query_grad_refs, dscore_refs, probs_refs = refs[4:6], refs[6:8], refs[8:10]
+    gain_rows_ref, own_ref = refs[10:12]
+    send_refs = refs[12:]
     arriving = arriving_from([waiting_ref])
-    inverse = inverse_ref[0]
+    normed_of = normed_from(x_ref, 0, inverse_ref[0])
     for turn in range(tp_count):
+        near, far = turn % near_count, turn // near_count
         columns_of = Group(sizes, turn)
         query = columns_of.stacked(lambda where: query_ref[0, :, where])
         grad = columns_of.stacked(arriving)
-        parts = (SCALE * dot(dscore_ref[turn], query, NN), dot(probs_ref[turn], grad, NN))
-        near, far = turn % (tp_count // 2), turn // (tp_count // 2)
+        parts = (
+            SCALE * dot(dscore_refs[far][near], query, NN),
+            dot(probs_refs[far][near], grad, NN),
+        )
         for kind, part in enumerate(parts):
             here = place_of(sizes, far, kind)
             own_ref[near, here, :] = part[:half]
             for step, ref in enumerate(send_refs, 1):
                 ref[near, here, :] = part[step * half : (step + 1) * half].astype(BF16)
-        gain_terms(
-            columns_of,
-            [query_grad_ref[:, columns_of.head(index)] for index in range(columns_of.group)],
-            lambda where: x_ref[0, 0, :, where].astype(F32) * inverse,
-            gain_rows_ref,
-        )
-
-
-def second_probs_kernel(sizes, kv_count, *refs):
+        gain_terms(columns_of, query_grad_refs[far][near], normed_of, gain_rows_ref)
+
+
+def both_sets(sizes, refs):
+    near_count = sizes[3] // 2
+    members = sizes[2] * near_count
+    sets = [Keys(sizes, 1, refs[:members]), Keys(sizes, 1, refs[members:])]
+    return lambda turn, kind: sets[turn // near_count](turn % near_count, kind)
+
+
+def second_probs_kernel(sizes, *refs):
     turns = range(sizes[3])
-    doc_ref, query_ref = refs[:2]
-    keys, probs_ref = Keys(sizes, 1, refs[2 : 2 + kv_count]), refs[2 + kv_count]
-    visible = visible_keys(sizes, 1, doc_ref)
+    mask_ref, query_ref = refs[:2]
+    keys, probs_ref = both_sets(sizes, refs[2:-1]), refs[-1]
+    mask = mask_ref[1]
     scores = []
     for turn in turns:
         query = Group(sizes, turn).stacked(lambda where: query_ref[1, :, where])
         scores.append(dot(keys(turn, 0), query, NT))
     for turn in turns:
-        probs_ref[turn] = probabilities(visible, scores[turn])
+        probs_ref[turn] = probabilities(mask, scores[turn])
 
 
 def second_keys_kernel(sizes, *refs):
     cycle, tp_count = sizes[2:4]
     turns = range(tp_count)
-    members = cycle * (tp_count // 2)
+    kv_count = cycle * tp_count
     x_ref, query_ref, inverse_ref, arrived_ref, output_ref, probs_ref, before_ref = refs[:7]
-    keys, refs = Keys(sizes, 1, refs[7 : 7 + 2 * members]), refs[7 + 2 * members :]
+    keys, refs = both_sets(sizes, refs[7 : 7 + kv_count]), refs[7 + kv_count :]
     query_grad_ref, gain_rows_ref, own_ref = refs[:3]
     message_refs, gain_scratch = refs[3:-1], refs[-1]
     arriving = arriving_from([arrived_ref, output_ref])
-    inverse = inverse_ref[1]
+    normed_of = normed_from(x_ref, 1, inverse_ref[1])
     columns_of = [Group(sizes, turn) for turn in turns]
     grads = [columns_of[turn].stacked(arriving) for turn in turns]
     prob_grads = [dot(keys(turn, 1), grads[turn], NT) for turn in turns]
@@ -277,15 +325,8 @@
         key_grad = SCALE * dot(dscores[turn], query, NN)
         put_key_grads(sizes, turn, (key_grad, value_grads[turn]), own_ref, message_refs)
     for turn in turns:
-        low_parts = columns_of[turn].unstacked(query_grads[turn])
-        for index, low in enumerate(low_parts):
-            query_grad_ref[:, columns_of[turn].head(index)] = low
-        gain_terms(
-            columns_of[turn],
-            low_parts,
-            lambda where: x_ref[0, 1, :, where].astype(F32) * inverse,
-            gain_scratch,
-        )
+        query_grad_ref[turn] = query_grads[turn]
+        gain_terms(columns_of[turn], query_grads[turn], normed_of, gain_scratch)
     gain_rows = gain_scratch[...] + before_ref[...]
     gain_rows_ref[...] = gain_rows
     gain_low = gain_rows.astype(BF16)
@@ -310,13 +351,26 @@
     x_ref, gain_ref, inverse_ref, arrived_ref, output_ref, query_grad_ref, first_ref = refs[:7]
     input_grads_ref = refs[7]
     input_grads_ref[0, 0] = first_ref[...]
-
-    def write(here, result):
-        input_grads_ref[0, 1, :, here] = result
-
-    arriving = arriving_from([arrived_ref, output_ref])
+    inverse = inverse_ref[1]
+    normed_of = normed_from(x_ref, 1, inverse)
+    coupled = jnp.zeros((sizes[0], HD), F32)
+    for turn in range(sizes[3]):
+        coupled = coupled_terms(
+            Group(sizes, turn), query_grad_ref[turn], normed_of, gain_ref, coupled
+        )
+
+    def write(where, result):
+        input_grads_ref[0, 1, :, where] = result
+
     write_input_grads(
-        sizes, 1, x_ref, gain_ref, inverse_ref[1], query_grad_ref, arriving, write
+        sizes,
+        coupled,
+        lambda turn: query_grad_ref[turn],
+        normed_of,
+        gain_ref,
+        inverse,
+        arriving_from([arrived_ref, output_ref]),
+        write,
     )
 
 
@@ -436,21 +490,34 @@
         for block in (own_kv, far_kv)
         for place in [(0, 0)] + places
     ]
-    queries, inverse = call(
-        norm_kernel,
+    own_set, far_set = kv[: len(kv) // 2], kv[len(kv) // 2 :]
+    queries, inverse, masks = call(
+        functools.partial(norm_kernel, sizes),
         "norm",
-        (segment_inputs, norm_gain),
-        [shape((ticks, rows, columns), BF16), shape((ticks, rows, HD), F32)],
+        (doc_lengths, segment_inputs, norm_gain),
+        [
+            shape((ticks, rows, columns), BF16),
+            shape((ticks, rows, HD), F32),
+            shape((ticks, key_count, stacked), F32),
+        ],
+        scalars=1,
     )
 
     low_rows = shape((rows, columns), BF16)
-    low_scores = shape((tp_count, key_count, stacked), BF16)
-    input_grad_first, query_grad_first, dscore_first, probs_first = call(
-        functools.partial(first_rows_kernel, sizes, len(kv)),
-        "first_rows",
-        (doc_lengths, segment_inputs, norm_gain, queries, inverse, waiting_grads, *kv),
-        [low_rows, low_rows, low_scores, low_scores],
-        scalars=1,
+    low_scores = shape((near_count, key_count, stacked), BF16)
+    low_grads = shape((near_count, stacked, HD), BF16)
+    rows_operands = (segment_inputs, norm_gain, queries, inverse, masks, waiting_grads)
+    query_grad_near, dscore_near, probs_near, coupled = call(
+        functools.partial(first_near_rows_kernel, sizes),
+        "first_near_rows",
+        (*rows_operands, *own_set),
+        [low_grads, low_scores, low_scores, shape((rows, HD), F32)],
+    )
+    input_grad_first, query_grad_far, dscore_far, probs_far = call(
+        functools.partial(first_far_rows_kernel, sizes),
+        "first_far_rows",
+        (*rows_operands, *far_set, query_grad_near, coupled),
+        [low_rows, low_grads, low_scores, low_scores],
     )
     arrived = lax.ppermute(
         input_grad_first, "pipe", [(i, (i - 1) % pipe_count) for i in range(pipe_count)]
@@ -467,9 +534,12 @@
             queries,
             inverse,
             waiting_grads,
-            query_grad_first,
-            dscore_first,
-            probs_first,
+            query_grad_near,
+            query_grad_far,
+            dscore_near,
+            dscore_far,
+            probs_near,
+            probs_far,
         ),
         [gain_shape, shape(first_sums, F32)] + [shape(first_sums, BF16)] * (cycle - 1),
     )
@@ -477,11 +547,10 @@
         to_near(value, -step, 0) for step, value in enumerate(sums_first[1:], 1)
     ]
     (probs_second,) = call(
-        functools.partial(second_probs_kernel, sizes, len(kv)),
+        functools.partial(second_probs_kernel, sizes),
         "second_probs",
-        (doc_lengths, queries, *kv),
+        (masks, queries, *kv),
         [shape((tp_count, key_count, stacked), F32)],
-        scalars=1,
     )
     message = shape((pair_rows + gain_count, HD), BF16)
     query_grad_second, gain_rows, own_second, *sends = call(
@@ -497,7 +566,7 @@
             gain_first,
             *kv,
         ),
-        [low_rows, gain_shape, own_shape] + [message] * len(places),
+        [shape((tp_count, stacked, HD), BF16), gain_shape, own_shape] + [message] * len(places),
         scratch=[pltpu.VMEM((gain_count, HD), F32)],
     )
     received = [to_near(value, -step, near) for value, (step, near) in zip(sends, places)]

time: 38.8 us -> 38.1 us (0.982)
  waiting for transfers between devices: 8.83 us -> 8.14 us
    ppermute x3, waiting for transfers between devices: 3.26 us -> 2.29 us  [to_near(): return lax.ppermute(value, ('ctx', 'tp'), pairs)]
    ppermute x1, waiting for transfers between devices: 0.81 us -> 1.47 us  [on_device(): lax.ppermute(input_grad_first, 'pipe', [(i, (i - 1) % pipe_count) for i i...]
    pallas_call x11 -> x12, Pallas kernels: 5.93 us -> 5.76 us  [call(): pl.pallas_call(kernel, out_shape=out_shape, in_specs=in_specs, out_specs=...]
  transfers between devices with their start and end apart: 15 -> 15, of which waited for: 7 -> 6; matrix products, arithmetic and copies ran while one was open for 0% -> 0% of each run, Pallas kernels for 9% -> 11%
where the time goes in v7:
time: 38.1 us; the launch traced here: 37.9 us
  starting transfers between devices  21.1 us (55%)
  waiting for transfers between devices  8.14 us (21%)
  Pallas kernels  5.76 us (15%)
  local copies, waits for them, and re-layouts  1.15 us (3%)
  other arithmetic  0.93 us (2%)
  between operations  0.79 us (2%)
    ppermute x3, starting transfers between devices, to_far(): lax.ppermute(value, 'tp', [(i, i ^ near_count) for i in range(tp_count)])  7.48 us
    ppermute x3, starting transfers between devices, to_near(): return lax.ppermute(value, ('ctx', 'tp'), pairs)  6.57 us
    pallas_call x12, Pallas kernels, call(): pl.pallas_call(kernel, out_shape=out_shape, in_specs=in_specs, out_specs=...  5.76 us
    ppermute x4, starting transfers between devices, to_near(): lax.ppermute(value, 'ctx', [(i, (i + step) % cycle) for i in range(cycle)])  3.66 us
    ppermute x4, starting transfers between devices, to_near(): return lax.ppermute(value, 'tp', [(i, i ^ near) for i in range(tp_count)])  3.32 us
    ppermute x3, waiting for transfers between devices, to_far(): lax.ppermute(value, 'tp', [(i, i ^ near_count) for i in range(tp_count)])  2.89 us
    ppermute x3, waiting for transfers between devices, to_near(): return lax.ppermute(value, ('ctx', 'tp'), pairs)  2.29 us
    ppermute x1, waiting for transfers between devices, on_device(): lax.ppermute(input_grad_first, 'pipe', [(i, (i - 1) % pipe_count) for i i...  1.47 us
  transfers between devices with their start and end apart: 15, of which 6 were waited for; matrix products, arithmetic and copies ran while one was open for 0% of the time, Pallas kernels for 11%

profile of v7, /device:TPU:0, one launch (start us, length us, event | category | flops | bytes accessed | tf_op | source)
XLA Modules:
  0.0 37.9 jit_solution(926027580439421311)
XLA Ops:
  0.6 0.0 copy-start.2
  0.6 0.9 %pad_maximum_fusion.both_ref = bf16[2,2,128,128]{3,2,1,0:T(8,128)(2,1)S(1)} fusion(bf16[1,2,128,128]{3,2,1,0:T(8,128)(2,1)} %param.9, bf16[1,2,128,128]{3,2,1,0:T(8,128)(2,1)} %param.8), kind=kLoop, calls=%fused_computation | loop fusion | flops 65536 | bytes 262144 | tf_op jit(solution)/shard_map/stack | solution.py:483
  1.6 0.0 copy-start.4
  1.6 0.0 copy-start.5
  1.6 4.1 %collective-permute-start = (bf16[2,2,64,128]{3,2,1,0:T(8,128)(2,1)S(1)}, bf16[2,2,64,128]{3,2,1,0:T(8,128)(2,1)S(1)}, u32[]{:S(2)}, u32[]{:S(2)}) collective-permute-start(bf16[2,2,64,128]{3,2,1,0:T(8,128)(2,1)S(1)} %get-tuple-element.39), channel_id=1, source_target_pairs={{0,2},{1,3},{2,0},{3,1},{4,6},{5,7},{6,4},{7,5},{8,10},{9,11},{10,... | collective-permute-start | bytes 196616 | tf_op jit(solution)/shard_map/ppermute | solution.py:477
  5.7 2.5 %collective-permute-start.6 = (bf16[2,2,64,128]{3,2,1,0:T(8,128)(2,1)S(1)}, bf16[2,2,64,128]{3,2,1,0:T(8,128)(2,1)S(1)}, u32[]{:S(2)}, u32[]{:S(2)}) collective-permute-start(bf16[2,2,64,128]{3,2,1,0:T(8,128)(2,1)S(1)} %get-tuple-element.40.refs_6_.refs_2_.refs_7_), channel_id=1, source_target_pairs={{0,5},{1,4},{2,7},{3,6},{4,1},{5,0},{6,3},{7,2},{8,13},{9,12},{10,... | collective-permute-start | bytes 196616 | tf_op jit(solution)/shard_map/ppermute | solution.py:474
  8.3 0.5 %collective-permute-start.5 = (bf16[2,2,64,128]{3,2,1,0:T(8,128)(2,1)S(1)}, bf16[2,2,64,128]{3,2,1,0:T(8,128)(2,1)S(1)}, u32[]{:S(2)}, u32[]{:S(2)}) collective-permute-start(bf16[2,2,64,128]{3,2,1,0:T(8,128)(2,1)S(1)} %get-tuple-element.40.refs_6_.refs_2_.refs_7_), channel_id=1, source_target_pairs={{0,4},{4,0},{1,5},{5,1},{2,6},{6,2},{3,7},{7,3},{8,12},{12,8},{9,1... | collective-permute-start | bytes 196616 | tf_op jit(solution)/shard_map/ppermute | solution.py:468
  8.8 0.4 %collective-permute-start.4 = (bf16[2,2,64,128]{3,2,1,0:T(8,128)(2,1)S(1)}, bf16[2,2,64,128]{3,2,1,0:T(8,128)(2,1)S(1)}, u32[]{:S(2)}, u32[]{:S(2)}) collective-permute-start(bf16[2,2,64,128]{3,2,1,0:T(8,128)(2,1)S(1)} %get-tuple-element.40.refs_6_.refs_2_.refs_7_), channel_id=1, source_target_pairs={{0,1},{1,0},{2,3},{3,2},{4,5},{5,4},{6,7},{7,6},{8,9},{9,8},{10,11... | collective-permute-start | bytes 196616 | tf_op jit(solution)/shard_map/ppermute | solution.py:466
  9.2 0.0 collective-permute-done.refs_6_.refs_11_
  9.2 2.5 %collective-permute-start.3 = (bf16[2,2,64,128]{3,2,1,0:T(8,128)(2,1)S(1)}, bf16[2,2,64,128]{3,2,1,0:T(8,128)(2,1)S(1)}, u32[]{:S(2)}, u32[]{:S(2)}) collective-permute-start(bf16[2,2,64,128]{3,2,1,0:T(8,128)(2,1)S(1)} %collective-permute-done.refs_6_.refs_11_), channel_id=1, source_target_pairs={{0,5},{1,4},{2,7},{3,6},{4,1},{5,0},{6,3},{7,2},{8,13},{9,12},{10,... | collective-permute-start | bytes 196616 | tf_op jit(solution)/shard_map/ppermute | solution.py:474
  11.8 0.5 %collective-permute-start.2 = (bf16[2,2,64,128]{3,2,1,0:T(8,128)(2,1)S(1)}, bf16[2,2,64,128]{3,2,1,0:T(8,128)(2,1)S(1)}, u32[]{:S(2)}, u32[]{:S(2)}) collective-permute-start(bf16[2,2,64,128]{3,2,1,0:T(8,128)(2,1)S(1)} %collective-permute-done.refs_6_.refs_11_), channel_id=1, source_target_pairs={{0,4},{4,0},{1,5},{5,1},{2,6},{6,2},{3,7},{7,3},{8,12},{12,8},{9,1... | collective-permute-start | bytes 196616 | tf_op jit(solution)/shard_map/ppermute | solution.py:468
  12.3 0.0 collective-permute-done.6.refs_9_.refs_5_.refs_10_
  12.3 0.9 %collective-permute-start.1 = (bf16[2,2,64,128]{3,2,1,0:T(8,128)(2,1)S(1)}, bf16[2,2,64,128]{3,2,1,0:T(8,128)(2,1)S(1)}, u32[]{:S(2)}, u32[]{:S(2)}) collective-permute-start(bf16[2,2,64,128]{3,2,1,0:T(8,128)(2,1)S(1)} %collective-permute-done.refs_6_.refs_11_), channel_id=1, source_target_pairs={{0,1},{1,0},{2,3},{3,2},{4,5},{5,4},{6,7},{7,6},{8,9},{9,8},{10,11... | collective-permute-start | bytes 196616 | tf_op jit(solution)/shard_map/ppermute | solution.py:466
  13.2 0.0 copy-done.4
  13.2 0.0 copy-done.5
  13.2 0.0 copy-start
  13.2 1.0 %copy-done = bf16[1,2,32,4096]{3,2,1,0:T(8,128)(2,1)S(1)} copy-done((bf16[1,2,32,4096]{3,2,1,0:T(8,128)(2,1)S(1)}, bf16[1,2,32,4096]{3,2,1,0:T(8,128)(2,1)}, u32[]{:S(2)}) %copy-start) | copy-done | bytes 524312
  14.2 0.0 copy-start.1
  14.2 0.9 %norm.1 = (bf16[2,32,4096]{2,1,0:T(8,128)(2,1)S(1)}, f32[2,32,128]{2,1,0:T(8,128)S(1)}, f32[2,128,256]{2,1,0:T(8,128)S(1)}) custom-call(s32[5,8]{1,0:T(8,128)S(1)} %copy-done.5, bf16[1,2,32,4096]{3,2,1,0:T(8,128)(2,1)S(1)} %copy-done, f32[1,4096]{1,0:T(1,128)S(1)} %copy-done.4), custom_call_target="tpu_custom_call" | custom-call | tf_op jit(solution)/shard_map/norm/pallas_call | solution.py:452
  15.2 0.0 collective-permute-done.5.refs_8_.refs_4_.refs_9_
  15.2 0.0 collective-permute-done.4.refs_7_.refs_3_.refs_8_
  15.2 0.0 copy-done.2
  15.2 0.1 copy-done.1
  15.3 0.5 %first_near_rows.1 = (bf16[2,256,128]{2,1,0:T(8,128)(2,1)S(1)}, bf16[2,128,256]{2,1,0:T(8,128)(2,1)S(1)}, bf16[2,128,256]{2,1,0:T(8,128)(2,1)S(1)}, f32[32,128]{1,0:T(8,128)S(1)}) custom-call(bf16[1,2,32,4096]{3,2,1,0:T(8,128)(2,1)S(1)} %copy-done.1, f32[1,4096]{1,0:T(1,128)S(1)} %copy-done.4, bf16[2,32,4096]{2,1,0:T(8,128)(2,1)S(1)} %get-tuple-element.37.refs_2_.refs_1_, ...), custom_call_target="tpu_custom_call" | custom-call | tf_op jit(solution)/shard_map/first_near_rows/pallas_call | solution.py:452
  15.8 0.0 collective-permute-done.3.refs_9_.refs_14_
  15.8 0.3 collective-permute-done.2.refs_8_.refs_13_
  16.1 0.4 %collective-permute-done.1.refs_7_.refs_12_ = bf16[2,2,64,128]{3,2,1,0:T(8,128)(2,1)S(1)} collective-permute-done((bf16[2,2,64,128]{3,2,1,0:T(8,128)(2,1)S(1)}, bf16[2,2,64,128]{3,2,1,0:T(8,128)(2,1)S(1)}, u32[]{:S(2)}, u32[]{:S(2)}) %collective-permute-start.1) | collective-permute-done | bytes 65568 | tf_op jit(solution)/shard_map/ppermute | solution.py:466
  16.5 0.8 %first_far_rows.1 = (bf16[32,4096]{1,0:T(8,128)(2,1)S(1)}, bf16[2,256,128]{2,1,0:T(8,128)(2,1)S(1)}, bf16[2,128,256]{2,1,0:T(8,128)(2,1)S(1)}, bf16[2,128,256]{2,1,0:T(8,128)(2,1)S(1)}) custom-call(bf16[1,2,32,4096]{3,2,1,0:T(8,128)(2,1)S(1)} %copy-done.1, f32[1,4096]{1,0:T(1,128)S(1)} %copy-done.4, ...), custom_call_target="tpu_custom_call" | custom-call | tf_op jit(solution)/shard_map/first_far_rows/pallas_call | solution.py:452
  17.4 0.1 collective-permute-start.7
  17.4 0.4 %first_keys.1 = (f32[32,128]{1,0:T(8,128)S(1)}, f32[2,256,128]{2,1,0:T(8,128)S(1)}, bf16[2,256,128]{2,1,0:T(8,128)(2,1)S(1)}) custom-call(bf16[1,2,32,4096]{3,2,1,0:T(8,128)(2,1)S(1)} %copy-done.1, bf16[2,32,4096]{2,1,0:T(8,128)(2,1)S(1)} %get-tuple-element.37.refs_2_.refs_1_, f32[2,32,128]{2,1,0:T(8,128)S(1)} %get-tuple-element.36.refs_3_.refs_2_, ...), custom_call_target="tpu_custom_call" | custom-call | tf_op jit(solution)/shard_map/first_keys/pallas_call | solution.py:452
  17.9 0.0 copy-start.3
  17.9 1.6 %collective-permute-start.8 = (bf16[2,256,128]{2,1,0:T(8,128)(2,1)S(1)}, bf16[2,256,128]{2,1,0:T(8,128)(2,1)S(1)}, u32[]{:S(2)}, u32[]{:S(2)}) collective-permute-start(bf16[2,256,128]{2,1,0:T(8,128)(2,1)S(1)} %get-tuple-element.52), channel_id=1, source_target_pairs={{0,4},{4,0},{1,5},{5,1},{2,6},{6,2},{3,7},{7,3},{8,12},{12,8},{9,1... | collective-permute-start | bytes 393224 | tf_op jit(solution)/shard_map/ppermute | solution.py:468
  19.5 0.4 second_probs.1.refs_5_
  19.8 1.5 %collective-permute-done.7.refs_3_ = bf16[32,4096]{1,0:T(8,128)(2,1)S(1)} collective-permute-done((bf16[32,4096]{1,0:T(8,128)(2,1)S(1)}, bf16[32,4096]{1,0:T(8,128)(2,1)S(1)}, u32[]{:S(2)}, u32[]{:S(2)}) %collective-permute-start.7) | collective-permute-done | bytes 262176 | tf_op jit(solution)/shard_map/ppermute | solution.py:522
  21.3 0.0 copy-done.3
  21.3 0.6 %second_keys.1 = (bf16[4,256,128]{2,1,0:T(8,128)(2,1)S(1)}, f32[32,128]{1,0:T(8,128)S(1)}, f32[256,128]{1,0:T(8,128)S(1)}, bf16[288,128]{1,0:T(8,128)(2,1)S(1)},...) custom-call(bf16[1,2,32,4096]{3,2,1,0:T(8,128)(2,1)S(1)} %copy-done.1, ...), custom_call_target="tpu_custom_call" | custom-call | tf_op jit(solution)/shard_map/second_keys/pallas_call | solution.py:452
  22.0 1.0 %collective-permute-start.10 = (bf16[288,128]{1,0:T(8,128)(2,1)S(1)}, bf16[288,128]{1,0:T(8,128)(2,1)S(1)}, u32[]{:S(2)}, u32[]{:S(2)}) collective-permute-start(bf16[288,128]{1,0:T(8,128)(2,1)S(1)} %get-tuple-element.58), channel_id=1, source_target_pairs={{0,1},{1,0},{2,3},{3,2},{4,5},{5,4},{6,7},{7,6},{8,9},{9,8},{10,11... | collective-permute-start | bytes 221192 | tf_op jit(solution)/shard_map/ppermute | solution.py:466
  22.9 1.1 %collective-permute-start.11 = (bf16[288,128]{1,0:T(8,128)(2,1)S(1)}, bf16[288,128]{1,0:T(8,128)(2,1)S(1)}, u32[]{:S(2)}, u32[]{:S(2)}) collective-permute-start(bf16[288,128]{1,0:T(8,128)(2,1)S(1)} %get-tuple-element.59), channel_id=1, source_target_pairs={{0,4},{4,0},{1,5},{5,1},{2,6},{6,2},{3,7},{7,3},{8,12},{12,8},{9,1... | collective-permute-start | bytes 221192 | tf_op jit(solution)/shard_map/ppermute | solution.py:468
  24.0 1.5 %collective-permute-start.12 = (bf16[288,128]{1,0:T(8,128)(2,1)S(1)}, bf16[288,128]{1,0:T(8,128)(2,1)S(1)}, u32[]{:S(2)}, u32[]{:S(2)}) collective-permute-start(bf16[288,128]{1,0:T(8,128)(2,1)S(1)} %get-tuple-element.60), channel_id=1, source_target_pairs={{0,5},{1,4},{2,7},{3,6},{4,1},{5,0},{6,3},{7,2},{8,13},{9,12},{10,... | collective-permute-start | bytes 221192 | tf_op jit(solution)/shard_map/ppermute | solution.py:474
  25.5 0.0 collective-permute-done.8.refs_1_
  25.5 1.0 %collective-permute-start.9 = (bf16[256,128]{1,0:T(8,128)(2,1)S(1)}, bf16[256,128]{1,0:T(8,128)(2,1)S(1)}, u32[]{:S(2)}, u32[]{:S(2)}) collective-permute-start(bf16[256,128]{1,0:T(8,128)(2,1)S(1)} %get-tuple-element.54), channel_id=1, source_target_pairs={{0,1},{1,0},{2,3},{3,2},{4,5},{5,4},{6,7},{7,6},{8,9},{9,8},{10,11... | collective-permute-start | bytes 196616 | tf_op jit(solution)/shard_map/ppermute | solution.py:466
  26.5 0.0 collective-permute-done.10.refs_2_
  26.5 0.8 %collective-permute-done.11.refs_3_ = bf16[288,128]{1,0:T(8,128)(2,1)S(1)} collective-permute-done((bf16[288,128]{1,0:T(8,128)(2,1)S(1)}, bf16[288,128]{1,0:T(8,128)(2,1)S(1)}, u32[]{:S(2)}, u32[]{:S(2)}) %collective-permute-start.11) | collective-permute-done | bytes 73760 | tf_op jit(solution)/shard_map/ppermute | solution.py:468
  27.3 2.3 %collective-permute-done.12.refs_4_ = bf16[288,128]{1,0:T(8,128)(2,1)S(1)} collective-permute-done((bf16[288,128]{1,0:T(8,128)(2,1)S(1)}, bf16[288,128]{1,0:T(8,128)(2,1)S(1)}, u32[]{:S(2)}, u32[]{:S(2)}) %collective-permute-start.12) | collective-permute-done | bytes 73760 | tf_op jit(solution)/shard_map/ppermute | solution.py:474
  29.6 0.1 second_near.1
  29.6 2.6 %collective-permute-start.14 = (bf16[160,128]{1,0:T(8,128)(2,1)S(1)}, bf16[160,128]{1,0:T(8,128)(2,1)S(1)}, u32[]{:S(2)}, u32[]{:S(2)}) collective-permute-start(bf16[160,128]{1,0:T(8,128)(2,1)S(1)} %get-tuple-element.63), channel_id=1, source_target_pairs={{0,2},{1,3},{2,0},{3,1},{4,6},{5,7},{6,4},{7,5},{8,10},{9,11},{10,... | collective-permute-start | bytes 122888 | tf_op jit(solution)/shard_map/ppermute | solution.py:477
  32.2 0.0 collective-permute-done.9.refs_0_
  32.3 0.8 %collective-permute-start.13 = (bf16[128,128]{1,0:T(8,128)(2,1)S(1)}, bf16[128,128]{1,0:T(8,128)(2,1)S(1)}, u32[]{:S(2)}, u32[]{:S(2)}) collective-permute-start(bf16[128,128]{1,0:T(8,128)(2,1)S(1)} %get-tuple-element.62), channel_id=1, source_target_pairs={{0,2},{1,3},{2,0},{3,1},{4,6},{5,7},{6,4},{7,5},{8,10},{9,11},{10,... | collective-permute-start | bytes 98312 | tf_op jit(solution)/shard_map/ppermute | solution.py:477
  33.0 1.2 %second_rows.1 = bf16[1,2,32,4096]{3,2,1,0:T(8,128)(2,1)} custom-call(bf16[1,2,32,4096]{3,2,1,0:T(8,128)(2,1)S(1)} %copy-done.1, f32[1,4096]{1,0:T(1,128)S(1)} %copy-done.4, f32[2,32,128]{2,1,0:T(8,128)S(1)} %get-tuple-element.36.refs_3_.refs_2_, bf16[32,4096]{1,0:T(8,128)(2,1)S(1)} %collective-permute-done.7.refs_3_, bf16[1,32,4096]{2,1,0:T(8,128)(2,1)S(1)} %copy-done.3, ...), custom_call_target="tpu_custom_call" | custom-call | tf_op jit(solution)/shard_map/second_rows/pallas_call | solution.py:452
  34.2 2.9 %collective-permute-done.13.refs_2_ = bf16[128,128]{1,0:T(8,128)(2,1)S(1)} collective-permute-done((bf16[128,128]{1,0:T(8,128)(2,1)S(1)}, bf16[128,128]{1,0:T(8,128)(2,1)S(1)}, u32[]{:S(2)}, u32[]{:S(2)}) %collective-permute-start.13) | collective-permute-done | bytes 32800 | tf_op jit(solution)/shard_map/ppermute | solution.py:477
  37.1 0.0 collective-permute-done.14.refs_3_
  37.1 0.7 %finish.1 = (f32[1,2,128,128]{3,2,1,0:T(8,128)}, f32[1,2,128,128]{3,2,1,0:T(8,128)}, f32[32,128]{1,0:T(8,128)}) custom-call(f32[128,128]{1,0:T(8,128)S(1)} %get-tuple-element.55.refs_0_, f32[128,128]{1,0:T(8,128)S(1)} %get-tuple-element.61.refs_1_, bf16[128,128]{1,0:T(8,128)(2,1)S(1)} %collective-permute-done.13.refs_2_, ...), custom_call_target="tpu_custom_call" | custom-call | tf_op jit(solution)/shard_map/finish/pallas_call | solution.py:452
  (3 shorter events, 0.1 us)
Async XLA Ops:
  0.6 14.5 %copy-start.2 = (bf16[1,32,4096]{2,1,0:T(8,128)(2,1)S(1)}, bf16[1,32,4096]{2,1,0:T(8,128)(2,1)}, u32[]{:S(2)}) copy-start(bf16[1,32,4096]{2,1,0:T(8,128)(2,1)} %refs_3_.1) | copy-start | bytes 786436
  1.6 11.6 %copy-start.4 = (f32[1,4096]{1,0:T(1,128)S(1)}, f32[1,4096]{1,0:T(1,128)}, u32[]{:S(2)}) copy-start(f32[1,4096]{1,0:T(1,128)} %refs_1_.5) | copy-start | bytes 49156
  1.6 11.6 %copy-start.5 = (s32[5,8]{1,0:T(8,128)S(1)}, s32[5,8]{1,0:T(8,128)}, u32[]{:S(2)}) copy-start(s32[5,8]{1,0:T(8,128)} %doc_ref.1) | copy-start | bytes 484
  1.6 7.6 %collective-permute-start = (bf16[2,2,64,128]{3,2,1,0:T(8,128)(2,1)S(1)}, bf16[2,2,64,128]{3,2,1,0:T(8,128)(2,1)S(1)}, u32[]{:S(2)}, u32[]{:S(2)}) collective-permute-start(bf16[2,2,64,128]{3,2,1,0:T(8,128)(2,1)S(1)} %get-tuple-element.39), channel_id=1, source_target_pairs={{0,2},{1,3},{2,0},{3,1},{4,6},{5,7},{6,4},{7,5},{8,10},{9,11},{10,... | collective-permute-start | bytes 196616 | tf_op jit(solution)/shard_map/ppermute | solution.py:477
  5.7 6.5 %collective-permute-start.6 = (bf16[2,2,64,128]{3,2,1,0:T(8,128)(2,1)S(1)}, bf16[2,2,64,128]{3,2,1,0:T(8,128)(2,1)S(1)}, u32[]{:S(2)}, u32[]{:S(2)}) collective-permute-start(bf16[2,2,64,128]{3,2,1,0:T(8,128)(2,1)S(1)} %get-tuple-element.40.refs_6_.refs_2_.refs_7_), channel_id=1, source_target_pairs={{0,5},{1,4},{2,7},{3,6},{4,1},{5,0},{6,3},{7,2},{8,13},{9,12},{10,... | collective-permute-start | bytes 196616 | tf_op jit(solution)/shard_map/ppermute | solution.py:474
  8.3 6.9 %collective-permute-start.5 = (bf16[2,2,64,128]{3,2,1,0:T(8,128)(2,1)S(1)}, bf16[2,2,64,128]{3,2,1,0:T(8,128)(2,1)S(1)}, u32[]{:S(2)}, u32[]{:S(2)}) collective-permute-start(bf16[2,2,64,128]{3,2,1,0:T(8,128)(2,1)S(1)} %get-tuple-element.40.refs_6_.refs_2_.refs_7_), channel_id=1, source_target_pairs={{0,4},{4,0},{1,5},{5,1},{2,6},{6,2},{3,7},{7,3},{8,12},{12,8},{9,1... | collective-permute-start | bytes 196616 | tf_op jit(solution)/shard_map/ppermute | solution.py:468
  8.8 6.4 %collective-permute-start.4 = (bf16[2,2,64,128]{3,2,1,0:T(8,128)(2,1)S(1)}, bf16[2,2,64,128]{3,2,1,0:T(8,128)(2,1)S(1)}, u32[]{:S(2)}, u32[]{:S(2)}) collective-permute-start(bf16[2,2,64,128]{3,2,1,0:T(8,128)(2,1)S(1)} %get-tuple-element.40.refs_6_.refs_2_.refs_7_), channel_id=1, source_target_pairs={{0,1},{1,0},{2,3},{3,2},{4,5},{5,4},{6,7},{7,6},{8,9},{9,8},{10,11... | collective-permute-start | bytes 196616 | tf_op jit(solution)/shard_map/ppermute | solution.py:466
  9.2 6.6 %collective-permute-start.3 = (bf16[2,2,64,128]{3,2,1,0:T(8,128)(2,1)S(1)}, bf16[2,2,64,128]{3,2,1,0:T(8,128)(2,1)S(1)}, u32[]{:S(2)}, u32[]{:S(2)}) collective-permute-start(bf16[2,2,64,128]{3,2,1,0:T(8,128)(2,1)S(1)} %collective-permute-done.refs_6_.refs_11_), channel_id=1, source_target_pairs={{0,5},{1,4},{2,7},{3,6},{4,1},{5,0},{6,3},{7,2},{8,13},{9,12},{10,... | collective-permute-start | bytes 196616 | tf_op jit(solution)/shard_map/ppermute | solution.py:474
  11.8 4.3 %collective-permute-start.2 = (bf16[2,2,64,128]{3,2,1,0:T(8,128)(2,1)S(1)}, bf16[2,2,64,128]{3,2,1,0:T(8,128)(2,1)S(1)}, u32[]{:S(2)}, u32[]{:S(2)}) collective-permute-start(bf16[2,2,64,128]{3,2,1,0:T(8,128)(2,1)S(1)} %collective-permute-done.refs_6_.refs_11_), channel_id=1, source_target_pairs={{0,4},{4,0},{1,5},{5,1},{2,6},{6,2},{3,7},{7,3},{8,12},{12,8},{9,1... | collective-permute-start | bytes 196616 | tf_op jit(solution)/shard_map/ppermute | solution.py:468
  12.3 4.3 %collective-permute-start.1 = (bf16[2,2,64,128]{3,2,1,0:T(8,128)(2,1)S(1)}, bf16[2,2,64,128]{3,2,1,0:T(8,128)(2,1)S(1)}, u32[]{:S(2)}, u32[]{:S(2)}) collective-permute-start(bf16[2,2,64,128]{3,2,1,0:T(8,128)(2,1)S(1)} %collective-permute-done.refs_6_.refs_11_), channel_id=1, source_target_pairs={{0,1},{1,0},{2,3},{3,2},{4,5},{5,4},{6,7},{7,6},{8,9},{9,8},{10,11... | collective-permute-start | bytes 196616 | tf_op jit(solution)/shard_map/ppermute | solution.py:466
  13.2 1.0 %copy-start = (bf16[1,2,32,4096]{3,2,1,0:T(8,128)(2,1)S(1)}, bf16[1,2,32,4096]{3,2,1,0:T(8,128)(2,1)}, u32[]{:S(2)}) copy-start(bf16[1,2,32,4096]{3,2,1,0:T(8,128)(2,1)} %refs_0_.9) | copy-start | bytes 1572868
  14.2 1.0 %copy-start.1 = (bf16[1,2,32,4096]{3,2,1,0:T(8,128)(2,1)S(1)}, bf16[1,2,32,4096]{3,2,1,0:T(8,128)(2,1)}, u32[]{:S(2)}) copy-start(bf16[1,2,32,4096]{3,2,1,0:T(8,128)(2,1)} %refs_0_.9) | copy-start | bytes 1572868
  17.4 3.9 %collective-permute-start.7 = (bf16[32,4096]{1,0:T(8,128)(2,1)S(1)}, bf16[32,4096]{1,0:T(8,128)(2,1)S(1)}, u32[]{:S(2)}, u32[]{:S(2)}) collective-permute-start(bf16[32,4096]{1,0:T(8,128)(2,1)S(1)} %get-tuple-element.43.refs_6_), channel_id=1, source_target_pairs={{0,24},{8,0},{16,8},{24,16},{1,25},{9,1},{17,9},{25,17},{2,26},{10... | collective-permute-start | bytes 786440 | tf_op jit(solution)/shard_map/ppermute | solution.py:522
  17.9 3.4 %copy-start.3 = (bf16[1,32,4096]{2,1,0:T(8,128)(2,1)S(1)}, bf16[1,32,4096]{2,1,0:T(8,128)(2,1)}, u32[]{:S(2)}) copy-start(bf16[1,32,4096]{2,1,0:T(8,128)(2,1)} %refs_4_.3) | copy-start | bytes 786436
  17.9 7.6 %collective-permute-start.8 = (bf16[2,256,128]{2,1,0:T(8,128)(2,1)S(1)}, bf16[2,256,128]{2,1,0:T(8,128)(2,1)S(1)}, u32[]{:S(2)}, u32[]{:S(2)}) collective-permute-start(bf16[2,256,128]{2,1,0:T(8,128)(2,1)S(1)} %get-tuple-element.52), channel_id=1, source_target_pairs={{0,4},{4,0},{1,5},{5,1},{2,6},{6,2},{3,7},{7,3},{8,12},{12,8},{9,1... | collective-permute-start | bytes 393224 | tf_op jit(solution)/shard_map/ppermute | solution.py:468
  22.0 4.6 %collective-permute-start.10 = (bf16[288,128]{1,0:T(8,128)(2,1)S(1)}, bf16[288,128]{1,0:T(8,128)(2,1)S(1)}, u32[]{:S(2)}, u32[]{:S(2)}) collective-permute-start(bf16[288,128]{1,0:T(8,128)(2,1)S(1)} %get-tuple-element.58), channel_id=1, source_target_pairs={{0,1},{1,0},{2,3},{3,2},{4,5},{5,4},{6,7},{7,6},{8,9},{9,8},{10,11... | collective-permute-start | bytes 221192 | tf_op jit(solution)/shard_map/ppermute | solution.py:466
  22.9 4.4 %collective-permute-start.11 = (bf16[288,128]{1,0:T(8,128)(2,1)S(1)}, bf16[288,128]{1,0:T(8,128)(2,1)S(1)}, u32[]{:S(2)}, u32[]{:S(2)}) collective-permute-start(bf16[288,128]{1,0:T(8,128)(2,1)S(1)} %get-tuple-element.59), channel_id=1, source_target_pairs={{0,4},{4,0},{1,5},{5,1},{2,6},{6,2},{3,7},{7,3},{8,12},{12,8},{9,1... | collective-permute-start | bytes 221192 | tf_op jit(solution)/shard_map/ppermute | solution.py:468
  24.0 5.6 %collective-permute-start.12 = (bf16[288,128]{1,0:T(8,128)(2,1)S(1)}, bf16[288,128]{1,0:T(8,128)(2,1)S(1)}, u32[]{:S(2)}, u32[]{:S(2)}) collective-permute-start(bf16[288,128]{1,0:T(8,128)(2,1)S(1)} %get-tuple-element.60), channel_id=1, source_target_pairs={{0,5},{1,4},{2,7},{3,6},{4,1},{5,0},{6,3},{7,2},{8,13},{9,12},{10,... | collective-permute-start | bytes 221192 | tf_op jit(solution)/shard_map/ppermute | solution.py:474
  25.5 6.7 %collective-permute-start.9 = (bf16[256,128]{1,0:T(8,128)(2,1)S(1)}, bf16[256,128]{1,0:T(8,128)(2,1)S(1)}, u32[]{:S(2)}, u32[]{:S(2)}) collective-permute-start(bf16[256,128]{1,0:T(8,128)(2,1)S(1)} %get-tuple-element.54), channel_id=1, source_target_pairs={{0,1},{1,0},{2,3},{3,2},{4,5},{5,4},{6,7},{7,6},{8,9},{9,8},{10,11... | collective-permute-start | bytes 196616 | tf_op jit(solution)/shard_map/ppermute | solution.py:466
  29.6 7.5 %collective-permute-start.14 = (bf16[160,128]{1,0:T(8,128)(2,1)S(1)}, bf16[160,128]{1,0:T(8,128)(2,1)S(1)}, u32[]{:S(2)}, u32[]{:S(2)}) collective-permute-start(bf16[160,128]{1,0:T(8,128)(2,1)S(1)} %get-tuple-element.63), channel_id=1, source_target_pairs={{0,2},{1,3},{2,0},{3,1},{4,6},{5,7},{6,4},{7,5},{8,10},{9,11},{10,... | collective-permute-start | bytes 122888 | tf_op jit(solution)/shard_map/ppermute | solution.py:477
  32.3 4.9 %collective-permute-start.13 = (bf16[128,128]{1,0:T(8,128)(2,1)S(1)}, bf16[128,128]{1,0:T(8,128)(2,1)S(1)}, u32[]{:S(2)}, u32[]{:S(2)}) collective-permute-start(bf16[128,128]{1,0:T(8,128)(2,1)S(1)} %get-tuple-element.62), channel_id=1, source_target_pairs={{0,2},{1,3},{2,0},{3,1},{4,6},{5,7},{6,4},{7,5},{8,10},{9,11},{10,... | collective-permute-start | bytes 98312 | tf_op jit(solution)/shard_map/ppermute | solution.py:477

commit v8 on v7

--- a/solution.py
+++ b/solution.py
@@ -78,11 +78,20 @@
         return [value[index * self.rows : (index + 1) * self.rows] for index in range(self.group)]
 
 
-def arriving_from(refs):
-    if len(refs) == 1:
-        return lambda where: refs[0][0, :, where]
-    last = lax.axis_index("pipe") == lax.axis_size("pipe") - 1
-    return lambda where: jnp.where(last, refs[1][0, :, where], refs[0][:, where])
+def waiting_from(waiting_ref):
+    return lambda where: waiting_ref[0, :, where]
+
+
+def arriving_from(output_ref, chip_ref, link_ref):
+    place = lax.axis_index("pipe")
+    last = place == lax.axis_size("pipe") - 1
+    even = place % 2 == 0
+
+    def arriving(where):
+        arrived = jnp.where(even, chip_ref[:, where], link_ref[:, where])
+        return jnp.where(last, output_ref[0, :, where], arrived)
+
+    return arriving
 
 
 def visible_keys(sizes, tick, doc_ref):
@@ -214,7 +223,7 @@
         keys,
         mask_ref[0],
         query_ref,
-        arriving_from([waiting_ref]),
+        waiting_from(waiting_ref),
         dscore_ref,
         probs_ref,
     )
@@ -233,7 +242,7 @@
     keys = Keys(sizes, 0, refs[6 : 6 + members])
     near_grad_ref, coupled_ref = refs[6 + members : 8 + members]
     input_grad_ref, query_grad_ref, dscore_ref, probs_ref = refs[8 + members :]
-    arriving = arriving_from([waiting_ref])
+    arriving = waiting_from(waiting_ref)
     query_grads = first_half(
         sizes, 1, keys, mask_ref[0], query_ref, arriving, dscore_ref, probs_ref
     )
@@ -263,7 +272,7 @@
     query_grad_refs, dscore_refs, probs_refs = refs[4:6], refs[6:8], refs[8:10]
     gain_rows_ref, own_ref = refs[10:12]
     send_refs = refs[12:]
-    arriving = arriving_from([waiting_ref])
+    arriving = waiting_from(waiting_ref)
     normed_of = normed_from(x_ref, 0, inverse_ref[0])
     for turn in range(tp_count):
         near, far = turn % near_count, turn // near_count
@@ -306,11 +315,12 @@
     cycle, tp_count = sizes[2:4]
     turns = range(tp_count)
     kv_count = cycle * tp_count
-    x_ref, query_ref, inverse_ref, arrived_ref, output_ref, probs_ref, before_ref = refs[:7]
-    keys, refs = both_sets(sizes, refs[7 : 7 + kv_count]), refs[7 + kv_count :]
+    x_ref, query_ref, inverse_ref, output_ref, chip_ref, link_ref = refs[:6]
+    probs_ref, before_ref, *refs = refs[6:]
+    keys, refs = both_sets(sizes, refs[:kv_count]), refs[kv_count:]
     query_grad_ref, gain_rows_ref, own_ref = refs[:3]
     message_refs, gain_scratch = refs[3:-1], refs[-1]
-    arriving = arriving_from([arrived_ref, output_ref])
+    arriving = arriving_from(output_ref, chip_ref, link_ref)
     normed_of = normed_from(x_ref, 1, inverse_ref[1])
     columns_of = [Group(sizes, turn) for turn in turns]
     grads = [columns_of[turn].stacked(arriving) for turn in turns]
@@ -348,8 +358,8 @@
 
 
 def second_rows_kernel(sizes, *refs):
-    x_ref, gain_ref, inverse_ref, arrived_ref, output_ref, query_grad_ref, first_ref = refs[:7]
-    input_grads_ref = refs[7]
+    x_ref, gain_ref, inverse_ref, output_ref, chip_ref, link_ref = refs[:6]
+    query_grad_ref, first_ref, input_grads_ref = refs[6:]
     input_grads_ref[0, 0] = first_ref[...]
     inverse = inverse_ref[1]
     normed_of = normed_from(x_ref, 1, inverse)
@@ -369,7 +379,7 @@
         normed_of,
         gain_ref,
         inverse,
-        arriving_from([arrived_ref, output_ref]),
+        arriving_from(output_ref, chip_ref, link_ref),
         write,
     )
 
@@ -519,9 +529,10 @@
         (*rows_operands, *far_set, query_grad_near, coupled),
         [low_rows, low_grads, low_scores, low_scores],
     )
-    arrived = lax.ppermute(
-        input_grad_first, "pipe", [(i, (i - 1) % pipe_count) for i in range(pipe_count)]
-    )
+    over_link = lax.ppermute(
+        input_grad_first, "pipe", [(i, i - 1) for i in range(2, pipe_count, 2)]
+    )
+    on_chip = lax.ppermute(input_grad_first, "pipe", [(i, i ^ 1) for i in range(pipe_count)])
     gain_shape = shape((gain_count, HD), F32)
     pair_rows = 2 * block
     own_shape = shape((pair_rows, HD), F32)
@@ -560,8 +571,9 @@
             segment_inputs,
             queries,
             inverse,
-            arrived,
             output_grads,
+            on_chip,
+            over_link,
             probs_second,
             gain_first,
             *kv,
@@ -584,8 +596,9 @@
             segment_inputs,
             norm_gain,
             inverse,
-            arrived,
             output_grads,
+            on_chip,
+            over_link,
             query_grad_second,
             input_grad_first,
         ),

time: 38.1 us -> 37.7 us (0.990)
  the two profiles are of different devices: /device:TPU:0 before, /device:TPU:1 now
where the time goes in v8:
time: 37.7 us; the launch traced here: 37.5 us
  starting transfers between devices  20.7 us (55%)
  waiting for transfers between devices  7.99 us (21%)
  Pallas kernels  5.95 us (16%)
  local copies, waits for them, and re-layouts  1.15 us (3%)
  other arithmetic  0.93 us (2%)
  between operations  0.8 us (2%)
    ppermute x3, starting transfers between devices, to_far(): lax.ppermute(value, 'tp', [(i, i ^ near_count) for i in range(tp_count)])  6.13 us
    pallas_call x12, Pallas kernels, call(): pl.pallas_call(kernel, out_shape=out_shape, in_specs=in_specs, out_specs=...  5.95 us
    ppermute x3, starting transfers between devices, to_near(): return lax.ppermute(value, ('ctx', 'tp'), pairs)  5.76 us
    ppermute x1, waiting for transfers between devices, on_device(): lax.ppermute(input_grad_first, 'pipe', [(i, i - 1) for i in range(2, pipe...  3.85 us
    ppermute x4, starting transfers between devices, to_near(): lax.ppermute(value, 'ctx', [(i, (i + step) % cycle) for i in range(cycle)])  2.53 us
    ppermute x1, starting transfers between devices, on_device(): lax.ppermute(input_grad_first, 'pipe', [(i, i ^ 1) for i in range(pipe_co...  2.52 us
    ppermute x4, starting transfers between devices, to_near(): return lax.ppermute(value, 'tp', [(i, i ^ near) for i in range(tp_count)])  2.43 us
    ppermute x3, waiting for transfers between devices, to_far(): lax.ppermute(value, 'tp', [(i, i ^ near_count) for i in range(tp_count)])  1.86 us
  transfers between devices with their start and end apart: 16, of which 5 were waited for; matrix products, arithmetic and copies ran while one was open for 0% of the time, Pallas kernels for 12%

profile of v8, /device:TPU:1, one launch (start us, length us, event | category | flops | bytes accessed | tf_op | source)
XLA Modules:
  0.0 37.5 jit_solution(7477538392431648955)
XLA Ops:
  0.6 0.0 copy-start.2
  0.6 0.9 %pad_maximum_fusion.both_ref = bf16[2,2,128,128]{3,2,1,0:T(8,128)(2,1)S(1)} fusion(bf16[1,2,128,128]{3,2,1,0:T(8,128)(2,1)} %param.9, bf16[1,2,128,128]{3,2,1,0:T(8,128)(2,1)} %param.8), kind=kLoop, calls=%fused_computation | loop fusion | flops 65536 | bytes 262144 | tf_op jit(solution)/shard_map/stack | solution.py:493
  1.6 0.0 copy-start.4
  1.6 0.0 copy-start.5
  1.6 3.2 %collective-permute-start = (bf16[2,2,64,128]{3,2,1,0:T(8,128)(2,1)S(1)}, bf16[2,2,64,128]{3,2,1,0:T(8,128)(2,1)S(1)}, u32[]{:S(2)}, u32[]{:S(2)}) collective-permute-start(bf16[2,2,64,128]{3,2,1,0:T(8,128)(2,1)S(1)} %get-tuple-element.39), channel_id=1, source_target_pairs={{0,2},{1,3},{2,0},{3,1},{4,6},{5,7},{6,4},{7,5},{8,10},{9,11},{10,... | collective-permute-start | bytes 196616 | tf_op jit(solution)/shard_map/ppermute | solution.py:487
  4.8 2.3 %collective-permute-start.6 = (bf16[2,2,64,128]{3,2,1,0:T(8,128)(2,1)S(1)}, bf16[2,2,64,128]{3,2,1,0:T(8,128)(2,1)S(1)}, u32[]{:S(2)}, u32[]{:S(2)}) collective-permute-start(bf16[2,2,64,128]{3,2,1,0:T(8,128)(2,1)S(1)} %get-tuple-element.40.refs_6_.refs_2_.refs_8_), channel_id=1, source_target_pairs={{0,5},{1,4},{2,7},{3,6},{4,1},{5,0},{6,3},{7,2},{8,13},{9,12},{10,... | collective-permute-start | bytes 196616 | tf_op jit(solution)/shard_map/ppermute | solution.py:484
  7.1 0.2 collective-permute-start.5
  7.3 0.2 collective-permute-start.4
  7.5 0.0 collective-permute-done.refs_6_.refs_12_
  7.5 2.3 %collective-permute-start.3 = (bf16[2,2,64,128]{3,2,1,0:T(8,128)(2,1)S(1)}, bf16[2,2,64,128]{3,2,1,0:T(8,128)(2,1)S(1)}, u32[]{:S(2)}, u32[]{:S(2)}) collective-permute-start(bf16[2,2,64,128]{3,2,1,0:T(8,128)(2,1)S(1)} %collective-permute-done.refs_6_.refs_12_), channel_id=1, source_target_pairs={{0,5},{1,4},{2,7},{3,6},{4,1},{5,0},{6,3},{7,2},{8,13},{9,12},{10,... | collective-permute-start | bytes 196616 | tf_op jit(solution)/shard_map/ppermute | solution.py:484
  9.7 0.2 collective-permute-start.2
  10.0 0.0 collective-permute-done.6.refs_9_.refs_5_.refs_11_
  10.0 0.9 %collective-permute-start.1 = (bf16[2,2,64,128]{3,2,1,0:T(8,128)(2,1)S(1)}, bf16[2,2,64,128]{3,2,1,0:T(8,128)(2,1)S(1)}, u32[]{:S(2)}, u32[]{:S(2)}) collective-permute-start(bf16[2,2,64,128]{3,2,1,0:T(8,128)(2,1)S(1)} %collective-permute-done.refs_6_.refs_12_), channel_id=1, source_target_pairs={{0,1},{1,0},{2,3},{3,2},{4,5},{5,4},{6,7},{7,6},{8,9},{9,8},{10,11... | collective-permute-start | bytes 196616 | tf_op jit(solution)/shard_map/ppermute | solution.py:476
  10.8 0.0 copy-done.4
  10.8 0.0 copy-done.5
  10.9 0.0 copy-start
  10.9 1.0 %copy-done = bf16[1,2,32,4096]{3,2,1,0:T(8,128)(2,1)S(1)} copy-done((bf16[1,2,32,4096]{3,2,1,0:T(8,128)(2,1)S(1)}, bf16[1,2,32,4096]{3,2,1,0:T(8,128)(2,1)}, u32[]{:S(2)}) %copy-start) | copy-done | bytes 524312
  11.9 0.0 copy-start.1
  11.9 0.9 %norm.1 = (bf16[2,32,4096]{2,1,0:T(8,128)(2,1)S(1)}, f32[2,32,128]{2,1,0:T(8,128)S(1)}, f32[2,128,256]{2,1,0:T(8,128)S(1)}) custom-call(s32[5,8]{1,0:T(8,128)S(1)} %copy-done.5, bf16[1,2,32,4096]{3,2,1,0:T(8,128)(2,1)S(1)} %copy-done, f32[1,4096]{1,0:T(1,128)S(1)} %copy-done.4), custom_call_target="tpu_custom_call" | custom-call | tf_op jit(solution)/shard_map/norm/pallas_call | solution.py:462
  12.8 0.0 collective-permute-done.5.refs_8_.refs_4_.refs_10_
  12.8 0.0 collective-permute-done.4.refs_7_.refs_3_.refs_9_
  12.8 0.0 copy-done.2
  12.9 0.1 copy-done.1
  12.9 0.5 %first_near_rows.1 = (bf16[2,256,128]{2,1,0:T(8,128)(2,1)S(1)}, bf16[2,128,256]{2,1,0:T(8,128)(2,1)S(1)}, bf16[2,128,256]{2,1,0:T(8,128)(2,1)S(1)}, f32[32,128]{1,0:T(8,128)S(1)}) custom-call(bf16[1,2,32,4096]{3,2,1,0:T(8,128)(2,1)S(1)} %copy-done.1, f32[1,4096]{1,0:T(1,128)S(1)} %copy-done.4, bf16[2,32,4096]{2,1,0:T(8,128)(2,1)S(1)} %get-tuple-element.37.refs_2_.refs_1_, ...), custom_call_target="tpu_custom_call" | custom-call | tf_op jit(solution)/shard_map/first_near_rows/pallas_call | solution.py:462
  13.5 0.0 collective-permute-done.3.refs_9_.refs_15_
  13.5 0.0 collective-permute-done.2.refs_8_.refs_14_
  13.5 0.0 collective-permute-done.1.refs_7_.refs_13_
  13.5 0.8 %first_far_rows.1 = (bf16[32,4096]{1,0:T(8,128)(2,1)S(1)}, bf16[2,256,128]{2,1,0:T(8,128)(2,1)S(1)}, bf16[2,128,256]{2,1,0:T(8,128)(2,1)S(1)}, bf16[2,128,256]{2,1,0:T(8,128)(2,1)S(1)}) custom-call(bf16[1,2,32,4096]{3,2,1,0:T(8,128)(2,1)S(1)} %copy-done.1, f32[1,4096]{1,0:T(1,128)S(1)} %copy-done.4, ...), custom_call_target="tpu_custom_call" | custom-call | tf_op jit(solution)/shard_map/first_far_rows/pallas_call | solution.py:462
  14.3 1.3 %collective-permute-start.8 = (bf16[32,4096]{1,0:T(8,128)(2,1)S(1)}, bf16[32,4096]{1,0:T(8,128)(2,1)S(1)}, u32[]{:S(2)}, u32[]{:S(2)}) collective-permute-start(bf16[32,4096]{1,0:T(8,128)(2,1)S(1)} %get-tuple-element.43.refs_7_), channel_id=1, source_target_pairs={{16,8},{17,9},{18,10},{19,11},{20,12},{21,13},{22,14},{23,15}} | collective-permute-start | bytes 786440 | tf_op jit(solution)/shard_map/ppermute | solution.py:532
  15.6 2.5 %collective-permute-start.7 = (bf16[32,4096]{1,0:T(8,128)(2,1)S(1)}, bf16[32,4096]{1,0:T(8,128)(2,1)S(1)}, u32[]{:S(2)}, u32[]{:S(2)}) collective-permute-start(bf16[32,4096]{1,0:T(8,128)(2,1)S(1)} %get-tuple-element.43.refs_7_), channel_id=1, source_target_pairs={{0,8},{8,0},{16,24},{24,16},{1,9},{9,1},{17,25},{25,17},{2,10},{10... | collective-permute-start | bytes 786440 | tf_op jit(solution)/shard_map/ppermute | solution.py:535
  18.2 0.4 %first_keys.1 = (f32[32,128]{1,0:T(8,128)S(1)}, f32[2,256,128]{2,1,0:T(8,128)S(1)}, bf16[2,256,128]{2,1,0:T(8,128)(2,1)S(1)}) custom-call(bf16[1,2,32,4096]{3,2,1,0:T(8,128)(2,1)S(1)} %copy-done.1, bf16[2,32,4096]{2,1,0:T(8,128)(2,1)S(1)} %get-tuple-element.37.refs_2_.refs_1_, f32[2,32,128]{2,1,0:T(8,128)S(1)} %get-tuple-element.36.refs_3_.refs_2_, ...), custom_call_target="tpu_custom_call" | custom-call | tf_op jit(solution)/shard_map/first_keys/pallas_call | solution.py:462
  18.6 0.0 copy-start.3
  18.6 1.3 %collective-permute-start.9 = (bf16[2,256,128]{2,1,0:T(8,128)(2,1)S(1)}, bf16[2,256,128]{2,1,0:T(8,128)(2,1)S(1)}, u32[]{:S(2)}, u32[]{:S(2)}) collective-permute-start(bf16[2,256,128]{2,1,0:T(8,128)(2,1)S(1)} %get-tuple-element.52), channel_id=1, source_target_pairs={{0,4},{4,0},{1,5},{5,1},{2,6},{6,2},{3,7},{7,3},{8,12},{12,8},{9,1... | collective-permute-start | bytes 393224 | tf_op jit(solution)/shard_map/ppermute | solution.py:478
  19.9 0.4 second_probs.1.refs_6_
  20.3 3.9 %collective-permute-done.8.refs_5_ = bf16[32,4096]{1,0:T(8,128)(2,1)S(1)} collective-permute-done((bf16[32,4096]{1,0:T(8,128)(2,1)S(1)}, bf16[32,4096]{1,0:T(8,128)(2,1)S(1)}, u32[]{:S(2)}, u32[]{:S(2)}) %collective-permute-start.8) | collective-permute-done | bytes 262176 | tf_op jit(solution)/shard_map/ppermute | solution.py:532
  24.1 0.0 collective-permute-done.7.refs_4_
  24.1 0.0 copy-done.3
  24.1 0.7 %second_keys.1 = (bf16[4,256,128]{2,1,0:T(8,128)(2,1)S(1)}, f32[32,128]{1,0:T(8,128)S(1)}, f32[256,128]{1,0:T(8,128)S(1)}, bf16[288,128]{1,0:T(8,128)(2,1)S(1)},...) custom-call(bf16[1,2,32,4096]{3,2,1,0:T(8,128)(2,1)S(1)} %copy-done.1, ...), custom_call_target="tpu_custom_call" | custom-call | tf_op jit(solution)/shard_map/second_keys/pallas_call | solution.py:462
  24.9 0.7 %collective-permute-start.11 = (bf16[288,128]{1,0:T(8,128)(2,1)S(1)}, bf16[288,128]{1,0:T(8,128)(2,1)S(1)}, u32[]{:S(2)}, u32[]{:S(2)}) collective-permute-start(bf16[288,128]{1,0:T(8,128)(2,1)S(1)} %get-tuple-element.58), channel_id=1, source_target_pairs={{0,1},{1,0},{2,3},{3,2},{4,5},{5,4},{6,7},{7,6},{8,9},{9,8},{10,11... | collective-permute-start | bytes 221192 | tf_op jit(solution)/shard_map/ppermute | solution.py:476
  25.6 0.8 %collective-permute-start.12 = (bf16[288,128]{1,0:T(8,128)(2,1)S(1)}, bf16[288,128]{1,0:T(8,128)(2,1)S(1)}, u32[]{:S(2)}, u32[]{:S(2)}) collective-permute-start(bf16[288,128]{1,0:T(8,128)(2,1)S(1)} %get-tuple-element.59), channel_id=1, source_target_pairs={{0,4},{4,0},{1,5},{5,1},{2,6},{6,2},{3,7},{7,3},{8,12},{12,8},{9,1... | collective-permute-start | bytes 221192 | tf_op jit(solution)/shard_map/ppermute | solution.py:478
  26.4 1.3 %collective-permute-start.13 = (bf16[288,128]{1,0:T(8,128)(2,1)S(1)}, bf16[288,128]{1,0:T(8,128)(2,1)S(1)}, u32[]{:S(2)}, u32[]{:S(2)}) collective-permute-start(bf16[288,128]{1,0:T(8,128)(2,1)S(1)} %get-tuple-element.60), channel_id=1, source_target_pairs={{0,5},{1,4},{2,7},{3,6},{4,1},{5,0},{6,3},{7,2},{8,13},{9,12},{10,... | collective-permute-start | bytes 221192 | tf_op jit(solution)/shard_map/ppermute | solution.py:484
  27.6 0.0 collective-permute-done.9.refs_1_
  27.7 0.7 %collective-permute-start.10 = (bf16[256,128]{1,0:T(8,128)(2,1)S(1)}, bf16[256,128]{1,0:T(8,128)(2,1)S(1)}, u32[]{:S(2)}, u32[]{:S(2)}) collective-permute-start(bf16[256,128]{1,0:T(8,128)(2,1)S(1)} %get-tuple-element.54), channel_id=1, source_target_pairs={{0,1},{1,0},{2,3},{3,2},{4,5},{5,4},{6,7},{7,6},{8,9},{9,8},{10,11... | collective-permute-start | bytes 196616 | tf_op jit(solution)/shard_map/ppermute | solution.py:476
  28.4 0.5 %collective-permute-done.11.refs_2_ = bf16[288,128]{1,0:T(8,128)(2,1)S(1)} collective-permute-done((bf16[288,128]{1,0:T(8,128)(2,1)S(1)}, bf16[288,128]{1,0:T(8,128)(2,1)S(1)}, u32[]{:S(2)}, u32[]{:S(2)}) %collective-permute-start.11) | collective-permute-done | bytes 73760 | tf_op jit(solution)/shard_map/ppermute | solution.py:476
  28.8 0.3 collective-permute-done.12.refs_3_
  29.1 1.5 %collective-permute-done.13.refs_4_ = bf16[288,128]{1,0:T(8,128)(2,1)S(1)} collective-permute-done((bf16[288,128]{1,0:T(8,128)(2,1)S(1)}, bf16[288,128]{1,0:T(8,128)(2,1)S(1)}, u32[]{:S(2)}, u32[]{:S(2)}) %collective-permute-start.13) | collective-permute-done | bytes 73760 | tf_op jit(solution)/shard_map/ppermute | solution.py:484
  30.6 0.1 second_near.1
  30.7 2.3 %collective-permute-start.15 = (bf16[160,128]{1,0:T(8,128)(2,1)S(1)}, bf16[160,128]{1,0:T(8,128)(2,1)S(1)}, u32[]{:S(2)}, u32[]{:S(2)}) collective-permute-start(bf16[160,128]{1,0:T(8,128)(2,1)S(1)} %get-tuple-element.63), channel_id=1, source_target_pairs={{0,2},{1,3},{2,0},{3,1},{4,6},{5,7},{6,4},{7,5},{8,10},{9,11},{10,... | collective-permute-start | bytes 122888 | tf_op jit(solution)/shard_map/ppermute | solution.py:487
  33.0 0.0 collective-permute-done.10.refs_0_
  33.0 0.6 %collective-permute-start.14 = (bf16[128,128]{1,0:T(8,128)(2,1)S(1)}, bf16[128,128]{1,0:T(8,128)(2,1)S(1)}, u32[]{:S(2)}, u32[]{:S(2)}) collective-permute-start(bf16[128,128]{1,0:T(8,128)(2,1)S(1)} %get-tuple-element.62), channel_id=1, source_target_pairs={{0,2},{1,3},{2,0},{3,1},{4,6},{5,7},{6,4},{7,5},{8,10},{9,11},{10,... | collective-permute-start | bytes 98312 | tf_op jit(solution)/shard_map/ppermute | solution.py:487
  33.6 1.3 %second_rows.1 = bf16[1,2,32,4096]{3,2,1,0:T(8,128)(2,1)} custom-call(bf16[1,2,32,4096]{3,2,1,0:T(8,128)(2,1)S(1)} %copy-done.1, f32[1,4096]{1,0:T(1,128)S(1)} %copy-done.4, f32[2,32,128]{2,1,0:T(8,128)S(1)} %get-tuple-element.36.refs_3_.refs_2_, bf16[1,32,4096]{2,1,0:T(8,128)(2,1)S(1)} %copy-done.3, bf16[32,4096]{1,0:T(8,128)(2,1)S(1)} %collective-permute-done.7.refs_4_, ...), custom_call_target="tpu_custom_call" | custom-call | tf_op jit(solution)/shard_map/second_rows/pallas_call | solution.py:462
  34.9 1.9 %collective-permute-done.14.refs_2_ = bf16[128,128]{1,0:T(8,128)(2,1)S(1)} collective-permute-done((bf16[128,128]{1,0:T(8,128)(2,1)S(1)}, bf16[128,128]{1,0:T(8,128)(2,1)S(1)}, u32[]{:S(2)}, u32[]{:S(2)}) %collective-permute-start.14) | collective-permute-done | bytes 32800 | tf_op jit(solution)/shard_map/ppermute | solution.py:487
  36.7 0.0 collective-permute-done.15.refs_3_
  36.7 0.7 %finish.1 = (f32[1,2,128,128]{3,2,1,0:T(8,128)}, f32[1,2,128,128]{3,2,1,0:T(8,128)}, f32[32,128]{1,0:T(8,128)}) custom-call(f32[128,128]{1,0:T(8,128)S(1)} %get-tuple-element.55.refs_0_, f32[128,128]{1,0:T(8,128)S(1)} %get-tuple-element.61.refs_1_, bf16[128,128]{1,0:T(8,128)(2,1)S(1)} %collective-permute-done.14.refs_2_, ...), custom_call_target="tpu_custom_call" | custom-call | tf_op jit(solution)/shard_map/finish/pallas_call | solution.py:462
  (3 shorter events, 0.1 us)
Async XLA Ops:
  0.6 12.2 %copy-start.2 = (bf16[1,32,4096]{2,1,0:T(8,128)(2,1)S(1)}, bf16[1,32,4096]{2,1,0:T(8,128)(2,1)}, u32[]{:S(2)}) copy-start(bf16[1,32,4096]{2,1,0:T(8,128)(2,1)} %refs_3_.3) | copy-start | bytes 786436
  1.6 9.3 %copy-start.4 = (f32[1,4096]{1,0:T(1,128)S(1)}, f32[1,4096]{1,0:T(1,128)}, u32[]{:S(2)}) copy-start(f32[1,4096]{1,0:T(1,128)} %refs_1_.5) | copy-start | bytes 49156
  1.6 9.3 %copy-start.5 = (s32[5,8]{1,0:T(8,128)S(1)}, s32[5,8]{1,0:T(8,128)}, u32[]{:S(2)}) copy-start(s32[5,8]{1,0:T(8,128)} %doc_ref.1) | copy-start | bytes 484
  1.6 5.9 %collective-permute-start = (bf16[2,2,64,128]{3,2,1,0:T(8,128)(2,1)S(1)}, bf16[2,2,64,128]{3,2,1,0:T(8,128)(2,1)S(1)}, u32[]{:S(2)}, u32[]{:S(2)}) collective-permute-start(bf16[2,2,64,128]{3,2,1,0:T(8,128)(2,1)S(1)} %get-tuple-element.39), channel_id=1, source_target_pairs={{0,2},{1,3},{2,0},{3,1},{4,6},{5,7},{6,4},{7,5},{8,10},{9,11},{10,... | collective-permute-start | bytes 196616 | tf_op jit(solution)/shard_map/ppermute | solution.py:487
  4.8 5.1 %collective-permute-start.6 = (bf16[2,2,64,128]{3,2,1,0:T(8,128)(2,1)S(1)}, bf16[2,2,64,128]{3,2,1,0:T(8,128)(2,1)S(1)}, u32[]{:S(2)}, u32[]{:S(2)}) collective-permute-start(bf16[2,2,64,128]{3,2,1,0:T(8,128)(2,1)S(1)} %get-tuple-element.40.refs_6_.refs_2_.refs_8_), channel_id=1, source_target_pairs={{0,5},{1,4},{2,7},{3,6},{4,1},{5,0},{6,3},{7,2},{8,13},{9,12},{10,... | collective-permute-start | bytes 196616 | tf_op jit(solution)/shard_map/ppermute | solution.py:484
  7.1 5.7 %collective-permute-start.5 = (bf16[2,2,64,128]{3,2,1,0:T(8,128)(2,1)S(1)}, bf16[2,2,64,128]{3,2,1,0:T(8,128)(2,1)S(1)}, u32[]{:S(2)}, u32[]{:S(2)}) collective-permute-start(bf16[2,2,64,128]{3,2,1,0:T(8,128)(2,1)S(1)} %get-tuple-element.40.refs_6_.refs_2_.refs_8_), channel_id=1, source_target_pairs={{0,4},{4,0},{1,5},{5,1},{2,6},{6,2},{3,7},{7,3},{8,12},{12,8},{9,1... | collective-permute-start | bytes 196616 | tf_op jit(solution)/shard_map/ppermute | solution.py:478
  7.3 5.5 %collective-permute-start.4 = (bf16[2,2,64,128]{3,2,1,0:T(8,128)(2,1)S(1)}, bf16[2,2,64,128]{3,2,1,0:T(8,128)(2,1)S(1)}, u32[]{:S(2)}, u32[]{:S(2)}) collective-permute-start(bf16[2,2,64,128]{3,2,1,0:T(8,128)(2,1)S(1)} %get-tuple-element.40.refs_6_.refs_2_.refs_8_), channel_id=1, source_target_pairs={{0,1},{1,0},{2,3},{3,2},{4,5},{5,4},{6,7},{7,6},{8,9},{9,8},{10,11... | collective-permute-start | bytes 196616 | tf_op jit(solution)/shard_map/ppermute | solution.py:476
  7.5 6.0 %collective-permute-start.3 = (bf16[2,2,64,128]{3,2,1,0:T(8,128)(2,1)S(1)}, bf16[2,2,64,128]{3,2,1,0:T(8,128)(2,1)S(1)}, u32[]{:S(2)}, u32[]{:S(2)}) collective-permute-start(bf16[2,2,64,128]{3,2,1,0:T(8,128)(2,1)S(1)} %collective-permute-done.refs_6_.refs_12_), channel_id=1, source_target_pairs={{0,5},{1,4},{2,7},{3,6},{4,1},{5,0},{6,3},{7,2},{8,13},{9,12},{10,... | collective-permute-start | bytes 196616 | tf_op jit(solution)/shard_map/ppermute | solution.py:484
  9.7 3.8 %collective-permute-start.2 = (bf16[2,2,64,128]{3,2,1,0:T(8,128)(2,1)S(1)}, bf16[2,2,64,128]{3,2,1,0:T(8,128)(2,1)S(1)}, u32[]{:S(2)}, u32[]{:S(2)}) collective-permute-start(bf16[2,2,64,128]{3,2,1,0:T(8,128)(2,1)S(1)} %collective-permute-done.refs_6_.refs_12_), channel_id=1, source_target_pairs={{0,4},{4,0},{1,5},{5,1},{2,6},{6,2},{3,7},{7,3},{8,12},{12,8},{9,1... | collective-permute-start | bytes 196616 | tf_op jit(solution)/shard_map/ppermute | solution.py:478
  10.0 3.5 %collective-permute-start.1 = (bf16[2,2,64,128]{3,2,1,0:T(8,128)(2,1)S(1)}, bf16[2,2,64,128]{3,2,1,0:T(8,128)(2,1)S(1)}, u32[]{:S(2)}, u32[]{:S(2)}) collective-permute-start(bf16[2,2,64,128]{3,2,1,0:T(8,128)(2,1)S(1)} %collective-permute-done.refs_6_.refs_12_), channel_id=1, source_target_pairs={{0,1},{1,0},{2,3},{3,2},{4,5},{5,4},{6,7},{7,6},{8,9},{9,8},{10,11... | collective-permute-start | bytes 196616 | tf_op jit(solution)/shard_map/ppermute | solution.py:476
  10.9 1.0 %copy-start = (bf16[1,2,32,4096]{3,2,1,0:T(8,128)(2,1)S(1)}, bf16[1,2,32,4096]{3,2,1,0:T(8,128)(2,1)}, u32[]{:S(2)}) copy-start(bf16[1,2,32,4096]{3,2,1,0:T(8,128)(2,1)} %refs_0_.9) | copy-start | bytes 1572868
  11.9 1.0 %copy-start.1 = (bf16[1,2,32,4096]{3,2,1,0:T(8,128)(2,1)S(1)}, bf16[1,2,32,4096]{3,2,1,0:T(8,128)(2,1)}, u32[]{:S(2)}) copy-start(bf16[1,2,32,4096]{3,2,1,0:T(8,128)(2,1)} %refs_0_.9) | copy-start | bytes 1572868
  14.3 9.8 %collective-permute-start.8 = (bf16[32,4096]{1,0:T(8,128)(2,1)S(1)}, bf16[32,4096]{1,0:T(8,128)(2,1)S(1)}, u32[]{:S(2)}, u32[]{:S(2)}) collective-permute-start(bf16[32,4096]{1,0:T(8,128)(2,1)S(1)} %get-tuple-element.43.refs_7_), channel_id=1, source_target_pairs={{16,8},{17,9},{18,10},{19,11},{20,12},{21,13},{22,14},{23,15}} | collective-permute-start | bytes 786440 | tf_op jit(solution)/shard_map/ppermute | solution.py:532
  15.6 8.5 %collective-permute-start.7 = (bf16[32,4096]{1,0:T(8,128)(2,1)S(1)}, bf16[32,4096]{1,0:T(8,128)(2,1)S(1)}, u32[]{:S(2)}, u32[]{:S(2)}) collective-permute-start(bf16[32,4096]{1,0:T(8,128)(2,1)S(1)} %get-tuple-element.43.refs_7_), channel_id=1, source_target_pairs={{0,8},{8,0},{16,24},{24,16},{1,9},{9,1},{17,25},{25,17},{2,10},{10... | collective-permute-start | bytes 786440 | tf_op jit(solution)/shard_map/ppermute | solution.py:535
  18.6 5.5 %copy-start.3 = (bf16[1,32,4096]{2,1,0:T(8,128)(2,1)S(1)}, bf16[1,32,4096]{2,1,0:T(8,128)(2,1)}, u32[]{:S(2)}) copy-start(bf16[1,32,4096]{2,1,0:T(8,128)(2,1)} %refs_3_.5) | copy-start | bytes 786436
  18.6 9.0 %collective-permute-start.9 = (bf16[2,256,128]{2,1,0:T(8,128)(2,1)S(1)}, bf16[2,256,128]{2,1,0:T(8,128)(2,1)S(1)}, u32[]{:S(2)}, u32[]{:S(2)}) collective-permute-start(bf16[2,256,128]{2,1,0:T(8,128)(2,1)S(1)} %get-tuple-element.52), channel_id=1, source_target_pairs={{0,4},{4,0},{1,5},{5,1},{2,6},{6,2},{3,7},{7,3},{8,12},{12,8},{9,1... | collective-permute-start | bytes 393224 | tf_op jit(solution)/shard_map/ppermute | solution.py:478
  24.9 3.9 %collective-permute-start.11 = (bf16[288,128]{1,0:T(8,128)(2,1)S(1)}, bf16[288,128]{1,0:T(8,128)(2,1)S(1)}, u32[]{:S(2)}, u32[]{:S(2)}) collective-permute-start(bf16[288,128]{1,0:T(8,128)(2,1)S(1)} %get-tuple-element.58), channel_id=1, source_target_pairs={{0,1},{1,0},{2,3},{3,2},{4,5},{5,4},{6,7},{7,6},{8,9},{9,8},{10,11... | collective-permute-start | bytes 221192 | tf_op jit(solution)/shard_map/ppermute | solution.py:476
  25.6 3.5 %collective-permute-start.12 = (bf16[288,128]{1,0:T(8,128)(2,1)S(1)}, bf16[288,128]{1,0:T(8,128)(2,1)S(1)}, u32[]{:S(2)}, u32[]{:S(2)}) collective-permute-start(bf16[288,128]{1,0:T(8,128)(2,1)S(1)} %get-tuple-element.59), channel_id=1, source_target_pairs={{0,4},{4,0},{1,5},{5,1},{2,6},{6,2},{3,7},{7,3},{8,12},{12,8},{9,1... | collective-permute-start | bytes 221192 | tf_op jit(solution)/shard_map/ppermute | solution.py:478
  26.4 4.2 %collective-permute-start.13 = (bf16[288,128]{1,0:T(8,128)(2,1)S(1)}, bf16[288,128]{1,0:T(8,128)(2,1)S(1)}, u32[]{:S(2)}, u32[]{:S(2)}) collective-permute-start(bf16[288,128]{1,0:T(8,128)(2,1)S(1)} %get-tuple-element.60), channel_id=1, source_target_pairs={{0,5},{1,4},{2,7},{3,6},{4,1},{5,0},{6,3},{7,2},{8,13},{9,12},{10,... | collective-permute-start | bytes 221192 | tf_op jit(solution)/shard_map/ppermute | solution.py:484
  27.7 5.3 %collective-permute-start.10 = (bf16[256,128]{1,0:T(8,128)(2,1)S(1)}, bf16[256,128]{1,0:T(8,128)(2,1)S(1)}, u32[]{:S(2)}, u32[]{:S(2)}) collective-permute-start(bf16[256,128]{1,0:T(8,128)(2,1)S(1)} %get-tuple-element.54), channel_id=1, source_target_pairs={{0,1},{1,0},{2,3},{3,2},{4,5},{5,4},{6,7},{7,6},{8,9},{9,8},{10,11... | collective-permute-start | bytes 196616 | tf_op jit(solution)/shard_map/ppermute | solution.py:476
  30.7 6.1 %collective-permute-start.15 = (bf16[160,128]{1,0:T(8,128)(2,1)S(1)}, bf16[160,128]{1,0:T(8,128)(2,1)S(1)}, u32[]{:S(2)}, u32[]{:S(2)}) collective-permute-start(bf16[160,128]{1,0:T(8,128)(2,1)S(1)} %get-tuple-element.63), channel_id=1, source_target_pairs={{0,2},{1,3},{2,0},{3,1},{4,6},{5,7},{6,4},{7,5},{8,10},{9,11},{10,... | collective-permute-start | bytes 122888 | tf_op jit(solution)/shard_map/ppermute | solution.py:487
  33.0 3.7 %collective-permute-start.14 = (bf16[128,128]{1,0:T(8,128)(2,1)S(1)}, bf16[128,128]{1,0:T(8,128)(2,1)S(1)}, u32[]{:S(2)}, u32[]{:S(2)}) collective-permute-start(bf16[128,128]{1,0:T(8,128)(2,1)S(1)} %get-tuple-element.62), channel_id=1, source_target_pairs={{0,2},{1,3},{2,0},{3,1},{4,6},{5,7},{6,4},{7,5},{8,10},{9,11},{10,... | collective-permute-start | bytes 98312 | tf_op jit(solution)/shard_map/ppermute | solution.py:487

commit v9 on v8

--- a/solution.py
+++ b/solution.py
@@ -384,29 +384,24 @@
     )
 
 
-def first_near_kernel(sizes, own_ref, *refs):
-    block = 2 * sizes[1]
-    keep_ref, send_ref = refs[-2:]
-    total = own_ref[...]
-    for ref in refs[:-2]:
-        total = total + ref[...].astype(F32)
-    keep_ref[...] = total[:block]
-    send_ref[...] = total[block:].astype(BF16)
-
-
-def second_near_kernel(sizes, *refs):
+def near_sum_kernel(sizes, *refs):
     rows, half, cycle, tp_count, group, columns = sizes
     near_count = tp_count // 2
     members = cycle * near_count
     own_ref, gain_ref = refs[:2]
-    message_refs = refs[2 : 1 + members]
-    keep_ref, gain_sum_ref, send_ref = refs[1 + members :]
+    message_refs, refs = refs[2 : 1 + members], refs[1 + members :]
+    own_first_ref, first_refs, refs = refs[0], refs[1:near_count], refs[near_count:]
+    keep_ref, gain_sum_ref, send_ref = refs
     block = 2 * half
-    total = own_ref[...]
+    first, second = own_first_ref[...], own_ref[...]
     for ref in message_refs:
-        total = total + ref[: 2 * block, :].astype(F32)
-    keep_ref[...] = total[:block]
-    send_ref[:block, :] = total[block:].astype(BF16)
+        second = second + ref[: 2 * block, :].astype(F32)
+    for ref in first_refs:
+        first = first + ref[...].astype(F32)
+    for tick, total in enumerate((first, second)):
+        here = slice(tick * block, (tick + 1) * block)
+        keep_ref[here, :] = total[:block]
+        send_ref[here, :] = total[block:].astype(BF16)
     cycle_place = lax.axis_index("ctx")
     near_place = lax.axis_index("tp") % near_count
     values = [gain_ref[...].astype(BF16).astype(F32)]
@@ -417,24 +412,22 @@
         owners.append(((cycle_place + step) % cycle) * near_count + (near_place ^ near))
     gain = in_order(values, owners)
     gain_sum_ref[...] = gain
-    send_ref[block:, :] = gain.astype(BF16)
-
-
-def finish_kernel(sizes, *refs):
+    send_ref[TICKS * block :, :] = gain.astype(BF16)
+
+
+def finish_kernel(sizes, keep_ref, gain_ref, receive_ref, key_ref, value_ref, gain_out_ref):
     half = sizes[1]
-    keep_refs, receive_refs, gain_ref = refs[:TICKS], refs[TICKS : 2 * TICKS], refs[2 * TICKS]
-    key_ref, value_ref, gain_out_ref = refs[2 * TICKS + 1 :]
     parity = lax.axis_index("tp") // (sizes[3] // 2)
-    block = 2 * half
     own_first = pl.multiple_of(parity * half, half)
     other_first = pl.multiple_of((1 - parity) * half, half)
     for tick in range(TICKS):
         for kind, out in enumerate((key_ref, value_ref)):
-            here = slice(kind * half, (kind + 1) * half)
-            out[0, tick, pl.ds(own_first, half), :] = keep_refs[tick][here, :]
-            out[0, tick, pl.ds(other_first, half), :] = receive_refs[tick][here, :].astype(F32)
+            begin = (tick * 2 + kind) * half
+            here = slice(begin, begin + half)
+            out[0, tick, pl.ds(own_first, half), :] = keep_ref[here, :]
+            out[0, tick, pl.ds(other_first, half), :] = receive_ref[here, :].astype(F32)
     own = gain_ref[...].astype(BF16).astype(F32)
-    gain_out_ref[...] = own + receive_refs[TICKS - 1][block:, :].astype(F32)
+    gain_out_ref[...] = own + receive_ref[TICKS * 2 * half :, :].astype(F32)
 
 
 def shape(dims, dtype):
@@ -604,24 +597,21 @@
         ),
         [shape((1, ticks, rows, columns), BF16)],
     )
-    keep_shape = shape((block, HD), F32)
-    keep_first, send_first = call(
-        functools.partial(first_near_kernel, sizes),
-        "first_near",
-        (own_first, *received_first),
-        [keep_shape, shape((block, HD), BF16)],
-    )
-    keep_second, gain_sum, send_second = call(
-        functools.partial(second_near_kernel, sizes),
-        "second_near",
-        (own_second, gain_rows, *received),
-        [keep_shape, gain_shape, shape((block + gain_count, HD), BF16)],
+    keep, gain_sum, send = call(
+        functools.partial(near_sum_kernel, sizes),
+        "near_sum",
+        (own_second, gain_rows, *received, own_first, *received_first),
+        [
+            shape((ticks * block, HD), F32),
+            gain_shape,
+            shape((ticks * block + gain_count, HD), BF16),
+        ],
     )
     grads_shape = shape((1, ticks, block, HD), F32)
     key_grads, value_grads, gain_grads = call(
         functools.partial(finish_kernel, sizes),
         "finish",
-        (keep_first, keep_second, to_far(send_first), to_far(send_second), gain_sum),
+        (keep, gain_sum, to_far(send)),
         [grads_shape, grads_shape, gain_shape],
     )
     return input_grads, key_grads, value_grads, gain_grads.reshape(1, columns)

time: 37.7 us -> 37.6 us (level)
  the two profiles are of different devices: /device:TPU:1 before, /device:TPU:0 now
where the time goes in v9:
time: 37.6 us; the launch traced here: 37.3 us
  starting transfers between devices  20.9 us (56%)
  waiting for transfers between devices  7.55 us (20%)
  Pallas kernels  5.95 us (16%)
  local copies, waits for them, and re-layouts  1.15 us (3%)
  other arithmetic  0.93 us (2%)
  between operations  0.82 us (2%)
    ppermute x3, starting transfers between devices, to_near(): return lax.ppermute(value, ('ctx', 'tp'), pairs)  7.14 us
    ppermute x2, starting transfers between devices, to_far(): lax.ppermute(value, 'tp', [(i, i ^ near_count) for i in range(tp_count)])  6.96 us
    pallas_call x11, Pallas kernels, call(): pl.pallas_call(kernel, out_shape=out_shape, in_specs=in_specs, out_specs=...  5.95 us
    ppermute x4, waiting for transfers between devices, to_near(): return lax.ppermute(value, 'tp', [(i, i ^ near) for i in range(tp_count)])  4.42 us
    ppermute x4, starting transfers between devices, to_near(): lax.ppermute(value, 'ctx', [(i, (i + step) % cycle) for i in range(cycle)])  3.56 us
    ppermute x2, waiting for transfers between devices, to_far(): lax.ppermute(value, 'tp', [(i, i ^ near_count) for i in range(tp_count)])  2.85 us
    ppermute x4, starting transfers between devices, to_near(): return lax.ppermute(value, 'tp', [(i, i ^ near) for i in range(tp_count)])  2.49 us
    unnamed x12, local copies, waits for them, and re-layouts  1.15 us
  transfers between devices with their start and end apart: 15, of which 4 were waited for; matrix products, arithmetic and copies ran while one was open for 0% of the time, Pallas kernels for 12%

profile of v9, /device:TPU:0, one launch (start us, length us, event | category | flops | bytes accessed | tf_op | source)
XLA Modules:
  0.0 37.3 jit_solution(2836068159252006056)
XLA Ops:
  0.6 0.0 copy-start.2
  0.6 0.9 %pad_maximum_fusion.both_ref = bf16[2,2,128,128]{3,2,1,0:T(8,128)(2,1)S(1)} fusion(bf16[1,2,128,128]{3,2,1,0:T(8,128)(2,1)} %param.9, bf16[1,2,128,128]{3,2,1,0:T(8,128)(2,1)} %param.8), kind=kLoop, calls=%fused_computation | loop fusion | flops 65536 | bytes 262144 | tf_op jit(solution)/shard_map/stack | solution.py:486
  1.6 0.0 copy-start.4
  1.6 0.0 copy-start.5
  1.6 4.1 %collective-permute-start = (bf16[2,2,64,128]{3,2,1,0:T(8,128)(2,1)S(1)}, bf16[2,2,64,128]{3,2,1,0:T(8,128)(2,1)S(1)}, u32[]{:S(2)}, u32[]{:S(2)}) collective-permute-start(bf16[2,2,64,128]{3,2,1,0:T(8,128)(2,1)S(1)} %get-tuple-element.37), channel_id=1, source_target_pairs={{0,2},{1,3},{2,0},{3,1},{4,6},{5,7},{6,4},{7,5},{8,10},{9,11},{10,... | collective-permute-start | bytes 196616 | tf_op jit(solution)/shard_map/ppermute | solution.py:480
  5.7 2.5 %collective-permute-start.6 = (bf16[2,2,64,128]{3,2,1,0:T(8,128)(2,1)S(1)}, bf16[2,2,64,128]{3,2,1,0:T(8,128)(2,1)S(1)}, u32[]{:S(2)}, u32[]{:S(2)}) collective-permute-start(bf16[2,2,64,128]{3,2,1,0:T(8,128)(2,1)S(1)} %get-tuple-element.38.refs_6_.refs_2_.refs_8_), channel_id=1, source_target_pairs={{0,5},{1,4},{2,7},{3,6},{4,1},{5,0},{6,3},{7,2},{8,13},{9,12},{10,... | collective-permute-start | bytes 196616 | tf_op jit(solution)/shard_map/ppermute | solution.py:477
  8.3 0.5 %collective-permute-start.5 = (bf16[2,2,64,128]{3,2,1,0:T(8,128)(2,1)S(1)}, bf16[2,2,64,128]{3,2,1,0:T(8,128)(2,1)S(1)}, u32[]{:S(2)}, u32[]{:S(2)}) collective-permute-start(bf16[2,2,64,128]{3,2,1,0:T(8,128)(2,1)S(1)} %get-tuple-element.38.refs_6_.refs_2_.refs_8_), channel_id=1, source_target_pairs={{0,4},{4,0},{1,5},{5,1},{2,6},{6,2},{3,7},{7,3},{8,12},{12,8},{9,1... | collective-permute-start | bytes 196616 | tf_op jit(solution)/shard_map/ppermute | solution.py:471
  8.8 0.4 %collective-permute-start.4 = (bf16[2,2,64,128]{3,2,1,0:T(8,128)(2,1)S(1)}, bf16[2,2,64,128]{3,2,1,0:T(8,128)(2,1)S(1)}, u32[]{:S(2)}, u32[]{:S(2)}) collective-permute-start(bf16[2,2,64,128]{3,2,1,0:T(8,128)(2,1)S(1)} %get-tuple-element.38.refs_6_.refs_2_.refs_8_), channel_id=1, source_target_pairs={{0,1},{1,0},{2,3},{3,2},{4,5},{5,4},{6,7},{7,6},{8,9},{9,8},{10,11... | collective-permute-start | bytes 196616 | tf_op jit(solution)/shard_map/ppermute | solution.py:469
  9.2 0.0 collective-permute-done.refs_6_.refs_12_
  9.2 2.5 %collective-permute-start.3 = (bf16[2,2,64,128]{3,2,1,0:T(8,128)(2,1)S(1)}, bf16[2,2,64,128]{3,2,1,0:T(8,128)(2,1)S(1)}, u32[]{:S(2)}, u32[]{:S(2)}) collective-permute-start(bf16[2,2,64,128]{3,2,1,0:T(8,128)(2,1)S(1)} %collective-permute-done.refs_6_.refs_12_), channel_id=1, source_target_pairs={{0,5},{1,4},{2,7},{3,6},{4,1},{5,0},{6,3},{7,2},{8,13},{9,12},{10,... | collective-permute-start | bytes 196616 | tf_op jit(solution)/shard_map/ppermute | solution.py:477
  11.8 0.5 %collective-permute-start.2 = (bf16[2,2,64,128]{3,2,1,0:T(8,128)(2,1)S(1)}, bf16[2,2,64,128]{3,2,1,0:T(8,128)(2,1)S(1)}, u32[]{:S(2)}, u32[]{:S(2)}) collective-permute-start(bf16[2,2,64,128]{3,2,1,0:T(8,128)(2,1)S(1)} %collective-permute-done.refs_6_.refs_12_), channel_id=1, source_target_pairs={{0,4},{4,0},{1,5},{5,1},{2,6},{6,2},{3,7},{7,3},{8,12},{12,8},{9,1... | collective-permute-start | bytes 196616 | tf_op jit(solution)/shard_map/ppermute | solution.py:471
  12.3 0.0 collective-permute-done.6.refs_9_.refs_5_.refs_11_
  12.3 0.9 %collective-permute-start.1 = (bf16[2,2,64,128]{3,2,1,0:T(8,128)(2,1)S(1)}, bf16[2,2,64,128]{3,2,1,0:T(8,128)(2,1)S(1)}, u32[]{:S(2)}, u32[]{:S(2)}) collective-permute-start(bf16[2,2,64,128]{3,2,1,0:T(8,128)(2,1)S(1)} %collective-permute-done.refs_6_.refs_12_), channel_id=1, source_target_pairs={{0,1},{1,0},{2,3},{3,2},{4,5},{5,4},{6,7},{7,6},{8,9},{9,8},{10,11... | collective-permute-start | bytes 196616 | tf_op jit(solution)/shard_map/ppermute | solution.py:469
  13.2 0.0 copy-done.4
  13.2 0.0 copy-done.5
  13.2 0.0 copy-start
  13.2 1.0 %copy-done = bf16[1,2,32,4096]{3,2,1,0:T(8,128)(2,1)S(1)} copy-done((bf16[1,2,32,4096]{3,2,1,0:T(8,128)(2,1)S(1)}, bf16[1,2,32,4096]{3,2,1,0:T(8,128)(2,1)}, u32[]{:S(2)}) %copy-start) | copy-done | bytes 524312
  14.2 0.0 copy-start.1
  14.2 0.9 %norm.1 = (bf16[2,32,4096]{2,1,0:T(8,128)(2,1)S(1)}, f32[2,32,128]{2,1,0:T(8,128)S(1)}, f32[2,128,256]{2,1,0:T(8,128)S(1)}) custom-call(s32[5,8]{1,0:T(8,128)S(1)} %copy-done.5, bf16[1,2,32,4096]{3,2,1,0:T(8,128)(2,1)S(1)} %copy-done, f32[1,4096]{1,0:T(1,128)S(1)} %copy-done.4), custom_call_target="tpu_custom_call" | custom-call | tf_op jit(solution)/shard_map/norm/pallas_call | solution.py:455
  15.2 0.0 collective-permute-done.5.refs_8_.refs_4_.refs_10_
  15.2 0.0 collective-permute-done.4.refs_7_.refs_3_.refs_9_
  15.2 0.0 copy-done.2
  15.2 0.1 copy-done.1
  15.3 0.5 %first_near_rows.1 = (bf16[2,256,128]{2,1,0:T(8,128)(2,1)S(1)}, bf16[2,128,256]{2,1,0:T(8,128)(2,1)S(1)}, bf16[2,128,256]{2,1,0:T(8,128)(2,1)S(1)}, f32[32,128]{1,0:T(8,128)S(1)}) custom-call(bf16[1,2,32,4096]{3,2,1,0:T(8,128)(2,1)S(1)} %copy-done.1, f32[1,4096]{1,0:T(1,128)S(1)} %copy-done.4, bf16[2,32,4096]{2,1,0:T(8,128)(2,1)S(1)} %get-tuple-element.35.refs_2_.refs_1_, ...), custom_call_target="tpu_custom_call" | custom-call | tf_op jit(solution)/shard_map/first_near_rows/pallas_call | solution.py:455
  15.8 0.0 collective-permute-done.3.refs_9_.refs_15_
  15.8 0.3 collective-permute-done.2.refs_8_.refs_14_
  16.1 0.4 %collective-permute-done.1.refs_7_.refs_13_ = bf16[2,2,64,128]{3,2,1,0:T(8,128)(2,1)S(1)} collective-permute-done((bf16[2,2,64,128]{3,2,1,0:T(8,128)(2,1)S(1)}, bf16[2,2,64,128]{3,2,1,0:T(8,128)(2,1)S(1)}, u32[]{:S(2)}, u32[]{:S(2)}) %collective-permute-start.1) | collective-permute-done | bytes 65568 | tf_op jit(solution)/shard_map/ppermute | solution.py:469
  16.5 0.8 %first_far_rows.1 = (bf16[32,4096]{1,0:T(8,128)(2,1)S(1)}, bf16[2,256,128]{2,1,0:T(8,128)(2,1)S(1)}, bf16[2,128,256]{2,1,0:T(8,128)(2,1)S(1)}, bf16[2,128,256]{2,1,0:T(8,128)(2,1)S(1)}) custom-call(bf16[1,2,32,4096]{3,2,1,0:T(8,128)(2,1)S(1)} %copy-done.1, f32[1,4096]{1,0:T(1,128)S(1)} %copy-done.4, ...), custom_call_target="tpu_custom_call" | custom-call | tf_op jit(solution)/shard_map/first_far_rows/pallas_call | solution.py:455
  17.4 0.7 %collective-permute-start.8 = (bf16[32,4096]{1,0:T(8,128)(2,1)S(1)}, bf16[32,4096]{1,0:T(8,128)(2,1)S(1)}, u32[]{:S(2)}, u32[]{:S(2)}) collective-permute-start(bf16[32,4096]{1,0:T(8,128)(2,1)S(1)} %get-tuple-element.41.refs_7_), channel_id=1, source_target_pairs={{16,8},{17,9},{18,10},{19,11},{20,12},{21,13},{22,14},{23,15}} | collective-permute-start | bytes 786440 | tf_op jit(solution)/shard_map/ppermute | solution.py:525
  18.0 0.1 collective-permute-start.7
  18.1 0.4 %first_keys.1 = (f32[32,128]{1,0:T(8,128)S(1)}, f32[2,256,128]{2,1,0:T(8,128)S(1)}, bf16[2,256,128]{2,1,0:T(8,128)(2,1)S(1)}) custom-call(bf16[1,2,32,4096]{3,2,1,0:T(8,128)(2,1)S(1)} %copy-done.1, bf16[2,32,4096]{2,1,0:T(8,128)(2,1)S(1)} %get-tuple-element.35.refs_2_.refs_1_, f32[2,32,128]{2,1,0:T(8,128)S(1)} %get-tuple-element.34.refs_3_.refs_2_, ...), custom_call_target="tpu_custom_call" | custom-call | tf_op jit(solution)/shard_map/first_keys/pallas_call | solution.py:455
  18.6 0.0 copy-start.3
  18.6 1.6 %collective-permute-start.12 = (bf16[2,256,128]{2,1,0:T(8,128)(2,1)S(1)}, bf16[2,256,128]{2,1,0:T(8,128)(2,1)S(1)}, u32[]{:S(2)}, u32[]{:S(2)}) collective-permute-start(bf16[2,256,128]{2,1,0:T(8,128)(2,1)S(1)} %get-tuple-element.55), channel_id=1, source_target_pairs={{0,4},{4,0},{1,5},{5,1},{2,6},{6,2},{3,7},{7,3},{8,12},{12,8},{9,1... | collective-permute-start | bytes 393224 | tf_op jit(solution)/shard_map/ppermute | solution.py:471
  20.2 0.4 second_probs.1.refs_6_
  20.5 0.0 collective-permute-done.8.refs_5_
  20.5 0.0 collective-permute-done.7.refs_4_
  20.6 0.0 copy-done.3
  20.6 0.8 %second_keys.1 = (bf16[4,256,128]{2,1,0:T(8,128)(2,1)S(1)}, f32[32,128]{1,0:T(8,128)S(1)}, f32[256,128]{1,0:T(8,128)S(1)}, bf16[288,128]{1,0:T(8,128)(2,1)S(1)},...) custom-call(bf16[1,2,32,4096]{3,2,1,0:T(8,128)(2,1)S(1)} %copy-done.1, ...), custom_call_target="tpu_custom_call" | custom-call | tf_op jit(solution)/shard_map/second_keys/pallas_call | solution.py:455
  21.3 0.5 %collective-permute-start.9 = (bf16[288,128]{1,0:T(8,128)(2,1)S(1)}, bf16[288,128]{1,0:T(8,128)(2,1)S(1)}, u32[]{:S(2)}, u32[]{:S(2)}) collective-permute-start(bf16[288,128]{1,0:T(8,128)(2,1)S(1)} %get-tuple-element.51), channel_id=1, source_target_pairs={{0,1},{1,0},{2,3},{3,2},{4,5},{5,4},{6,7},{7,6},{8,9},{9,8},{10,11... | collective-permute-start | bytes 221192 | tf_op jit(solution)/shard_map/ppermute | solution.py:469
  21.8 1.0 %collective-permute-start.10 = (bf16[288,128]{1,0:T(8,128)(2,1)S(1)}, bf16[288,128]{1,0:T(8,128)(2,1)S(1)}, u32[]{:S(2)}, u32[]{:S(2)}) collective-permute-start(bf16[288,128]{1,0:T(8,128)(2,1)S(1)} %get-tuple-element.52), channel_id=1, source_target_pairs={{0,4},{4,0},{1,5},{5,1},{2,6},{6,2},{3,7},{7,3},{8,12},{12,8},{9,1... | collective-permute-start | bytes 221192 | tf_op jit(solution)/shard_map/ppermute | solution.py:471
  22.8 2.1 %collective-permute-start.11 = (bf16[288,128]{1,0:T(8,128)(2,1)S(1)}, bf16[288,128]{1,0:T(8,128)(2,1)S(1)}, u32[]{:S(2)}, u32[]{:S(2)}) collective-permute-start(bf16[288,128]{1,0:T(8,128)(2,1)S(1)} %get-tuple-element.53), channel_id=1, source_target_pairs={{0,5},{1,4},{2,7},{3,6},{4,1},{5,0},{6,3},{7,2},{8,13},{9,12},{10,... | collective-permute-start | bytes 221192 | tf_op jit(solution)/shard_map/ppermute | solution.py:477
  24.9 0.0 collective-permute-done.12.refs_1_
  24.9 0.6 %collective-permute-start.13 = (bf16[256,128]{1,0:T(8,128)(2,1)S(1)}, bf16[256,128]{1,0:T(8,128)(2,1)S(1)}, u32[]{:S(2)}, u32[]{:S(2)}) collective-permute-start(bf16[256,128]{1,0:T(8,128)(2,1)S(1)} %get-tuple-element.57), channel_id=1, source_target_pairs={{0,1},{1,0},{2,3},{3,2},{4,5},{5,4},{6,7},{7,6},{8,9},{9,8},{10,11... | collective-permute-start | bytes 196616 | tf_op jit(solution)/shard_map/ppermute | solution.py:469
  25.5 4.0 %collective-permute-done.13.refs_6_ = bf16[256,128]{1,0:T(8,128)(2,1)S(1)} collective-permute-done((bf16[256,128]{1,0:T(8,128)(2,1)S(1)}, bf16[256,128]{1,0:T(8,128)(2,1)S(1)}, u32[]{:S(2)}, u32[]{:S(2)}) %collective-permute-start.13) | collective-permute-done | bytes 65568 | tf_op jit(solution)/shard_map/ppermute | solution.py:469
  29.5 0.0 collective-permute-done.9.refs_2_
  29.5 0.0 collective-permute-done.10.refs_3_
  29.5 0.0 collective-permute-done.11.refs_4_
  29.5 0.1 near_sum.1
  29.6 2.9 %collective-permute-start.14 = (bf16[288,128]{1,0:T(8,128)(2,1)S(1)}, bf16[288,128]{1,0:T(8,128)(2,1)S(1)}, u32[]{:S(2)}, u32[]{:S(2)}) collective-permute-start(bf16[288,128]{1,0:T(8,128)(2,1)S(1)} %get-tuple-element.60), channel_id=1, source_target_pairs={{0,2},{1,3},{2,0},{3,1},{4,6},{5,7},{6,4},{7,5},{8,10},{9,11},{10,... | collective-permute-start | bytes 221192 | tf_op jit(solution)/shard_map/ppermute | solution.py:480
  32.5 1.3 %second_rows.1 = bf16[1,2,32,4096]{3,2,1,0:T(8,128)(2,1)} custom-call(bf16[1,2,32,4096]{3,2,1,0:T(8,128)(2,1)S(1)} %copy-done.1, f32[1,4096]{1,0:T(1,128)S(1)} %copy-done.4, f32[2,32,128]{2,1,0:T(8,128)S(1)} %get-tuple-element.34.refs_3_.refs_2_, bf16[1,32,4096]{2,1,0:T(8,128)(2,1)S(1)} %copy-done.3, bf16[32,4096]{1,0:T(8,128)(2,1)S(1)} %collective-permute-done.7.refs_4_, ...), custom_call_target="tpu_custom_call" | custom-call | tf_op jit(solution)/shard_map/second_rows/pallas_call | solution.py:455
  33.7 2.8 %collective-permute-done.14.receive_ref = bf16[288,128]{1,0:T(8,128)(2,1)S(1)} collective-permute-done((bf16[288,128]{1,0:T(8,128)(2,1)S(1)}, bf16[288,128]{1,0:T(8,128)(2,1)S(1)}, u32[]{:S(2)}, u32[]{:S(2)}) %collective-permute-start.14) | collective-permute-done | bytes 73760 | tf_op jit(solution)/shard_map/ppermute | solution.py:480
  36.6 0.7 %finish.1 = (f32[1,2,128,128]{3,2,1,0:T(8,128)}, f32[1,2,128,128]{3,2,1,0:T(8,128)}, f32[32,128]{1,0:T(8,128)}) custom-call(f32[256,128]{1,0:T(8,128)S(1)} %get-tuple-element.58.keep_ref, f32[32,128]{1,0:T(8,128)S(1)} %get-tuple-element.59.gain_ref, bf16[288,128]{1,0:T(8,128)(2,1)S(1)} %collective-permute-done.14.receive_ref), custom_call_target="tpu_custom_call" | custom-call | tf_op jit(solution)/shard_map/finish/pallas_call | solution.py:455
  (2 shorter events, 0.1 us)
Async XLA Ops:
  0.6 14.5 %copy-start.2 = (bf16[1,32,4096]{2,1,0:T(8,128)(2,1)S(1)}, bf16[1,32,4096]{2,1,0:T(8,128)(2,1)}, u32[]{:S(2)}) copy-start(bf16[1,32,4096]{2,1,0:T(8,128)(2,1)} %refs_3_.3) | copy-start | bytes 786436
  1.6 11.6 %copy-start.4 = (f32[1,4096]{1,0:T(1,128)S(1)}, f32[1,4096]{1,0:T(1,128)}, u32[]{:S(2)}) copy-start(f32[1,4096]{1,0:T(1,128)} %refs_1_.5) | copy-start | bytes 49156
  1.6 11.6 %copy-start.5 = (s32[5,8]{1,0:T(8,128)S(1)}, s32[5,8]{1,0:T(8,128)}, u32[]{:S(2)}) copy-start(s32[5,8]{1,0:T(8,128)} %doc_ref.1) | copy-start | bytes 484
  1.6 7.6 %collective-permute-start = (bf16[2,2,64,128]{3,2,1,0:T(8,128)(2,1)S(1)}, bf16[2,2,64,128]{3,2,1,0:T(8,128)(2,1)S(1)}, u32[]{:S(2)}, u32[]{:S(2)}) collective-permute-start(bf16[2,2,64,128]{3,2,1,0:T(8,128)(2,1)S(1)} %get-tuple-element.37), channel_id=1, source_target_pairs={{0,2},{1,3},{2,0},{3,1},{4,6},{5,7},{6,4},{7,5},{8,10},{9,11},{10,... | collective-permute-start | bytes 196616 | tf_op jit(solution)/shard_map/ppermute | solution.py:480
  5.7 6.5 %collective-permute-start.6 = (bf16[2,2,64,128]{3,2,1,0:T(8,128)(2,1)S(1)}, bf16[2,2,64,128]{3,2,1,0:T(8,128)(2,1)S(1)}, u32[]{:S(2)}, u32[]{:S(2)}) collective-permute-start(bf16[2,2,64,128]{3,2,1,0:T(8,128)(2,1)S(1)} %get-tuple-element.38.refs_6_.refs_2_.refs_8_), channel_id=1, source_target_pairs={{0,5},{1,4},{2,7},{3,6},{4,1},{5,0},{6,3},{7,2},{8,13},{9,12},{10,... | collective-permute-start | bytes 196616 | tf_op jit(solution)/shard_map/ppermute | solution.py:477
  8.3 6.9 %collective-permute-start.5 = (bf16[2,2,64,128]{3,2,1,0:T(8,128)(2,1)S(1)}, bf16[2,2,64,128]{3,2,1,0:T(8,128)(2,1)S(1)}, u32[]{:S(2)}, u32[]{:S(2)}) collective-permute-start(bf16[2,2,64,128]{3,2,1,0:T(8,128)(2,1)S(1)} %get-tuple-element.38.refs_6_.refs_2_.refs_8_), channel_id=1, source_target_pairs={{0,4},{4,0},{1,5},{5,1},{2,6},{6,2},{3,7},{7,3},{8,12},{12,8},{9,1... | collective-permute-start | bytes 196616 | tf_op jit(solution)/shard_map/ppermute | solution.py:471
  8.8 6.4 %collective-permute-start.4 = (bf16[2,2,64,128]{3,2,1,0:T(8,128)(2,1)S(1)}, bf16[2,2,64,128]{3,2,1,0:T(8,128)(2,1)S(1)}, u32[]{:S(2)}, u32[]{:S(2)}) collective-permute-start(bf16[2,2,64,128]{3,2,1,0:T(8,128)(2,1)S(1)} %get-tuple-element.38.refs_6_.refs_2_.refs_8_), channel_id=1, source_target_pairs={{0,1},{1,0},{2,3},{3,2},{4,5},{5,4},{6,7},{7,6},{8,9},{9,8},{10,11... | collective-permute-start | bytes 196616 | tf_op jit(solution)/shard_map/ppermute | solution.py:469
  9.2 6.6 %collective-permute-start.3 = (bf16[2,2,64,128]{3,2,1,0:T(8,128)(2,1)S(1)}, bf16[2,2,64,128]{3,2,1,0:T(8,128)(2,1)S(1)}, u32[]{:S(2)}, u32[]{:S(2)}) collective-permute-start(bf16[2,2,64,128]{3,2,1,0:T(8,128)(2,1)S(1)} %collective-permute-done.refs_6_.refs_12_), channel_id=1, source_target_pairs={{0,5},{1,4},{2,7},{3,6},{4,1},{5,0},{6,3},{7,2},{8,13},{9,12},{10,... | collective-permute-start | bytes 196616 | tf_op jit(solution)/shard_map/ppermute | solution.py:477
  11.8 4.3 %collective-permute-start.2 = (bf16[2,2,64,128]{3,2,1,0:T(8,128)(2,1)S(1)}, bf16[2,2,64,128]{3,2,1,0:T(8,128)(2,1)S(1)}, u32[]{:S(2)}, u32[]{:S(2)}) collective-permute-start(bf16[2,2,64,128]{3,2,1,0:T(8,128)(2,1)S(1)} %collective-permute-done.refs_6_.refs_12_), channel_id=1, source_target_pairs={{0,4},{4,0},{1,5},{5,1},{2,6},{6,2},{3,7},{7,3},{8,12},{12,8},{9,1... | collective-permute-start | bytes 196616 | tf_op jit(solution)/shard_map/ppermute | solution.py:471
  12.3 4.3 %collective-permute-start.1 = (bf16[2,2,64,128]{3,2,1,0:T(8,128)(2,1)S(1)}, bf16[2,2,64,128]{3,2,1,0:T(8,128)(2,1)S(1)}, u32[]{:S(2)}, u32[]{:S(2)}) collective-permute-start(bf16[2,2,64,128]{3,2,1,0:T(8,128)(2,1)S(1)} %collective-permute-done.refs_6_.refs_12_), channel_id=1, source_target_pairs={{0,1},{1,0},{2,3},{3,2},{4,5},{5,4},{6,7},{7,6},{8,9},{9,8},{10,11... | collective-permute-start | bytes 196616 | tf_op jit(solution)/shard_map/ppermute | solution.py:469
  13.2 1.0 %copy-start = (bf16[1,2,32,4096]{3,2,1,0:T(8,128)(2,1)S(1)}, bf16[1,2,32,4096]{3,2,1,0:T(8,128)(2,1)}, u32[]{:S(2)}) copy-start(bf16[1,2,32,4096]{3,2,1,0:T(8,128)(2,1)} %refs_0_.9) | copy-start | bytes 1572868
  14.2 1.0 %copy-start.1 = (bf16[1,2,32,4096]{3,2,1,0:T(8,128)(2,1)S(1)}, bf16[1,2,32,4096]{3,2,1,0:T(8,128)(2,1)}, u32[]{:S(2)}) copy-start(bf16[1,2,32,4096]{3,2,1,0:T(8,128)(2,1)} %refs_0_.9) | copy-start | bytes 1572868
  17.4 3.2 %collective-permute-start.8 = (bf16[32,4096]{1,0:T(8,128)(2,1)S(1)}, bf16[32,4096]{1,0:T(8,128)(2,1)S(1)}, u32[]{:S(2)}, u32[]{:S(2)}) collective-permute-start(bf16[32,4096]{1,0:T(8,128)(2,1)S(1)} %get-tuple-element.41.refs_7_), channel_id=1, source_target_pairs={{16,8},{17,9},{18,10},{19,11},{20,12},{21,13},{22,14},{23,15}} | collective-permute-start | bytes 786440 | tf_op jit(solution)/shard_map/ppermute | solution.py:525
  18.0 2.5 %collective-permute-start.7 = (bf16[32,4096]{1,0:T(8,128)(2,1)S(1)}, bf16[32,4096]{1,0:T(8,128)(2,1)S(1)}, u32[]{:S(2)}, u32[]{:S(2)}) collective-permute-start(bf16[32,4096]{1,0:T(8,128)(2,1)S(1)} %get-tuple-element.41.refs_7_), channel_id=1, source_target_pairs={{0,8},{8,0},{16,24},{24,16},{1,9},{9,1},{17,25},{25,17},{2,10},{10... | collective-permute-start | bytes 786440 | tf_op jit(solution)/shard_map/ppermute | solution.py:528
  18.6 2.0 %copy-start.3 = (bf16[1,32,4096]{2,1,0:T(8,128)(2,1)S(1)}, bf16[1,32,4096]{2,1,0:T(8,128)(2,1)}, u32[]{:S(2)}) copy-start(bf16[1,32,4096]{2,1,0:T(8,128)(2,1)} %refs_3_.5) | copy-start | bytes 786436
  18.6 6.3 %collective-permute-start.12 = (bf16[2,256,128]{2,1,0:T(8,128)(2,1)S(1)}, bf16[2,256,128]{2,1,0:T(8,128)(2,1)S(1)}, u32[]{:S(2)}, u32[]{:S(2)}) collective-permute-start(bf16[2,256,128]{2,1,0:T(8,128)(2,1)S(1)} %get-tuple-element.55), channel_id=1, source_target_pairs={{0,4},{4,0},{1,5},{5,1},{2,6},{6,2},{3,7},{7,3},{8,12},{12,8},{9,1... | collective-permute-start | bytes 393224 | tf_op jit(solution)/shard_map/ppermute | solution.py:471
  21.3 8.2 %collective-permute-start.9 = (bf16[288,128]{1,0:T(8,128)(2,1)S(1)}, bf16[288,128]{1,0:T(8,128)(2,1)S(1)}, u32[]{:S(2)}, u32[]{:S(2)}) collective-permute-start(bf16[288,128]{1,0:T(8,128)(2,1)S(1)} %get-tuple-element.51), channel_id=1, source_target_pairs={{0,1},{1,0},{2,3},{3,2},{4,5},{5,4},{6,7},{7,6},{8,9},{9,8},{10,11... | collective-permute-start | bytes 221192 | tf_op jit(solution)/shard_map/ppermute | solution.py:469
  21.8 7.7 %collective-permute-start.10 = (bf16[288,128]{1,0:T(8,128)(2,1)S(1)}, bf16[288,128]{1,0:T(8,128)(2,1)S(1)}, u32[]{:S(2)}, u32[]{:S(2)}) collective-permute-start(bf16[288,128]{1,0:T(8,128)(2,1)S(1)} %get-tuple-element.52), channel_id=1, source_target_pairs={{0,4},{4,0},{1,5},{5,1},{2,6},{6,2},{3,7},{7,3},{8,12},{12,8},{9,1... | collective-permute-start | bytes 221192 | tf_op jit(solution)/shard_map/ppermute | solution.py:471
  22.8 6.7 %collective-permute-start.11 = (bf16[288,128]{1,0:T(8,128)(2,1)S(1)}, bf16[288,128]{1,0:T(8,128)(2,1)S(1)}, u32[]{:S(2)}, u32[]{:S(2)}) collective-permute-start(bf16[288,128]{1,0:T(8,128)(2,1)S(1)} %get-tuple-element.53), channel_id=1, source_target_pairs={{0,5},{1,4},{2,7},{3,6},{4,1},{5,0},{6,3},{7,2},{8,13},{9,12},{10,... | collective-permute-start | bytes 221192 | tf_op jit(solution)/shard_map/ppermute | solution.py:477
  24.9 4.6 %collective-permute-start.13 = (bf16[256,128]{1,0:T(8,128)(2,1)S(1)}, bf16[256,128]{1,0:T(8,128)(2,1)S(1)}, u32[]{:S(2)}, u32[]{:S(2)}) collective-permute-start(bf16[256,128]{1,0:T(8,128)(2,1)S(1)} %get-tuple-element.57), channel_id=1, source_target_pairs={{0,1},{1,0},{2,3},{3,2},{4,5},{5,4},{6,7},{7,6},{8,9},{9,8},{10,11... | collective-permute-start | bytes 196616 | tf_op jit(solution)/shard_map/ppermute | solution.py:469
  29.6 7.0 %collective-permute-start.14 = (bf16[288,128]{1,0:T(8,128)(2,1)S(1)}, bf16[288,128]{1,0:T(8,128)(2,1)S(1)}, u32[]{:S(2)}, u32[]{:S(2)}) collective-permute-start(bf16[288,128]{1,0:T(8,128)(2,1)S(1)} %get-tuple-element.60), channel_id=1, source_target_pairs={{0,2},{1,3},{2,0},{3,1},{4,6},{5,7},{6,4},{7,5},{8,10},{9,11},{10,... | collective-permute-start | bytes 221192 | tf_op jit(solution)/shard_map/ppermute | solution.py:480

commit v10 on v9

--- a/solution.py
+++ b/solution.py
@@ -82,16 +82,22 @@
     return lambda where: waiting_ref[0, :, where]
 
 
-def arriving_from(output_ref, chip_ref, link_ref):
+def choose_arriving(output_ref, chip_ref, link_ref, target_ref):
     place = lax.axis_index("pipe")
     last = place == lax.axis_size("pipe") - 1
     even = place % 2 == 0
 
-    def arriving(where):
-        arrived = jnp.where(even, chip_ref[:, where], link_ref[:, where])
-        return jnp.where(last, output_ref[0, :, where], arrived)
-
-    return arriving
+    @pl.when(last)
+    def _():
+        target_ref[...] = output_ref[0]
+
+    @pl.when(jnp.logical_not(last) & even)
+    def _():
+        target_ref[...] = chip_ref[...]
+
+    @pl.when(jnp.logical_not(last) & jnp.logical_not(even))
+    def _():
+        target_ref[...] = link_ref[...]
 
 
 def visible_keys(sizes, tick, doc_ref):
@@ -194,58 +200,55 @@
     return lambda where: x_ref[0, tick, :, where].astype(F32) * inverse
 
 
-def first_half(sizes, far, keys, mask, query_ref, arriving, dscore_ref, probs_ref):
-    near_count = sizes[3] // 2
-    nears = range(near_count)
-    columns_of = [Group(sizes, far * near_count + near) for near in nears]
-    scores, prob_grads = [], []
-    for near in nears:
-        query = columns_of[near].stacked(lambda where: query_ref[0, :, where])
-        scores.append(dot(keys(near, 0), query, NT))
-        prob_grads.append(dot(keys(near, 1), columns_of[near].stacked(arriving), NT))
+def first_half(keys, mask, products, dscore_ref, probs_ref):
     dscores = []
-    for near in nears:
-        probs = probabilities(mask, scores[near])
-        dscores.append(score_grads(probs, prob_grads[near]))
+    for near, (scores, prob_grads) in enumerate(products):
+        probs = probabilities(mask, scores)
+        dscores.append(score_grads(probs, prob_grads))
         dscore_ref[near] = dscores[near]
         probs_ref[near] = probs.astype(BF16)
-    return [(SCALE * dot(dscores[near], keys(near, 0), TN)).astype(BF16) for near in nears]
+    return [
+        (SCALE * dot(dscore, keys(near, 0), TN)).astype(BF16)
+        for near, dscore in enumerate(dscores)
+    ]
 
 
 def first_near_rows_kernel(sizes, *refs):
-    members = sizes[2] * sizes[3] // 2
+    near_count = sizes[3] // 2
+    members = sizes[2] * near_count
     x_ref, gain_ref, query_ref, inverse_ref, mask_ref, waiting_ref = refs[:6]
     keys = Keys(sizes, 0, refs[6 : 6 + members])
-    query_grad_ref, dscore_ref, probs_ref, coupled_ref = refs[6 + members :]
-    query_grads = first_half(
-        sizes,
-        0,
-        keys,
-        mask_ref[0],
-        query_ref,
-        waiting_from(waiting_ref),
-        dscore_ref,
-        probs_ref,
-    )
+    query_grad_ref, dscore_ref, probs_ref, coupled_ref, turned_ref = refs[6 + members :]
+    loads = (lambda where: query_ref[0, :, where], waiting_from(waiting_ref))
+    products = []
+    for near in range(near_count):
+        operands = [Group(sizes, near).stacked(load) for load in loads]
+        products.append([dot(keys(near, kind), operands[kind], NT) for kind in range(2)])
+    query_grads = first_half(keys, mask_ref[0], products, dscore_ref, probs_ref)
     normed_of = normed_from(x_ref, 0, inverse_ref[0])
     coupled = jnp.zeros((sizes[0], HD), F32)
     for near, query_grad in enumerate(query_grads):
         query_grad_ref[near] = query_grad
         coupled = coupled_terms(Group(sizes, near), query_grad, normed_of, gain_ref, coupled)
     coupled_ref[...] = coupled
+    for near in range(near_count):
+        columns_of = Group(sizes, near_count + near)
+        for kind, load in enumerate(loads):
+            turned_ref[near, kind] = columns_of.stacked(load).T
 
 
 def first_far_rows_kernel(sizes, *refs):
     near_count = sizes[3] // 2
     members = sizes[2] * near_count
-    x_ref, gain_ref, query_ref, inverse_ref, mask_ref, waiting_ref = refs[:6]
-    keys = Keys(sizes, 0, refs[6 : 6 + members])
-    near_grad_ref, coupled_ref = refs[6 + members : 8 + members]
-    input_grad_ref, query_grad_ref, dscore_ref, probs_ref = refs[8 + members :]
-    arriving = waiting_from(waiting_ref)
-    query_grads = first_half(
-        sizes, 1, keys, mask_ref[0], query_ref, arriving, dscore_ref, probs_ref
-    )
+    x_ref, gain_ref, inverse_ref, mask_ref, waiting_ref = refs[:5]
+    keys, refs = Keys(sizes, 0, refs[5 : 5 + members]), refs[5 + members :]
+    near_grad_ref, coupled_ref, turned_ref = refs[:3]
+    input_grad_ref, query_grad_ref, dscore_ref, probs_ref = refs[3:]
+    products = [
+        [dot(keys(near, kind), turned_ref[near, kind], NN) for kind in range(2)]
+        for near in range(near_count)
+    ]
+    query_grads = first_half(keys, mask_ref[0], products, dscore_ref, probs_ref)
     normed_of = normed_from(x_ref, 0, inverse_ref[0])
     coupled = coupled_ref[...]
     for near, query_grad in enumerate(query_grads):
@@ -261,7 +264,14 @@
         input_grad_ref[:, where] = result
 
     write_input_grads(
-        sizes, coupled, query_grad_of, normed_of, gain_ref, inverse_ref[0], arriving, write
+        sizes,
+        coupled,
+        query_grad_of,
+        normed_of,
+        gain_ref,
+        inverse_ref[0],
+        waiting_from(waiting_ref),
+        write,
     )
 
 
@@ -318,9 +328,13 @@
     x_ref, query_ref, inverse_ref, output_ref, chip_ref, link_ref = refs[:6]
     probs_ref, before_ref, *refs = refs[6:]
     keys, refs = both_sets(sizes, refs[:kv_count]), refs[kv_count:]
-    query_grad_ref, gain_rows_ref, own_ref = refs[:3]
-    message_refs, gain_scratch = refs[3:-1], refs[-1]
-    arriving = arriving_from(output_ref, chip_ref, link_ref)
+    query_grad_ref, gain_rows_ref, own_ref, arriving_ref = refs[:4]
+    message_refs, gain_scratch = refs[4:-1], refs[-1]
+    choose_arriving(output_ref, chip_ref, link_ref, arriving_ref)
+
+    def arriving(where):
+        return arriving_ref[:, where]
+
     normed_of = normed_from(x_ref, 1, inverse_ref[1])
     columns_of = [Group(sizes, turn) for turn in turns]
     grads = [columns_of[turn].stacked(arriving) for turn in turns]
@@ -358,8 +372,7 @@
 
 
 def second_rows_kernel(sizes, *refs):
-    x_ref, gain_ref, inverse_ref, output_ref, chip_ref, link_ref = refs[:6]
-    query_grad_ref, first_ref, input_grads_ref = refs[6:]
+    x_ref, gain_ref, inverse_ref, arriving_ref, query_grad_ref, first_ref, input_grads_ref = refs
     input_grads_ref[0, 0] = first_ref[...]
     inverse = inverse_ref[1]
     normed_of = normed_from(x_ref, 1, inverse)
@@ -379,7 +392,7 @@
         normed_of,
         gain_ref,
         inverse,
-        arriving_from(output_ref, chip_ref, link_ref),
+        lambda where: arriving_ref[:, where],
         write,
     )
 
@@ -509,17 +522,32 @@
     low_rows = shape((rows, columns), BF16)
     low_scores = shape((near_count, key_count, stacked), BF16)
     low_grads = shape((near_count, stacked, HD), BF16)
-    rows_operands = (segment_inputs, norm_gain, queries, inverse, masks, waiting_grads)
-    query_grad_near, dscore_near, probs_near, coupled = call(
+    query_grad_near, dscore_near, probs_near, coupled, turned = call(
         functools.partial(first_near_rows_kernel, sizes),
         "first_near_rows",
-        (*rows_operands, *own_set),
-        [low_grads, low_scores, low_scores, shape((rows, HD), F32)],
+        (segment_inputs, norm_gain, queries, inverse, masks, waiting_grads, *own_set),
+        [
+            low_grads,
+            low_scores,
+            low_scores,
+            shape((rows, HD), F32),
+            shape((near_count, 2, HD, stacked), BF16),
+        ],
     )
     input_grad_first, query_grad_far, dscore_far, probs_far = call(
         functools.partial(first_far_rows_kernel, sizes),
         "first_far_rows",
-        (*rows_operands, *far_set, query_grad_near, coupled),
+        (
+            segment_inputs,
+            norm_gain,
+            inverse,
+            masks,
+            waiting_grads,
+            *far_set,
+            query_grad_near,
+            coupled,
+            turned,
+        ),
         [low_rows, low_grads, low_scores, low_scores],
     )
     over_link = lax.ppermute(
@@ -557,7 +585,7 @@
         [shape((tp_count, key_count, stacked), F32)],
     )
     message = shape((pair_rows + gain_count, HD), BF16)
-    query_grad_second, gain_rows, own_second, *sends = call(
+    query_grad_second, gain_rows, own_second, arriving, *sends = call(
         functools.partial(second_keys_kernel, sizes),
         "second_keys",
         (
@@ -571,7 +599,8 @@
             gain_first,
             *kv,
         ),
-        [shape((tp_count, stacked, HD), BF16), gain_shape, own_shape] + [message] * len(places),
+        [shape((tp_count, stacked, HD), BF16), gain_shape, own_shape, low_rows]
+        + [message] * len(places),
         scratch=[pltpu.VMEM((gain_count, HD), F32)],
     )
     received = [to_near(value, -step, near) for value, (step, near) in zip(sends, places)]
@@ -589,9 +618,7 @@
             segment_inputs,
             norm_gain,
             inverse,
-            output_grads,
-            on_chip,
-            over_link,
+            arriving,
             query_grad_second,
             input_grad_first,
         ),

time: 37.6 us -> 37.4 us (level)
  transfers between devices with their start and end apart: 15 -> 15, of which waited for: 4 -> 4; matrix products, arithmetic and copies ran while one was open for 0% -> 0% of each run, Pallas kernels for 12% -> 11%
where the time goes in v10:
time: 37.4 us; the launch traced here: 37.1 us
  starting transfers between devices  21 us (56%)
  waiting for transfers between devices  7.54 us (20%)
  Pallas kernels  5.67 us (15%)
  local copies, waits for them, and re-layouts  1.15 us (3%)
  other arithmetic  0.93 us (2%)
  between operations  0.81 us (2%)
    ppermute x3, starting transfers between devices, to_near(): return lax.ppermute(value, ('ctx', 'tp'), pairs)  7.13 us
    ppermute x2, starting transfers between devices, to_far(): lax.ppermute(value, 'tp', [(i, i ^ near_count) for i in range(tp_count)])  6.95 us
    pallas_call x11, Pallas kernels, call(): pl.pallas_call(kernel, out_shape=out_shape, in_specs=in_specs, out_specs=...  5.67 us
    ppermute x4, waiting for transfers between devices, to_near(): return lax.ppermute(value, 'tp', [(i, i ^ near) for i in range(tp_count)])  4.29 us
    ppermute x4, starting transfers between devices, to_near(): lax.ppermute(value, 'ctx', [(i, (i + step) % cycle) for i in range(cycle)])  3.57 us
    ppermute x2, waiting for transfers between devices, to_far(): lax.ppermute(value, 'tp', [(i, i ^ near_count) for i in range(tp_count)])  2.96 us
    ppermute x4, starting transfers between devices, to_near(): return lax.ppermute(value, 'tp', [(i, i ^ near) for i in range(tp_count)])  2.61 us
    unnamed x12, local copies, waits for them, and re-layouts  1.15 us
  transfers between devices with their start and end apart: 15, of which 4 were waited for; matrix products, arithmetic and copies ran while one was open for 0% of the time, Pallas kernels for 11%

profile of v10, /device:TPU:0, one launch (start us, length us, event | category | flops | bytes accessed | tf_op | source)
XLA Modules:
  0.0 37.1 jit_solution(17225759666875199532)
XLA Ops:
  0.6 0.0 copy-start.2
  0.6 0.9 %pad_maximum_fusion.both_ref = bf16[2,2,128,128]{3,2,1,0:T(8,128)(2,1)S(1)} fusion(bf16[1,2,128,128]{3,2,1,0:T(8,128)(2,1)} %param.9, bf16[1,2,128,128]{3,2,1,0:T(8,128)(2,1)} %param.8), kind=kLoop, calls=%fused_computation | loop fusion | flops 65536 | bytes 262144 | tf_op jit(solution)/shard_map/stack | solution.py:499
  1.6 0.0 copy-start.3
  1.6 0.0 copy-start.5
  1.6 4.1 %collective-permute-start = (bf16[2,2,64,128]{3,2,1,0:T(8,128)(2,1)S(1)}, bf16[2,2,64,128]{3,2,1,0:T(8,128)(2,1)S(1)}, u32[]{:S(2)}, u32[]{:S(2)}) collective-permute-start(bf16[2,2,64,128]{3,2,1,0:T(8,128)(2,1)S(1)} %get-tuple-element.39), channel_id=1, source_target_pairs={{0,2},{1,3},{2,0},{3,1},{4,6},{5,7},{6,4},{7,5},{8,10},{9,11},{10,... | collective-permute-start | bytes 196616 | tf_op jit(solution)/shard_map/ppermute | solution.py:493
  5.7 2.5 %collective-permute-start.6 = (bf16[2,2,64,128]{3,2,1,0:T(8,128)(2,1)S(1)}, bf16[2,2,64,128]{3,2,1,0:T(8,128)(2,1)S(1)}, u32[]{:S(2)}, u32[]{:S(2)}) collective-permute-start(bf16[2,2,64,128]{3,2,1,0:T(8,128)(2,1)S(1)} %get-tuple-element.40.refs_6_.refs_2_.refs_8_), channel_id=1, source_target_pairs={{0,5},{1,4},{2,7},{3,6},{4,1},{5,0},{6,3},{7,2},{8,13},{9,12},{10,... | collective-permute-start | bytes 196616 | tf_op jit(solution)/shard_map/ppermute | solution.py:490
  8.3 0.5 %collective-permute-start.5 = (bf16[2,2,64,128]{3,2,1,0:T(8,128)(2,1)S(1)}, bf16[2,2,64,128]{3,2,1,0:T(8,128)(2,1)S(1)}, u32[]{:S(2)}, u32[]{:S(2)}) collective-permute-start(bf16[2,2,64,128]{3,2,1,0:T(8,128)(2,1)S(1)} %get-tuple-element.40.refs_6_.refs_2_.refs_8_), channel_id=1, source_target_pairs={{0,4},{4,0},{1,5},{5,1},{2,6},{6,2},{3,7},{7,3},{8,12},{12,8},{9,1... | collective-permute-start | bytes 196616 | tf_op jit(solution)/shard_map/ppermute | solution.py:484
  8.8 0.4 %collective-permute-start.4 = (bf16[2,2,64,128]{3,2,1,0:T(8,128)(2,1)S(1)}, bf16[2,2,64,128]{3,2,1,0:T(8,128)(2,1)S(1)}, u32[]{:S(2)}, u32[]{:S(2)}) collective-permute-start(bf16[2,2,64,128]{3,2,1,0:T(8,128)(2,1)S(1)} %get-tuple-element.40.refs_6_.refs_2_.refs_8_), channel_id=1, source_target_pairs={{0,1},{1,0},{2,3},{3,2},{4,5},{5,4},{6,7},{7,6},{8,9},{9,8},{10,11... | collective-permute-start | bytes 196616 | tf_op jit(solution)/shard_map/ppermute | solution.py:482
  9.2 0.0 collective-permute-done.refs_5_.refs_6_.refs_12_
  9.2 2.5 %collective-permute-start.3 = (bf16[2,2,64,128]{3,2,1,0:T(8,128)(2,1)S(1)}, bf16[2,2,64,128]{3,2,1,0:T(8,128)(2,1)S(1)}, u32[]{:S(2)}, u32[]{:S(2)}) collective-permute-start(bf16[2,2,64,128]{3,2,1,0:T(8,128)(2,1)S(1)} %collective-permute-done.refs_5_.refs_6_.refs_12_), channel_id=1, source_target_pairs={{0,5},{1,4},{2,7},{3,6},{4,1},{5,0},{6,3},{7,2},{8,13},{9,12},{10,... | collective-permute-start | bytes 196616 | tf_op jit(solution)/shard_map/ppermute | solution.py:490
  11.8 0.5 %collective-permute-start.2 = (bf16[2,2,64,128]{3,2,1,0:T(8,128)(2,1)S(1)}, bf16[2,2,64,128]{3,2,1,0:T(8,128)(2,1)S(1)}, u32[]{:S(2)}, u32[]{:S(2)}) collective-permute-start(bf16[2,2,64,128]{3,2,1,0:T(8,128)(2,1)S(1)} %collective-permute-done.refs_5_.refs_6_.refs_12_), channel_id=1, source_target_pairs={{0,4},{4,0},{1,5},{5,1},{2,6},{6,2},{3,7},{7,3},{8,12},{12,8},{9,1... | collective-permute-start | bytes 196616 | tf_op jit(solution)/shard_map/ppermute | solution.py:484
  12.3 0.0 collective-permute-done.6.refs_9_.refs_5_.refs_11_
  12.3 0.9 %collective-permute-start.1 = (bf16[2,2,64,128]{3,2,1,0:T(8,128)(2,1)S(1)}, bf16[2,2,64,128]{3,2,1,0:T(8,128)(2,1)S(1)}, u32[]{:S(2)}, u32[]{:S(2)}) collective-permute-start(bf16[2,2,64,128]{3,2,1,0:T(8,128)(2,1)S(1)} %collective-permute-done.refs_5_.refs_6_.refs_12_), channel_id=1, source_target_pairs={{0,1},{1,0},{2,3},{3,2},{4,5},{5,4},{6,7},{7,6},{8,9},{9,8},{10,11... | collective-permute-start | bytes 196616 | tf_op jit(solution)/shard_map/ppermute | solution.py:482
  13.2 0.0 copy-done.3
  13.2 0.0 copy-done.5
  13.2 0.0 copy-start
  13.2 1.0 %copy-done = bf16[1,2,32,4096]{3,2,1,0:T(8,128)(2,1)S(1)} copy-done((bf16[1,2,32,4096]{3,2,1,0:T(8,128)(2,1)S(1)}, bf16[1,2,32,4096]{3,2,1,0:T(8,128)(2,1)}, u32[]{:S(2)}) %copy-start) | copy-done | bytes 524312
  14.2 0.0 copy-start.1
  14.2 0.9 %norm.1 = (bf16[2,32,4096]{2,1,0:T(8,128)(2,1)S(1)}, f32[2,32,128]{2,1,0:T(8,128)S(1)}, f32[2,128,256]{2,1,0:T(8,128)S(1)}) custom-call(s32[5,8]{1,0:T(8,128)S(1)} %copy-done.5, bf16[1,2,32,4096]{3,2,1,0:T(8,128)(2,1)S(1)} %copy-done, f32[1,4096]{1,0:T(1,128)S(1)} %copy-done.3), custom_call_target="tpu_custom_call" | custom-call | tf_op jit(solution)/shard_map/norm/pallas_call | solution.py:468
  15.2 0.0 collective-permute-done.5.refs_8_.refs_4_.refs_10_
  15.2 0.0 collective-permute-done.4.refs_7_.refs_3_.refs_9_
  15.2 0.0 copy-done.2
  15.2 0.1 copy-done.1
  15.3 0.5 %first_near_rows.1 = (bf16[2,256,128]{2,1,0:T(8,128)(2,1)S(1)}, bf16[2,128,256]{2,1,0:T(8,128)(2,1)S(1)}, bf16[2,128,256]{2,1,0:T(8,128)(2,1)S(1)}, f32[32,128]{1,0:T(8,128)S(1)}, bf16[2,2,128,256]{3,2,1,0:T(8,128)(2,1)S(1)}) custom-call(bf16[1,2,32,4096]{3,2,1,0:T(8,128)(2,1)S(1)} %copy-done.1, f32[1,4096]{1,0:T(1,128)S(1)} %copy-done.3, ...), custom_call_target="tpu_custom_call" | custom-call | tf_op jit(solution)/shard_map/first_near_rows/pallas_call | solution.py:468
  15.8 0.0 collective-permute-done.3.refs_8_.refs_9_.refs_15_
  15.8 0.3 collective-permute-done.2.refs_7_.refs_8_.refs_14_
  16.1 0.4 %collective-permute-done.1.refs_6_.refs_7_.refs_13_ = bf16[2,2,64,128]{3,2,1,0:T(8,128)(2,1)S(1)} collective-permute-done((bf16[2,2,64,128]{3,2,1,0:T(8,128)(2,1)S(1)}, bf16[2,2,64,128]{3,2,1,0:T(8,128)(2,1)S(1)}, u32[]{:S(2)}, u32[]{:S(2)}) %collective-permute-start.1) | collective-permute-done | bytes 65568 | tf_op jit(solution)/shard_map/ppermute | solution.py:482
  16.5 0.8 %first_far_rows.1 = (bf16[32,4096]{1,0:T(8,128)(2,1)S(1)}, bf16[2,256,128]{2,1,0:T(8,128)(2,1)S(1)}, bf16[2,128,256]{2,1,0:T(8,128)(2,1)S(1)}, bf16[2,128,256]{2,1,0:T(8,128)(2,1)S(1)}) custom-call(bf16[1,2,32,4096]{3,2,1,0:T(8,128)(2,1)S(1)} %copy-done.1, f32[1,4096]{1,0:T(1,128)S(1)} %copy-done.3, f32[2,32,128]{2,1,0:T(8,128)S(1)} %get-tuple-element.36.refs_3_.refs_2_, ...), custom_call_target="tpu_custom_call" | custom-call | tf_op jit(solution)/shard_map/first_far_rows/pallas_call | solution.py:468
  17.3 0.7 %collective-permute-start.8 = (bf16[32,4096]{1,0:T(8,128)(2,1)S(1)}, bf16[32,4096]{1,0:T(8,128)(2,1)S(1)}, u32[]{:S(2)}, u32[]{:S(2)}) collective-permute-start(bf16[32,4096]{1,0:T(8,128)(2,1)S(1)} %get-tuple-element.44.refs_5_), channel_id=1, source_target_pairs={{16,8},{17,9},{18,10},{19,11},{20,12},{21,13},{22,14},{23,15}} | collective-permute-start | bytes 786440 | tf_op jit(solution)/shard_map/ppermute | solution.py:553
  18.0 0.1 collective-permute-start.7
  18.1 0.4 %first_keys.1 = (f32[32,128]{1,0:T(8,128)S(1)}, f32[2,256,128]{2,1,0:T(8,128)S(1)}, bf16[2,256,128]{2,1,0:T(8,128)(2,1)S(1)}) custom-call(bf16[1,2,32,4096]{3,2,1,0:T(8,128)(2,1)S(1)} %copy-done.1, bf16[2,32,4096]{2,1,0:T(8,128)(2,1)S(1)} %get-tuple-element.37.refs_2_.refs_1_, f32[2,32,128]{2,1,0:T(8,128)S(1)} %get-tuple-element.36.refs_3_.refs_2_, ...), custom_call_target="tpu_custom_call" | custom-call | tf_op jit(solution)/shard_map/first_keys/pallas_call | solution.py:468
  18.5 0.0 copy-start.4
  18.5 1.6 %collective-permute-start.12 = (bf16[2,256,128]{2,1,0:T(8,128)(2,1)S(1)}, bf16[2,256,128]{2,1,0:T(8,128)(2,1)S(1)}, u32[]{:S(2)}, u32[]{:S(2)}) collective-permute-start(bf16[2,256,128]{2,1,0:T(8,128)(2,1)S(1)} %get-tuple-element.59), channel_id=1, source_target_pairs={{0,4},{4,0},{1,5},{5,1},{2,6},{6,2},{3,7},{7,3},{8,12},{12,8},{9,1... | collective-permute-start | bytes 393224 | tf_op jit(solution)/shard_map/ppermute | solution.py:484
  20.1 0.4 second_probs.1.refs_6_
  20.5 0.0 collective-permute-done.8.refs_5_
  20.5 0.0 collective-permute-done.7.refs_4_
  20.5 0.0 copy-done.4
  20.5 0.6 %second_keys.1 = (bf16[4,256,128]{2,1,0:T(8,128)(2,1)S(1)}, f32[32,128]{1,0:T(8,128)S(1)}, f32[256,128]{1,0:T(8,128)S(1)}, bf16[32,4096]{1,0:T(8,128)(2,1)S(1)},...) custom-call(bf16[1,2,32,4096]{3,2,1,0:T(8,128)(2,1)S(1)} %copy-done.1, ...), custom_call_target="tpu_custom_call" | custom-call | tf_op jit(solution)/shard_map/second_keys/pallas_call | solution.py:468
  21.2 0.5 %collective-permute-start.9 = (bf16[288,128]{1,0:T(8,128)(2,1)S(1)}, bf16[288,128]{1,0:T(8,128)(2,1)S(1)}, u32[]{:S(2)}, u32[]{:S(2)}) collective-permute-start(bf16[288,128]{1,0:T(8,128)(2,1)S(1)} %get-tuple-element.55), channel_id=1, source_target_pairs={{0,1},{1,0},{2,3},{3,2},{4,5},{5,4},{6,7},{7,6},{8,9},{9,8},{10,11... | collective-permute-start | bytes 221192 | tf_op jit(solution)/shard_map/ppermute | solution.py:482
  21.7 1.0 %collective-permute-start.10 = (bf16[288,128]{1,0:T(8,128)(2,1)S(1)}, bf16[288,128]{1,0:T(8,128)(2,1)S(1)}, u32[]{:S(2)}, u32[]{:S(2)}) collective-permute-start(bf16[288,128]{1,0:T(8,128)(2,1)S(1)} %get-tuple-element.56), channel_id=1, source_target_pairs={{0,4},{4,0},{1,5},{5,1},{2,6},{6,2},{3,7},{7,3},{8,12},{12,8},{9,1... | collective-permute-start | bytes 221192 | tf_op jit(solution)/shard_map/ppermute | solution.py:484
  22.6 2.1 %collective-permute-start.11 = (bf16[288,128]{1,0:T(8,128)(2,1)S(1)}, bf16[288,128]{1,0:T(8,128)(2,1)S(1)}, u32[]{:S(2)}, u32[]{:S(2)}) collective-permute-start(bf16[288,128]{1,0:T(8,128)(2,1)S(1)} %get-tuple-element.57), channel_id=1, source_target_pairs={{0,5},{1,4},{2,7},{3,6},{4,1},{5,0},{6,3},{7,2},{8,13},{9,12},{10,... | collective-permute-start | bytes 221192 | tf_op jit(solution)/shard_map/ppermute | solution.py:490
  24.7 0.0 collective-permute-done.12.refs_1_
  24.8 0.7 %collective-permute-start.13 = (bf16[256,128]{1,0:T(8,128)(2,1)S(1)}, bf16[256,128]{1,0:T(8,128)(2,1)S(1)}, u32[]{:S(2)}, u32[]{:S(2)}) collective-permute-start(bf16[256,128]{1,0:T(8,128)(2,1)S(1)} %get-tuple-element.61), channel_id=1, source_target_pairs={{0,1},{1,0},{2,3},{3,2},{4,5},{5,4},{6,7},{7,6},{8,9},{9,8},{10,11... | collective-permute-start | bytes 196616 | tf_op jit(solution)/shard_map/ppermute | solution.py:482
  25.5 3.8 %collective-permute-done.13.refs_6_ = bf16[256,128]{1,0:T(8,128)(2,1)S(1)} collective-permute-done((bf16[256,128]{1,0:T(8,128)(2,1)S(1)}, bf16[256,128]{1,0:T(8,128)(2,1)S(1)}, u32[]{:S(2)}, u32[]{:S(2)}) %collective-permute-start.13) | collective-permute-done | bytes 65568 | tf_op jit(solution)/shard_map/ppermute | solution.py:482
  29.3 0.0 collective-permute-done.9.refs_2_
  29.3 0.0 collective-permute-done.10.refs_3_
  29.3 0.0 collective-permute-done.11.refs_4_
  29.3 0.1 near_sum.1
  29.4 2.8 %collective-permute-start.14 = (bf16[288,128]{1,0:T(8,128)(2,1)S(1)}, bf16[288,128]{1,0:T(8,128)(2,1)S(1)}, u32[]{:S(2)}, u32[]{:S(2)}) collective-permute-start(bf16[288,128]{1,0:T(8,128)(2,1)S(1)} %get-tuple-element.64), channel_id=1, source_target_pairs={{0,2},{1,3},{2,0},{3,1},{4,6},{5,7},{6,4},{7,5},{8,10},{9,11},{10,... | collective-permute-start | bytes 221192 | tf_op jit(solution)/shard_map/ppermute | solution.py:493
  32.3 1.2 %second_rows.1 = bf16[1,2,32,4096]{3,2,1,0:T(8,128)(2,1)} custom-call(bf16[1,2,32,4096]{3,2,1,0:T(8,128)(2,1)S(1)} %copy-done.1, f32[1,4096]{1,0:T(1,128)S(1)} %copy-done.3, f32[2,32,128]{2,1,0:T(8,128)S(1)} %get-tuple-element.36.refs_3_.refs_2_, bf16[32,4096]{1,0:T(8,128)(2,1)S(1)} %get-tuple-element.51.refs_3_, ...), custom_call_target="tpu_custom_call" | custom-call | tf_op jit(solution)/shard_map/second_rows/pallas_call | solution.py:468
  33.4 3.0 %collective-permute-done.14.receive_ref = bf16[288,128]{1,0:T(8,128)(2,1)S(1)} collective-permute-done((bf16[288,128]{1,0:T(8,128)(2,1)S(1)}, bf16[288,128]{1,0:T(8,128)(2,1)S(1)}, u32[]{:S(2)}, u32[]{:S(2)}) %collective-permute-start.14) | collective-permute-done | bytes 73760 | tf_op jit(solution)/shard_map/ppermute | solution.py:493
  36.4 0.7 %finish.1 = (f32[1,2,128,128]{3,2,1,0:T(8,128)}, f32[1,2,128,128]{3,2,1,0:T(8,128)}, f32[32,128]{1,0:T(8,128)}) custom-call(f32[256,128]{1,0:T(8,128)S(1)} %get-tuple-element.62.keep_ref, f32[32,128]{1,0:T(8,128)S(1)} %get-tuple-element.63.gain_ref, bf16[288,128]{1,0:T(8,128)(2,1)S(1)} %collective-permute-done.14.receive_ref), custom_call_target="tpu_custom_call" | custom-call | tf_op jit(solution)/shard_map/finish/pallas_call | solution.py:468
  (2 shorter events, 0.1 us)
Async XLA Ops:
  0.6 14.5 %copy-start.2 = (bf16[1,32,4096]{2,1,0:T(8,128)(2,1)S(1)}, bf16[1,32,4096]{2,1,0:T(8,128)(2,1)}, u32[]{:S(2)}) copy-start(bf16[1,32,4096]{2,1,0:T(8,128)(2,1)} %refs_3_.2) | copy-start | bytes 786436
  1.6 11.6 %copy-start.3 = (f32[1,4096]{1,0:T(1,128)S(1)}, f32[1,4096]{1,0:T(1,128)}, u32[]{:S(2)}) copy-start(f32[1,4096]{1,0:T(1,128)} %refs_1_.5) | copy-start | bytes 49156
  1.6 11.6 %copy-start.5 = (s32[5,8]{1,0:T(8,128)S(1)}, s32[5,8]{1,0:T(8,128)}, u32[]{:S(2)}) copy-start(s32[5,8]{1,0:T(8,128)} %doc_ref.1) | copy-start | bytes 484
  1.6 7.6 %collective-permute-start = (bf16[2,2,64,128]{3,2,1,0:T(8,128)(2,1)S(1)}, bf16[2,2,64,128]{3,2,1,0:T(8,128)(2,1)S(1)}, u32[]{:S(2)}, u32[]{:S(2)}) collective-permute-start(bf16[2,2,64,128]{3,2,1,0:T(8,128)(2,1)S(1)} %get-tuple-element.39), channel_id=1, source_target_pairs={{0,2},{1,3},{2,0},{3,1},{4,6},{5,7},{6,4},{7,5},{8,10},{9,11},{10,... | collective-permute-start | bytes 196616 | tf_op jit(solution)/shard_map/ppermute | solution.py:493
  5.7 6.5 %collective-permute-start.6 = (bf16[2,2,64,128]{3,2,1,0:T(8,128)(2,1)S(1)}, bf16[2,2,64,128]{3,2,1,0:T(8,128)(2,1)S(1)}, u32[]{:S(2)}, u32[]{:S(2)}) collective-permute-start(bf16[2,2,64,128]{3,2,1,0:T(8,128)(2,1)S(1)} %get-tuple-element.40.refs_6_.refs_2_.refs_8_), channel_id=1, source_target_pairs={{0,5},{1,4},{2,7},{3,6},{4,1},{5,0},{6,3},{7,2},{8,13},{9,12},{10,... | collective-permute-start | bytes 196616 | tf_op jit(solution)/shard_map/ppermute | solution.py:490
  8.3 6.9 %collective-permute-start.5 = (bf16[2,2,64,128]{3,2,1,0:T(8,128)(2,1)S(1)}, bf16[2,2,64,128]{3,2,1,0:T(8,128)(2,1)S(1)}, u32[]{:S(2)}, u32[]{:S(2)}) collective-permute-start(bf16[2,2,64,128]{3,2,1,0:T(8,128)(2,1)S(1)} %get-tuple-element.40.refs_6_.refs_2_.refs_8_), channel_id=1, source_target_pairs={{0,4},{4,0},{1,5},{5,1},{2,6},{6,2},{3,7},{7,3},{8,12},{12,8},{9,1... | collective-permute-start | bytes 196616 | tf_op jit(solution)/shard_map/ppermute | solution.py:484
  8.8 6.4 %collective-permute-start.4 = (bf16[2,2,64,128]{3,2,1,0:T(8,128)(2,1)S(1)}, bf16[2,2,64,128]{3,2,1,0:T(8,128)(2,1)S(1)}, u32[]{:S(2)}, u32[]{:S(2)}) collective-permute-start(bf16[2,2,64,128]{3,2,1,0:T(8,128)(2,1)S(1)} %get-tuple-element.40.refs_6_.refs_2_.refs_8_), channel_id=1, source_target_pairs={{0,1},{1,0},{2,3},{3,2},{4,5},{5,4},{6,7},{7,6},{8,9},{9,8},{10,11... | collective-permute-start | bytes 196616 | tf_op jit(solution)/shard_map/ppermute | solution.py:482
  9.2 6.6 %collective-permute-start.3 = (bf16[2,2,64,128]{3,2,1,0:T(8,128)(2,1)S(1)}, bf16[2,2,64,128]{3,2,1,0:T(8,128)(2,1)S(1)}, u32[]{:S(2)}, u32[]{:S(2)}) collective-permute-start(bf16[2,2,64,128]{3,2,1,0:T(8,128)(2,1)S(1)} %collective-permute-done.refs_5_.refs_6_.refs_12_), channel_id=1, source_target_pairs={{0,5},{1,4},{2,7},{3,6},{4,1},{5,0},{6,3},{7,2},{8,13},{9,12},{10,... | collective-permute-start | bytes 196616 | tf_op jit(solution)/shard_map/ppermute | solution.py:490
  11.8 4.3 %collective-permute-start.2 = (bf16[2,2,64,128]{3,2,1,0:T(8,128)(2,1)S(1)}, bf16[2,2,64,128]{3,2,1,0:T(8,128)(2,1)S(1)}, u32[]{:S(2)}, u32[]{:S(2)}) collective-permute-start(bf16[2,2,64,128]{3,2,1,0:T(8,128)(2,1)S(1)} %collective-permute-done.refs_5_.refs_6_.refs_12_), channel_id=1, source_target_pairs={{0,4},{4,0},{1,5},{5,1},{2,6},{6,2},{3,7},{7,3},{8,12},{12,8},{9,1... | collective-permute-start | bytes 196616 | tf_op jit(solution)/shard_map/ppermute | solution.py:484
  12.3 4.3 %collective-permute-start.1 = (bf16[2,2,64,128]{3,2,1,0:T(8,128)(2,1)S(1)}, bf16[2,2,64,128]{3,2,1,0:T(8,128)(2,1)S(1)}, u32[]{:S(2)}, u32[]{:S(2)}) collective-permute-start(bf16[2,2,64,128]{3,2,1,0:T(8,128)(2,1)S(1)} %collective-permute-done.refs_5_.refs_6_.refs_12_), channel_id=1, source_target_pairs={{0,1},{1,0},{2,3},{3,2},{4,5},{5,4},{6,7},{7,6},{8,9},{9,8},{10,11... | collective-permute-start | bytes 196616 | tf_op jit(solution)/shard_map/ppermute | solution.py:482
  13.2 1.0 %copy-start = (bf16[1,2,32,4096]{3,2,1,0:T(8,128)(2,1)S(1)}, bf16[1,2,32,4096]{3,2,1,0:T(8,128)(2,1)}, u32[]{:S(2)}) copy-start(bf16[1,2,32,4096]{3,2,1,0:T(8,128)(2,1)} %refs_0_.9) | copy-start | bytes 1572868
  14.2 1.0 %copy-start.1 = (bf16[1,2,32,4096]{3,2,1,0:T(8,128)(2,1)S(1)}, bf16[1,2,32,4096]{3,2,1,0:T(8,128)(2,1)}, u32[]{:S(2)}) copy-start(bf16[1,2,32,4096]{3,2,1,0:T(8,128)(2,1)} %refs_0_.9) | copy-start | bytes 1572868
  17.3 3.2 %collective-permute-start.8 = (bf16[32,4096]{1,0:T(8,128)(2,1)S(1)}, bf16[32,4096]{1,0:T(8,128)(2,1)S(1)}, u32[]{:S(2)}, u32[]{:S(2)}) collective-permute-start(bf16[32,4096]{1,0:T(8,128)(2,1)S(1)} %get-tuple-element.44.refs_5_), channel_id=1, source_target_pairs={{16,8},{17,9},{18,10},{19,11},{20,12},{21,13},{22,14},{23,15}} | collective-permute-start | bytes 786440 | tf_op jit(solution)/shard_map/ppermute | solution.py:553
  18.0 2.5 %collective-permute-start.7 = (bf16[32,4096]{1,0:T(8,128)(2,1)S(1)}, bf16[32,4096]{1,0:T(8,128)(2,1)S(1)}, u32[]{:S(2)}, u32[]{:S(2)}) collective-permute-start(bf16[32,4096]{1,0:T(8,128)(2,1)S(1)} %get-tuple-element.44.refs_5_), channel_id=1, source_target_pairs={{0,8},{8,0},{16,24},{24,16},{1,9},{9,1},{17,25},{25,17},{2,10},{10... | collective-permute-start | bytes 786440 | tf_op jit(solution)/shard_map/ppermute | solution.py:556
  18.5 2.0 %copy-start.4 = (bf16[1,32,4096]{2,1,0:T(8,128)(2,1)S(1)}, bf16[1,32,4096]{2,1,0:T(8,128)(2,1)}, u32[]{:S(2)}) copy-start(bf16[1,32,4096]{2,1,0:T(8,128)(2,1)} %refs_3_.3) | copy-start | bytes 786436
  18.5 6.2 %collective-permute-start.12 = (bf16[2,256,128]{2,1,0:T(8,128)(2,1)S(1)}, bf16[2,256,128]{2,1,0:T(8,128)(2,1)S(1)}, u32[]{:S(2)}, u32[]{:S(2)}) collective-permute-start(bf16[2,256,128]{2,1,0:T(8,128)(2,1)S(1)} %get-tuple-element.59), channel_id=1, source_target_pairs={{0,4},{4,0},{1,5},{5,1},{2,6},{6,2},{3,7},{7,3},{8,12},{12,8},{9,1... | collective-permute-start | bytes 393224 | tf_op jit(solution)/shard_map/ppermute | solution.py:484
  21.2 8.2 %collective-permute-start.9 = (bf16[288,128]{1,0:T(8,128)(2,1)S(1)}, bf16[288,128]{1,0:T(8,128)(2,1)S(1)}, u32[]{:S(2)}, u32[]{:S(2)}) collective-permute-start(bf16[288,128]{1,0:T(8,128)(2,1)S(1)} %get-tuple-element.55), channel_id=1, source_target_pairs={{0,1},{1,0},{2,3},{3,2},{4,5},{5,4},{6,7},{7,6},{8,9},{9,8},{10,11... | collective-permute-start | bytes 221192 | tf_op jit(solution)/shard_map/ppermute | solution.py:482
  21.7 7.7 %collective-permute-start.10 = (bf16[288,128]{1,0:T(8,128)(2,1)S(1)}, bf16[288,128]{1,0:T(8,128)(2,1)S(1)}, u32[]{:S(2)}, u32[]{:S(2)}) collective-permute-start(bf16[288,128]{1,0:T(8,128)(2,1)S(1)} %get-tuple-element.56), channel_id=1, source_target_pairs={{0,4},{4,0},{1,5},{5,1},{2,6},{6,2},{3,7},{7,3},{8,12},{12,8},{9,1... | collective-permute-start | bytes 221192 | tf_op jit(solution)/shard_map/ppermute | solution.py:484
  22.6 6.7 %collective-permute-start.11 = (bf16[288,128]{1,0:T(8,128)(2,1)S(1)}, bf16[288,128]{1,0:T(8,128)(2,1)S(1)}, u32[]{:S(2)}, u32[]{:S(2)}) collective-permute-start(bf16[288,128]{1,0:T(8,128)(2,1)S(1)} %get-tuple-element.57), channel_id=1, source_target_pairs={{0,5},{1,4},{2,7},{3,6},{4,1},{5,0},{6,3},{7,2},{8,13},{9,12},{10,... | collective-permute-start | bytes 221192 | tf_op jit(solution)/shard_map/ppermute | solution.py:490
  24.8 4.6 %collective-permute-start.13 = (bf16[256,128]{1,0:T(8,128)(2,1)S(1)}, bf16[256,128]{1,0:T(8,128)(2,1)S(1)}, u32[]{:S(2)}, u32[]{:S(2)}) collective-permute-start(bf16[256,128]{1,0:T(8,128)(2,1)S(1)} %get-tuple-element.61), channel_id=1, source_target_pairs={{0,1},{1,0},{2,3},{3,2},{4,5},{5,4},{6,7},{7,6},{8,9},{9,8},{10,11... | collective-permute-start | bytes 196616 | tf_op jit(solution)/shard_map/ppermute | solution.py:482
  29.4 7.0 %collective-permute-start.14 = (bf16[288,128]{1,0:T(8,128)(2,1)S(1)}, bf16[288,128]{1,0:T(8,128)(2,1)S(1)}, u32[]{:S(2)}, u32[]{:S(2)}) collective-permute-start(bf16[288,128]{1,0:T(8,128)(2,1)S(1)} %get-tuple-element.64), channel_id=1, source_target_pairs={{0,2},{1,3},{2,0},{3,1},{4,6},{5,7},{6,4},{7,5},{8,10},{9,11},{10,... | collective-permute-start | bytes 221192 | tf_op jit(solution)/shard_map/ppermute | solution.py:493

commit v11 on v10

--- a/solution.py
+++ b/solution.py
@@ -397,24 +397,29 @@
     )
 
 
-def near_sum_kernel(sizes, *refs):
+def first_near_kernel(sizes, own_ref, *refs):
+    block = 2 * sizes[1]
+    keep_ref, send_ref = refs[-2:]
+    total = own_ref[...]
+    for ref in refs[:-2]:
+        total = total + ref[...].astype(F32)
+    keep_ref[...] = total[:block]
+    send_ref[...] = total[block:].astype(BF16)
+
+
+def second_near_kernel(sizes, *refs):
     rows, half, cycle, tp_count, group, columns = sizes
     near_count = tp_count // 2
     members = cycle * near_count
     own_ref, gain_ref = refs[:2]
-    message_refs, refs = refs[2 : 1 + members], refs[1 + members :]
-    own_first_ref, first_refs, refs = refs[0], refs[1:near_count], refs[near_count:]
-    keep_ref, gain_sum_ref, send_ref = refs
+    message_refs = refs[2 : 1 + members][::-1]
+    keep_ref, gain_sum_ref, send_ref = refs[1 + members :]
     block = 2 * half
-    first, second = own_first_ref[...], own_ref[...]
+    total = own_ref[...]
     for ref in message_refs:
-        second = second + ref[: 2 * block, :].astype(F32)
-    for ref in first_refs:
-        first = first + ref[...].astype(F32)
-    for tick, total in enumerate((first, second)):
-        here = slice(tick * block, (tick + 1) * block)
-        keep_ref[here, :] = total[:block]
-        send_ref[here, :] = total[block:].astype(BF16)
+        total = total + ref[: 2 * block, :].astype(F32)
+    keep_ref[...] = total[:block]
+    send_ref[:block, :] = total[block:].astype(BF16)
     cycle_place = lax.axis_index("ctx")
     near_place = lax.axis_index("tp") % near_count
     values = [gain_ref[...].astype(BF16).astype(F32)]
@@ -425,22 +430,24 @@
         owners.append(((cycle_place + step) % cycle) * near_count + (near_place ^ near))
     gain = in_order(values, owners)
     gain_sum_ref[...] = gain
-    send_ref[TICKS * block :, :] = gain.astype(BF16)
-
-
-def finish_kernel(sizes, keep_ref, gain_ref, receive_ref, key_ref, value_ref, gain_out_ref):
+    send_ref[block:, :] = gain.astype(BF16)
+
+
+def finish_kernel(sizes, *refs):
     half = sizes[1]
+    keep_refs, receive_refs, gain_ref = refs[:TICKS], refs[TICKS : 2 * TICKS], refs[2 * TICKS]
+    key_ref, value_ref, gain_out_ref = refs[2 * TICKS + 1 :]
     parity = lax.axis_index("tp") // (sizes[3] // 2)
+    block = 2 * half
     own_first = pl.multiple_of(parity * half, half)
     other_first = pl.multiple_of((1 - parity) * half, half)
     for tick in range(TICKS):
         for kind, out in enumerate((key_ref, value_ref)):
-            begin = (tick * 2 + kind) * half
-            here = slice(begin, begin + half)
-            out[0, tick, pl.ds(own_first, half), :] = keep_ref[here, :]
-            out[0, tick, pl.ds(other_first, half), :] = receive_ref[here, :].astype(F32)
+            here = slice(kind * half, (kind + 1) * half)
+            out[0, tick, pl.ds(own_first, half), :] = keep_refs[tick][here, :]
+            out[0, tick, pl.ds(other_first, half), :] = receive_refs[tick][here, :].astype(F32)
     own = gain_ref[...].astype(BF16).astype(F32)
-    gain_out_ref[...] = own + receive_ref[TICKS * 2 * half :, :].astype(F32)
+    gain_out_ref[...] = own + receive_refs[TICKS - 1][block:, :].astype(F32)
 
 
 def shape(dims, dtype):
@@ -624,21 +631,24 @@
         ),
         [shape((1, ticks, rows, columns), BF16)],
     )
-    keep, gain_sum, send = call(
-        functools.partial(near_sum_kernel, sizes),
-        "near_sum",
-        (own_second, gain_rows, *received, own_first, *received_first),
-        [
-            shape((ticks * block, HD), F32),
-            gain_shape,
-            shape((ticks * block + gain_count, HD), BF16),
-        ],
+    keep_shape = shape((block, HD), F32)
+    keep_first, send_first = call(
+        functools.partial(first_near_kernel, sizes),
+        "first_near",
+        (own_first, *received_first),
+        [keep_shape, shape((block, HD), BF16)],
+    )
+    keep_second, gain_sum, send_second = call(
+        functools.partial(second_near_kernel, sizes),
+        "second_near",
+        (own_second, gain_rows, *received[::-1]),
+        [keep_shape, gain_shape, shape((block + gain_count, HD), BF16)],
     )
     grads_shape = shape((1, ticks, block, HD), F32)
     key_grads, value_grads, gain_grads = call(
         functools.partial(finish_kernel, sizes),
         "finish",
-        (keep, gain_sum, to_far(send)),
+        (keep_first, keep_second, to_far(send_first), to_far(send_second), gain_sum),
         [grads_shape, grads_shape, gain_shape],
     )
     return input_grads, key_grads, value_grads, gain_grads.reshape(1, columns)

time: 37.4 us -> 37.1 us (level)
  the two profiles are of different devices: /device:TPU:0 before, /device:TPU:1 now
where the time goes in v11:
time: 37.1 us; the launch traced here: 36.9 us
  starting transfers between devices  21 us (57%)
  waiting for transfers between devices  7.35 us (20%)
  Pallas kernels  5.63 us (15%)
  local copies, waits for them, and re-layouts  1.15 us (3%)
  other arithmetic  0.93 us (3%)
  between operations  0.8 us (2%)
    ppermute x3, starting transfers between devices, to_far(): lax.ppermute(value, 'tp', [(i, i ^ near_count) for i in range(tp_count)])  6.51 us
    ppermute x3, starting transfers between devices, to_near(): return lax.ppermute(value, ('ctx', 'tp'), pairs)  5.69 us
    pallas_call x12, Pallas kernels, call(): pl.pallas_call(kernel, out_shape=out_shape, in_specs=in_specs, out_specs=...  5.63 us
    ppermute x1, waiting for transfers between devices, on_device(): lax.ppermute(input_grad_first, 'pipe', [(i, i - 1) for i in range(2, pipe...  3.85 us
    ppermute x4, starting transfers between devices, to_near(): return lax.ppermute(value, 'tp', [(i, i ^ near) for i in range(tp_count)])  2.58 us
    ppermute x1, starting transfers between devices, on_device(): lax.ppermute(input_grad_first, 'pipe', [(i, i ^ 1) for i in range(pipe_co...  2.52 us
    ppermute x4, starting transfers between devices, to_near(): lax.ppermute(value, 'ctx', [(i, (i + step) % cycle) for i in range(cycle)])  2.44 us
    ppermute x3, waiting for transfers between devices, to_far(): lax.ppermute(value, 'tp', [(i, i ^ near_count) for i in range(tp_count)])  1.59 us
  transfers between devices with their start and end apart: 16, of which 5 were waited for; matrix products, arithmetic and copies ran while one was open for 0% of the time, Pallas kernels for 11%

profile of v11, /device:TPU:1, one launch (start us, length us, event | category | flops | bytes accessed | tf_op | source)
XLA Modules:
  0.0 36.9 jit_solution(18038432993034737325)
XLA Ops:
  0.6 0.0 copy-start.2
  0.6 0.9 %pad_maximum_fusion.both_ref = bf16[2,2,128,128]{3,2,1,0:T(8,128)(2,1)S(1)} fusion(bf16[1,2,128,128]{3,2,1,0:T(8,128)(2,1)} %param.9, bf16[1,2,128,128]{3,2,1,0:T(8,128)(2,1)} %param.8), kind=kLoop, calls=%fused_computation | loop fusion | flops 65536 | bytes 262144 | tf_op jit(solution)/shard_map/stack | solution.py:506
  1.6 0.0 copy-start.3
  1.6 0.0 copy-start.5
  1.6 3.2 %collective-permute-start = (bf16[2,2,64,128]{3,2,1,0:T(8,128)(2,1)S(1)}, bf16[2,2,64,128]{3,2,1,0:T(8,128)(2,1)S(1)}, u32[]{:S(2)}, u32[]{:S(2)}) collective-permute-start(bf16[2,2,64,128]{3,2,1,0:T(8,128)(2,1)S(1)} %get-tuple-element.41), channel_id=1, source_target_pairs={{0,2},{1,3},{2,0},{3,1},{4,6},{5,7},{6,4},{7,5},{8,10},{9,11},{10,... | collective-permute-start | bytes 196616 | tf_op jit(solution)/shard_map/ppermute | solution.py:500
  4.8 2.3 %collective-permute-start.6 = (bf16[2,2,64,128]{3,2,1,0:T(8,128)(2,1)S(1)}, bf16[2,2,64,128]{3,2,1,0:T(8,128)(2,1)S(1)}, u32[]{:S(2)}, u32[]{:S(2)}) collective-permute-start(bf16[2,2,64,128]{3,2,1,0:T(8,128)(2,1)S(1)} %get-tuple-element.42.refs_6_.refs_2_.refs_8_), channel_id=1, source_target_pairs={{0,5},{1,4},{2,7},{3,6},{4,1},{5,0},{6,3},{7,2},{8,13},{9,12},{10,... | collective-permute-start | bytes 196616 | tf_op jit(solution)/shard_map/ppermute | solution.py:497
  7.1 0.2 collective-permute-start.5
  7.3 0.2 collective-permute-start.4
  7.5 0.0 collective-permute-done.refs_5_.refs_6_.refs_12_
  7.5 2.3 %collective-permute-start.3 = (bf16[2,2,64,128]{3,2,1,0:T(8,128)(2,1)S(1)}, bf16[2,2,64,128]{3,2,1,0:T(8,128)(2,1)S(1)}, u32[]{:S(2)}, u32[]{:S(2)}) collective-permute-start(bf16[2,2,64,128]{3,2,1,0:T(8,128)(2,1)S(1)} %collective-permute-done.refs_5_.refs_6_.refs_12_), channel_id=1, source_target_pairs={{0,5},{1,4},{2,7},{3,6},{4,1},{5,0},{6,3},{7,2},{8,13},{9,12},{10,... | collective-permute-start | bytes 196616 | tf_op jit(solution)/shard_map/ppermute | solution.py:497
  9.7 0.2 collective-permute-start.2
  10.0 0.0 collective-permute-done.6.refs_9_.refs_5_.refs_11_
  10.0 0.9 %collective-permute-start.1 = (bf16[2,2,64,128]{3,2,1,0:T(8,128)(2,1)S(1)}, bf16[2,2,64,128]{3,2,1,0:T(8,128)(2,1)S(1)}, u32[]{:S(2)}, u32[]{:S(2)}) collective-permute-start(bf16[2,2,64,128]{3,2,1,0:T(8,128)(2,1)S(1)} %collective-permute-done.refs_5_.refs_6_.refs_12_), channel_id=1, source_target_pairs={{0,1},{1,0},{2,3},{3,2},{4,5},{5,4},{6,7},{7,6},{8,9},{9,8},{10,11... | collective-permute-start | bytes 196616 | tf_op jit(solution)/shard_map/ppermute | solution.py:489
  10.8 0.0 copy-done.3
  10.8 0.0 copy-done.5
  10.9 0.0 copy-start
  10.9 1.0 %copy-done = bf16[1,2,32,4096]{3,2,1,0:T(8,128)(2,1)S(1)} copy-done((bf16[1,2,32,4096]{3,2,1,0:T(8,128)(2,1)S(1)}, bf16[1,2,32,4096]{3,2,1,0:T(8,128)(2,1)}, u32[]{:S(2)}) %copy-start) | copy-done | bytes 524312
  11.9 0.0 copy-start.1
  11.9 0.9 %norm.1 = (bf16[2,32,4096]{2,1,0:T(8,128)(2,1)S(1)}, f32[2,32,128]{2,1,0:T(8,128)S(1)}, f32[2,128,256]{2,1,0:T(8,128)S(1)}) custom-call(s32[5,8]{1,0:T(8,128)S(1)} %copy-done.5, bf16[1,2,32,4096]{3,2,1,0:T(8,128)(2,1)S(1)} %copy-done, f32[1,4096]{1,0:T(1,128)S(1)} %copy-done.3), custom_call_target="tpu_custom_call" | custom-call | tf_op jit(solution)/shard_map/norm/pallas_call | solution.py:475
  12.8 0.0 collective-permute-done.5.refs_8_.refs_4_.refs_10_
  12.8 0.0 collective-permute-done.4.refs_7_.refs_3_.refs_9_
  12.8 0.0 copy-done.2
  12.9 0.1 copy-done.1
  12.9 0.5 %first_near_rows.1 = (bf16[2,256,128]{2,1,0:T(8,128)(2,1)S(1)}, bf16[2,128,256]{2,1,0:T(8,128)(2,1)S(1)}, bf16[2,128,256]{2,1,0:T(8,128)(2,1)S(1)}, f32[32,128]{1,0:T(8,128)S(1)}, bf16[2,2,128,256]{3,2,1,0:T(8,128)(2,1)S(1)}) custom-call(bf16[1,2,32,4096]{3,2,1,0:T(8,128)(2,1)S(1)} %copy-done.1, f32[1,4096]{1,0:T(1,128)S(1)} %copy-done.3, ...), custom_call_target="tpu_custom_call" | custom-call | tf_op jit(solution)/shard_map/first_near_rows/pallas_call | solution.py:475
  13.5 0.0 collective-permute-done.3.refs_8_.refs_9_.refs_15_
  13.5 0.0 collective-permute-done.2.refs_7_.refs_8_.refs_14_
  13.5 0.0 collective-permute-done.1.refs_6_.refs_7_.refs_13_
  13.5 0.8 %first_far_rows.1 = (bf16[32,4096]{1,0:T(8,128)(2,1)S(1)}, bf16[2,256,128]{2,1,0:T(8,128)(2,1)S(1)}, bf16[2,128,256]{2,1,0:T(8,128)(2,1)S(1)}, bf16[2,128,256]{2,1,0:T(8,128)(2,1)S(1)}) custom-call(bf16[1,2,32,4096]{3,2,1,0:T(8,128)(2,1)S(1)} %copy-done.1, f32[1,4096]{1,0:T(1,128)S(1)} %copy-done.3, f32[2,32,128]{2,1,0:T(8,128)S(1)} %get-tuple-element.38.refs_3_.refs_2_, ...), custom_call_target="tpu_custom_call" | custom-call | tf_op jit(solution)/shard_map/first_far_rows/pallas_call | solution.py:475
  14.3 1.3 %collective-permute-start.8 = (bf16[32,4096]{1,0:T(8,128)(2,1)S(1)}, bf16[32,4096]{1,0:T(8,128)(2,1)S(1)}, u32[]{:S(2)}, u32[]{:S(2)}) collective-permute-start(bf16[32,4096]{1,0:T(8,128)(2,1)S(1)} %get-tuple-element.46.refs_5_), channel_id=1, source_target_pairs={{16,8},{17,9},{18,10},{19,11},{20,12},{21,13},{22,14},{23,15}} | collective-permute-start | bytes 786440 | tf_op jit(solution)/shard_map/ppermute | solution.py:560
  15.6 2.5 %collective-permute-start.7 = (bf16[32,4096]{1,0:T(8,128)(2,1)S(1)}, bf16[32,4096]{1,0:T(8,128)(2,1)S(1)}, u32[]{:S(2)}, u32[]{:S(2)}) collective-permute-start(bf16[32,4096]{1,0:T(8,128)(2,1)S(1)} %get-tuple-element.46.refs_5_), channel_id=1, source_target_pairs={{0,8},{8,0},{16,24},{24,16},{1,9},{9,1},{17,25},{25,17},{2,10},{10... | collective-permute-start | bytes 786440 | tf_op jit(solution)/shard_map/ppermute | solution.py:563
  18.1 0.4 %first_keys.1 = (f32[32,128]{1,0:T(8,128)S(1)}, f32[2,256,128]{2,1,0:T(8,128)S(1)}, bf16[2,256,128]{2,1,0:T(8,128)(2,1)S(1)}) custom-call(bf16[1,2,32,4096]{3,2,1,0:T(8,128)(2,1)S(1)} %copy-done.1, bf16[2,32,4096]{2,1,0:T(8,128)(2,1)S(1)} %get-tuple-element.39.refs_2_.refs_1_, f32[2,32,128]{2,1,0:T(8,128)S(1)} %get-tuple-element.38.refs_3_.refs_2_, ...), custom_call_target="tpu_custom_call" | custom-call | tf_op jit(solution)/shard_map/first_keys/pallas_call | solution.py:475
  18.5 0.0 copy-start.4
  18.6 1.3 %collective-permute-start.9 = (bf16[2,256,128]{2,1,0:T(8,128)(2,1)S(1)}, bf16[2,256,128]{2,1,0:T(8,128)(2,1)S(1)}, u32[]{:S(2)}, u32[]{:S(2)}) collective-permute-start(bf16[2,256,128]{2,1,0:T(8,128)(2,1)S(1)} %get-tuple-element.56), channel_id=1, source_target_pairs={{0,4},{4,0},{1,5},{5,1},{2,6},{6,2},{3,7},{7,3},{8,12},{12,8},{9,1... | collective-permute-start | bytes 393224 | tf_op jit(solution)/shard_map/ppermute | solution.py:491
  19.9 0.4 second_probs.1.refs_6_
  20.2 3.9 %collective-permute-done.8.refs_5_ = bf16[32,4096]{1,0:T(8,128)(2,1)S(1)} collective-permute-done((bf16[32,4096]{1,0:T(8,128)(2,1)S(1)}, bf16[32,4096]{1,0:T(8,128)(2,1)S(1)}, u32[]{:S(2)}, u32[]{:S(2)}) %collective-permute-start.8) | collective-permute-done | bytes 262176 | tf_op jit(solution)/shard_map/ppermute | solution.py:560
  24.1 0.0 collective-permute-done.7.refs_4_
  24.1 0.0 copy-done.4
  24.1 0.6 %second_keys.1 = (bf16[4,256,128]{2,1,0:T(8,128)(2,1)S(1)}, f32[32,128]{1,0:T(8,128)S(1)}, f32[256,128]{1,0:T(8,128)S(1)}, bf16[32,4096]{1,0:T(8,128)(2,1)S(1)},...) custom-call(bf16[1,2,32,4096]{3,2,1,0:T(8,128)(2,1)S(1)} %copy-done.1, ...), custom_call_target="tpu_custom_call" | custom-call | tf_op jit(solution)/shard_map/second_keys/pallas_call | solution.py:475
  24.7 1.2 %collective-permute-start.11 = (bf16[288,128]{1,0:T(8,128)(2,1)S(1)}, bf16[288,128]{1,0:T(8,128)(2,1)S(1)}, u32[]{:S(2)}, u32[]{:S(2)}) collective-permute-start(bf16[288,128]{1,0:T(8,128)(2,1)S(1)} %get-tuple-element.62), channel_id=1, source_target_pairs={{0,5},{1,4},{2,7},{3,6},{4,1},{5,0},{6,3},{7,2},{8,13},{9,12},{10,... | collective-permute-start | bytes 221192 | tf_op jit(solution)/shard_map/ppermute | solution.py:497
  25.9 0.7 %collective-permute-start.12 = (bf16[288,128]{1,0:T(8,128)(2,1)S(1)}, bf16[288,128]{1,0:T(8,128)(2,1)S(1)}, u32[]{:S(2)}, u32[]{:S(2)}) collective-permute-start(bf16[288,128]{1,0:T(8,128)(2,1)S(1)} %get-tuple-element.63), channel_id=1, source_target_pairs={{0,4},{4,0},{1,5},{5,1},{2,6},{6,2},{3,7},{7,3},{8,12},{12,8},{9,1... | collective-permute-start | bytes 221192 | tf_op jit(solution)/shard_map/ppermute | solution.py:491
  26.6 0.8 %collective-permute-start.13 = (bf16[288,128]{1,0:T(8,128)(2,1)S(1)}, bf16[288,128]{1,0:T(8,128)(2,1)S(1)}, u32[]{:S(2)}, u32[]{:S(2)}) collective-permute-start(bf16[288,128]{1,0:T(8,128)(2,1)S(1)} %get-tuple-element.64), channel_id=1, source_target_pairs={{0,1},{1,0},{2,3},{3,2},{4,5},{5,4},{6,7},{7,6},{8,9},{9,8},{10,11... | collective-permute-start | bytes 221192 | tf_op jit(solution)/shard_map/ppermute | solution.py:489
  27.4 0.0 collective-permute-done.9.refs_1_
  27.5 0.7 %collective-permute-start.10 = (bf16[256,128]{1,0:T(8,128)(2,1)S(1)}, bf16[256,128]{1,0:T(8,128)(2,1)S(1)}, u32[]{:S(2)}, u32[]{:S(2)}) collective-permute-start(bf16[256,128]{1,0:T(8,128)(2,1)S(1)} %get-tuple-element.58), channel_id=1, source_target_pairs={{0,1},{1,0},{2,3},{3,2},{4,5},{5,4},{6,7},{7,6},{8,9},{9,8},{10,11... | collective-permute-start | bytes 196616 | tf_op jit(solution)/shard_map/ppermute | solution.py:489
  28.2 1.2 %collective-permute-done.11.refs_2_ = bf16[288,128]{1,0:T(8,128)(2,1)S(1)} collective-permute-done((bf16[288,128]{1,0:T(8,128)(2,1)S(1)}, bf16[288,128]{1,0:T(8,128)(2,1)S(1)}, u32[]{:S(2)}, u32[]{:S(2)}) %collective-permute-start.11) | collective-permute-done | bytes 73760 | tf_op jit(solution)/shard_map/ppermute | solution.py:497
  29.4 0.3 collective-permute-done.12.refs_3_
  29.7 0.4 collective-permute-done.13.refs_4_
  30.0 0.1 second_near.1
  30.1 2.3 %collective-permute-start.15 = (bf16[160,128]{1,0:T(8,128)(2,1)S(1)}, bf16[160,128]{1,0:T(8,128)(2,1)S(1)}, u32[]{:S(2)}, u32[]{:S(2)}) collective-permute-start(bf16[160,128]{1,0:T(8,128)(2,1)S(1)} %get-tuple-element.67), channel_id=1, source_target_pairs={{0,2},{1,3},{2,0},{3,1},{4,6},{5,7},{6,4},{7,5},{8,10},{9,11},{10,... | collective-permute-start | bytes 122888 | tf_op jit(solution)/shard_map/ppermute | solution.py:500
  32.4 0.0 collective-permute-done.10.refs_0_
  32.4 1.0 %collective-permute-start.14 = (bf16[128,128]{1,0:T(8,128)(2,1)S(1)}, bf16[128,128]{1,0:T(8,128)(2,1)S(1)}, u32[]{:S(2)}, u32[]{:S(2)}) collective-permute-start(bf16[128,128]{1,0:T(8,128)(2,1)S(1)} %get-tuple-element.66), channel_id=1, source_target_pairs={{0,2},{1,3},{2,0},{3,1},{4,6},{5,7},{6,4},{7,5},{8,10},{9,11},{10,... | collective-permute-start | bytes 98312 | tf_op jit(solution)/shard_map/ppermute | solution.py:500
  33.4 1.2 %second_rows.1 = bf16[1,2,32,4096]{3,2,1,0:T(8,128)(2,1)} custom-call(bf16[1,2,32,4096]{3,2,1,0:T(8,128)(2,1)S(1)} %copy-done.1, f32[1,4096]{1,0:T(1,128)S(1)} %copy-done.3, f32[2,32,128]{2,1,0:T(8,128)S(1)} %get-tuple-element.38.refs_3_.refs_2_, bf16[32,4096]{1,0:T(8,128)(2,1)S(1)} %get-tuple-element.53.refs_3_, ...), custom_call_target="tpu_custom_call" | custom-call | tf_op jit(solution)/shard_map/second_rows/pallas_call | solution.py:475
  34.6 1.6 %collective-permute-done.14.refs_2_ = bf16[128,128]{1,0:T(8,128)(2,1)S(1)} collective-permute-done((bf16[128,128]{1,0:T(8,128)(2,1)S(1)}, bf16[128,128]{1,0:T(8,128)(2,1)S(1)}, u32[]{:S(2)}, u32[]{:S(2)}) %collective-permute-start.14) | collective-permute-done | bytes 32800 | tf_op jit(solution)/shard_map/ppermute | solution.py:500
  36.2 0.0 collective-permute-done.15.refs_3_
  36.2 0.7 %finish.1 = (f32[1,2,128,128]{3,2,1,0:T(8,128)}, f32[1,2,128,128]{3,2,1,0:T(8,128)}, f32[32,128]{1,0:T(8,128)}) custom-call(f32[128,128]{1,0:T(8,128)S(1)} %get-tuple-element.59.refs_0_, f32[128,128]{1,0:T(8,128)S(1)} %get-tuple-element.65.refs_1_, bf16[128,128]{1,0:T(8,128)(2,1)S(1)} %collective-permute-done.14.refs_2_, ...), custom_call_target="tpu_custom_call" | custom-call | tf_op jit(solution)/shard_map/finish/pallas_call | solution.py:475
  (3 shorter events, 0.1 us)
Async XLA Ops:
  0.6 12.2 %copy-start.2 = (bf16[1,32,4096]{2,1,0:T(8,128)(2,1)S(1)}, bf16[1,32,4096]{2,1,0:T(8,128)(2,1)}, u32[]{:S(2)}) copy-start(bf16[1,32,4096]{2,1,0:T(8,128)(2,1)} %refs_3_.2) | copy-start | bytes 786436
  1.6 9.3 %copy-start.3 = (f32[1,4096]{1,0:T(1,128)S(1)}, f32[1,4096]{1,0:T(1,128)}, u32[]{:S(2)}) copy-start(f32[1,4096]{1,0:T(1,128)} %refs_1_.5) | copy-start | bytes 49156
  1.6 9.3 %copy-start.5 = (s32[5,8]{1,0:T(8,128)S(1)}, s32[5,8]{1,0:T(8,128)}, u32[]{:S(2)}) copy-start(s32[5,8]{1,0:T(8,128)} %doc_ref.1) | copy-start | bytes 484
  1.6 5.9 %collective-permute-start = (bf16[2,2,64,128]{3,2,1,0:T(8,128)(2,1)S(1)}, bf16[2,2,64,128]{3,2,1,0:T(8,128)(2,1)S(1)}, u32[]{:S(2)}, u32[]{:S(2)}) collective-permute-start(bf16[2,2,64,128]{3,2,1,0:T(8,128)(2,1)S(1)} %get-tuple-element.41), channel_id=1, source_target_pairs={{0,2},{1,3},{2,0},{3,1},{4,6},{5,7},{6,4},{7,5},{8,10},{9,11},{10,... | collective-permute-start | bytes 196616 | tf_op jit(solution)/shard_map/ppermute | solution.py:500
  4.8 5.1 %collective-permute-start.6 = (bf16[2,2,64,128]{3,2,1,0:T(8,128)(2,1)S(1)}, bf16[2,2,64,128]{3,2,1,0:T(8,128)(2,1)S(1)}, u32[]{:S(2)}, u32[]{:S(2)}) collective-permute-start(bf16[2,2,64,128]{3,2,1,0:T(8,128)(2,1)S(1)} %get-tuple-element.42.refs_6_.refs_2_.refs_8_), channel_id=1, source_target_pairs={{0,5},{1,4},{2,7},{3,6},{4,1},{5,0},{6,3},{7,2},{8,13},{9,12},{10,... | collective-permute-start | bytes 196616 | tf_op jit(solution)/shard_map/ppermute | solution.py:497
  7.1 5.7 %collective-permute-start.5 = (bf16[2,2,64,128]{3,2,1,0:T(8,128)(2,1)S(1)}, bf16[2,2,64,128]{3,2,1,0:T(8,128)(2,1)S(1)}, u32[]{:S(2)}, u32[]{:S(2)}) collective-permute-start(bf16[2,2,64,128]{3,2,1,0:T(8,128)(2,1)S(1)} %get-tuple-element.42.refs_6_.refs_2_.refs_8_), channel_id=1, source_target_pairs={{0,4},{4,0},{1,5},{5,1},{2,6},{6,2},{3,7},{7,3},{8,12},{12,8},{9,1... | collective-permute-start | bytes 196616 | tf_op jit(solution)/shard_map/ppermute | solution.py:491
  7.3 5.5 %collective-permute-start.4 = (bf16[2,2,64,128]{3,2,1,0:T(8,128)(2,1)S(1)}, bf16[2,2,64,128]{3,2,1,0:T(8,128)(2,1)S(1)}, u32[]{:S(2)}, u32[]{:S(2)}) collective-permute-start(bf16[2,2,64,128]{3,2,1,0:T(8,128)(2,1)S(1)} %get-tuple-element.42.refs_6_.refs_2_.refs_8_), channel_id=1, source_target_pairs={{0,1},{1,0},{2,3},{3,2},{4,5},{5,4},{6,7},{7,6},{8,9},{9,8},{10,11... | collective-permute-start | bytes 196616 | tf_op jit(solution)/shard_map/ppermute | solution.py:489
  7.5 6.0 %collective-permute-start.3 = (bf16[2,2,64,128]{3,2,1,0:T(8,128)(2,1)S(1)}, bf16[2,2,64,128]{3,2,1,0:T(8,128)(2,1)S(1)}, u32[]{:S(2)}, u32[]{:S(2)}) collective-permute-start(bf16[2,2,64,128]{3,2,1,0:T(8,128)(2,1)S(1)} %collective-permute-done.refs_5_.refs_6_.refs_12_), channel_id=1, source_target_pairs={{0,5},{1,4},{2,7},{3,6},{4,1},{5,0},{6,3},{7,2},{8,13},{9,12},{10,... | collective-permute-start | bytes 196616 | tf_op jit(solution)/shard_map/ppermute | solution.py:497
  9.7 3.8 %collective-permute-start.2 = (bf16[2,2,64,128]{3,2,1,0:T(8,128)(2,1)S(1)}, bf16[2,2,64,128]{3,2,1,0:T(8,128)(2,1)S(1)}, u32[]{:S(2)}, u32[]{:S(2)}) collective-permute-start(bf16[2,2,64,128]{3,2,1,0:T(8,128)(2,1)S(1)} %collective-permute-done.refs_5_.refs_6_.refs_12_), channel_id=1, source_target_pairs={{0,4},{4,0},{1,5},{5,1},{2,6},{6,2},{3,7},{7,3},{8,12},{12,8},{9,1... | collective-permute-start | bytes 196616 | tf_op jit(solution)/shard_map/ppermute | solution.py:491
  10.0 3.5 %collective-permute-start.1 = (bf16[2,2,64,128]{3,2,1,0:T(8,128)(2,1)S(1)}, bf16[2,2,64,128]{3,2,1,0:T(8,128)(2,1)S(1)}, u32[]{:S(2)}, u32[]{:S(2)}) collective-permute-start(bf16[2,2,64,128]{3,2,1,0:T(8,128)(2,1)S(1)} %collective-permute-done.refs_5_.refs_6_.refs_12_), channel_id=1, source_target_pairs={{0,1},{1,0},{2,3},{3,2},{4,5},{5,4},{6,7},{7,6},{8,9},{9,8},{10,11... | collective-permute-start | bytes 196616 | tf_op jit(solution)/shard_map/ppermute | solution.py:489
  10.9 1.0 %copy-start = (bf16[1,2,32,4096]{3,2,1,0:T(8,128)(2,1)S(1)}, bf16[1,2,32,4096]{3,2,1,0:T(8,128)(2,1)}, u32[]{:S(2)}) copy-start(bf16[1,2,32,4096]{3,2,1,0:T(8,128)(2,1)} %refs_0_.9) | copy-start | bytes 1572868
  11.9 1.0 %copy-start.1 = (bf16[1,2,32,4096]{3,2,1,0:T(8,128)(2,1)S(1)}, bf16[1,2,32,4096]{3,2,1,0:T(8,128)(2,1)}, u32[]{:S(2)}) copy-start(bf16[1,2,32,4096]{3,2,1,0:T(8,128)(2,1)} %refs_0_.9) | copy-start | bytes 1572868
  14.3 9.8 %collective-permute-start.8 = (bf16[32,4096]{1,0:T(8,128)(2,1)S(1)}, bf16[32,4096]{1,0:T(8,128)(2,1)S(1)}, u32[]{:S(2)}, u32[]{:S(2)}) collective-permute-start(bf16[32,4096]{1,0:T(8,128)(2,1)S(1)} %get-tuple-element.46.refs_5_), channel_id=1, source_target_pairs={{16,8},{17,9},{18,10},{19,11},{20,12},{21,13},{22,14},{23,15}} | collective-permute-start | bytes 786440 | tf_op jit(solution)/shard_map/ppermute | solution.py:560
  15.6 8.5 %collective-permute-start.7 = (bf16[32,4096]{1,0:T(8,128)(2,1)S(1)}, bf16[32,4096]{1,0:T(8,128)(2,1)S(1)}, u32[]{:S(2)}, u32[]{:S(2)}) collective-permute-start(bf16[32,4096]{1,0:T(8,128)(2,1)S(1)} %get-tuple-element.46.refs_5_), channel_id=1, source_target_pairs={{0,8},{8,0},{16,24},{24,16},{1,9},{9,1},{17,25},{25,17},{2,10},{10... | collective-permute-start | bytes 786440 | tf_op jit(solution)/shard_map/ppermute | solution.py:563
  18.5 5.5 %copy-start.4 = (bf16[1,32,4096]{2,1,0:T(8,128)(2,1)S(1)}, bf16[1,32,4096]{2,1,0:T(8,128)(2,1)}, u32[]{:S(2)}) copy-start(bf16[1,32,4096]{2,1,0:T(8,128)(2,1)} %refs_3_.3) | copy-start | bytes 786436
  18.6 8.9 %collective-permute-start.9 = (bf16[2,256,128]{2,1,0:T(8,128)(2,1)S(1)}, bf16[2,256,128]{2,1,0:T(8,128)(2,1)S(1)}, u32[]{:S(2)}, u32[]{:S(2)}) collective-permute-start(bf16[2,256,128]{2,1,0:T(8,128)(2,1)S(1)} %get-tuple-element.56), channel_id=1, source_target_pairs={{0,4},{4,0},{1,5},{5,1},{2,6},{6,2},{3,7},{7,3},{8,12},{12,8},{9,1... | collective-permute-start | bytes 393224 | tf_op jit(solution)/shard_map/ppermute | solution.py:491
  24.7 4.7 %collective-permute-start.11 = (bf16[288,128]{1,0:T(8,128)(2,1)S(1)}, bf16[288,128]{1,0:T(8,128)(2,1)S(1)}, u32[]{:S(2)}, u32[]{:S(2)}) collective-permute-start(bf16[288,128]{1,0:T(8,128)(2,1)S(1)} %get-tuple-element.62), channel_id=1, source_target_pairs={{0,5},{1,4},{2,7},{3,6},{4,1},{5,0},{6,3},{7,2},{8,13},{9,12},{10,... | collective-permute-start | bytes 221192 | tf_op jit(solution)/shard_map/ppermute | solution.py:497
  25.9 3.8 %collective-permute-start.12 = (bf16[288,128]{1,0:T(8,128)(2,1)S(1)}, bf16[288,128]{1,0:T(8,128)(2,1)S(1)}, u32[]{:S(2)}, u32[]{:S(2)}) collective-permute-start(bf16[288,128]{1,0:T(8,128)(2,1)S(1)} %get-tuple-element.63), channel_id=1, source_target_pairs={{0,4},{4,0},{1,5},{5,1},{2,6},{6,2},{3,7},{7,3},{8,12},{12,8},{9,1... | collective-permute-start | bytes 221192 | tf_op jit(solution)/shard_map/ppermute | solution.py:491
  26.6 3.5 %collective-permute-start.13 = (bf16[288,128]{1,0:T(8,128)(2,1)S(1)}, bf16[288,128]{1,0:T(8,128)(2,1)S(1)}, u32[]{:S(2)}, u32[]{:S(2)}) collective-permute-start(bf16[288,128]{1,0:T(8,128)(2,1)S(1)} %get-tuple-element.64), channel_id=1, source_target_pairs={{0,1},{1,0},{2,3},{3,2},{4,5},{5,4},{6,7},{7,6},{8,9},{9,8},{10,11... | collective-permute-start | bytes 221192 | tf_op jit(solution)/shard_map/ppermute | solution.py:489
  27.5 4.9 %collective-permute-start.10 = (bf16[256,128]{1,0:T(8,128)(2,1)S(1)}, bf16[256,128]{1,0:T(8,128)(2,1)S(1)}, u32[]{:S(2)}, u32[]{:S(2)}) collective-permute-start(bf16[256,128]{1,0:T(8,128)(2,1)S(1)} %get-tuple-element.58), channel_id=1, source_target_pairs={{0,1},{1,0},{2,3},{3,2},{4,5},{5,4},{6,7},{7,6},{8,9},{9,8},{10,11... | collective-permute-start | bytes 196616 | tf_op jit(solution)/shard_map/ppermute | solution.py:489
  30.1 6.1 %collective-permute-start.15 = (bf16[160,128]{1,0:T(8,128)(2,1)S(1)}, bf16[160,128]{1,0:T(8,128)(2,1)S(1)}, u32[]{:S(2)}, u32[]{:S(2)}) collective-permute-start(bf16[160,128]{1,0:T(8,128)(2,1)S(1)} %get-tuple-element.67), channel_id=1, source_target_pairs={{0,2},{1,3},{2,0},{3,1},{4,6},{5,7},{6,4},{7,5},{8,10},{9,11},{10,... | collective-permute-start | bytes 122888 | tf_op jit(solution)/shard_map/ppermute | solution.py:500
  32.4 3.7 %collective-permute-start.14 = (bf16[128,128]{1,0:T(8,128)(2,1)S(1)}, bf16[128,128]{1,0:T(8,128)(2,1)S(1)}, u32[]{:S(2)}, u32[]{:S(2)}) collective-permute-start(bf16[128,128]{1,0:T(8,128)(2,1)S(1)} %get-tuple-element.66), channel_id=1, source_target_pairs={{0,2},{1,3},{2,0},{3,1},{4,6},{5,7},{6,4},{7,5},{8,10},{9,11},{10,... | collective-permute-start | bytes 98312 | tf_op jit(solution)/shard_map/ppermute | solution.py:500

commit v12 on v11

--- a/solution.py
+++ b/solution.py
@@ -435,7 +435,8 @@
 
 def finish_kernel(sizes, *refs):
     half = sizes[1]
-    keep_refs, receive_refs, gain_ref = refs[:TICKS], refs[TICKS : 2 * TICKS], refs[2 * TICKS]
+    keep_refs, receive_refs = refs[:TICKS][::-1], refs[TICKS : 2 * TICKS][::-1]
+    gain_ref = refs[2 * TICKS]
     key_ref, value_ref, gain_out_ref = refs[2 * TICKS + 1 :]
     parity = lax.axis_index("tp") // (sizes[3] // 2)
     block = 2 * half
@@ -648,7 +649,7 @@
     key_grads, value_grads, gain_grads = call(
         functools.partial(finish_kernel, sizes),
         "finish",
-        (keep_first, keep_second, to_far(send_first), to_far(send_second), gain_sum),
+        (keep_second, keep_first, to_far(send_second), to_far(send_first), gain_sum),
         [grads_shape, grads_shape, gain_shape],
     )
     return input_grads, key_grads, value_grads, gain_grads.reshape(1, columns)

time: 37.1 us -> 37.1 us (level)
  no operation moved by 1% of the time
where the time goes in v12:
time: 37.1 us; the launch traced here: 36.9 us
  starting transfers between devices  21 us (57%)
  waiting for transfers between devices  7.35 us (20%)
  Pallas kernels  5.63 us (15%)
  local copies, waits for them, and re-layouts  1.15 us (3%)
  other arithmetic  0.93 us (3%)
  between operations  0.8 us (2%)
    ppermute x3, starting transfers between devices, to_far(): lax.ppermute(value, 'tp', [(i, i ^ near_count) for i in range(tp_count)])  6.51 us
    ppermute x3, starting transfers between devices, to_near(): return lax.ppermute(value, ('ctx', 'tp'), pairs)  5.69 us
    pallas_call x12, Pallas kernels, call(): pl.pallas_call(kernel, out_shape=out_shape, in_specs=in_specs, out_specs=...  5.63 us
    ppermute x1, waiting for transfers between devices, on_device(): lax.ppermute(input_grad_first, 'pipe', [(i, i - 1) for i in range(2, pipe...  3.85 us
    ppermute x4, starting transfers between devices, to_near(): return lax.ppermute(value, 'tp', [(i, i ^ near) for i in range(tp_count)])  2.58 us
    ppermute x1, starting transfers between devices, on_device(): lax.ppermute(input_grad_first, 'pipe', [(i, i ^ 1) for i in range(pipe_co...  2.52 us
    ppermute x4, starting transfers between devices, to_near(): lax.ppermute(value, 'ctx', [(i, (i + step) % cycle) for i in range(cycle)])  2.44 us
    ppermute x3, waiting for transfers between devices, to_far(): lax.ppermute(value, 'tp', [(i, i ^ near_count) for i in range(tp_count)])  1.59 us
  transfers between devices with their start and end apart: 16, of which 5 were waited for; matrix products, arithmetic and copies ran while one was open for 0% of the time, Pallas kernels for 11%

profile of v12, /device:TPU:1, one launch (start us, length us, event | category | flops | bytes accessed | tf_op | source)
XLA Modules:
  0.0 36.9 jit_solution(6160661721038489932)
XLA Ops:
  0.6 0.0 copy-start.2
  0.6 0.9 %pad_maximum_fusion.both_ref = bf16[2,2,128,128]{3,2,1,0:T(8,128)(2,1)S(1)} fusion(bf16[1,2,128,128]{3,2,1,0:T(8,128)(2,1)} %param.9, bf16[1,2,128,128]{3,2,1,0:T(8,128)(2,1)} %param.8), kind=kLoop, calls=%fused_computation | loop fusion | flops 65536 | bytes 262144 | tf_op jit(solution)/shard_map/stack | solution.py:507
  1.6 0.0 copy-start.3
  1.6 0.0 copy-start.5
  1.6 3.2 %collective-permute-start = (bf16[2,2,64,128]{3,2,1,0:T(8,128)(2,1)S(1)}, bf16[2,2,64,128]{3,2,1,0:T(8,128)(2,1)S(1)}, u32[]{:S(2)}, u32[]{:S(2)}) collective-permute-start(bf16[2,2,64,128]{3,2,1,0:T(8,128)(2,1)S(1)} %get-tuple-element.41), channel_id=1, source_target_pairs={{0,2},{1,3},{2,0},{3,1},{4,6},{5,7},{6,4},{7,5},{8,10},{9,11},{10,... | collective-permute-start | bytes 196616 | tf_op jit(solution)/shard_map/ppermute | solution.py:501
  4.8 2.3 %collective-permute-start.6 = (bf16[2,2,64,128]{3,2,1,0:T(8,128)(2,1)S(1)}, bf16[2,2,64,128]{3,2,1,0:T(8,128)(2,1)S(1)}, u32[]{:S(2)}, u32[]{:S(2)}) collective-permute-start(bf16[2,2,64,128]{3,2,1,0:T(8,128)(2,1)S(1)} %get-tuple-element.42.refs_6_.refs_2_.refs_8_), channel_id=1, source_target_pairs={{0,5},{1,4},{2,7},{3,6},{4,1},{5,0},{6,3},{7,2},{8,13},{9,12},{10,... | collective-permute-start | bytes 196616 | tf_op jit(solution)/shard_map/ppermute | solution.py:498
  7.1 0.2 collective-permute-start.5
  7.3 0.2 collective-permute-start.4
  7.5 0.0 collective-permute-done.refs_5_.refs_6_.refs_12_
  7.5 2.3 %collective-permute-start.3 = (bf16[2,2,64,128]{3,2,1,0:T(8,128)(2,1)S(1)}, bf16[2,2,64,128]{3,2,1,0:T(8,128)(2,1)S(1)}, u32[]{:S(2)}, u32[]{:S(2)}) collective-permute-start(bf16[2,2,64,128]{3,2,1,0:T(8,128)(2,1)S(1)} %collective-permute-done.refs_5_.refs_6_.refs_12_), channel_id=1, source_target_pairs={{0,5},{1,4},{2,7},{3,6},{4,1},{5,0},{6,3},{7,2},{8,13},{9,12},{10,... | collective-permute-start | bytes 196616 | tf_op jit(solution)/shard_map/ppermute | solution.py:498
  9.7 0.2 collective-permute-start.2
  10.0 0.0 collective-permute-done.6.refs_9_.refs_5_.refs_11_
  10.0 0.9 %collective-permute-start.1 = (bf16[2,2,64,128]{3,2,1,0:T(8,128)(2,1)S(1)}, bf16[2,2,64,128]{3,2,1,0:T(8,128)(2,1)S(1)}, u32[]{:S(2)}, u32[]{:S(2)}) collective-permute-start(bf16[2,2,64,128]{3,2,1,0:T(8,128)(2,1)S(1)} %collective-permute-done.refs_5_.refs_6_.refs_12_), channel_id=1, source_target_pairs={{0,1},{1,0},{2,3},{3,2},{4,5},{5,4},{6,7},{7,6},{8,9},{9,8},{10,11... | collective-permute-start | bytes 196616 | tf_op jit(solution)/shard_map/ppermute | solution.py:490
  10.8 0.0 copy-done.3
  10.8 0.0 copy-done.5
  10.9 0.0 copy-start
  10.9 1.0 %copy-done = bf16[1,2,32,4096]{3,2,1,0:T(8,128)(2,1)S(1)} copy-done((bf16[1,2,32,4096]{3,2,1,0:T(8,128)(2,1)S(1)}, bf16[1,2,32,4096]{3,2,1,0:T(8,128)(2,1)}, u32[]{:S(2)}) %copy-start) | copy-done | bytes 524312
  11.9 0.0 copy-start.1
  11.9 0.9 %norm.1 = (bf16[2,32,4096]{2,1,0:T(8,128)(2,1)S(1)}, f32[2,32,128]{2,1,0:T(8,128)S(1)}, f32[2,128,256]{2,1,0:T(8,128)S(1)}) custom-call(s32[5,8]{1,0:T(8,128)S(1)} %copy-done.5, bf16[1,2,32,4096]{3,2,1,0:T(8,128)(2,1)S(1)} %copy-done, f32[1,4096]{1,0:T(1,128)S(1)} %copy-done.3), custom_call_target="tpu_custom_call" | custom-call | tf_op jit(solution)/shard_map/norm/pallas_call | solution.py:476
  12.8 0.0 collective-permute-done.5.refs_8_.refs_4_.refs_10_
  12.8 0.0 collective-permute-done.4.refs_7_.refs_3_.refs_9_
  12.8 0.0 copy-done.2
  12.9 0.1 copy-done.1
  12.9 0.5 %first_near_rows.1 = (bf16[2,256,128]{2,1,0:T(8,128)(2,1)S(1)}, bf16[2,128,256]{2,1,0:T(8,128)(2,1)S(1)}, bf16[2,128,256]{2,1,0:T(8,128)(2,1)S(1)}, f32[32,128]{1,0:T(8,128)S(1)}, bf16[2,2,128,256]{3,2,1,0:T(8,128)(2,1)S(1)}) custom-call(bf16[1,2,32,4096]{3,2,1,0:T(8,128)(2,1)S(1)} %copy-done.1, f32[1,4096]{1,0:T(1,128)S(1)} %copy-done.3, ...), custom_call_target="tpu_custom_call" | custom-call | tf_op jit(solution)/shard_map/first_near_rows/pallas_call | solution.py:476
  13.5 0.0 collective-permute-done.3.refs_8_.refs_9_.refs_15_
  13.5 0.0 collective-permute-done.2.refs_7_.refs_8_.refs_14_
  13.5 0.0 collective-permute-done.1.refs_6_.refs_7_.refs_13_
  13.5 0.8 %first_far_rows.1 = (bf16[32,4096]{1,0:T(8,128)(2,1)S(1)}, bf16[2,256,128]{2,1,0:T(8,128)(2,1)S(1)}, bf16[2,128,256]{2,1,0:T(8,128)(2,1)S(1)}, bf16[2,128,256]{2,1,0:T(8,128)(2,1)S(1)}) custom-call(bf16[1,2,32,4096]{3,2,1,0:T(8,128)(2,1)S(1)} %copy-done.1, f32[1,4096]{1,0:T(1,128)S(1)} %copy-done.3, f32[2,32,128]{2,1,0:T(8,128)S(1)} %get-tuple-element.38.refs_3_.refs_2_, ...), custom_call_target="tpu_custom_call" | custom-call | tf_op jit(solution)/shard_map/first_far_rows/pallas_call | solution.py:476
  14.3 1.3 %collective-permute-start.8 = (bf16[32,4096]{1,0:T(8,128)(2,1)S(1)}, bf16[32,4096]{1,0:T(8,128)(2,1)S(1)}, u32[]{:S(2)}, u32[]{:S(2)}) collective-permute-start(bf16[32,4096]{1,0:T(8,128)(2,1)S(1)} %get-tuple-element.46.refs_5_), channel_id=1, source_target_pairs={{16,8},{17,9},{18,10},{19,11},{20,12},{21,13},{22,14},{23,15}} | collective-permute-start | bytes 786440 | tf_op jit(solution)/shard_map/ppermute | solution.py:561
  15.6 2.5 %collective-permute-start.7 = (bf16[32,4096]{1,0:T(8,128)(2,1)S(1)}, bf16[32,4096]{1,0:T(8,128)(2,1)S(1)}, u32[]{:S(2)}, u32[]{:S(2)}) collective-permute-start(bf16[32,4096]{1,0:T(8,128)(2,1)S(1)} %get-tuple-element.46.refs_5_), channel_id=1, source_target_pairs={{0,8},{8,0},{16,24},{24,16},{1,9},{9,1},{17,25},{25,17},{2,10},{10... | collective-permute-start | bytes 786440 | tf_op jit(solution)/shard_map/ppermute | solution.py:564
  18.1 0.4 %first_keys.1 = (f32[32,128]{1,0:T(8,128)S(1)}, f32[2,256,128]{2,1,0:T(8,128)S(1)}, bf16[2,256,128]{2,1,0:T(8,128)(2,1)S(1)}) custom-call(bf16[1,2,32,4096]{3,2,1,0:T(8,128)(2,1)S(1)} %copy-done.1, bf16[2,32,4096]{2,1,0:T(8,128)(2,1)S(1)} %get-tuple-element.39.refs_2_.refs_1_, f32[2,32,128]{2,1,0:T(8,128)S(1)} %get-tuple-element.38.refs_3_.refs_2_, ...), custom_call_target="tpu_custom_call" | custom-call | tf_op jit(solution)/shard_map/first_keys/pallas_call | solution.py:476
  18.5 0.0 copy-start.4
  18.6 1.3 %collective-permute-start.12 = (bf16[2,256,128]{2,1,0:T(8,128)(2,1)S(1)}, bf16[2,256,128]{2,1,0:T(8,128)(2,1)S(1)}, u32[]{:S(2)}, u32[]{:S(2)}) collective-permute-start(bf16[2,256,128]{2,1,0:T(8,128)(2,1)S(1)} %get-tuple-element.62), channel_id=1, source_target_pairs={{0,4},{4,0},{1,5},{5,1},{2,6},{6,2},{3,7},{7,3},{8,12},{12,8},{9,1... | collective-permute-start | bytes 393224 | tf_op jit(solution)/shard_map/ppermute | solution.py:492
  19.9 0.4 second_probs.1.refs_6_
  20.2 3.9 %collective-permute-done.8.refs_5_ = bf16[32,4096]{1,0:T(8,128)(2,1)S(1)} collective-permute-done((bf16[32,4096]{1,0:T(8,128)(2,1)S(1)}, bf16[32,4096]{1,0:T(8,128)(2,1)S(1)}, u32[]{:S(2)}, u32[]{:S(2)}) %collective-permute-start.8) | collective-permute-done | bytes 262176 | tf_op jit(solution)/shard_map/ppermute | solution.py:561
  24.1 0.0 collective-permute-done.7.refs_4_
  24.1 0.0 copy-done.4
  24.1 0.6 %second_keys.1 = (bf16[4,256,128]{2,1,0:T(8,128)(2,1)S(1)}, f32[32,128]{1,0:T(8,128)S(1)}, f32[256,128]{1,0:T(8,128)S(1)}, bf16[32,4096]{1,0:T(8,128)(2,1)S(1)},...) custom-call(bf16[1,2,32,4096]{3,2,1,0:T(8,128)(2,1)S(1)} %copy-done.1, ...), custom_call_target="tpu_custom_call" | custom-call | tf_op jit(solution)/shard_map/second_keys/pallas_call | solution.py:476
  24.7 1.2 %collective-permute-start.9 = (bf16[288,128]{1,0:T(8,128)(2,1)S(1)}, bf16[288,128]{1,0:T(8,128)(2,1)S(1)}, u32[]{:S(2)}, u32[]{:S(2)}) collective-permute-start(bf16[288,128]{1,0:T(8,128)(2,1)S(1)} %get-tuple-element.57), channel_id=1, source_target_pairs={{0,5},{1,4},{2,7},{3,6},{4,1},{5,0},{6,3},{7,2},{8,13},{9,12},{10,... | collective-permute-start | bytes 221192 | tf_op jit(solution)/shard_map/ppermute | solution.py:498
  25.9 0.7 %collective-permute-start.10 = (bf16[288,128]{1,0:T(8,128)(2,1)S(1)}, bf16[288,128]{1,0:T(8,128)(2,1)S(1)}, u32[]{:S(2)}, u32[]{:S(2)}) collective-permute-start(bf16[288,128]{1,0:T(8,128)(2,1)S(1)} %get-tuple-element.58), channel_id=1, source_target_pairs={{0,4},{4,0},{1,5},{5,1},{2,6},{6,2},{3,7},{7,3},{8,12},{12,8},{9,1... | collective-permute-start | bytes 221192 | tf_op jit(solution)/shard_map/ppermute | solution.py:492
  26.6 0.8 %collective-permute-start.11 = (bf16[288,128]{1,0:T(8,128)(2,1)S(1)}, bf16[288,128]{1,0:T(8,128)(2,1)S(1)}, u32[]{:S(2)}, u32[]{:S(2)}) collective-permute-start(bf16[288,128]{1,0:T(8,128)(2,1)S(1)} %get-tuple-element.59), channel_id=1, source_target_pairs={{0,1},{1,0},{2,3},{3,2},{4,5},{5,4},{6,7},{7,6},{8,9},{9,8},{10,11... | collective-permute-start | bytes 221192 | tf_op jit(solution)/shard_map/ppermute | solution.py:490
  27.4 0.0 collective-permute-done.12.refs_1_
  27.5 0.7 %collective-permute-start.13 = (bf16[256,128]{1,0:T(8,128)(2,1)S(1)}, bf16[256,128]{1,0:T(8,128)(2,1)S(1)}, u32[]{:S(2)}, u32[]{:S(2)}) collective-permute-start(bf16[256,128]{1,0:T(8,128)(2,1)S(1)} %get-tuple-element.64), channel_id=1, source_target_pairs={{0,1},{1,0},{2,3},{3,2},{4,5},{5,4},{6,7},{7,6},{8,9},{9,8},{10,11... | collective-permute-start | bytes 196616 | tf_op jit(solution)/shard_map/ppermute | solution.py:490
  28.2 1.2 %collective-permute-done.9.refs_2_ = bf16[288,128]{1,0:T(8,128)(2,1)S(1)} collective-permute-done((bf16[288,128]{1,0:T(8,128)(2,1)S(1)}, bf16[288,128]{1,0:T(8,128)(2,1)S(1)}, u32[]{:S(2)}, u32[]{:S(2)}) %collective-permute-start.9) | collective-permute-done | bytes 73760 | tf_op jit(solution)/shard_map/ppermute | solution.py:498
  29.4 0.3 collective-permute-done.10.refs_3_
  29.7 0.4 collective-permute-done.11.refs_4_
  30.0 0.1 second_near.1
  30.1 2.3 %collective-permute-start.14 = (bf16[160,128]{1,0:T(8,128)(2,1)S(1)}, bf16[160,128]{1,0:T(8,128)(2,1)S(1)}, u32[]{:S(2)}, u32[]{:S(2)}) collective-permute-start(bf16[160,128]{1,0:T(8,128)(2,1)S(1)} %get-tuple-element.66), channel_id=1, source_target_pairs={{0,2},{1,3},{2,0},{3,1},{4,6},{5,7},{6,4},{7,5},{8,10},{9,11},{10,... | collective-permute-start | bytes 122888 | tf_op jit(solution)/shard_map/ppermute | solution.py:501
  32.4 0.0 collective-permute-done.13.refs_0_
  32.4 1.0 %collective-permute-start.15 = (bf16[128,128]{1,0:T(8,128)(2,1)S(1)}, bf16[128,128]{1,0:T(8,128)(2,1)S(1)}, u32[]{:S(2)}, u32[]{:S(2)}) collective-permute-start(bf16[128,128]{1,0:T(8,128)(2,1)S(1)} %get-tuple-element.67), channel_id=1, source_target_pairs={{0,2},{1,3},{2,0},{3,1},{4,6},{5,7},{6,4},{7,5},{8,10},{9,11},{10,... | collective-permute-start | bytes 98312 | tf_op jit(solution)/shard_map/ppermute | solution.py:501
  33.4 1.2 %second_rows.1 = bf16[1,2,32,4096]{3,2,1,0:T(8,128)(2,1)} custom-call(bf16[1,2,32,4096]{3,2,1,0:T(8,128)(2,1)S(1)} %copy-done.1, f32[1,4096]{1,0:T(1,128)S(1)} %copy-done.3, f32[2,32,128]{2,1,0:T(8,128)S(1)} %get-tuple-element.38.refs_3_.refs_2_, bf16[32,4096]{1,0:T(8,128)(2,1)S(1)} %get-tuple-element.53.refs_3_, ...), custom_call_target="tpu_custom_call" | custom-call | tf_op jit(solution)/shard_map/second_rows/pallas_call | solution.py:476
  34.6 1.6 %collective-permute-done.15.refs_3_ = bf16[128,128]{1,0:T(8,128)(2,1)S(1)} collective-permute-done((bf16[128,128]{1,0:T(8,128)(2,1)S(1)}, bf16[128,128]{1,0:T(8,128)(2,1)S(1)}, u32[]{:S(2)}, u32[]{:S(2)}) %collective-permute-start.15) | collective-permute-done | bytes 32800 | tf_op jit(solution)/shard_map/ppermute | solution.py:501
  36.2 0.0 collective-permute-done.14.refs_2_
  36.2 0.7 %finish.1 = (f32[1,2,128,128]{3,2,1,0:T(8,128)}, f32[1,2,128,128]{3,2,1,0:T(8,128)}, f32[32,128]{1,0:T(8,128)}) custom-call(f32[128,128]{1,0:T(8,128)S(1)} %get-tuple-element.60.refs_0_, f32[128,128]{1,0:T(8,128)S(1)} %get-tuple-element.65.refs_1_, bf16[160,128]{1,0:T(8,128)(2,1)S(1)} %collective-permute-done.14.refs_2_, ...), custom_call_target="tpu_custom_call" | custom-call | tf_op jit(solution)/shard_map/finish/pallas_call | solution.py:476
  (3 shorter events, 0.1 us)
Async XLA Ops:
  0.6 12.2 %copy-start.2 = (bf16[1,32,4096]{2,1,0:T(8,128)(2,1)S(1)}, bf16[1,32,4096]{2,1,0:T(8,128)(2,1)}, u32[]{:S(2)}) copy-start(bf16[1,32,4096]{2,1,0:T(8,128)(2,1)} %refs_3_.2) | copy-start | bytes 786436
  1.6 9.3 %copy-start.3 = (f32[1,4096]{1,0:T(1,128)S(1)}, f32[1,4096]{1,0:T(1,128)}, u32[]{:S(2)}) copy-start(f32[1,4096]{1,0:T(1,128)} %refs_1_.5) | copy-start | bytes 49156
  1.6 9.3 %copy-start.5 = (s32[5,8]{1,0:T(8,128)S(1)}, s32[5,8]{1,0:T(8,128)}, u32[]{:S(2)}) copy-start(s32[5,8]{1,0:T(8,128)} %doc_ref.1) | copy-start | bytes 484
  1.6 5.9 %collective-permute-start = (bf16[2,2,64,128]{3,2,1,0:T(8,128)(2,1)S(1)}, bf16[2,2,64,128]{3,2,1,0:T(8,128)(2,1)S(1)}, u32[]{:S(2)}, u32[]{:S(2)}) collective-permute-start(bf16[2,2,64,128]{3,2,1,0:T(8,128)(2,1)S(1)} %get-tuple-element.41), channel_id=1, source_target_pairs={{0,2},{1,3},{2,0},{3,1},{4,6},{5,7},{6,4},{7,5},{8,10},{9,11},{10,... | collective-permute-start | bytes 196616 | tf_op jit(solution)/shard_map/ppermute | solution.py:501
  4.8 5.1 %collective-permute-start.6 = (bf16[2,2,64,128]{3,2,1,0:T(8,128)(2,1)S(1)}, bf16[2,2,64,128]{3,2,1,0:T(8,128)(2,1)S(1)}, u32[]{:S(2)}, u32[]{:S(2)}) collective-permute-start(bf16[2,2,64,128]{3,2,1,0:T(8,128)(2,1)S(1)} %get-tuple-element.42.refs_6_.refs_2_.refs_8_), channel_id=1, source_target_pairs={{0,5},{1,4},{2,7},{3,6},{4,1},{5,0},{6,3},{7,2},{8,13},{9,12},{10,... | collective-permute-start | bytes 196616 | tf_op jit(solution)/shard_map/ppermute | solution.py:498
  7.1 5.7 %collective-permute-start.5 = (bf16[2,2,64,128]{3,2,1,0:T(8,128)(2,1)S(1)}, bf16[2,2,64,128]{3,2,1,0:T(8,128)(2,1)S(1)}, u32[]{:S(2)}, u32[]{:S(2)}) collective-permute-start(bf16[2,2,64,128]{3,2,1,0:T(8,128)(2,1)S(1)} %get-tuple-element.42.refs_6_.refs_2_.refs_8_), channel_id=1, source_target_pairs={{0,4},{4,0},{1,5},{5,1},{2,6},{6,2},{3,7},{7,3},{8,12},{12,8},{9,1... | collective-permute-start | bytes 196616 | tf_op jit(solution)/shard_map/ppermute | solution.py:492
  7.3 5.5 %collective-permute-start.4 = (bf16[2,2,64,128]{3,2,1,0:T(8,128)(2,1)S(1)}, bf16[2,2,64,128]{3,2,1,0:T(8,128)(2,1)S(1)}, u32[]{:S(2)}, u32[]{:S(2)}) collective-permute-start(bf16[2,2,64,128]{3,2,1,0:T(8,128)(2,1)S(1)} %get-tuple-element.42.refs_6_.refs_2_.refs_8_), channel_id=1, source_target_pairs={{0,1},{1,0},{2,3},{3,2},{4,5},{5,4},{6,7},{7,6},{8,9},{9,8},{10,11... | collective-permute-start | bytes 196616 | tf_op jit(solution)/shard_map/ppermute | solution.py:490
  7.5 6.0 %collective-permute-start.3 = (bf16[2,2,64,128]{3,2,1,0:T(8,128)(2,1)S(1)}, bf16[2,2,64,128]{3,2,1,0:T(8,128)(2,1)S(1)}, u32[]{:S(2)}, u32[]{:S(2)}) collective-permute-start(bf16[2,2,64,128]{3,2,1,0:T(8,128)(2,1)S(1)} %collective-permute-done.refs_5_.refs_6_.refs_12_), channel_id=1, source_target_pairs={{0,5},{1,4},{2,7},{3,6},{4,1},{5,0},{6,3},{7,2},{8,13},{9,12},{10,... | collective-permute-start | bytes 196616 | tf_op jit(solution)/shard_map/ppermute | solution.py:498
  9.7 3.8 %collective-permute-start.2 = (bf16[2,2,64,128]{3,2,1,0:T(8,128)(2,1)S(1)}, bf16[2,2,64,128]{3,2,1,0:T(8,128)(2,1)S(1)}, u32[]{:S(2)}, u32[]{:S(2)}) collective-permute-start(bf16[2,2,64,128]{3,2,1,0:T(8,128)(2,1)S(1)} %collective-permute-done.refs_5_.refs_6_.refs_12_), channel_id=1, source_target_pairs={{0,4},{4,0},{1,5},{5,1},{2,6},{6,2},{3,7},{7,3},{8,12},{12,8},{9,1... | collective-permute-start | bytes 196616 | tf_op jit(solution)/shard_map/ppermute | solution.py:492
  10.0 3.5 %collective-permute-start.1 = (bf16[2,2,64,128]{3,2,1,0:T(8,128)(2,1)S(1)}, bf16[2,2,64,128]{3,2,1,0:T(8,128)(2,1)S(1)}, u32[]{:S(2)}, u32[]{:S(2)}) collective-permute-start(bf16[2,2,64,128]{3,2,1,0:T(8,128)(2,1)S(1)} %collective-permute-done.refs_5_.refs_6_.refs_12_), channel_id=1, source_target_pairs={{0,1},{1,0},{2,3},{3,2},{4,5},{5,4},{6,7},{7,6},{8,9},{9,8},{10,11... | collective-permute-start | bytes 196616 | tf_op jit(solution)/shard_map/ppermute | solution.py:490
  10.9 1.0 %copy-start = (bf16[1,2,32,4096]{3,2,1,0:T(8,128)(2,1)S(1)}, bf16[1,2,32,4096]{3,2,1,0:T(8,128)(2,1)}, u32[]{:S(2)}) copy-start(bf16[1,2,32,4096]{3,2,1,0:T(8,128)(2,1)} %refs_0_.9) | copy-start | bytes 1572868
  11.9 1.0 %copy-start.1 = (bf16[1,2,32,4096]{3,2,1,0:T(8,128)(2,1)S(1)}, bf16[1,2,32,4096]{3,2,1,0:T(8,128)(2,1)}, u32[]{:S(2)}) copy-start(bf16[1,2,32,4096]{3,2,1,0:T(8,128)(2,1)} %refs_0_.9) | copy-start | bytes 1572868
  14.3 9.8 %collective-permute-start.8 = (bf16[32,4096]{1,0:T(8,128)(2,1)S(1)}, bf16[32,4096]{1,0:T(8,128)(2,1)S(1)}, u32[]{:S(2)}, u32[]{:S(2)}) collective-permute-start(bf16[32,4096]{1,0:T(8,128)(2,1)S(1)} %get-tuple-element.46.refs_5_), channel_id=1, source_target_pairs={{16,8},{17,9},{18,10},{19,11},{20,12},{21,13},{22,14},{23,15}} | collective-permute-start | bytes 786440 | tf_op jit(solution)/shard_map/ppermute | solution.py:561
  15.6 8.5 %collective-permute-start.7 = (bf16[32,4096]{1,0:T(8,128)(2,1)S(1)}, bf16[32,4096]{1,0:T(8,128)(2,1)S(1)}, u32[]{:S(2)}, u32[]{:S(2)}) collective-permute-start(bf16[32,4096]{1,0:T(8,128)(2,1)S(1)} %get-tuple-element.46.refs_5_), channel_id=1, source_target_pairs={{0,8},{8,0},{16,24},{24,16},{1,9},{9,1},{17,25},{25,17},{2,10},{10... | collective-permute-start | bytes 786440 | tf_op jit(solution)/shard_map/ppermute | solution.py:564
  18.5 5.5 %copy-start.4 = (bf16[1,32,4096]{2,1,0:T(8,128)(2,1)S(1)}, bf16[1,32,4096]{2,1,0:T(8,128)(2,1)}, u32[]{:S(2)}) copy-start(bf16[1,32,4096]{2,1,0:T(8,128)(2,1)} %refs_3_.3) | copy-start | bytes 786436
  18.6 8.9 %collective-permute-start.12 = (bf16[2,256,128]{2,1,0:T(8,128)(2,1)S(1)}, bf16[2,256,128]{2,1,0:T(8,128)(2,1)S(1)}, u32[]{:S(2)}, u32[]{:S(2)}) collective-permute-start(bf16[2,256,128]{2,1,0:T(8,128)(2,1)S(1)} %get-tuple-element.62), channel_id=1, source_target_pairs={{0,4},{4,0},{1,5},{5,1},{2,6},{6,2},{3,7},{7,3},{8,12},{12,8},{9,1... | collective-permute-start | bytes 393224 | tf_op jit(solution)/shard_map/ppermute | solution.py:492
  24.7 4.7 %collective-permute-start.9 = (bf16[288,128]{1,0:T(8,128)(2,1)S(1)}, bf16[288,128]{1,0:T(8,128)(2,1)S(1)}, u32[]{:S(2)}, u32[]{:S(2)}) collective-permute-start(bf16[288,128]{1,0:T(8,128)(2,1)S(1)} %get-tuple-element.57), channel_id=1, source_target_pairs={{0,5},{1,4},{2,7},{3,6},{4,1},{5,0},{6,3},{7,2},{8,13},{9,12},{10,... | collective-permute-start | bytes 221192 | tf_op jit(solution)/shard_map/ppermute | solution.py:498
  25.9 3.8 %collective-permute-start.10 = (bf16[288,128]{1,0:T(8,128)(2,1)S(1)}, bf16[288,128]{1,0:T(8,128)(2,1)S(1)}, u32[]{:S(2)}, u32[]{:S(2)}) collective-permute-start(bf16[288,128]{1,0:T(8,128)(2,1)S(1)} %get-tuple-element.58), channel_id=1, source_target_pairs={{0,4},{4,0},{1,5},{5,1},{2,6},{6,2},{3,7},{7,3},{8,12},{12,8},{9,1... | collective-permute-start | bytes 221192 | tf_op jit(solution)/shard_map/ppermute | solution.py:492
  26.6 3.5 %collective-permute-start.11 = (bf16[288,128]{1,0:T(8,128)(2,1)S(1)}, bf16[288,128]{1,0:T(8,128)(2,1)S(1)}, u32[]{:S(2)}, u32[]{:S(2)}) collective-permute-start(bf16[288,128]{1,0:T(8,128)(2,1)S(1)} %get-tuple-element.59), channel_id=1, source_target_pairs={{0,1},{1,0},{2,3},{3,2},{4,5},{5,4},{6,7},{7,6},{8,9},{9,8},{10,11... | collective-permute-start | bytes 221192 | tf_op jit(solution)/shard_map/ppermute | solution.py:490
  27.5 4.9 %collective-permute-start.13 = (bf16[256,128]{1,0:T(8,128)(2,1)S(1)}, bf16[256,128]{1,0:T(8,128)(2,1)S(1)}, u32[]{:S(2)}, u32[]{:S(2)}) collective-permute-start(bf16[256,128]{1,0:T(8,128)(2,1)S(1)} %get-tuple-element.64), channel_id=1, source_target_pairs={{0,1},{1,0},{2,3},{3,2},{4,5},{5,4},{6,7},{7,6},{8,9},{9,8},{10,11... | collective-permute-start | bytes 196616 | tf_op jit(solution)/shard_map/ppermute | solution.py:490
  30.1 6.1 %collective-permute-start.14 = (bf16[160,128]{1,0:T(8,128)(2,1)S(1)}, bf16[160,128]{1,0:T(8,128)(2,1)S(1)}, u32[]{:S(2)}, u32[]{:S(2)}) collective-permute-start(bf16[160,128]{1,0:T(8,128)(2,1)S(1)} %get-tuple-element.66), channel_id=1, source_target_pairs={{0,2},{1,3},{2,0},{3,1},{4,6},{5,7},{6,4},{7,5},{8,10},{9,11},{10,... | collective-permute-start | bytes 122888 | tf_op jit(solution)/shard_map/ppermute | solution.py:501
  32.4 3.7 %collective-permute-start.15 = (bf16[128,128]{1,0:T(8,128)(2,1)S(1)}, bf16[128,128]{1,0:T(8,128)(2,1)S(1)}, u32[]{:S(2)}, u32[]{:S(2)}) collective-permute-start(bf16[128,128]{1,0:T(8,128)(2,1)S(1)} %get-tuple-element.67), channel_id=1, source_target_pairs={{0,2},{1,3},{2,0},{3,1},{4,6},{5,7},{6,4},{7,5},{8,10},{9,11},{10,... | collective-permute-start | bytes 98312 | tf_op jit(solution)/shard_map/ppermute | solution.py:501

commit v13 on v12

--- a/solution.py
+++ b/solution.py
@@ -295,9 +295,12 @@
         )
         for kind, part in enumerate(parts):
             here = place_of(sizes, far, kind)
-            own_ref[near, here, :] = part[:half]
-            for step, ref in enumerate(send_refs, 1):
-                ref[near, here, :] = part[step * half : (step + 1) * half].astype(BF16)
+            for step in range(cycle):
+                piece = part[step * half : (step + 1) * half]
+                if near == 0:
+                    own_ref[step, here, :] = piece
+                else:
+                    send_refs[near - 1][step, here, :] = piece.astype(BF16)
         gain_terms(columns_of, query_grad_refs[far][near], normed_of, gain_rows_ref)
 
 
@@ -359,16 +362,16 @@
 
 
 def first_sum_kernel(sizes, *refs):
-    cycle = sizes[2]
-    parts, own_ref, message_refs = refs[:cycle], refs[cycle], refs[cycle + 1 :]
-    for near in range(sizes[3] // 2):
-        total = parts[0][near]
+    near_count = sizes[3] // 2
+    parts, own_ref, message_refs = refs[:near_count], refs[near_count], refs[near_count + 1 :]
+    for step in range(sizes[2]):
+        total = parts[0][step]
         for ref in parts[1:]:
-            total = total + ref[near].astype(F32)
-        if near == 0:
+            total = total + ref[step].astype(F32)
+        if step == 0:
             own_ref[...] = total
         else:
-            message_refs[near - 1][...] = total.astype(BF16)
+            message_refs[step - 1][...] = total.astype(BF16)
 
 
 def second_rows_kernel(sizes, *refs):
@@ -565,7 +568,7 @@
     gain_shape = shape((gain_count, HD), F32)
     pair_rows = 2 * block
     own_shape = shape((pair_rows, HD), F32)
-    first_sums = (near_count, pair_rows, HD)
+    first_sums = (cycle, pair_rows, HD)
     gain_first, *sums_first = call(
         functools.partial(first_keys_kernel, sizes),
         "first_keys",
@@ -581,10 +584,10 @@
             probs_near,
             probs_far,
         ),
-        [gain_shape, shape(first_sums, F32)] + [shape(first_sums, BF16)] * (cycle - 1),
+        [gain_shape, shape(first_sums, F32)] + [shape(first_sums, BF16)] * (near_count - 1),
     )
     sums_first = sums_first[:1] + [
-        to_near(value, -step, 0) for step, value in enumerate(sums_first[1:], 1)
+        to_near(value, 0, near) for near, value in enumerate(sums_first[1:], 1)
     ]
     (probs_second,) = call(
         functools.partial(second_probs_kernel, sizes),
@@ -616,9 +619,9 @@
         functools.partial(first_sum_kernel, sizes),
         "first_sum",
         sums_first,
-        [own_shape] + [shape((pair_rows, HD), BF16)] * (near_count - 1),
-    )
-    received_first = [to_near(value, 0, near) for near, value in enumerate(sends_first, 1)]
+        [own_shape] + [shape((pair_rows, HD), BF16)] * (cycle - 1),
+    )
+    received_first = [to_near(value, -step, 0) for step, value in enumerate(sends_first, 1)]
     (input_grads,) = call(
         functools.partial(second_rows_kernel, sizes),
         "second_rows",

time: 37.1 us -> 37 us (level)
  the two profiles are of different devices: /device:TPU:1 before, /device:TPU:2 now
where the time goes in v13:
time: 37 us; the launch traced here: 36.8 us
  starting transfers between devices  21.3 us (58%)
  waiting for transfers between devices  6.94 us (19%)
  Pallas kernels  5.63 us (15%)
  local copies, waits for them, and re-layouts  1.15 us (3%)
  other arithmetic  0.93 us (3%)
  between operations  0.79 us (2%)
    ppermute x3, starting transfers between devices, to_near(): return lax.ppermute(value, ('ctx', 'tp'), pairs)  6.53 us
    ppermute x3, starting transfers between devices, to_far(): lax.ppermute(value, 'tp', [(i, i ^ near_count) for i in range(tp_count)])  6.43 us
    pallas_call x12, Pallas kernels, call(): pl.pallas_call(kernel, out_shape=out_shape, in_specs=in_specs, out_specs=...  5.63 us
    ppermute x4, starting transfers between devices, to_near(): lax.ppermute(value, 'ctx', [(i, (i + step) % cycle) for i in range(cycle)])  3.57 us
    ppermute x4, starting transfers between devices, to_near(): return lax.ppermute(value, 'tp', [(i, i ^ near) for i in range(tp_count)])  3.44 us
    ppermute x3, waiting for transfers between devices, to_far(): lax.ppermute(value, 'tp', [(i, i ^ near_count) for i in range(tp_count)])  2.62 us
    ppermute x1, waiting for transfers between devices, on_device(): lax.ppermute(input_grad_first, 'pipe', [(i, i - 1) for i in range(2, pipe...  1.98 us
    ppermute x4, waiting for transfers between devices, to_near(): lax.ppermute(value, 'ctx', [(i, (i + step) % cycle) for i in range(cycle)])  1.41 us
  transfers between devices with their start and end apart: 16, of which 7 were waited for; matrix products, arithmetic and copies ran while one was open for 0% of the time, Pallas kernels for 11%

profile of v13, /device:TPU:2, one launch (start us, length us, event | category | flops | bytes accessed | tf_op | source)
XLA Modules:
  0.0 36.8 jit_solution(6779161182418023477)
XLA Ops:
  0.6 0.0 copy-start.2
  0.6 0.9 %pad_maximum_fusion.both_ref = bf16[2,2,128,128]{3,2,1,0:T(8,128)(2,1)S(1)} fusion(bf16[1,2,128,128]{3,2,1,0:T(8,128)(2,1)} %param.9, bf16[1,2,128,128]{3,2,1,0:T(8,128)(2,1)} %param.8), kind=kLoop, calls=%fused_computation | loop fusion | flops 65536 | bytes 262144 | tf_op jit(solution)/shard_map/stack | solution.py:510
  1.6 0.0 copy-start.3
  1.6 0.0 copy-start.5
  1.6 2.7 %collective-permute-start = (bf16[2,2,64,128]{3,2,1,0:T(8,128)(2,1)S(1)}, bf16[2,2,64,128]{3,2,1,0:T(8,128)(2,1)S(1)}, u32[]{:S(2)}, u32[]{:S(2)}) collective-permute-start(bf16[2,2,64,128]{3,2,1,0:T(8,128)(2,1)S(1)} %get-tuple-element.41), channel_id=1, source_target_pairs={{0,2},{1,3},{2,0},{3,1},{4,6},{5,7},{6,4},{7,5},{8,10},{9,11},{10,... | collective-permute-start | bytes 196616 | tf_op jit(solution)/shard_map/ppermute | solution.py:504
  4.3 2.5 %collective-permute-start.6 = (bf16[2,2,64,128]{3,2,1,0:T(8,128)(2,1)S(1)}, bf16[2,2,64,128]{3,2,1,0:T(8,128)(2,1)S(1)}, u32[]{:S(2)}, u32[]{:S(2)}) collective-permute-start(bf16[2,2,64,128]{3,2,1,0:T(8,128)(2,1)S(1)} %get-tuple-element.42.refs_6_.refs_2_.refs_8_), channel_id=1, source_target_pairs={{0,5},{1,4},{2,7},{3,6},{4,1},{5,0},{6,3},{7,2},{8,13},{9,12},{10,... | collective-permute-start | bytes 196616 | tf_op jit(solution)/shard_map/ppermute | solution.py:501
  6.8 0.5 %collective-permute-start.5 = (bf16[2,2,64,128]{3,2,1,0:T(8,128)(2,1)S(1)}, bf16[2,2,64,128]{3,2,1,0:T(8,128)(2,1)S(1)}, u32[]{:S(2)}, u32[]{:S(2)}) collective-permute-start(bf16[2,2,64,128]{3,2,1,0:T(8,128)(2,1)S(1)} %get-tuple-element.42.refs_6_.refs_2_.refs_8_), channel_id=1, source_target_pairs={{0,4},{4,0},{1,5},{5,1},{2,6},{6,2},{3,7},{7,3},{8,12},{12,8},{9,1... | collective-permute-start | bytes 196616 | tf_op jit(solution)/shard_map/ppermute | solution.py:495
  7.3 0.4 %collective-permute-start.4 = (bf16[2,2,64,128]{3,2,1,0:T(8,128)(2,1)S(1)}, bf16[2,2,64,128]{3,2,1,0:T(8,128)(2,1)S(1)}, u32[]{:S(2)}, u32[]{:S(2)}) collective-permute-start(bf16[2,2,64,128]{3,2,1,0:T(8,128)(2,1)S(1)} %get-tuple-element.42.refs_6_.refs_2_.refs_8_), channel_id=1, source_target_pairs={{0,1},{1,0},{2,3},{3,2},{4,5},{5,4},{6,7},{7,6},{8,9},{9,8},{10,11... | collective-permute-start | bytes 196616 | tf_op jit(solution)/shard_map/ppermute | solution.py:493
  7.8 0.0 collective-permute-done.refs_5_.refs_6_.refs_12_
  7.8 2.5 %collective-permute-start.3 = (bf16[2,2,64,128]{3,2,1,0:T(8,128)(2,1)S(1)}, bf16[2,2,64,128]{3,2,1,0:T(8,128)(2,1)S(1)}, u32[]{:S(2)}, u32[]{:S(2)}) collective-permute-start(bf16[2,2,64,128]{3,2,1,0:T(8,128)(2,1)S(1)} %collective-permute-done.refs_5_.refs_6_.refs_12_), channel_id=1, source_target_pairs={{0,5},{1,4},{2,7},{3,6},{4,1},{5,0},{6,3},{7,2},{8,13},{9,12},{10,... | collective-permute-start | bytes 196616 | tf_op jit(solution)/shard_map/ppermute | solution.py:501
  10.3 0.5 %collective-permute-start.2 = (bf16[2,2,64,128]{3,2,1,0:T(8,128)(2,1)S(1)}, bf16[2,2,64,128]{3,2,1,0:T(8,128)(2,1)S(1)}, u32[]{:S(2)}, u32[]{:S(2)}) collective-permute-start(bf16[2,2,64,128]{3,2,1,0:T(8,128)(2,1)S(1)} %collective-permute-done.refs_5_.refs_6_.refs_12_), channel_id=1, source_target_pairs={{0,4},{4,0},{1,5},{5,1},{2,6},{6,2},{3,7},{7,3},{8,12},{12,8},{9,1... | collective-permute-start | bytes 196616 | tf_op jit(solution)/shard_map/ppermute | solution.py:495
  10.8 0.0 collective-permute-done.6.refs_9_.refs_5_.refs_11_
  10.8 0.9 %collective-permute-start.1 = (bf16[2,2,64,128]{3,2,1,0:T(8,128)(2,1)S(1)}, bf16[2,2,64,128]{3,2,1,0:T(8,128)(2,1)S(1)}, u32[]{:S(2)}, u32[]{:S(2)}) collective-permute-start(bf16[2,2,64,128]{3,2,1,0:T(8,128)(2,1)S(1)} %collective-permute-done.refs_5_.refs_6_.refs_12_), channel_id=1, source_target_pairs={{0,1},{1,0},{2,3},{3,2},{4,5},{5,4},{6,7},{7,6},{8,9},{9,8},{10,11... | collective-permute-start | bytes 196616 | tf_op jit(solution)/shard_map/ppermute | solution.py:493
  11.7 0.0 copy-done.3
  11.7 0.0 copy-done.5
  11.7 0.0 copy-start
  11.7 1.0 %copy-done = bf16[1,2,32,4096]{3,2,1,0:T(8,128)(2,1)S(1)} copy-done((bf16[1,2,32,4096]{3,2,1,0:T(8,128)(2,1)S(1)}, bf16[1,2,32,4096]{3,2,1,0:T(8,128)(2,1)}, u32[]{:S(2)}) %copy-start) | copy-done | bytes 524312
  12.8 0.0 copy-start.1
  12.8 0.9 %norm.1 = (bf16[2,32,4096]{2,1,0:T(8,128)(2,1)S(1)}, f32[2,32,128]{2,1,0:T(8,128)S(1)}, f32[2,128,256]{2,1,0:T(8,128)S(1)}) custom-call(s32[5,8]{1,0:T(8,128)S(1)} %copy-done.5, bf16[1,2,32,4096]{3,2,1,0:T(8,128)(2,1)S(1)} %copy-done, f32[1,4096]{1,0:T(1,128)S(1)} %copy-done.3), custom_call_target="tpu_custom_call" | custom-call | tf_op jit(solution)/shard_map/norm/pallas_call | solution.py:479
  13.7 0.0 collective-permute-done.5.refs_8_.refs_4_.refs_10_
  13.7 0.0 collective-permute-done.4.refs_7_.refs_3_.refs_9_
  13.7 0.0 copy-done.2
  13.7 0.1 copy-done.1
  13.8 0.5 %first_near_rows.1 = (bf16[2,256,128]{2,1,0:T(8,128)(2,1)S(1)}, bf16[2,128,256]{2,1,0:T(8,128)(2,1)S(1)}, bf16[2,128,256]{2,1,0:T(8,128)(2,1)S(1)}, f32[32,128]{1,0:T(8,128)S(1)}, bf16[2,2,128,256]{3,2,1,0:T(8,128)(2,1)S(1)}) custom-call(bf16[1,2,32,4096]{3,2,1,0:T(8,128)(2,1)S(1)} %copy-done.1, f32[1,4096]{1,0:T(1,128)S(1)} %copy-done.3, ...), custom_call_target="tpu_custom_call" | custom-call | tf_op jit(solution)/shard_map/first_near_rows/pallas_call | solution.py:479
  14.4 0.0 collective-permute-done.3.refs_8_.refs_9_.refs_15_
  14.4 0.3 collective-permute-done.2.refs_7_.refs_8_.refs_14_
  14.6 0.4 %collective-permute-done.1.refs_6_.refs_7_.refs_13_ = bf16[2,2,64,128]{3,2,1,0:T(8,128)(2,1)S(1)} collective-permute-done((bf16[2,2,64,128]{3,2,1,0:T(8,128)(2,1)S(1)}, bf16[2,2,64,128]{3,2,1,0:T(8,128)(2,1)S(1)}, u32[]{:S(2)}, u32[]{:S(2)}) %collective-permute-start.1) | collective-permute-done | bytes 65568 | tf_op jit(solution)/shard_map/ppermute | solution.py:493
  15.1 0.8 %first_far_rows.1 = (bf16[32,4096]{1,0:T(8,128)(2,1)S(1)}, bf16[2,256,128]{2,1,0:T(8,128)(2,1)S(1)}, bf16[2,128,256]{2,1,0:T(8,128)(2,1)S(1)}, bf16[2,128,256]{2,1,0:T(8,128)(2,1)S(1)}) custom-call(bf16[1,2,32,4096]{3,2,1,0:T(8,128)(2,1)S(1)} %copy-done.1, f32[1,4096]{1,0:T(1,128)S(1)} %copy-done.3, f32[2,32,128]{2,1,0:T(8,128)S(1)} %get-tuple-element.38.refs_3_.refs_2_, ...), custom_call_target="tpu_custom_call" | custom-call | tf_op jit(solution)/shard_map/first_far_rows/pallas_call | solution.py:479
  15.9 1.3 %collective-permute-start.8 = (bf16[32,4096]{1,0:T(8,128)(2,1)S(1)}, bf16[32,4096]{1,0:T(8,128)(2,1)S(1)}, u32[]{:S(2)}, u32[]{:S(2)}) collective-permute-start(bf16[32,4096]{1,0:T(8,128)(2,1)S(1)} %get-tuple-element.46.refs_5_), channel_id=1, source_target_pairs={{16,8},{17,9},{18,10},{19,11},{20,12},{21,13},{22,14},{23,15}} | collective-permute-start | bytes 786440 | tf_op jit(solution)/shard_map/ppermute | solution.py:564
  17.2 0.1 collective-permute-start.7
  17.2 0.4 %first_keys.1 = (f32[32,128]{1,0:T(8,128)S(1)}, f32[2,256,128]{2,1,0:T(8,128)S(1)}, bf16[2,256,128]{2,1,0:T(8,128)(2,1)S(1)}) custom-call(bf16[1,2,32,4096]{3,2,1,0:T(8,128)(2,1)S(1)} %copy-done.1, bf16[2,32,4096]{2,1,0:T(8,128)(2,1)S(1)} %get-tuple-element.39.refs_2_.refs_1_, f32[2,32,128]{2,1,0:T(8,128)S(1)} %get-tuple-element.38.refs_3_.refs_2_, ...), custom_call_target="tpu_custom_call" | custom-call | tf_op jit(solution)/shard_map/first_keys/pallas_call | solution.py:479
  17.7 0.0 copy-start.4
  17.7 1.0 %collective-permute-start.12 = (bf16[2,256,128]{2,1,0:T(8,128)(2,1)S(1)}, bf16[2,256,128]{2,1,0:T(8,128)(2,1)S(1)}, u32[]{:S(2)}, u32[]{:S(2)}) collective-permute-start(bf16[2,256,128]{2,1,0:T(8,128)(2,1)S(1)} %get-tuple-element.62), channel_id=1, source_target_pairs={{0,1},{1,0},{2,3},{3,2},{4,5},{5,4},{6,7},{7,6},{8,9},{9,8},{10,11... | collective-permute-start | bytes 393224 | tf_op jit(solution)/shard_map/ppermute | solution.py:493
  18.7 0.4 second_probs.1.refs_6_
  19.0 2.0 %collective-permute-done.8.refs_5_ = bf16[32,4096]{1,0:T(8,128)(2,1)S(1)} collective-permute-done((bf16[32,4096]{1,0:T(8,128)(2,1)S(1)}, bf16[32,4096]{1,0:T(8,128)(2,1)S(1)}, u32[]{:S(2)}, u32[]{:S(2)}) %collective-permute-start.8) | collective-permute-done | bytes 262176 | tf_op jit(solution)/shard_map/ppermute | solution.py:564
  21.0 0.0 collective-permute-done.7.refs_4_
  21.0 0.0 copy-done.4
  21.0 0.6 %second_keys.1 = (bf16[4,256,128]{2,1,0:T(8,128)(2,1)S(1)}, f32[32,128]{1,0:T(8,128)S(1)}, f32[256,128]{1,0:T(8,128)S(1)}, bf16[32,4096]{1,0:T(8,128)(2,1)S(1)},...) custom-call(bf16[1,2,32,4096]{3,2,1,0:T(8,128)(2,1)S(1)} %copy-done.1, ...), custom_call_target="tpu_custom_call" | custom-call | tf_op jit(solution)/shard_map/second_keys/pallas_call | solution.py:479
  21.6 1.5 %collective-permute-start.9 = (bf16[288,128]{1,0:T(8,128)(2,1)S(1)}, bf16[288,128]{1,0:T(8,128)(2,1)S(1)}, u32[]{:S(2)}, u32[]{:S(2)}) collective-permute-start(bf16[288,128]{1,0:T(8,128)(2,1)S(1)} %get-tuple-element.57), channel_id=1, source_target_pairs={{0,5},{1,4},{2,7},{3,6},{4,1},{5,0},{6,3},{7,2},{8,13},{9,12},{10,... | collective-permute-start | bytes 221192 | tf_op jit(solution)/shard_map/ppermute | solution.py:501
  23.1 1.0 %collective-permute-start.10 = (bf16[288,128]{1,0:T(8,128)(2,1)S(1)}, bf16[288,128]{1,0:T(8,128)(2,1)S(1)}, u32[]{:S(2)}, u32[]{:S(2)}) collective-permute-start(bf16[288,128]{1,0:T(8,128)(2,1)S(1)} %get-tuple-element.58), channel_id=1, source_target_pairs={{0,4},{4,0},{1,5},{5,1},{2,6},{6,2},{3,7},{7,3},{8,12},{12,8},{9,1... | collective-permute-start | bytes 221192 | tf_op jit(solution)/shard_map/ppermute | solution.py:495
  24.1 1.1 %collective-permute-start.11 = (bf16[288,128]{1,0:T(8,128)(2,1)S(1)}, bf16[288,128]{1,0:T(8,128)(2,1)S(1)}, u32[]{:S(2)}, u32[]{:S(2)}) collective-permute-start(bf16[288,128]{1,0:T(8,128)(2,1)S(1)} %get-tuple-element.59), channel_id=1, source_target_pairs={{0,1},{1,0},{2,3},{3,2},{4,5},{5,4},{6,7},{7,6},{8,9},{9,8},{10,11... | collective-permute-start | bytes 221192 | tf_op jit(solution)/shard_map/ppermute | solution.py:493
  25.2 0.0 collective-permute-done.12.refs_1_
  25.2 1.6 %collective-permute-start.13 = (bf16[256,128]{1,0:T(8,128)(2,1)S(1)}, bf16[256,128]{1,0:T(8,128)(2,1)S(1)}, u32[]{:S(2)}, u32[]{:S(2)}) collective-permute-start(bf16[256,128]{1,0:T(8,128)(2,1)S(1)} %get-tuple-element.64), channel_id=1, source_target_pairs={{0,4},{4,0},{1,5},{5,1},{2,6},{6,2},{3,7},{7,3},{8,12},{12,8},{9,1... | collective-permute-start | bytes 196616 | tf_op jit(solution)/shard_map/ppermute | solution.py:495
  26.8 0.4 %collective-permute-done.9.refs_2_ = bf16[288,128]{1,0:T(8,128)(2,1)S(1)} collective-permute-done((bf16[288,128]{1,0:T(8,128)(2,1)S(1)}, bf16[288,128]{1,0:T(8,128)(2,1)S(1)}, u32[]{:S(2)}, u32[]{:S(2)}) %collective-permute-start.9) | collective-permute-done | bytes 73760 | tf_op jit(solution)/shard_map/ppermute | solution.py:501
  27.2 1.1 %collective-permute-done.10.refs_3_ = bf16[288,128]{1,0:T(8,128)(2,1)S(1)} collective-permute-done((bf16[288,128]{1,0:T(8,128)(2,1)S(1)}, bf16[288,128]{1,0:T(8,128)(2,1)S(1)}, u32[]{:S(2)}, u32[]{:S(2)}) %collective-permute-start.10) | collective-permute-done | bytes 73760 | tf_op jit(solution)/shard_map/ppermute | solution.py:495
  28.3 0.1 collective-permute-done.11.refs_4_
  28.4 0.1 second_near.1
  28.5 2.7 %collective-permute-start.14 = (bf16[160,128]{1,0:T(8,128)(2,1)S(1)}, bf16[160,128]{1,0:T(8,128)(2,1)S(1)}, u32[]{:S(2)}, u32[]{:S(2)}) collective-permute-start(bf16[160,128]{1,0:T(8,128)(2,1)S(1)} %get-tuple-element.66), channel_id=1, source_target_pairs={{0,2},{1,3},{2,0},{3,1},{4,6},{5,7},{6,4},{7,5},{8,10},{9,11},{10,... | collective-permute-start | bytes 122888 | tf_op jit(solution)/shard_map/ppermute | solution.py:504
  31.2 0.0 collective-permute-done.13.refs_0_
  31.2 1.1 %collective-permute-start.15 = (bf16[128,128]{1,0:T(8,128)(2,1)S(1)}, bf16[128,128]{1,0:T(8,128)(2,1)S(1)}, u32[]{:S(2)}, u32[]{:S(2)}) collective-permute-start(bf16[128,128]{1,0:T(8,128)(2,1)S(1)} %get-tuple-element.67), channel_id=1, source_target_pairs={{0,2},{1,3},{2,0},{3,1},{4,6},{5,7},{6,4},{7,5},{8,10},{9,11},{10,... | collective-permute-start | bytes 98312 | tf_op jit(solution)/shard_map/ppermute | solution.py:504
  32.3 1.2 %second_rows.1 = bf16[1,2,32,4096]{3,2,1,0:T(8,128)(2,1)} custom-call(bf16[1,2,32,4096]{3,2,1,0:T(8,128)(2,1)S(1)} %copy-done.1, f32[1,4096]{1,0:T(1,128)S(1)} %copy-done.3, f32[2,32,128]{2,1,0:T(8,128)S(1)} %get-tuple-element.38.refs_3_.refs_2_, bf16[32,4096]{1,0:T(8,128)(2,1)S(1)} %get-tuple-element.53.refs_3_, ...), custom_call_target="tpu_custom_call" | custom-call | tf_op jit(solution)/shard_map/second_rows/pallas_call | solution.py:479
  33.4 2.6 %collective-permute-done.15.refs_3_ = bf16[128,128]{1,0:T(8,128)(2,1)S(1)} collective-permute-done((bf16[128,128]{1,0:T(8,128)(2,1)S(1)}, bf16[128,128]{1,0:T(8,128)(2,1)S(1)}, u32[]{:S(2)}, u32[]{:S(2)}) %collective-permute-start.15) | collective-permute-done | bytes 32800 | tf_op jit(solution)/shard_map/ppermute | solution.py:504
  36.1 0.0 collective-permute-done.14.refs_2_
  36.1 0.7 %finish.1 = (f32[1,2,128,128]{3,2,1,0:T(8,128)}, f32[1,2,128,128]{3,2,1,0:T(8,128)}, f32[32,128]{1,0:T(8,128)}) custom-call(f32[128,128]{1,0:T(8,128)S(1)} %get-tuple-element.60.refs_0_, f32[128,128]{1,0:T(8,128)S(1)} %get-tuple-element.65.refs_1_, bf16[160,128]{1,0:T(8,128)(2,1)S(1)} %collective-permute-done.14.refs_2_, ...), custom_call_target="tpu_custom_call" | custom-call | tf_op jit(solution)/shard_map/finish/pallas_call | solution.py:479
  (3 shorter events, 0.1 us)
Async XLA Ops:
  0.6 13.1 %copy-start.2 = (bf16[1,32,4096]{2,1,0:T(8,128)(2,1)S(1)}, bf16[1,32,4096]{2,1,0:T(8,128)(2,1)}, u32[]{:S(2)}) copy-start(bf16[1,32,4096]{2,1,0:T(8,128)(2,1)} %refs_3_.2) | copy-start | bytes 786436
  1.6 10.2 %copy-start.3 = (f32[1,4096]{1,0:T(1,128)S(1)}, f32[1,4096]{1,0:T(1,128)}, u32[]{:S(2)}) copy-start(f32[1,4096]{1,0:T(1,128)} %refs_1_.5) | copy-start | bytes 49156
  1.6 10.2 %copy-start.5 = (s32[5,8]{1,0:T(8,128)S(1)}, s32[5,8]{1,0:T(8,128)}, u32[]{:S(2)}) copy-start(s32[5,8]{1,0:T(8,128)} %doc_ref.1) | copy-start | bytes 484
  1.6 6.1 %collective-permute-start = (bf16[2,2,64,128]{3,2,1,0:T(8,128)(2,1)S(1)}, bf16[2,2,64,128]{3,2,1,0:T(8,128)(2,1)S(1)}, u32[]{:S(2)}, u32[]{:S(2)}) collective-permute-start(bf16[2,2,64,128]{3,2,1,0:T(8,128)(2,1)S(1)} %get-tuple-element.41), channel_id=1, source_target_pairs={{0,2},{1,3},{2,0},{3,1},{4,6},{5,7},{6,4},{7,5},{8,10},{9,11},{10,... | collective-permute-start | bytes 196616 | tf_op jit(solution)/shard_map/ppermute | solution.py:504
  4.3 6.5 %collective-permute-start.6 = (bf16[2,2,64,128]{3,2,1,0:T(8,128)(2,1)S(1)}, bf16[2,2,64,128]{3,2,1,0:T(8,128)(2,1)S(1)}, u32[]{:S(2)}, u32[]{:S(2)}) collective-permute-start(bf16[2,2,64,128]{3,2,1,0:T(8,128)(2,1)S(1)} %get-tuple-element.42.refs_6_.refs_2_.refs_8_), channel_id=1, source_target_pairs={{0,5},{1,4},{2,7},{3,6},{4,1},{5,0},{6,3},{7,2},{8,13},{9,12},{10,... | collective-permute-start | bytes 196616 | tf_op jit(solution)/shard_map/ppermute | solution.py:501
  6.8 6.9 %collective-permute-start.5 = (bf16[2,2,64,128]{3,2,1,0:T(8,128)(2,1)S(1)}, bf16[2,2,64,128]{3,2,1,0:T(8,128)(2,1)S(1)}, u32[]{:S(2)}, u32[]{:S(2)}) collective-permute-start(bf16[2,2,64,128]{3,2,1,0:T(8,128)(2,1)S(1)} %get-tuple-element.42.refs_6_.refs_2_.refs_8_), channel_id=1, source_target_pairs={{0,4},{4,0},{1,5},{5,1},{2,6},{6,2},{3,7},{7,3},{8,12},{12,8},{9,1... | collective-permute-start | bytes 196616 | tf_op jit(solution)/shard_map/ppermute | solution.py:495
  7.3 6.4 %collective-permute-start.4 = (bf16[2,2,64,128]{3,2,1,0:T(8,128)(2,1)S(1)}, bf16[2,2,64,128]{3,2,1,0:T(8,128)(2,1)S(1)}, u32[]{:S(2)}, u32[]{:S(2)}) collective-permute-start(bf16[2,2,64,128]{3,2,1,0:T(8,128)(2,1)S(1)} %get-tuple-element.42.refs_6_.refs_2_.refs_8_), channel_id=1, source_target_pairs={{0,1},{1,0},{2,3},{3,2},{4,5},{5,4},{6,7},{7,6},{8,9},{9,8},{10,11... | collective-permute-start | bytes 196616 | tf_op jit(solution)/shard_map/ppermute | solution.py:493
  7.8 6.6 %collective-permute-start.3 = (bf16[2,2,64,128]{3,2,1,0:T(8,128)(2,1)S(1)}, bf16[2,2,64,128]{3,2,1,0:T(8,128)(2,1)S(1)}, u32[]{:S(2)}, u32[]{:S(2)}) collective-permute-start(bf16[2,2,64,128]{3,2,1,0:T(8,128)(2,1)S(1)} %collective-permute-done.refs_5_.refs_6_.refs_12_), channel_id=1, source_target_pairs={{0,5},{1,4},{2,7},{3,6},{4,1},{5,0},{6,3},{7,2},{8,13},{9,12},{10,... | collective-permute-start | bytes 196616 | tf_op jit(solution)/shard_map/ppermute | solution.py:501
  10.3 4.3 %collective-permute-start.2 = (bf16[2,2,64,128]{3,2,1,0:T(8,128)(2,1)S(1)}, bf16[2,2,64,128]{3,2,1,0:T(8,128)(2,1)S(1)}, u32[]{:S(2)}, u32[]{:S(2)}) collective-permute-start(bf16[2,2,64,128]{3,2,1,0:T(8,128)(2,1)S(1)} %collective-permute-done.refs_5_.refs_6_.refs_12_), channel_id=1, source_target_pairs={{0,4},{4,0},{1,5},{5,1},{2,6},{6,2},{3,7},{7,3},{8,12},{12,8},{9,1... | collective-permute-start | bytes 196616 | tf_op jit(solution)/shard_map/ppermute | solution.py:495
  10.8 4.3 %collective-permute-start.1 = (bf16[2,2,64,128]{3,2,1,0:T(8,128)(2,1)S(1)}, bf16[2,2,64,128]{3,2,1,0:T(8,128)(2,1)S(1)}, u32[]{:S(2)}, u32[]{:S(2)}) collective-permute-start(bf16[2,2,64,128]{3,2,1,0:T(8,128)(2,1)S(1)} %collective-permute-done.refs_5_.refs_6_.refs_12_), channel_id=1, source_target_pairs={{0,1},{1,0},{2,3},{3,2},{4,5},{5,4},{6,7},{7,6},{8,9},{9,8},{10,11... | collective-permute-start | bytes 196616 | tf_op jit(solution)/shard_map/ppermute | solution.py:493
  11.7 1.0 %copy-start = (bf16[1,2,32,4096]{3,2,1,0:T(8,128)(2,1)S(1)}, bf16[1,2,32,4096]{3,2,1,0:T(8,128)(2,1)}, u32[]{:S(2)}) copy-start(bf16[1,2,32,4096]{3,2,1,0:T(8,128)(2,1)} %refs_0_.9) | copy-start | bytes 1572868
  12.8 1.0 %copy-start.1 = (bf16[1,2,32,4096]{3,2,1,0:T(8,128)(2,1)S(1)}, bf16[1,2,32,4096]{3,2,1,0:T(8,128)(2,1)}, u32[]{:S(2)}) copy-start(bf16[1,2,32,4096]{3,2,1,0:T(8,128)(2,1)} %refs_0_.9) | copy-start | bytes 1572868
  15.9 5.2 %collective-permute-start.8 = (bf16[32,4096]{1,0:T(8,128)(2,1)S(1)}, bf16[32,4096]{1,0:T(8,128)(2,1)S(1)}, u32[]{:S(2)}, u32[]{:S(2)}) collective-permute-start(bf16[32,4096]{1,0:T(8,128)(2,1)S(1)} %get-tuple-element.46.refs_5_), channel_id=1, source_target_pairs={{16,8},{17,9},{18,10},{19,11},{20,12},{21,13},{22,14},{23,15}} | collective-permute-start | bytes 786440 | tf_op jit(solution)/shard_map/ppermute | solution.py:564
  17.2 3.9 %collective-permute-start.7 = (bf16[32,4096]{1,0:T(8,128)(2,1)S(1)}, bf16[32,4096]{1,0:T(8,128)(2,1)S(1)}, u32[]{:S(2)}, u32[]{:S(2)}) collective-permute-start(bf16[32,4096]{1,0:T(8,128)(2,1)S(1)} %get-tuple-element.46.refs_5_), channel_id=1, source_target_pairs={{0,8},{8,0},{16,24},{24,16},{1,9},{9,1},{17,25},{25,17},{2,10},{10... | collective-permute-start | bytes 786440 | tf_op jit(solution)/shard_map/ppermute | solution.py:567
  17.7 3.3 %copy-start.4 = (bf16[1,32,4096]{2,1,0:T(8,128)(2,1)S(1)}, bf16[1,32,4096]{2,1,0:T(8,128)(2,1)}, u32[]{:S(2)}) copy-start(bf16[1,32,4096]{2,1,0:T(8,128)(2,1)} %refs_3_.3) | copy-start | bytes 786436
  17.7 7.5 %collective-permute-start.12 = (bf16[2,256,128]{2,1,0:T(8,128)(2,1)S(1)}, bf16[2,256,128]{2,1,0:T(8,128)(2,1)S(1)}, u32[]{:S(2)}, u32[]{:S(2)}) collective-permute-start(bf16[2,256,128]{2,1,0:T(8,128)(2,1)S(1)} %get-tuple-element.62), channel_id=1, source_target_pairs={{0,1},{1,0},{2,3},{3,2},{4,5},{5,4},{6,7},{7,6},{8,9},{9,8},{10,11... | collective-permute-start | bytes 393224 | tf_op jit(solution)/shard_map/ppermute | solution.py:493
  21.6 5.6 %collective-permute-start.9 = (bf16[288,128]{1,0:T(8,128)(2,1)S(1)}, bf16[288,128]{1,0:T(8,128)(2,1)S(1)}, u32[]{:S(2)}, u32[]{:S(2)}) collective-permute-start(bf16[288,128]{1,0:T(8,128)(2,1)S(1)} %get-tuple-element.57), channel_id=1, source_target_pairs={{0,5},{1,4},{2,7},{3,6},{4,1},{5,0},{6,3},{7,2},{8,13},{9,12},{10,... | collective-permute-start | bytes 221192 | tf_op jit(solution)/shard_map/ppermute | solution.py:501
  23.1 5.2 %collective-permute-start.10 = (bf16[288,128]{1,0:T(8,128)(2,1)S(1)}, bf16[288,128]{1,0:T(8,128)(2,1)S(1)}, u32[]{:S(2)}, u32[]{:S(2)}) collective-permute-start(bf16[288,128]{1,0:T(8,128)(2,1)S(1)} %get-tuple-element.58), channel_id=1, source_target_pairs={{0,4},{4,0},{1,5},{5,1},{2,6},{6,2},{3,7},{7,3},{8,12},{12,8},{9,1... | collective-permute-start | bytes 221192 | tf_op jit(solution)/shard_map/ppermute | solution.py:495
  24.1 4.4 %collective-permute-start.11 = (bf16[288,128]{1,0:T(8,128)(2,1)S(1)}, bf16[288,128]{1,0:T(8,128)(2,1)S(1)}, u32[]{:S(2)}, u32[]{:S(2)}) collective-permute-start(bf16[288,128]{1,0:T(8,128)(2,1)S(1)} %get-tuple-element.59), channel_id=1, source_target_pairs={{0,1},{1,0},{2,3},{3,2},{4,5},{5,4},{6,7},{7,6},{8,9},{9,8},{10,11... | collective-permute-start | bytes 221192 | tf_op jit(solution)/shard_map/ppermute | solution.py:493
  25.2 5.9 %collective-permute-start.13 = (bf16[256,128]{1,0:T(8,128)(2,1)S(1)}, bf16[256,128]{1,0:T(8,128)(2,1)S(1)}, u32[]{:S(2)}, u32[]{:S(2)}) collective-permute-start(bf16[256,128]{1,0:T(8,128)(2,1)S(1)} %get-tuple-element.64), channel_id=1, source_target_pairs={{0,4},{4,0},{1,5},{5,1},{2,6},{6,2},{3,7},{7,3},{8,12},{12,8},{9,1... | collective-permute-start | bytes 196616 | tf_op jit(solution)/shard_map/ppermute | solution.py:495
  28.5 7.6 %collective-permute-start.14 = (bf16[160,128]{1,0:T(8,128)(2,1)S(1)}, bf16[160,128]{1,0:T(8,128)(2,1)S(1)}, u32[]{:S(2)}, u32[]{:S(2)}) collective-permute-start(bf16[160,128]{1,0:T(8,128)(2,1)S(1)} %get-tuple-element.66), channel_id=1, source_target_pairs={{0,2},{1,3},{2,0},{3,1},{4,6},{5,7},{6,4},{7,5},{8,10},{9,11},{10,... | collective-permute-start | bytes 122888 | tf_op jit(solution)/shard_map/ppermute | solution.py:504
  31.2 4.9 %collective-permute-start.15 = (bf16[128,128]{1,0:T(8,128)(2,1)S(1)}, bf16[128,128]{1,0:T(8,128)(2,1)S(1)}, u32[]{:S(2)}, u32[]{:S(2)}) collective-permute-start(bf16[128,128]{1,0:T(8,128)(2,1)S(1)} %get-tuple-element.67), channel_id=1, source_target_pairs={{0,2},{1,3},{2,0},{3,1},{4,6},{5,7},{6,4},{7,5},{8,10},{9,11},{10,... | collective-permute-start | bytes 98312 | tf_op jit(solution)/shard_map/ppermute | solution.py:504

commit v14 on v11

--- a/solution.py
+++ b/solution.py
@@ -142,7 +142,7 @@
     def __init__(self, sizes, tick, refs):
         self.near_count = sizes[3] // 2
         self.tick = tick
-        self.refs = refs
+        self.refs = [refs[0], *refs[1:][::-1]]
 
     def __call__(self, near, kind):
         parts = [ref[self.tick, kind] for ref in self.refs[near :: self.near_count]]
@@ -218,7 +218,8 @@
     members = sizes[2] * near_count
     x_ref, gain_ref, query_ref, inverse_ref, mask_ref, waiting_ref = refs[:6]
     keys = Keys(sizes, 0, refs[6 : 6 + members])
-    query_grad_ref, dscore_ref, probs_ref, coupled_ref, turned_ref = refs[6 + members :]
+    query_grad_ref, dscore_ref, probs_ref, coupled_ref, turned_ref = refs[6 + members : 11 + members]
+    base_ref, pull_ref, rate_ref, weight_ref = refs[11 + members :]
     loads = (lambda where: query_ref[0, :, where], waiting_from(waiting_ref))
     products = []
     for near in range(near_count):
@@ -231,48 +232,56 @@
         query_grad_ref[near] = query_grad
         coupled = coupled_terms(Group(sizes, near), query_grad, normed_of, gain_ref, coupled)
     coupled_ref[...] = coupled
+    inverse = inverse_ref[0]
     for near in range(near_count):
+        columns_of = Group(sizes, near)
+        for index, low in enumerate(columns_of.unstacked(query_grads[near])):
+            where = columns_of.head(index)
+            scaled = low.astype(F32) * gain_ref[:, where]
+            base_ref[:, where] = loads[1](where).astype(F32) + inverse * scaled
+            pull_ref[:, where] = inverse * normed_of(where)
         columns_of = Group(sizes, near_count + near)
         for kind, load in enumerate(loads):
             turned_ref[near, kind] = columns_of.stacked(load).T
+        for index in range(columns_of.group):
+            where = columns_of.head(index)
+            normed = normed_of(where)
+            pull_ref[:, where] = inverse * normed
+            rate_ref[:, where] = inverse * gain_ref[:, where]
+            weight_ref[:, where] = normed * gain_ref[:, where]
 
 
 def first_far_rows_kernel(sizes, *refs):
     near_count = sizes[3] // 2
     members = sizes[2] * near_count
-    x_ref, gain_ref, inverse_ref, mask_ref, waiting_ref = refs[:5]
-    keys, refs = Keys(sizes, 0, refs[5 : 5 + members]), refs[5 + members :]
-    near_grad_ref, coupled_ref, turned_ref = refs[:3]
-    input_grad_ref, query_grad_ref, dscore_ref, probs_ref = refs[3:]
+    mask_ref, waiting_ref = refs[:2]
+    keys, refs = Keys(sizes, 0, refs[2 : 2 + members]), refs[2 + members :]
+    coupled_ref, turned_ref, base_ref, pull_ref, rate_ref, weight_ref = refs[:6]
+    input_grad_ref, query_grad_ref, dscore_ref, probs_ref = refs[6:]
     products = [
         [dot(keys(near, kind), turned_ref[near, kind], NN) for kind in range(2)]
         for near in range(near_count)
     ]
     query_grads = first_half(keys, mask_ref[0], products, dscore_ref, probs_ref)
-    normed_of = normed_from(x_ref, 0, inverse_ref[0])
     coupled = coupled_ref[...]
+    groups = [Group(sizes, turn) for turn in range(2 * near_count)]
     for near, query_grad in enumerate(query_grads):
         query_grad_ref[near] = query_grad
-        coupled = coupled_terms(
-            Group(sizes, near_count + near), query_grad, normed_of, gain_ref, coupled
-        )
-
-    def query_grad_of(turn):
-        return near_grad_ref[turn] if turn < near_count else query_grads[turn - near_count]
-
-    def write(where, result):
-        input_grad_ref[:, where] = result
-
-    write_input_grads(
-        sizes,
-        coupled,
-        query_grad_of,
-        normed_of,
-        gain_ref,
-        inverse_ref[0],
-        waiting_from(waiting_ref),
-        write,
-    )
+        columns_of = groups[near_count + near]
+        for index, low in enumerate(columns_of.unstacked(query_grad)):
+            coupled = coupled + low.astype(F32) * weight_ref[:, columns_of.head(index)]
+    coupling = jnp.sum(coupled, axis=1, keepdims=True) * (1.0 / sizes[5])
+    for near, query_grad in enumerate(query_grads):
+        for index in range(groups[near].group):
+            where = groups[near].head(index)
+            input_grad_ref[:, where] = (base_ref[:, where] - pull_ref[:, where] * coupling).astype(
+                BF16
+            )
+        columns_of = groups[near_count + near]
+        for index, low in enumerate(columns_of.unstacked(query_grad)):
+            where = columns_of.head(index)
+            base = waiting_ref[0, :, where].astype(F32) + low.astype(F32) * rate_ref[:, where]
+            input_grad_ref[:, where] = (base - pull_ref[:, where] * coupling).astype(BF16)
 
 
 def first_keys_kernel(sizes, *refs):
@@ -325,7 +334,7 @@
     cycle, tp_count = sizes[2:4]
     turns = range(tp_count)
     kv_count = cycle * tp_count
-    x_ref, query_ref, inverse_ref, output_ref, chip_ref, link_ref = refs[:6]
+    x_ref, query_ref, inverse_ref, output_ref, link_ref, chip_ref = refs[:6]
     probs_ref, before_ref, *refs = refs[6:]
     keys, refs = both_sets(sizes, refs[:kv_count]), refs[kv_count:]
     query_grad_ref, gain_rows_ref, own_ref, arriving_ref = refs[:4]
@@ -511,7 +520,7 @@
     kv = [
         block if place == (0, 0) else to_near(block, *place)
         for block in (own_kv, far_kv)
-        for place in [(0, 0)] + places
+        for place in [(0, 0)] + places[::-1]
     ]
     own_set, far_set = kv[: len(kv) // 2], kv[len(kv) // 2 :]
     queries, inverse, masks = call(
@@ -529,7 +538,7 @@
     low_rows = shape((rows, columns), BF16)
     low_scores = shape((near_count, key_count, stacked), BF16)
     low_grads = shape((near_count, stacked, HD), BF16)
-    query_grad_near, dscore_near, probs_near, coupled, turned = call(
+    query_grad_near, dscore_near, probs_near, coupled, turned, *factors = call(
         functools.partial(first_near_rows_kernel, sizes),
         "first_near_rows",
         (segment_inputs, norm_gain, queries, inverse, masks, waiting_grads, *own_set),
@@ -539,21 +548,19 @@
             low_scores,
             shape((rows, HD), F32),
             shape((near_count, 2, HD, stacked), BF16),
-        ],
+        ]
+        + [shape((rows, columns), F32)] * 4,
     )
     input_grad_first, query_grad_far, dscore_far, probs_far = call(
         functools.partial(first_far_rows_kernel, sizes),
         "first_far_rows",
         (
-            segment_inputs,
-            norm_gain,
-            inverse,
             masks,
             waiting_grads,
             *far_set,
-            query_grad_near,
             coupled,
             turned,
+            *factors,
         ),
         [low_rows, low_grads, low_scores, low_scores],
     )
@@ -600,8 +607,8 @@
             queries,
             inverse,
             output_grads,
+            over_link,
             on_chip,
-            over_link,
             probs_second,
             gain_first,
             *kv,

time: 37.1 us -> 37.1 us (level)
  no operation moved by 1% of the time
where the time goes in v14:
time: 37.1 us; the launch traced here: 36.8 us
  starting transfers between devices  21 us (57%)
  waiting for transfers between devices  7.31 us (20%)
  Pallas kernels  5.67 us (15%)
  local copies, waits for them, and re-layouts  1.15 us (3%)
  other arithmetic  0.93 us (3%)
  between operations  0.8 us (2%)
    ppermute x3, starting transfers between devices, to_far(): lax.ppermute(value, 'tp', [(i, i ^ near_count) for i in range(tp_count)])  6.55 us
    ppermute x3, starting transfers between devices, to_near(): return lax.ppermute(value, ('ctx', 'tp'), pairs)  5.78 us
    pallas_call x12, Pallas kernels, call(): pl.pallas_call(kernel, out_shape=out_shape, in_specs=in_specs, out_specs=...  5.67 us
    ppermute x1, waiting for transfers between devices, on_device(): lax.ppermute(input_grad_first, 'pipe', [(i, i - 1) for i in range(2, pipe...  3.87 us
    ppermute x4, starting transfers between devices, to_near(): return lax.ppermute(value, 'tp', [(i, i ^ near) for i in range(tp_count)])  2.58 us
    ppermute x1, starting transfers between devices, on_device(): lax.ppermute(input_grad_first, 'pipe', [(i, i ^ 1) for i in range(pipe_co...  2.42 us
    ppermute x4, starting transfers between devices, to_near(): lax.ppermute(value, 'ctx', [(i, (i + step) % cycle) for i in range(cycle)])  2.36 us
    ppermute x3, waiting for transfers between devices, to_far(): lax.ppermute(value, 'tp', [(i, i ^ near_count) for i in range(tp_count)])  1.56 us
  transfers between devices with their start and end apart: 16, of which 5 were waited for; matrix products, arithmetic and copies ran while one was open for 0% of the time, Pallas kernels for 11%

profile of v14, /device:TPU:1, one launch (start us, length us, event | category | flops | bytes accessed | tf_op | source)
XLA Modules:
  0.0 36.8 jit_solution(16228215487751624749)
XLA Ops:
  0.6 0.0 copy-start.2
  0.6 0.9 %pad_maximum_fusion.both_ref = bf16[2,2,128,128]{3,2,1,0:T(8,128)(2,1)S(1)} fusion(bf16[1,2,128,128]{3,2,1,0:T(8,128)(2,1)} %param.9, bf16[1,2,128,128]{3,2,1,0:T(8,128)(2,1)} %param.8), kind=kLoop, calls=%fused_computation | loop fusion | flops 65536 | bytes 262144 | tf_op jit(solution)/shard_map/stack | solution.py:515
  1.6 0.0 copy-start.4
  1.6 0.0 copy-start.5
  1.6 3.2 %collective-permute-start = (bf16[2,2,64,128]{3,2,1,0:T(8,128)(2,1)S(1)}, bf16[2,2,64,128]{3,2,1,0:T(8,128)(2,1)S(1)}, u32[]{:S(2)}, u32[]{:S(2)}) collective-permute-start(bf16[2,2,64,128]{3,2,1,0:T(8,128)(2,1)S(1)} %get-tuple-element.45), channel_id=1, source_target_pairs={{0,2},{1,3},{2,0},{3,1},{4,6},{5,7},{6,4},{7,5},{8,10},{9,11},{10,... | collective-permute-start | bytes 196616 | tf_op jit(solution)/shard_map/ppermute | solution.py:509
  4.8 2.3 %collective-permute-start.4 = (bf16[2,2,64,128]{3,2,1,0:T(8,128)(2,1)S(1)}, bf16[2,2,64,128]{3,2,1,0:T(8,128)(2,1)S(1)}, u32[]{:S(2)}, u32[]{:S(2)}) collective-permute-start(bf16[2,2,64,128]{3,2,1,0:T(8,128)(2,1)S(1)} %get-tuple-element.46.refs_6_.refs_2_.refs_8_), channel_id=1, source_target_pairs={{0,5},{1,4},{2,7},{3,6},{4,1},{5,0},{6,3},{7,2},{8,13},{9,12},{10,... | collective-permute-start | bytes 196616 | tf_op jit(solution)/shard_map/ppermute | solution.py:506
  7.1 0.2 collective-permute-start.5
  7.3 0.2 collective-permute-start.6
  7.5 0.0 collective-permute-done.refs_2_.refs_6_.refs_12_
  7.5 2.3 %collective-permute-start.1 = (bf16[2,2,64,128]{3,2,1,0:T(8,128)(2,1)S(1)}, bf16[2,2,64,128]{3,2,1,0:T(8,128)(2,1)S(1)}, u32[]{:S(2)}, u32[]{:S(2)}) collective-permute-start(bf16[2,2,64,128]{3,2,1,0:T(8,128)(2,1)S(1)} %collective-permute-done.refs_2_.refs_6_.refs_12_), channel_id=1, source_target_pairs={{0,5},{1,4},{2,7},{3,6},{4,1},{5,0},{6,3},{7,2},{8,13},{9,12},{10,... | collective-permute-start | bytes 196616 | tf_op jit(solution)/shard_map/ppermute | solution.py:506
  9.7 0.2 collective-permute-start.2
  10.0 0.0 collective-permute-done.4.refs_7_.refs_3_.refs_9_
  10.0 0.9 %collective-permute-start.3 = (bf16[2,2,64,128]{3,2,1,0:T(8,128)(2,1)S(1)}, bf16[2,2,64,128]{3,2,1,0:T(8,128)(2,1)S(1)}, u32[]{:S(2)}, u32[]{:S(2)}) collective-permute-start(bf16[2,2,64,128]{3,2,1,0:T(8,128)(2,1)S(1)} %collective-permute-done.refs_2_.refs_6_.refs_12_), channel_id=1, source_target_pairs={{0,1},{1,0},{2,3},{3,2},{4,5},{5,4},{6,7},{7,6},{8,9},{9,8},{10,11... | collective-permute-start | bytes 196616 | tf_op jit(solution)/shard_map/ppermute | solution.py:498
  10.8 0.0 copy-done.4
  10.8 0.0 copy-done.5
  10.9 0.0 copy-start
  10.9 1.0 %copy-done = bf16[1,2,32,4096]{3,2,1,0:T(8,128)(2,1)S(1)} copy-done((bf16[1,2,32,4096]{3,2,1,0:T(8,128)(2,1)S(1)}, bf16[1,2,32,4096]{3,2,1,0:T(8,128)(2,1)}, u32[]{:S(2)}) %copy-start) | copy-done | bytes 524312
  11.9 0.0 copy-start.1
  11.9 0.9 %norm.1 = (bf16[2,32,4096]{2,1,0:T(8,128)(2,1)S(1)}, f32[2,32,128]{2,1,0:T(8,128)S(1)}, f32[2,128,256]{2,1,0:T(8,128)S(1)}) custom-call(s32[5,8]{1,0:T(8,128)S(1)} %copy-done.5, bf16[1,2,32,4096]{3,2,1,0:T(8,128)(2,1)S(1)} %copy-done, f32[1,4096]{1,0:T(1,128)S(1)} %copy-done.4), custom_call_target="tpu_custom_call" | custom-call | tf_op jit(solution)/shard_map/norm/pallas_call | solution.py:484
  12.8 0.0 collective-permute-done.5.refs_8_.refs_4_.refs_10_
  12.8 0.0 collective-permute-done.6.refs_9_.refs_5_.refs_11_
  12.8 0.0 copy-done.2
  12.9 0.1 copy-done.1
  12.9 0.6 %first_near_rows.1 = (bf16[2,256,128]{2,1,0:T(8,128)(2,1)S(1)}, bf16[2,128,256]{2,1,0:T(8,128)(2,1)S(1)}, bf16[2,128,256]{2,1,0:T(8,128)(2,1)S(1)}, f32[32,128]{...) custom-call(bf16[1,2,32,4096]{3,2,1,0:T(8,128)(2,1)S(1)} %copy-done., ...), custom_call_target="tpu_custom_call" | custom-call | tf_op jit(solution)/shard_map/first_near_rows/pallas_call | solution.py:484
  13.6 0.0 collective-permute-done.1.refs_3_.refs_7_.refs_13_
  13.6 0.0 collective-permute-done.2.refs_4_.refs_8_.refs_14_
  13.6 0.0 collective-permute-done.3.refs_5_.refs_9_.refs_15_
  13.6 0.7 %first_far_rows.1 = (bf16[32,4096]{1,0:T(8,128)(2,1)S(1)}, bf16[2,256,128]{2,1,0:T(8,128)(2,1)S(1)}, bf16[2,128,256]{2,1,0:T(8,128)(2,1)S(1)}, bf16[2,128,256]{2,1,0:T(8,128)(2,1)S(1)}) custom-call(f32[2,128,256]{2,1,0:T(8,128)S(1)} %get-tuple-element.44.refs_4_.refs_0_, bf16[1,32,4096]{2,1,0:T(8,128)(2,1)S(1)} %copy-done.2, ...), custom_call_target="tpu_custom_call" | custom-call | tf_op jit(solution)/shard_map/first_far_rows/pallas_call | solution.py:484
  14.4 1.3 %collective-permute-start.7 = (bf16[32,4096]{1,0:T(8,128)(2,1)S(1)}, bf16[32,4096]{1,0:T(8,128)(2,1)S(1)}, u32[]{:S(2)}, u32[]{:S(2)}) collective-permute-start(bf16[32,4096]{1,0:T(8,128)(2,1)S(1)} %get-tuple-element.53.refs_5_), channel_id=1, source_target_pairs={{16,8},{17,9},{18,10},{19,11},{20,12},{21,13},{22,14},{23,15}} | collective-permute-start | bytes 786440 | tf_op jit(solution)/shard_map/ppermute | solution.py:567
  15.7 2.4 %collective-permute-start.8 = (bf16[32,4096]{1,0:T(8,128)(2,1)S(1)}, bf16[32,4096]{1,0:T(8,128)(2,1)S(1)}, u32[]{:S(2)}, u32[]{:S(2)}) collective-permute-start(bf16[32,4096]{1,0:T(8,128)(2,1)S(1)} %get-tuple-element.53.refs_5_), channel_id=1, source_target_pairs={{0,8},{8,0},{16,24},{24,16},{1,9},{9,1},{17,25},{25,17},{2,10},{10... | collective-permute-start | bytes 786440 | tf_op jit(solution)/shard_map/ppermute | solution.py:570
  18.1 0.4 %first_keys.1 = (f32[32,128]{1,0:T(8,128)S(1)}, f32[2,256,128]{2,1,0:T(8,128)S(1)}, bf16[2,256,128]{2,1,0:T(8,128)(2,1)S(1)}) custom-call(bf16[1,2,32,4096]{3,2,1,0:T(8,128)(2,1)S(1)} %copy-done.1, bf16[2,32,4096]{2,1,0:T(8,128)(2,1)S(1)} %get-tuple-element.43.refs_2_.refs_1_, f32[2,32,128]{2,1,0:T(8,128)S(1)} %get-tuple-element.42.refs_3_.refs_2_, ...), custom_call_target="tpu_custom_call" | custom-call | tf_op jit(solution)/shard_map/first_keys/pallas_call | solution.py:484
  18.5 0.0 copy-start.3
  18.5 1.3 %collective-permute-start.9 = (bf16[2,256,128]{2,1,0:T(8,128)(2,1)S(1)}, bf16[2,256,128]{2,1,0:T(8,128)(2,1)S(1)}, u32[]{:S(2)}, u32[]{:S(2)}) collective-permute-start(bf16[2,256,128]{2,1,0:T(8,128)(2,1)S(1)} %get-tuple-element.64), channel_id=1, source_target_pairs={{0,4},{4,0},{1,5},{5,1},{2,6},{6,2},{3,7},{7,3},{8,12},{12,8},{9,1... | collective-permute-start | bytes 393224 | tf_op jit(solution)/shard_map/ppermute | solution.py:500
  19.8 0.4 second_probs.1.refs_6_
  20.2 3.9 %collective-permute-done.7.refs_4_ = bf16[32,4096]{1,0:T(8,128)(2,1)S(1)} collective-permute-done((bf16[32,4096]{1,0:T(8,128)(2,1)S(1)}, bf16[32,4096]{1,0:T(8,128)(2,1)S(1)}, u32[]{:S(2)}, u32[]{:S(2)}) %collective-permute-start.7) | collective-permute-done | bytes 262176 | tf_op jit(solution)/shard_map/ppermute | solution.py:567
  24.0 0.0 collective-permute-done.8.refs_5_
  24.1 0.0 copy-done.3
  24.1 0.6 %second_keys.1 = (bf16[4,256,128]{2,1,0:T(8,128)(2,1)S(1)}, f32[32,128]{1,0:T(8,128)S(1)}, f32[256,128]{1,0:T(8,128)S(1)}, bf16[32,4096]{1,0:T(8,128)(2,1)S(1)},...) custom-call(bf16[1,2,32,4096]{3,2,1,0:T(8,128)(2,1)S(1)} %copy-done.1, ...), custom_call_target="tpu_custom_call" | custom-call | tf_op jit(solution)/shard_map/second_keys/pallas_call | solution.py:484
  24.7 1.3 %collective-permute-start.11 = (bf16[288,128]{1,0:T(8,128)(2,1)S(1)}, bf16[288,128]{1,0:T(8,128)(2,1)S(1)}, u32[]{:S(2)}, u32[]{:S(2)}) collective-permute-start(bf16[288,128]{1,0:T(8,128)(2,1)S(1)} %get-tuple-element.70), channel_id=1, source_target_pairs={{0,5},{1,4},{2,7},{3,6},{4,1},{5,0},{6,3},{7,2},{8,13},{9,12},{10,... | collective-permute-start | bytes 221192 | tf_op jit(solution)/shard_map/ppermute | solution.py:506
  25.9 0.6 %collective-permute-start.12 = (bf16[288,128]{1,0:T(8,128)(2,1)S(1)}, bf16[288,128]{1,0:T(8,128)(2,1)S(1)}, u32[]{:S(2)}, u32[]{:S(2)}) collective-permute-start(bf16[288,128]{1,0:T(8,128)(2,1)S(1)} %get-tuple-element.71), channel_id=1, source_target_pairs={{0,4},{4,0},{1,5},{5,1},{2,6},{6,2},{3,7},{7,3},{8,12},{12,8},{9,1... | collective-permute-start | bytes 221192 | tf_op jit(solution)/shard_map/ppermute | solution.py:500
  26.5 0.8 %collective-permute-start.13 = (bf16[288,128]{1,0:T(8,128)(2,1)S(1)}, bf16[288,128]{1,0:T(8,128)(2,1)S(1)}, u32[]{:S(2)}, u32[]{:S(2)}) collective-permute-start(bf16[288,128]{1,0:T(8,128)(2,1)S(1)} %get-tuple-element.72), channel_id=1, source_target_pairs={{0,1},{1,0},{2,3},{3,2},{4,5},{5,4},{6,7},{7,6},{8,9},{9,8},{10,11... | collective-permute-start | bytes 221192 | tf_op jit(solution)/shard_map/ppermute | solution.py:498
  27.4 0.0 collective-permute-done.9.refs_1_
  27.4 0.7 %collective-permute-start.10 = (bf16[256,128]{1,0:T(8,128)(2,1)S(1)}, bf16[256,128]{1,0:T(8,128)(2,1)S(1)}, u32[]{:S(2)}, u32[]{:S(2)}) collective-permute-start(bf16[256,128]{1,0:T(8,128)(2,1)S(1)} %get-tuple-element.66), channel_id=1, source_target_pairs={{0,1},{1,0},{2,3},{3,2},{4,5},{5,4},{6,7},{7,6},{8,9},{9,8},{10,11... | collective-permute-start | bytes 196616 | tf_op jit(solution)/shard_map/ppermute | solution.py:498
  28.1 1.2 %collective-permute-done.11.refs_2_ = bf16[288,128]{1,0:T(8,128)(2,1)S(1)} collective-permute-done((bf16[288,128]{1,0:T(8,128)(2,1)S(1)}, bf16[288,128]{1,0:T(8,128)(2,1)S(1)}, u32[]{:S(2)}, u32[]{:S(2)}) %collective-permute-start.11) | collective-permute-done | bytes 73760 | tf_op jit(solution)/shard_map/ppermute | solution.py:506
  29.4 0.3 collective-permute-done.12.refs_3_
  29.6 0.3 collective-permute-done.13.refs_4_
  30.0 0.1 second_near.1
  30.0 2.3 %collective-permute-start.15 = (bf16[160,128]{1,0:T(8,128)(2,1)S(1)}, bf16[160,128]{1,0:T(8,128)(2,1)S(1)}, u32[]{:S(2)}, u32[]{:S(2)}) collective-permute-start(bf16[160,128]{1,0:T(8,128)(2,1)S(1)} %get-tuple-element.75), channel_id=1, source_target_pairs={{0,2},{1,3},{2,0},{3,1},{4,6},{5,7},{6,4},{7,5},{8,10},{9,11},{10,... | collective-permute-start | bytes 122888 | tf_op jit(solution)/shard_map/ppermute | solution.py:509
  32.3 0.0 collective-permute-done.10.refs_0_
  32.4 1.0 %collective-permute-start.14 = (bf16[128,128]{1,0:T(8,128)(2,1)S(1)}, bf16[128,128]{1,0:T(8,128)(2,1)S(1)}, u32[]{:S(2)}, u32[]{:S(2)}) collective-permute-start(bf16[128,128]{1,0:T(8,128)(2,1)S(1)} %get-tuple-element.74), channel_id=1, source_target_pairs={{0,2},{1,3},{2,0},{3,1},{4,6},{5,7},{6,4},{7,5},{8,10},{9,11},{10,... | collective-permute-start | bytes 98312 | tf_op jit(solution)/shard_map/ppermute | solution.py:509
  33.4 1.2 %second_rows.1 = bf16[1,2,32,4096]{3,2,1,0:T(8,128)(2,1)} custom-call(bf16[1,2,32,4096]{3,2,1,0:T(8,128)(2,1)S(1)} %copy-done.1, f32[1,4096]{1,0:T(1,128)S(1)} %copy-done.4, f32[2,32,128]{2,1,0:T(8,128)S(1)} %get-tuple-element.42.refs_3_.refs_2_, bf16[32,4096]{1,0:T(8,128)(2,1)S(1)} %get-tuple-element.61.refs_3_, ...), custom_call_target="tpu_custom_call" | custom-call | tf_op jit(solution)/shard_map/second_rows/pallas_call | solution.py:484
  34.5 1.6 %collective-permute-done.14.refs_2_ = bf16[128,128]{1,0:T(8,128)(2,1)S(1)} collective-permute-done((bf16[128,128]{1,0:T(8,128)(2,1)S(1)}, bf16[128,128]{1,0:T(8,128)(2,1)S(1)}, u32[]{:S(2)}, u32[]{:S(2)}) %collective-permute-start.14) | collective-permute-done | bytes 32800 | tf_op jit(solution)/shard_map/ppermute | solution.py:509
  36.1 0.0 collective-permute-done.15.refs_3_
  36.1 0.7 %finish.1 = (f32[1,2,128,128]{3,2,1,0:T(8,128)}, f32[1,2,128,128]{3,2,1,0:T(8,128)}, f32[32,128]{1,0:T(8,128)}) custom-call(f32[128,128]{1,0:T(8,128)S(1)} %get-tuple-element.67.refs_0_, f32[128,128]{1,0:T(8,128)S(1)} %get-tuple-element.73.refs_1_, bf16[128,128]{1,0:T(8,128)(2,1)S(1)} %collective-permute-done.14.refs_2_, ...), custom_call_target="tpu_custom_call" | custom-call | tf_op jit(solution)/shard_map/finish/pallas_call | solution.py:484
  (3 shorter events, 0.1 us)
Async XLA Ops:
  0.6 12.2 %copy-start.2 = (bf16[1,32,4096]{2,1,0:T(8,128)(2,1)S(1)}, bf16[1,32,4096]{2,1,0:T(8,128)(2,1)}, u32[]{:S(2)}) copy-start(bf16[1,32,4096]{2,1,0:T(8,128)(2,1)} %refs_3_.2) | copy-start | bytes 786436
  1.6 9.3 %copy-start.4 = (f32[1,4096]{1,0:T(1,128)S(1)}, f32[1,4096]{1,0:T(1,128)}, u32[]{:S(2)}) copy-start(f32[1,4096]{1,0:T(1,128)} %refs_1_.5) | copy-start | bytes 49156
  1.6 9.3 %copy-start.5 = (s32[5,8]{1,0:T(8,128)S(1)}, s32[5,8]{1,0:T(8,128)}, u32[]{:S(2)}) copy-start(s32[5,8]{1,0:T(8,128)} %doc_ref.1) | copy-start | bytes 484
  1.6 5.9 %collective-permute-start = (bf16[2,2,64,128]{3,2,1,0:T(8,128)(2,1)S(1)}, bf16[2,2,64,128]{3,2,1,0:T(8,128)(2,1)S(1)}, u32[]{:S(2)}, u32[]{:S(2)}) collective-permute-start(bf16[2,2,64,128]{3,2,1,0:T(8,128)(2,1)S(1)} %get-tuple-element.45), channel_id=1, source_target_pairs={{0,2},{1,3},{2,0},{3,1},{4,6},{5,7},{6,4},{7,5},{8,10},{9,11},{10,... | collective-permute-start | bytes 196616 | tf_op jit(solution)/shard_map/ppermute | solution.py:509
  4.8 5.1 %collective-permute-start.4 = (bf16[2,2,64,128]{3,2,1,0:T(8,128)(2,1)S(1)}, bf16[2,2,64,128]{3,2,1,0:T(8,128)(2,1)S(1)}, u32[]{:S(2)}, u32[]{:S(2)}) collective-permute-start(bf16[2,2,64,128]{3,2,1,0:T(8,128)(2,1)S(1)} %get-tuple-element.46.refs_6_.refs_2_.refs_8_), channel_id=1, source_target_pairs={{0,5},{1,4},{2,7},{3,6},{4,1},{5,0},{6,3},{7,2},{8,13},{9,12},{10,... | collective-permute-start | bytes 196616 | tf_op jit(solution)/shard_map/ppermute | solution.py:506
  7.1 5.7 %collective-permute-start.5 = (bf16[2,2,64,128]{3,2,1,0:T(8,128)(2,1)S(1)}, bf16[2,2,64,128]{3,2,1,0:T(8,128)(2,1)S(1)}, u32[]{:S(2)}, u32[]{:S(2)}) collective-permute-start(bf16[2,2,64,128]{3,2,1,0:T(8,128)(2,1)S(1)} %get-tuple-element.46.refs_6_.refs_2_.refs_8_), channel_id=1, source_target_pairs={{0,4},{4,0},{1,5},{5,1},{2,6},{6,2},{3,7},{7,3},{8,12},{12,8},{9,1... | collective-permute-start | bytes 196616 | tf_op jit(solution)/shard_map/ppermute | solution.py:500
  7.3 5.5 %collective-permute-start.6 = (bf16[2,2,64,128]{3,2,1,0:T(8,128)(2,1)S(1)}, bf16[2,2,64,128]{3,2,1,0:T(8,128)(2,1)S(1)}, u32[]{:S(2)}, u32[]{:S(2)}) collective-permute-start(bf16[2,2,64,128]{3,2,1,0:T(8,128)(2,1)S(1)} %get-tuple-element.46.refs_6_.refs_2_.refs_8_), channel_id=1, source_target_pairs={{0,1},{1,0},{2,3},{3,2},{4,5},{5,4},{6,7},{7,6},{8,9},{9,8},{10,11... | collective-permute-start | bytes 196616 | tf_op jit(solution)/shard_map/ppermute | solution.py:498
  7.5 6.1 %collective-permute-start.1 = (bf16[2,2,64,128]{3,2,1,0:T(8,128)(2,1)S(1)}, bf16[2,2,64,128]{3,2,1,0:T(8,128)(2,1)S(1)}, u32[]{:S(2)}, u32[]{:S(2)}) collective-permute-start(bf16[2,2,64,128]{3,2,1,0:T(8,128)(2,1)S(1)} %collective-permute-done.refs_2_.refs_6_.refs_12_), channel_id=1, source_target_pairs={{0,5},{1,4},{2,7},{3,6},{4,1},{5,0},{6,3},{7,2},{8,13},{9,12},{10,... | collective-permute-start | bytes 196616 | tf_op jit(solution)/shard_map/ppermute | solution.py:506
  9.7 3.9 %collective-permute-start.2 = (bf16[2,2,64,128]{3,2,1,0:T(8,128)(2,1)S(1)}, bf16[2,2,64,128]{3,2,1,0:T(8,128)(2,1)S(1)}, u32[]{:S(2)}, u32[]{:S(2)}) collective-permute-start(bf16[2,2,64,128]{3,2,1,0:T(8,128)(2,1)S(1)} %collective-permute-done.refs_2_.refs_6_.refs_12_), channel_id=1, source_target_pairs={{0,4},{4,0},{1,5},{5,1},{2,6},{6,2},{3,7},{7,3},{8,12},{12,8},{9,1... | collective-permute-start | bytes 196616 | tf_op jit(solution)/shard_map/ppermute | solution.py:500
  10.0 3.6 %collective-permute-start.3 = (bf16[2,2,64,128]{3,2,1,0:T(8,128)(2,1)S(1)}, bf16[2,2,64,128]{3,2,1,0:T(8,128)(2,1)S(1)}, u32[]{:S(2)}, u32[]{:S(2)}) collective-permute-start(bf16[2,2,64,128]{3,2,1,0:T(8,128)(2,1)S(1)} %collective-permute-done.refs_2_.refs_6_.refs_12_), channel_id=1, source_target_pairs={{0,1},{1,0},{2,3},{3,2},{4,5},{5,4},{6,7},{7,6},{8,9},{9,8},{10,11... | collective-permute-start | bytes 196616 | tf_op jit(solution)/shard_map/ppermute | solution.py:498
  10.9 1.0 %copy-start = (bf16[1,2,32,4096]{3,2,1,0:T(8,128)(2,1)S(1)}, bf16[1,2,32,4096]{3,2,1,0:T(8,128)(2,1)}, u32[]{:S(2)}) copy-start(bf16[1,2,32,4096]{3,2,1,0:T(8,128)(2,1)} %refs_0_.7) | copy-start | bytes 1572868
  11.9 1.0 %copy-start.1 = (bf16[1,2,32,4096]{3,2,1,0:T(8,128)(2,1)S(1)}, bf16[1,2,32,4096]{3,2,1,0:T(8,128)(2,1)}, u32[]{:S(2)}) copy-start(bf16[1,2,32,4096]{3,2,1,0:T(8,128)(2,1)} %refs_0_.7) | copy-start | bytes 1572868
  14.4 9.7 %collective-permute-start.7 = (bf16[32,4096]{1,0:T(8,128)(2,1)S(1)}, bf16[32,4096]{1,0:T(8,128)(2,1)S(1)}, u32[]{:S(2)}, u32[]{:S(2)}) collective-permute-start(bf16[32,4096]{1,0:T(8,128)(2,1)S(1)} %get-tuple-element.53.refs_5_), channel_id=1, source_target_pairs={{16,8},{17,9},{18,10},{19,11},{20,12},{21,13},{22,14},{23,15}} | collective-permute-start | bytes 786440 | tf_op jit(solution)/shard_map/ppermute | solution.py:567
  15.7 8.4 %collective-permute-start.8 = (bf16[32,4096]{1,0:T(8,128)(2,1)S(1)}, bf16[32,4096]{1,0:T(8,128)(2,1)S(1)}, u32[]{:S(2)}, u32[]{:S(2)}) collective-permute-start(bf16[32,4096]{1,0:T(8,128)(2,1)S(1)} %get-tuple-element.53.refs_5_), channel_id=1, source_target_pairs={{0,8},{8,0},{16,24},{24,16},{1,9},{9,1},{17,25},{25,17},{2,10},{10... | collective-permute-start | bytes 786440 | tf_op jit(solution)/shard_map/ppermute | solution.py:570
  18.5 5.6 %copy-start.3 = (bf16[1,32,4096]{2,1,0:T(8,128)(2,1)S(1)}, bf16[1,32,4096]{2,1,0:T(8,128)(2,1)}, u32[]{:S(2)}) copy-start(bf16[1,32,4096]{2,1,0:T(8,128)(2,1)} %refs_3_.3) | copy-start | bytes 786436
  18.5 8.9 %collective-permute-start.9 = (bf16[2,256,128]{2,1,0:T(8,128)(2,1)S(1)}, bf16[2,256,128]{2,1,0:T(8,128)(2,1)S(1)}, u32[]{:S(2)}, u32[]{:S(2)}) collective-permute-start(bf16[2,256,128]{2,1,0:T(8,128)(2,1)S(1)} %get-tuple-element.64), channel_id=1, source_target_pairs={{0,4},{4,0},{1,5},{5,1},{2,6},{6,2},{3,7},{7,3},{8,12},{12,8},{9,1... | collective-permute-start | bytes 393224 | tf_op jit(solution)/shard_map/ppermute | solution.py:500
  24.7 4.7 %collective-permute-start.11 = (bf16[288,128]{1,0:T(8,128)(2,1)S(1)}, bf16[288,128]{1,0:T(8,128)(2,1)S(1)}, u32[]{:S(2)}, u32[]{:S(2)}) collective-permute-start(bf16[288,128]{1,0:T(8,128)(2,1)S(1)} %get-tuple-element.70), channel_id=1, source_target_pairs={{0,5},{1,4},{2,7},{3,6},{4,1},{5,0},{6,3},{7,2},{8,13},{9,12},{10,... | collective-permute-start | bytes 221192 | tf_op jit(solution)/shard_map/ppermute | solution.py:506
  25.9 3.7 %collective-permute-start.12 = (bf16[288,128]{1,0:T(8,128)(2,1)S(1)}, bf16[288,128]{1,0:T(8,128)(2,1)S(1)}, u32[]{:S(2)}, u32[]{:S(2)}) collective-permute-start(bf16[288,128]{1,0:T(8,128)(2,1)S(1)} %get-tuple-element.71), channel_id=1, source_target_pairs={{0,4},{4,0},{1,5},{5,1},{2,6},{6,2},{3,7},{7,3},{8,12},{12,8},{9,1... | collective-permute-start | bytes 221192 | tf_op jit(solution)/shard_map/ppermute | solution.py:500
  26.5 3.4 %collective-permute-start.13 = (bf16[288,128]{1,0:T(8,128)(2,1)S(1)}, bf16[288,128]{1,0:T(8,128)(2,1)S(1)}, u32[]{:S(2)}, u32[]{:S(2)}) collective-permute-start(bf16[288,128]{1,0:T(8,128)(2,1)S(1)} %get-tuple-element.72), channel_id=1, source_target_pairs={{0,1},{1,0},{2,3},{3,2},{4,5},{5,4},{6,7},{7,6},{8,9},{9,8},{10,11... | collective-permute-start | bytes 221192 | tf_op jit(solution)/shard_map/ppermute | solution.py:498
  27.4 4.9 %collective-permute-start.10 = (bf16[256,128]{1,0:T(8,128)(2,1)S(1)}, bf16[256,128]{1,0:T(8,128)(2,1)S(1)}, u32[]{:S(2)}, u32[]{:S(2)}) collective-permute-start(bf16[256,128]{1,0:T(8,128)(2,1)S(1)} %get-tuple-element.66), channel_id=1, source_target_pairs={{0,1},{1,0},{2,3},{3,2},{4,5},{5,4},{6,7},{7,6},{8,9},{9,8},{10,11... | collective-permute-start | bytes 196616 | tf_op jit(solution)/shard_map/ppermute | solution.py:498
  30.0 6.1 %collective-permute-start.15 = (bf16[160,128]{1,0:T(8,128)(2,1)S(1)}, bf16[160,128]{1,0:T(8,128)(2,1)S(1)}, u32[]{:S(2)}, u32[]{:S(2)}) collective-permute-start(bf16[160,128]{1,0:T(8,128)(2,1)S(1)} %get-tuple-element.75), channel_id=1, source_target_pairs={{0,2},{1,3},{2,0},{3,1},{4,6},{5,7},{6,4},{7,5},{8,10},{9,11},{10,... | collective-permute-start | bytes 122888 | tf_op jit(solution)/shard_map/ppermute | solution.py:509
  32.4 3.7 %collective-permute-start.14 = (bf16[128,128]{1,0:T(8,128)(2,1)S(1)}, bf16[128,128]{1,0:T(8,128)(2,1)S(1)}, u32[]{:S(2)}, u32[]{:S(2)}) collective-permute-start(bf16[128,128]{1,0:T(8,128)(2,1)S(1)} %get-tuple-element.74), channel_id=1, source_target_pairs={{0,2},{1,3},{2,0},{3,1},{4,6},{5,7},{6,4},{7,5},{8,10},{9,11},{10,... | collective-permute-start | bytes 98312 | tf_op jit(solution)/shard_map/ppermute | solution.py:509

commit v15 on v11

--- a/solution.py
+++ b/solution.py
@@ -310,22 +310,28 @@
 
 def second_probs_kernel(sizes, *refs):
     turns = range(sizes[3])
-    mask_ref, query_ref = refs[:2]
-    keys, probs_ref = both_sets(sizes, refs[2:-1]), refs[-1]
+    mask_ref, query_ref, x_ref, inverse_ref = refs[:4]
+    keys, (probs_ref, low_ref, normed_ref) = both_sets(sizes, refs[4:-3]), refs[-3:]
     mask = mask_ref[1]
     scores = []
     for turn in turns:
         query = Group(sizes, turn).stacked(lambda where: query_ref[1, :, where])
         scores.append(dot(keys(turn, 0), query, NT))
     for turn in turns:
-        probs_ref[turn] = probabilities(mask, scores[turn])
+        probs = probabilities(mask, scores[turn])
+        probs_ref[turn] = probs
+        low_ref[turn] = probs.astype(BF16)
+    inverse = inverse_ref[1]
+    for first in range(0, sizes[5], HD):
+        here = slice(first, first + HD)
+        normed_ref[:, here] = x_ref[0, 1, :, here].astype(F32) * inverse
 
 
 def second_keys_kernel(sizes, *refs):
     cycle, tp_count = sizes[2:4]
     turns = range(tp_count)
     kv_count = cycle * tp_count
-    x_ref, query_ref, inverse_ref, output_ref, chip_ref, link_ref = refs[:6]
+    normed_ref, query_ref, low_ref, output_ref, chip_ref, link_ref = refs[:6]
     probs_ref, before_ref, *refs = refs[6:]
     keys, refs = both_sets(sizes, refs[:kv_count]), refs[kv_count:]
     query_grad_ref, gain_rows_ref, own_ref, arriving_ref = refs[:4]
@@ -335,11 +341,10 @@
     def arriving(where):
         return arriving_ref[:, where]
 
-    normed_of = normed_from(x_ref, 1, inverse_ref[1])
     columns_of = [Group(sizes, turn) for turn in turns]
     grads = [columns_of[turn].stacked(arriving) for turn in turns]
     prob_grads = [dot(keys(turn, 1), grads[turn], NT) for turn in turns]
-    value_grads = [dot(probs_ref[turn].astype(BF16), grads[turn], NN) for turn in turns]
+    value_grads = [dot(low_ref[turn], grads[turn], NN) for turn in turns]
     dscores = [score_grads(probs_ref[turn], prob_grads[turn]) for turn in turns]
     query_grads = [
         (SCALE * dot(dscores[turn], keys(turn, 0), TN)).astype(BF16) for turn in turns
@@ -350,7 +355,9 @@
         put_key_grads(sizes, turn, (key_grad, value_grads[turn]), own_ref, message_refs)
     for turn in turns:
         query_grad_ref[turn] = query_grads[turn]
-        gain_terms(columns_of[turn], query_grads[turn], normed_of, gain_scratch)
+        gain_terms(
+            columns_of[turn], query_grads[turn], lambda where: normed_ref[:, where], gain_scratch
+        )
     gain_rows = gain_scratch[...] + before_ref[...]
     gain_rows_ref[...] = gain_rows
     gain_low = gain_rows.astype(BF16)
@@ -585,20 +592,24 @@
     sums_first = sums_first[:1] + [
         to_near(value, -step, 0) for step, value in enumerate(sums_first[1:], 1)
     ]
-    (probs_second,) = call(
+    probs_second, probs_low, normed_second = call(
         functools.partial(second_probs_kernel, sizes),
         "second_probs",
-        (masks, queries, *kv),
-        [shape((tp_count, key_count, stacked), F32)],
+        (masks, queries, segment_inputs, inverse, *kv),
+        [
+            shape((tp_count, key_count, stacked), F32),
+            shape((tp_count, key_count, stacked), BF16),
+            shape((rows, columns), F32),
+        ],
     )
     message = shape((pair_rows + gain_count, HD), BF16)
     query_grad_second, gain_rows, own_second, arriving, *sends = call(
         functools.partial(second_keys_kernel, sizes),
         "second_keys",
         (
-            segment_inputs,
+            normed_second,
             queries,
-            inverse,
+            probs_low,
             output_grads,
             on_chip,
             over_link,

time: 37.1 us -> 37.1 us (level)
  no operation moved by 1% of the time
where the time goes in v15:
time: 37.1 us; the launch traced here: 36.9 us
  starting transfers between devices  20.9 us (56%)
  waiting for transfers between devices  7.52 us (20%)
  Pallas kernels  5.64 us (15%)
  local copies, waits for them, and re-layouts  1.15 us (3%)
  other arithmetic  0.93 us (3%)
  between operations  0.8 us (2%)
    ppermute x3, starting transfers between devices, to_far(): lax.ppermute(value, 'tp', [(i, i ^ near_count) for i in range(tp_count)])  6.35 us
    ppermute x3, starting transfers between devices, to_near(): return lax.ppermute(value, ('ctx', 'tp'), pairs)  5.69 us
    pallas_call x12, Pallas kernels, call(): pl.pallas_call(kernel, out_shape=out_shape, in_specs=in_specs, out_specs=...  5.64 us
    ppermute x1, waiting for transfers between devices, on_device(): lax.ppermute(input_grad_first, 'pipe', [(i, i - 1) for i in range(2, pipe...  3.82 us
    ppermute x4, starting transfers between devices, to_near(): return lax.ppermute(value, 'tp', [(i, i ^ near) for i in range(tp_count)])  2.58 us
    ppermute x1, starting transfers between devices, on_device(): lax.ppermute(input_grad_first, 'pipe', [(i, i ^ 1) for i in range(pipe_co...  2.53 us
    ppermute x4, starting transfers between devices, to_near(): lax.ppermute(value, 'ctx', [(i, (i + step) % cycle) for i in range(cycle)])  2.44 us
    ppermute x3, waiting for transfers between devices, to_far(): lax.ppermute(value, 'tp', [(i, i ^ near_count) for i in range(tp_count)])  1.75 us
  transfers between devices with their start and end apart: 16, of which 5 were waited for; matrix products, arithmetic and copies ran while one was open for 0% of the time, Pallas kernels for 11%

profile of v15, /device:TPU:1, one launch (start us, length us, event | category | flops | bytes accessed | tf_op | source)
XLA Modules:
  0.0 36.9 jit_solution(13711980375672857660)
XLA Ops:
  0.6 0.0 copy-start.2
  0.6 0.9 %pad_maximum_fusion.both_ref = bf16[2,2,128,128]{3,2,1,0:T(8,128)(2,1)S(1)} fusion(bf16[1,2,128,128]{3,2,1,0:T(8,128)(2,1)} %param.9, bf16[1,2,128,128]{3,2,1,0:T(8,128)(2,1)} %param.8), kind=kLoop, calls=%fused_computation | loop fusion | flops 65536 | bytes 262144 | tf_op jit(solution)/shard_map/stack | solution.py:513
  1.6 0.0 copy-start.3
  1.6 0.0 copy-start.5
  1.6 3.2 %collective-permute-start.3 = (bf16[2,2,64,128]{3,2,1,0:T(8,128)(2,1)S(1)}, bf16[2,2,64,128]{3,2,1,0:T(8,128)(2,1)S(1)}, u32[]{:S(2)}, u32[]{:S(2)}) collective-permute-start(bf16[2,2,64,128]{3,2,1,0:T(8,128)(2,1)S(1)} %get-tuple-element.45), channel_id=1, source_target_pairs={{0,2},{1,3},{2,0},{3,1},{4,6},{5,7},{6,4},{7,5},{8,10},{9,11},{10,... | collective-permute-start | bytes 196616 | tf_op jit(solution)/shard_map/ppermute | solution.py:507
  4.8 2.3 %collective-permute-start.2 = (bf16[2,2,64,128]{3,2,1,0:T(8,128)(2,1)S(1)}, bf16[2,2,64,128]{3,2,1,0:T(8,128)(2,1)S(1)}, u32[]{:S(2)}, u32[]{:S(2)}) collective-permute-start(bf16[2,2,64,128]{3,2,1,0:T(8,128)(2,1)S(1)} %get-tuple-element.44.refs_4_.refs_6_.refs_8_), channel_id=1, source_target_pairs={{0,5},{1,4},{2,7},{3,6},{4,1},{5,0},{6,3},{7,2},{8,13},{9,12},{10,... | collective-permute-start | bytes 196616 | tf_op jit(solution)/shard_map/ppermute | solution.py:504
  7.1 0.2 collective-permute-start.1
  7.3 0.2 collective-permute-start
  7.5 0.0 collective-permute-done.3.refs_8_.refs_5_.refs_12_
  7.5 2.3 %collective-permute-start.6 = (bf16[2,2,64,128]{3,2,1,0:T(8,128)(2,1)S(1)}, bf16[2,2,64,128]{3,2,1,0:T(8,128)(2,1)S(1)}, u32[]{:S(2)}, u32[]{:S(2)}) collective-permute-start(bf16[2,2,64,128]{3,2,1,0:T(8,128)(2,1)S(1)} %collective-permute-done.3.refs_8_.refs_5_.refs_12_), channel_id=1, source_target_pairs={{0,5},{1,4},{2,7},{3,6},{4,1},{5,0},{6,3},{7,2},{8,13},{9,12},{10,... | collective-permute-start | bytes 196616 | tf_op jit(solution)/shard_map/ppermute | solution.py:504
  9.7 0.2 collective-permute-start.5
  10.0 0.0 collective-permute-done.2.refs_7_.refs_9_.refs_11_
  10.0 0.9 %collective-permute-start.4 = (bf16[2,2,64,128]{3,2,1,0:T(8,128)(2,1)S(1)}, bf16[2,2,64,128]{3,2,1,0:T(8,128)(2,1)S(1)}, u32[]{:S(2)}, u32[]{:S(2)}) collective-permute-start(bf16[2,2,64,128]{3,2,1,0:T(8,128)(2,1)S(1)} %collective-permute-done.3.refs_8_.refs_5_.refs_12_), channel_id=1, source_target_pairs={{0,1},{1,0},{2,3},{3,2},{4,5},{5,4},{6,7},{7,6},{8,9},{9,8},{10,11... | collective-permute-start | bytes 196616 | tf_op jit(solution)/shard_map/ppermute | solution.py:496
  10.8 0.0 copy-done.3
  10.8 0.0 copy-done.5
  10.9 0.0 copy-start
  10.9 1.0 %copy-done = bf16[1,2,32,4096]{3,2,1,0:T(8,128)(2,1)S(1)} copy-done((bf16[1,2,32,4096]{3,2,1,0:T(8,128)(2,1)S(1)}, bf16[1,2,32,4096]{3,2,1,0:T(8,128)(2,1)}, u32[]{:S(2)}) %copy-start) | copy-done | bytes 524312
  11.9 0.0 copy-start.1
  11.9 0.9 %norm.1 = (bf16[2,32,4096]{2,1,0:T(8,128)(2,1)S(1)}, f32[2,32,128]{2,1,0:T(8,128)S(1)}, f32[2,128,256]{2,1,0:T(8,128)S(1)}) custom-call(s32[5,8]{1,0:T(8,128)S(1)} %copy-done.5, bf16[1,2,32,4096]{3,2,1,0:T(8,128)(2,1)S(1)} %copy-done, f32[1,4096]{1,0:T(1,128)S(1)} %copy-done.3), custom_call_target="tpu_custom_call" | custom-call | tf_op jit(solution)/shard_map/norm/pallas_call | solution.py:482
  12.8 0.0 collective-permute-done.1.refs_6_.refs_8_.refs_10_
  12.8 0.0 collective-permute-done.refs_5_.refs_7_.refs_9_
  12.8 0.0 copy-done.2
  12.9 0.1 copy-done.1
  12.9 0.5 %first_near_rows.1 = (bf16[2,256,128]{2,1,0:T(8,128)(2,1)S(1)}, bf16[2,128,256]{2,1,0:T(8,128)(2,1)S(1)}, bf16[2,128,256]{2,1,0:T(8,128)(2,1)S(1)}, f32[32,128]{1,0:T(8,128)S(1)}, bf16[2,2,128,256]{3,2,1,0:T(8,128)(2,1)S(1)}) custom-call(bf16[1,2,32,4096]{3,2,1,0:T(8,128)(2,1)S(1)} %copy-done.1, f32[1,4096]{1,0:T(1,128)S(1)} %copy-done.3, ...), custom_call_target="tpu_custom_call" | custom-call | tf_op jit(solution)/shard_map/first_near_rows/pallas_call | solution.py:482
  13.5 0.0 collective-permute-done.6.refs_11_.refs_8_.refs_15_
  13.5 0.0 collective-permute-done.5.refs_10_.refs_7_.refs_14_
  13.5 0.0 collective-permute-done.4.refs_9_.refs_6_.refs_13_
  13.5 0.8 %first_far_rows.1 = (bf16[32,4096]{1,0:T(8,128)(2,1)S(1)}, bf16[2,256,128]{2,1,0:T(8,128)(2,1)S(1)}, bf16[2,128,256]{2,1,0:T(8,128)(2,1)S(1)}, bf16[2,128,256]{2,1,0:T(8,128)(2,1)S(1)}) custom-call(bf16[1,2,32,4096]{3,2,1,0:T(8,128)(2,1)S(1)} %copy-done.1, f32[1,4096]{1,0:T(1,128)S(1)} %copy-done.3, f32[2,32,128]{2,1,0:T(8,128)S(1)} %get-tuple-element.41.refs_3_.refs_2_, ...), custom_call_target="tpu_custom_call" | custom-call | tf_op jit(solution)/shard_map/first_far_rows/pallas_call | solution.py:482
  14.3 1.3 %collective-permute-start.8 = (bf16[32,4096]{1,0:T(8,128)(2,1)S(1)}, bf16[32,4096]{1,0:T(8,128)(2,1)S(1)}, u32[]{:S(2)}, u32[]{:S(2)}) collective-permute-start(bf16[32,4096]{1,0:T(8,128)(2,1)S(1)} %get-tuple-element.51.refs_5_), channel_id=1, source_target_pairs={{16,8},{17,9},{18,10},{19,11},{20,12},{21,13},{22,14},{23,15}} | collective-permute-start | bytes 786440 | tf_op jit(solution)/shard_map/ppermute | solution.py:567
  15.6 2.5 %collective-permute-start.7 = (bf16[32,4096]{1,0:T(8,128)(2,1)S(1)}, bf16[32,4096]{1,0:T(8,128)(2,1)S(1)}, u32[]{:S(2)}, u32[]{:S(2)}) collective-permute-start(bf16[32,4096]{1,0:T(8,128)(2,1)S(1)} %get-tuple-element.51.refs_5_), channel_id=1, source_target_pairs={{0,8},{8,0},{16,24},{24,16},{1,9},{9,1},{17,25},{25,17},{2,10},{10... | collective-permute-start | bytes 786440 | tf_op jit(solution)/shard_map/ppermute | solution.py:570
  18.1 0.4 %first_keys.1 = (f32[32,128]{1,0:T(8,128)S(1)}, f32[2,256,128]{2,1,0:T(8,128)S(1)}, bf16[2,256,128]{2,1,0:T(8,128)(2,1)S(1)}) custom-call(bf16[1,2,32,4096]{3,2,1,0:T(8,128)(2,1)S(1)} %copy-done.1, bf16[2,32,4096]{2,1,0:T(8,128)(2,1)S(1)} %get-tuple-element.43.refs_1_.refs_2_, f32[2,32,128]{2,1,0:T(8,128)S(1)} %get-tuple-element.41.refs_3_.refs_2_, ...), custom_call_target="tpu_custom_call" | custom-call | tf_op jit(solution)/shard_map/first_keys/pallas_call | solution.py:482
  18.5 0.0 copy-start.4
  18.6 1.3 %collective-permute-start.9 = (bf16[2,256,128]{2,1,0:T(8,128)(2,1)S(1)}, bf16[2,256,128]{2,1,0:T(8,128)(2,1)S(1)}, u32[]{:S(2)}, u32[]{:S(2)}) collective-permute-start(bf16[2,256,128]{2,1,0:T(8,128)(2,1)S(1)} %get-tuple-element.62), channel_id=1, source_target_pairs={{0,4},{4,0},{1,5},{5,1},{2,6},{6,2},{3,7},{7,3},{8,12},{12,8},{9,1... | collective-permute-start | bytes 393224 | tf_op jit(solution)/shard_map/ppermute | solution.py:498
  19.9 0.4 %second_probs.1 = (f32[4,128,256]{2,1,0:T(8,128)S(1)}, bf16[4,128,256]{2,1,0:T(8,128)(2,1)S(1)}, f32[32,4096]{1,0:T(8,128)S(1)}) custom-call(f32[2,128,256]{2,1,0:T(8,128)S(1)} %get-tuple-element.42.refs_0_.refs_4_.refs_3_, bf16[2,32,4096]{2,1,0:T(8,128)(2,1)S(1)} %get-tuple-element.43.refs_1_.refs_2_, bf16[1,2,32,4096]{3,2,1,0:T(8,128)(2,1)S(1)} %copy-done.1, ...), custom_call_target="tpu_custom_call" | custom-call | tf_op jit(solution)/shard_map/second_probs/pallas_call | solution.py:482
  20.3 3.8 %collective-permute-done.8.refs_5_ = bf16[32,4096]{1,0:T(8,128)(2,1)S(1)} collective-permute-done((bf16[32,4096]{1,0:T(8,128)(2,1)S(1)}, bf16[32,4096]{1,0:T(8,128)(2,1)S(1)}, u32[]{:S(2)}, u32[]{:S(2)}) %collective-permute-start.8) | collective-permute-done | bytes 262176 | tf_op jit(solution)/shard_map/ppermute | solution.py:567
  24.1 0.0 collective-permute-done.7.refs_4_
  24.1 0.0 copy-done.4
  24.1 0.6 %second_keys.1 = (bf16[4,256,128]{2,1,0:T(8,128)(2,1)S(1)}, f32[32,128]{1,0:T(8,128)S(1)}, f32[256,128]{1,0:T(8,128)S(1)}, bf16[32,4096]{1,0:T(8,128)(2,1)S(1)},...) custom-call(f32[32,4096]{1,0:T(8,128)S(1)} %get-tuple-element.46.refs_0_, ...), custom_call_target="tpu_custom_call" | custom-call | tf_op jit(solution)/shard_map/second_keys/pallas_call | solution.py:482
  24.7 1.2 %collective-permute-start.11 = (bf16[288,128]{1,0:T(8,128)(2,1)S(1)}, bf16[288,128]{1,0:T(8,128)(2,1)S(1)}, u32[]{:S(2)}, u32[]{:S(2)}) collective-permute-start(bf16[288,128]{1,0:T(8,128)(2,1)S(1)} %get-tuple-element.68), channel_id=1, source_target_pairs={{0,5},{1,4},{2,7},{3,6},{4,1},{5,0},{6,3},{7,2},{8,13},{9,12},{10,... | collective-permute-start | bytes 221192 | tf_op jit(solution)/shard_map/ppermute | solution.py:504
  25.9 0.7 %collective-permute-start.12 = (bf16[288,128]{1,0:T(8,128)(2,1)S(1)}, bf16[288,128]{1,0:T(8,128)(2,1)S(1)}, u32[]{:S(2)}, u32[]{:S(2)}) collective-permute-start(bf16[288,128]{1,0:T(8,128)(2,1)S(1)} %get-tuple-element.69), channel_id=1, source_target_pairs={{0,4},{4,0},{1,5},{5,1},{2,6},{6,2},{3,7},{7,3},{8,12},{12,8},{9,1... | collective-permute-start | bytes 221192 | tf_op jit(solution)/shard_map/ppermute | solution.py:498
  26.5 0.8 %collective-permute-start.13 = (bf16[288,128]{1,0:T(8,128)(2,1)S(1)}, bf16[288,128]{1,0:T(8,128)(2,1)S(1)}, u32[]{:S(2)}, u32[]{:S(2)}) collective-permute-start(bf16[288,128]{1,0:T(8,128)(2,1)S(1)} %get-tuple-element.70), channel_id=1, source_target_pairs={{0,1},{1,0},{2,3},{3,2},{4,5},{5,4},{6,7},{7,6},{8,9},{9,8},{10,11... | collective-permute-start | bytes 221192 | tf_op jit(solution)/shard_map/ppermute | solution.py:496
  27.4 0.0 collective-permute-done.9.refs_1_
  27.4 0.7 %collective-permute-start.10 = (bf16[256,128]{1,0:T(8,128)(2,1)S(1)}, bf16[256,128]{1,0:T(8,128)(2,1)S(1)}, u32[]{:S(2)}, u32[]{:S(2)}) collective-permute-start(bf16[256,128]{1,0:T(8,128)(2,1)S(1)} %get-tuple-element.64), channel_id=1, source_target_pairs={{0,1},{1,0},{2,3},{3,2},{4,5},{5,4},{6,7},{7,6},{8,9},{9,8},{10,11... | collective-permute-start | bytes 196616 | tf_op jit(solution)/shard_map/ppermute | solution.py:496
  28.1 1.2 %collective-permute-done.11.refs_2_ = bf16[288,128]{1,0:T(8,128)(2,1)S(1)} collective-permute-done((bf16[288,128]{1,0:T(8,128)(2,1)S(1)}, bf16[288,128]{1,0:T(8,128)(2,1)S(1)}, u32[]{:S(2)}, u32[]{:S(2)}) %collective-permute-start.11) | collective-permute-done | bytes 73760 | tf_op jit(solution)/shard_map/ppermute | solution.py:504
  29.3 0.3 collective-permute-done.12.refs_3_
  29.6 0.4 %collective-permute-done.13.refs_4_ = bf16[288,128]{1,0:T(8,128)(2,1)S(1)} collective-permute-done((bf16[288,128]{1,0:T(8,128)(2,1)S(1)}, bf16[288,128]{1,0:T(8,128)(2,1)S(1)}, u32[]{:S(2)}, u32[]{:S(2)}) %collective-permute-start.13) | collective-permute-done | bytes 73760 | tf_op jit(solution)/shard_map/ppermute | solution.py:496
  30.0 0.1 second_near.1
  30.1 2.3 %collective-permute-start.15 = (bf16[160,128]{1,0:T(8,128)(2,1)S(1)}, bf16[160,128]{1,0:T(8,128)(2,1)S(1)}, u32[]{:S(2)}, u32[]{:S(2)}) collective-permute-start(bf16[160,128]{1,0:T(8,128)(2,1)S(1)} %get-tuple-element.73), channel_id=1, source_target_pairs={{0,2},{1,3},{2,0},{3,1},{4,6},{5,7},{6,4},{7,5},{8,10},{9,11},{10,... | collective-permute-start | bytes 122888 | tf_op jit(solution)/shard_map/ppermute | solution.py:507
  32.4 0.0 collective-permute-done.10.refs_0_
  32.4 0.8 %collective-permute-start.14 = (bf16[128,128]{1,0:T(8,128)(2,1)S(1)}, bf16[128,128]{1,0:T(8,128)(2,1)S(1)}, u32[]{:S(2)}, u32[]{:S(2)}) collective-permute-start(bf16[128,128]{1,0:T(8,128)(2,1)S(1)} %get-tuple-element.72), channel_id=1, source_target_pairs={{0,2},{1,3},{2,0},{3,1},{4,6},{5,7},{6,4},{7,5},{8,10},{9,11},{10,... | collective-permute-start | bytes 98312 | tf_op jit(solution)/shard_map/ppermute | solution.py:507
  33.3 1.2 %second_rows.1 = bf16[1,2,32,4096]{3,2,1,0:T(8,128)(2,1)} custom-call(bf16[1,2,32,4096]{3,2,1,0:T(8,128)(2,1)S(1)} %copy-done.1, f32[1,4096]{1,0:T(1,128)S(1)} %copy-done.3, f32[2,32,128]{2,1,0:T(8,128)S(1)} %get-tuple-element.41.refs_3_.refs_2_, bf16[32,4096]{1,0:T(8,128)(2,1)S(1)} %get-tuple-element.59.refs_3_, ...), custom_call_target="tpu_custom_call" | custom-call | tf_op jit(solution)/shard_map/second_rows/pallas_call | solution.py:482
  34.4 1.7 %collective-permute-done.14.refs_2_ = bf16[128,128]{1,0:T(8,128)(2,1)S(1)} collective-permute-done((bf16[128,128]{1,0:T(8,128)(2,1)S(1)}, bf16[128,128]{1,0:T(8,128)(2,1)S(1)}, u32[]{:S(2)}, u32[]{:S(2)}) %collective-permute-start.14) | collective-permute-done | bytes 32800 | tf_op jit(solution)/shard_map/ppermute | solution.py:507
  36.2 0.0 collective-permute-done.15.refs_3_
  36.2 0.7 %finish.1 = (f32[1,2,128,128]{3,2,1,0:T(8,128)}, f32[1,2,128,128]{3,2,1,0:T(8,128)}, f32[32,128]{1,0:T(8,128)}) custom-call(f32[128,128]{1,0:T(8,128)S(1)} %get-tuple-element.65.refs_0_, f32[128,128]{1,0:T(8,128)S(1)} %get-tuple-element.71.refs_1_, bf16[128,128]{1,0:T(8,128)(2,1)S(1)} %collective-permute-done.14.refs_2_, ...), custom_call_target="tpu_custom_call" | custom-call | tf_op jit(solution)/shard_map/finish/pallas_call | solution.py:482
  (3 shorter events, 0.1 us)
Async XLA Ops:
  0.6 12.2 %copy-start.2 = (bf16[1,32,4096]{2,1,0:T(8,128)(2,1)S(1)}, bf16[1,32,4096]{2,1,0:T(8,128)(2,1)}, u32[]{:S(2)}) copy-start(bf16[1,32,4096]{2,1,0:T(8,128)(2,1)} %refs_3_.2) | copy-start | bytes 786436
  1.6 9.3 %copy-start.3 = (f32[1,4096]{1,0:T(1,128)S(1)}, f32[1,4096]{1,0:T(1,128)}, u32[]{:S(2)}) copy-start(f32[1,4096]{1,0:T(1,128)} %refs_1_.5) | copy-start | bytes 49156
  1.6 9.3 %copy-start.5 = (s32[5,8]{1,0:T(8,128)S(1)}, s32[5,8]{1,0:T(8,128)}, u32[]{:S(2)}) copy-start(s32[5,8]{1,0:T(8,128)} %doc_ref.1) | copy-start | bytes 484
  1.6 5.9 %collective-permute-start.3 = (bf16[2,2,64,128]{3,2,1,0:T(8,128)(2,1)S(1)}, bf16[2,2,64,128]{3,2,1,0:T(8,128)(2,1)S(1)}, u32[]{:S(2)}, u32[]{:S(2)}) collective-permute-start(bf16[2,2,64,128]{3,2,1,0:T(8,128)(2,1)S(1)} %get-tuple-element.45), channel_id=1, source_target_pairs={{0,2},{1,3},{2,0},{3,1},{4,6},{5,7},{6,4},{7,5},{8,10},{9,11},{10,... | collective-permute-start | bytes 196616 | tf_op jit(solution)/shard_map/ppermute | solution.py:507
  4.8 5.1 %collective-permute-start.2 = (bf16[2,2,64,128]{3,2,1,0:T(8,128)(2,1)S(1)}, bf16[2,2,64,128]{3,2,1,0:T(8,128)(2,1)S(1)}, u32[]{:S(2)}, u32[]{:S(2)}) collective-permute-start(bf16[2,2,64,128]{3,2,1,0:T(8,128)(2,1)S(1)} %get-tuple-element.44.refs_4_.refs_6_.refs_8_), channel_id=1, source_target_pairs={{0,5},{1,4},{2,7},{3,6},{4,1},{5,0},{6,3},{7,2},{8,13},{9,12},{10,... | collective-permute-start | bytes 196616 | tf_op jit(solution)/shard_map/ppermute | solution.py:504
  7.1 5.7 %collective-permute-start.1 = (bf16[2,2,64,128]{3,2,1,0:T(8,128)(2,1)S(1)}, bf16[2,2,64,128]{3,2,1,0:T(8,128)(2,1)S(1)}, u32[]{:S(2)}, u32[]{:S(2)}) collective-permute-start(bf16[2,2,64,128]{3,2,1,0:T(8,128)(2,1)S(1)} %get-tuple-element.44.refs_4_.refs_6_.refs_8_), channel_id=1, source_target_pairs={{0,4},{4,0},{1,5},{5,1},{2,6},{6,2},{3,7},{7,3},{8,12},{12,8},{9,1... | collective-permute-start | bytes 196616 | tf_op jit(solution)/shard_map/ppermute | solution.py:498
  7.3 5.5 %collective-permute-start = (bf16[2,2,64,128]{3,2,1,0:T(8,128)(2,1)S(1)}, bf16[2,2,64,128]{3,2,1,0:T(8,128)(2,1)S(1)}, u32[]{:S(2)}, u32[]{:S(2)}) collective-permute-start(bf16[2,2,64,128]{3,2,1,0:T(8,128)(2,1)S(1)} %get-tuple-element.44.refs_4_.refs_6_.refs_8_), channel_id=1, source_target_pairs={{0,1},{1,0},{2,3},{3,2},{4,5},{5,4},{6,7},{7,6},{8,9},{9,8},{10,11... | collective-permute-start | bytes 196616 | tf_op jit(solution)/shard_map/ppermute | solution.py:496
  7.5 6.0 %collective-permute-start.6 = (bf16[2,2,64,128]{3,2,1,0:T(8,128)(2,1)S(1)}, bf16[2,2,64,128]{3,2,1,0:T(8,128)(2,1)S(1)}, u32[]{:S(2)}, u32[]{:S(2)}) collective-permute-start(bf16[2,2,64,128]{3,2,1,0:T(8,128)(2,1)S(1)} %collective-permute-done.3.refs_8_.refs_5_.refs_12_), channel_id=1, source_target_pairs={{0,5},{1,4},{2,7},{3,6},{4,1},{5,0},{6,3},{7,2},{8,13},{9,12},{10,... | collective-permute-start | bytes 196616 | tf_op jit(solution)/shard_map/ppermute | solution.py:504
  9.7 3.8 %collective-permute-start.5 = (bf16[2,2,64,128]{3,2,1,0:T(8,128)(2,1)S(1)}, bf16[2,2,64,128]{3,2,1,0:T(8,128)(2,1)S(1)}, u32[]{:S(2)}, u32[]{:S(2)}) collective-permute-start(bf16[2,2,64,128]{3,2,1,0:T(8,128)(2,1)S(1)} %collective-permute-done.3.refs_8_.refs_5_.refs_12_), channel_id=1, source_target_pairs={{0,4},{4,0},{1,5},{5,1},{2,6},{6,2},{3,7},{7,3},{8,12},{12,8},{9,1... | collective-permute-start | bytes 196616 | tf_op jit(solution)/shard_map/ppermute | solution.py:498
  10.0 3.5 %collective-permute-start.4 = (bf16[2,2,64,128]{3,2,1,0:T(8,128)(2,1)S(1)}, bf16[2,2,64,128]{3,2,1,0:T(8,128)(2,1)S(1)}, u32[]{:S(2)}, u32[]{:S(2)}) collective-permute-start(bf16[2,2,64,128]{3,2,1,0:T(8,128)(2,1)S(1)} %collective-permute-done.3.refs_8_.refs_5_.refs_12_), channel_id=1, source_target_pairs={{0,1},{1,0},{2,3},{3,2},{4,5},{5,4},{6,7},{7,6},{8,9},{9,8},{10,11... | collective-permute-start | bytes 196616 | tf_op jit(solution)/shard_map/ppermute | solution.py:496
  10.9 1.0 %copy-start = (bf16[1,2,32,4096]{3,2,1,0:T(8,128)(2,1)S(1)}, bf16[1,2,32,4096]{3,2,1,0:T(8,128)(2,1)}, u32[]{:S(2)}) copy-start(bf16[1,2,32,4096]{3,2,1,0:T(8,128)(2,1)} %refs_0_.7) | copy-start | bytes 1572868
  11.9 1.0 %copy-start.1 = (bf16[1,2,32,4096]{3,2,1,0:T(8,128)(2,1)S(1)}, bf16[1,2,32,4096]{3,2,1,0:T(8,128)(2,1)}, u32[]{:S(2)}) copy-start(bf16[1,2,32,4096]{3,2,1,0:T(8,128)(2,1)} %refs_0_.7) | copy-start | bytes 1572868
  14.3 9.8 %collective-permute-start.8 = (bf16[32,4096]{1,0:T(8,128)(2,1)S(1)}, bf16[32,4096]{1,0:T(8,128)(2,1)S(1)}, u32[]{:S(2)}, u32[]{:S(2)}) collective-permute-start(bf16[32,4096]{1,0:T(8,128)(2,1)S(1)} %get-tuple-element.51.refs_5_), channel_id=1, source_target_pairs={{16,8},{17,9},{18,10},{19,11},{20,12},{21,13},{22,14},{23,15}} | collective-permute-start | bytes 786440 | tf_op jit(solution)/shard_map/ppermute | solution.py:567
  15.6 8.5 %collective-permute-start.7 = (bf16[32,4096]{1,0:T(8,128)(2,1)S(1)}, bf16[32,4096]{1,0:T(8,128)(2,1)S(1)}, u32[]{:S(2)}, u32[]{:S(2)}) collective-permute-start(bf16[32,4096]{1,0:T(8,128)(2,1)S(1)} %get-tuple-element.51.refs_5_), channel_id=1, source_target_pairs={{0,8},{8,0},{16,24},{24,16},{1,9},{9,1},{17,25},{25,17},{2,10},{10... | collective-permute-start | bytes 786440 | tf_op jit(solution)/shard_map/ppermute | solution.py:570
  18.5 5.5 %copy-start.4 = (bf16[1,32,4096]{2,1,0:T(8,128)(2,1)S(1)}, bf16[1,32,4096]{2,1,0:T(8,128)(2,1)}, u32[]{:S(2)}) copy-start(bf16[1,32,4096]{2,1,0:T(8,128)(2,1)} %refs_3_.3) | copy-start | bytes 786436
  18.6 8.8 %collective-permute-start.9 = (bf16[2,256,128]{2,1,0:T(8,128)(2,1)S(1)}, bf16[2,256,128]{2,1,0:T(8,128)(2,1)S(1)}, u32[]{:S(2)}, u32[]{:S(2)}) collective-permute-start(bf16[2,256,128]{2,1,0:T(8,128)(2,1)S(1)} %get-tuple-element.62), channel_id=1, source_target_pairs={{0,4},{4,0},{1,5},{5,1},{2,6},{6,2},{3,7},{7,3},{8,12},{12,8},{9,1... | collective-permute-start | bytes 393224 | tf_op jit(solution)/shard_map/ppermute | solution.py:498
  24.7 4.6 %collective-permute-start.11 = (bf16[288,128]{1,0:T(8,128)(2,1)S(1)}, bf16[288,128]{1,0:T(8,128)(2,1)S(1)}, u32[]{:S(2)}, u32[]{:S(2)}) collective-permute-start(bf16[288,128]{1,0:T(8,128)(2,1)S(1)} %get-tuple-element.68), channel_id=1, source_target_pairs={{0,5},{1,4},{2,7},{3,6},{4,1},{5,0},{6,3},{7,2},{8,13},{9,12},{10,... | collective-permute-start | bytes 221192 | tf_op jit(solution)/shard_map/ppermute | solution.py:504
  25.9 3.8 %collective-permute-start.12 = (bf16[288,128]{1,0:T(8,128)(2,1)S(1)}, bf16[288,128]{1,0:T(8,128)(2,1)S(1)}, u32[]{:S(2)}, u32[]{:S(2)}) collective-permute-start(bf16[288,128]{1,0:T(8,128)(2,1)S(1)} %get-tuple-element.69), channel_id=1, source_target_pairs={{0,4},{4,0},{1,5},{5,1},{2,6},{6,2},{3,7},{7,3},{8,12},{12,8},{9,1... | collective-permute-start | bytes 221192 | tf_op jit(solution)/shard_map/ppermute | solution.py:498
  26.5 3.5 %collective-permute-start.13 = (bf16[288,128]{1,0:T(8,128)(2,1)S(1)}, bf16[288,128]{1,0:T(8,128)(2,1)S(1)}, u32[]{:S(2)}, u32[]{:S(2)}) collective-permute-start(bf16[288,128]{1,0:T(8,128)(2,1)S(1)} %get-tuple-element.70), channel_id=1, source_target_pairs={{0,1},{1,0},{2,3},{3,2},{4,5},{5,4},{6,7},{7,6},{8,9},{9,8},{10,11... | collective-permute-start | bytes 221192 | tf_op jit(solution)/shard_map/ppermute | solution.py:496
  27.4 5.0 %collective-permute-start.10 = (bf16[256,128]{1,0:T(8,128)(2,1)S(1)}, bf16[256,128]{1,0:T(8,128)(2,1)S(1)}, u32[]{:S(2)}, u32[]{:S(2)}) collective-permute-start(bf16[256,128]{1,0:T(8,128)(2,1)S(1)} %get-tuple-element.64), channel_id=1, source_target_pairs={{0,1},{1,0},{2,3},{3,2},{4,5},{5,4},{6,7},{7,6},{8,9},{9,8},{10,11... | collective-permute-start | bytes 196616 | tf_op jit(solution)/shard_map/ppermute | solution.py:496
  30.1 6.1 %collective-permute-start.15 = (bf16[160,128]{1,0:T(8,128)(2,1)S(1)}, bf16[160,128]{1,0:T(8,128)(2,1)S(1)}, u32[]{:S(2)}, u32[]{:S(2)}) collective-permute-start(bf16[160,128]{1,0:T(8,128)(2,1)S(1)} %get-tuple-element.73), channel_id=1, source_target_pairs={{0,2},{1,3},{2,0},{3,1},{4,6},{5,7},{6,4},{7,5},{8,10},{9,11},{10,... | collective-permute-start | bytes 122888 | tf_op jit(solution)/shard_map/ppermute | solution.py:507
  32.4 3.7 %collective-permute-start.14 = (bf16[128,128]{1,0:T(8,128)(2,1)S(1)}, bf16[128,128]{1,0:T(8,128)(2,1)S(1)}, u32[]{:S(2)}, u32[]{:S(2)}) collective-permute-start(bf16[128,128]{1,0:T(8,128)(2,1)S(1)} %get-tuple-element.72), channel_id=1, source_target_pairs={{0,2},{1,3},{2,0},{3,1},{4,6},{5,7},{6,4},{7,5},{8,10},{9,11},{10,... | collective-permute-start | bytes 98312 | tf_op jit(solution)/shard_map/ppermute | solution.py:507

commit v16 on v14

--- a/solution.py
+++ b/solution.py
@@ -319,22 +319,28 @@
 
 def second_probs_kernel(sizes, *refs):
     turns = range(sizes[3])
-    mask_ref, query_ref = refs[:2]
-    keys, probs_ref = both_sets(sizes, refs[2:-1]), refs[-1]
+    mask_ref, query_ref, x_ref, inverse_ref = refs[:4]
+    keys, (probs_ref, low_ref, normed_ref) = both_sets(sizes, refs[4:-3]), refs[-3:]
     mask = mask_ref[1]
     scores = []
     for turn in turns:
         query = Group(sizes, turn).stacked(lambda where: query_ref[1, :, where])
         scores.append(dot(keys(turn, 0), query, NT))
     for turn in turns:
-        probs_ref[turn] = probabilities(mask, scores[turn])
+        probs = probabilities(mask, scores[turn])
+        probs_ref[turn] = probs
+        low_ref[turn] = probs.astype(BF16)
+    inverse = inverse_ref[1]
+    for first in range(0, sizes[5], HD):
+        here = slice(first, first + HD)
+        normed_ref[:, here] = x_ref[0, 1, :, here].astype(F32) * inverse
 
 
 def second_keys_kernel(sizes, *refs):
     cycle, tp_count = sizes[2:4]
     turns = range(tp_count)
     kv_count = cycle * tp_count
-    x_ref, query_ref, inverse_ref, output_ref, link_ref, chip_ref = refs[:6]
+    normed_ref, query_ref, low_ref, output_ref, link_ref, chip_ref = refs[:6]
     probs_ref, before_ref, *refs = refs[6:]
     keys, refs = both_sets(sizes, refs[:kv_count]), refs[kv_count:]
     query_grad_ref, gain_rows_ref, own_ref, arriving_ref = refs[:4]
@@ -344,11 +350,10 @@
     def arriving(where):
         return arriving_ref[:, where]
 
-    normed_of = normed_from(x_ref, 1, inverse_ref[1])
     columns_of = [Group(sizes, turn) for turn in turns]
     grads = [columns_of[turn].stacked(arriving) for turn in turns]
     prob_grads = [dot(keys(turn, 1), grads[turn], NT) for turn in turns]
-    value_grads = [dot(probs_ref[turn].astype(BF16), grads[turn], NN) for turn in turns]
+    value_grads = [dot(low_ref[turn], grads[turn], NN) for turn in turns]
     dscores = [score_grads(probs_ref[turn], prob_grads[turn]) for turn in turns]
     query_grads = [
         (SCALE * dot(dscores[turn], keys(turn, 0), TN)).astype(BF16) for turn in turns
@@ -359,7 +364,9 @@
         put_key_grads(sizes, turn, (key_grad, value_grads[turn]), own_ref, message_refs)
     for turn in turns:
         query_grad_ref[turn] = query_grads[turn]
-        gain_terms(columns_of[turn], query_grads[turn], normed_of, gain_scratch)
+        gain_terms(
+            columns_of[turn], query_grads[turn], lambda where: normed_ref[:, where], gain_scratch
+        )
     gain_rows = gain_scratch[...] + before_ref[...]
     gain_rows_ref[...] = gain_rows
     gain_low = gain_rows.astype(BF16)
@@ -592,20 +599,24 @@
     sums_first = sums_first[:1] + [
         to_near(value, -step, 0) for step, value in enumerate(sums_first[1:], 1)
     ]
-    (probs_second,) = call(
+    probs_second, probs_low, normed_second = call(
         functools.partial(second_probs_kernel, sizes),
         "second_probs",
-        (masks, queries, *kv),
-        [shape((tp_count, key_count, stacked), F32)],
+        (masks, queries, segment_inputs, inverse, *kv),
+        [
+            shape((tp_count, key_count, stacked), F32),
+            shape((tp_count, key_count, stacked), BF16),
+            shape((rows, columns), F32),
+        ],
     )
     message = shape((pair_rows + gain_count, HD), BF16)
     query_grad_second, gain_rows, own_second, arriving, *sends = call(
         functools.partial(second_keys_kernel, sizes),
         "second_keys",
         (
-            segment_inputs,
+            normed_second,
             queries,
-            inverse,
+            probs_low,
             output_grads,
             over_link,
             on_chip,

time: 37.1 us -> 37.1 us (level)
  no operation moved by 1% of the time
where the time goes in v16:
time: 37.1 us; the launch traced here: 36.8 us
  starting transfers between devices  20.8 us (56%)
  waiting for transfers between devices  7.5 us (20%)
  Pallas kernels  5.69 us (15%)
  local copies, waits for them, and re-layouts  1.15 us (3%)
  other arithmetic  0.93 us (3%)
  between operations  0.8 us (2%)
    ppermute x3, starting transfers between devices, to_far(): lax.ppermute(value, 'tp', [(i, i ^ near_count) for i in range(tp_count)])  6.35 us
    ppermute x3, starting transfers between devices, to_near(): return lax.ppermute(value, ('ctx', 'tp'), pairs)  5.79 us
    pallas_call x12, Pallas kernels, call(): pl.pallas_call(kernel, out_shape=out_shape, in_specs=in_specs, out_specs=...  5.69 us
    ppermute x1, waiting for transfers between devices, on_device(): lax.ppermute(input_grad_first, 'pipe', [(i, i - 1) for i in range(2, pipe...  3.83 us
    ppermute x4, starting transfers between devices, to_near(): return lax.ppermute(value, 'tp', [(i, i ^ near) for i in range(tp_count)])  2.58 us
    ppermute x1, starting transfers between devices, on_device(): lax.ppermute(input_grad_first, 'pipe', [(i, i ^ 1) for i in range(pipe_co...  2.41 us
    ppermute x4, starting transfers between devices, to_near(): lax.ppermute(value, 'ctx', [(i, (i + step) % cycle) for i in range(cycle)])  2.36 us
    ppermute x3, waiting for transfers between devices, to_far(): lax.ppermute(value, 'tp', [(i, i ^ near_count) for i in range(tp_count)])  1.75 us
  transfers between devices with their start and end apart: 16, of which 5 were waited for; matrix products, arithmetic and copies ran while one was open for 0% of the time, Pallas kernels for 11%

profile of v16, /device:TPU:1, one launch (start us, length us, event | category | flops | bytes accessed | tf_op | source)
XLA Modules:
  0.0 36.8 jit_solution(13267113575465515530)
XLA Ops:
  0.6 0.0 copy-start.2
  0.6 0.9 %pad_maximum_fusion.both_ref = bf16[2,2,128,128]{3,2,1,0:T(8,128)(2,1)S(1)} fusion(bf16[1,2,128,128]{3,2,1,0:T(8,128)(2,1)} %param.9, bf16[1,2,128,128]{3,2,1,0:T(8,128)(2,1)} %param.8), kind=kLoop, calls=%fused_computation | loop fusion | flops 65536 | bytes 262144 | tf_op jit(solution)/shard_map/stack | solution.py:522
  1.6 0.0 copy-start.4
  1.6 0.0 copy-start.5
  1.6 3.2 %collective-permute-start.3 = (bf16[2,2,64,128]{3,2,1,0:T(8,128)(2,1)S(1)}, bf16[2,2,64,128]{3,2,1,0:T(8,128)(2,1)S(1)}, u32[]{:S(2)}, u32[]{:S(2)}) collective-permute-start(bf16[2,2,64,128]{3,2,1,0:T(8,128)(2,1)S(1)} %get-tuple-element.49), channel_id=1, source_target_pairs={{0,2},{1,3},{2,0},{3,1},{4,6},{5,7},{6,4},{7,5},{8,10},{9,11},{10,... | collective-permute-start | bytes 196616 | tf_op jit(solution)/shard_map/ppermute | solution.py:516
  4.8 2.3 %collective-permute-start = (bf16[2,2,64,128]{3,2,1,0:T(8,128)(2,1)S(1)}, bf16[2,2,64,128]{3,2,1,0:T(8,128)(2,1)S(1)}, u32[]{:S(2)}, u32[]{:S(2)}) collective-permute-start(bf16[2,2,64,128]{3,2,1,0:T(8,128)(2,1)S(1)} %get-tuple-element.48.refs_4_.refs_6_.refs_8_), channel_id=1, source_target_pairs={{0,5},{1,4},{2,7},{3,6},{4,1},{5,0},{6,3},{7,2},{8,13},{9,12},{10,... | collective-permute-start | bytes 196616 | tf_op jit(solution)/shard_map/ppermute | solution.py:513
  7.1 0.2 collective-permute-start.1
  7.3 0.2 collective-permute-start.2
  7.5 0.0 collective-permute-done.3.refs_8_.refs_2_.refs_12_
  7.5 2.3 %collective-permute-start.4 = (bf16[2,2,64,128]{3,2,1,0:T(8,128)(2,1)S(1)}, bf16[2,2,64,128]{3,2,1,0:T(8,128)(2,1)S(1)}, u32[]{:S(2)}, u32[]{:S(2)}) collective-permute-start(bf16[2,2,64,128]{3,2,1,0:T(8,128)(2,1)S(1)} %collective-permute-done.3.refs_8_.refs_2_.refs_12_), channel_id=1, source_target_pairs={{0,5},{1,4},{2,7},{3,6},{4,1},{5,0},{6,3},{7,2},{8,13},{9,12},{10,... | collective-permute-start | bytes 196616 | tf_op jit(solution)/shard_map/ppermute | solution.py:513
  9.7 0.2 collective-permute-start.5
  10.0 0.0 collective-permute-done.refs_5_.refs_7_.refs_9_
  10.0 0.9 %collective-permute-start.6 = (bf16[2,2,64,128]{3,2,1,0:T(8,128)(2,1)S(1)}, bf16[2,2,64,128]{3,2,1,0:T(8,128)(2,1)S(1)}, u32[]{:S(2)}, u32[]{:S(2)}) collective-permute-start(bf16[2,2,64,128]{3,2,1,0:T(8,128)(2,1)S(1)} %collective-permute-done.3.refs_8_.refs_2_.refs_12_), channel_id=1, source_target_pairs={{0,1},{1,0},{2,3},{3,2},{4,5},{5,4},{6,7},{7,6},{8,9},{9,8},{10,11... | collective-permute-start | bytes 196616 | tf_op jit(solution)/shard_map/ppermute | solution.py:505
  10.8 0.0 copy-done.4
  10.8 0.0 copy-done.5
  10.9 0.0 copy-start
  10.9 1.0 %copy-done = bf16[1,2,32,4096]{3,2,1,0:T(8,128)(2,1)S(1)} copy-done((bf16[1,2,32,4096]{3,2,1,0:T(8,128)(2,1)S(1)}, bf16[1,2,32,4096]{3,2,1,0:T(8,128)(2,1)}, u32[]{:S(2)}) %copy-start) | copy-done | bytes 524312
  11.9 0.0 copy-start.1
  11.9 0.9 %norm.1 = (bf16[2,32,4096]{2,1,0:T(8,128)(2,1)S(1)}, f32[2,32,128]{2,1,0:T(8,128)S(1)}, f32[2,128,256]{2,1,0:T(8,128)S(1)}) custom-call(s32[5,8]{1,0:T(8,128)S(1)} %copy-done.5, bf16[1,2,32,4096]{3,2,1,0:T(8,128)(2,1)S(1)} %copy-done, f32[1,4096]{1,0:T(1,128)S(1)} %copy-done.4), custom_call_target="tpu_custom_call" | custom-call | tf_op jit(solution)/shard_map/norm/pallas_call | solution.py:491
  12.8 0.0 collective-permute-done.1.refs_6_.refs_8_.refs_10_
  12.8 0.0 collective-permute-done.2.refs_7_.refs_9_.refs_11_
  12.8 0.0 copy-done.2
  12.9 0.1 copy-done.1
  12.9 0.6 %first_near_rows.1 = (bf16[2,256,128]{2,1,0:T(8,128)(2,1)S(1)}, bf16[2,128,256]{2,1,0:T(8,128)(2,1)S(1)}, bf16[2,128,256]{2,1,0:T(8,128)(2,1)S(1)}, f32[32,128]{...) custom-call(bf16[1,2,32,4096]{3,2,1,0:T(8,128)(2,1)S(1)} %copy-done., ...), custom_call_target="tpu_custom_call" | custom-call | tf_op jit(solution)/shard_map/first_near_rows/pallas_call | solution.py:491
  13.6 0.0 collective-permute-done.4.refs_9_.refs_3_.refs_13_
  13.6 0.0 collective-permute-done.5.refs_10_.refs_4_.refs_14_
  13.6 0.0 collective-permute-done.6.refs_11_.refs_5_.refs_15_
  13.6 0.7 %first_far_rows.1 = (bf16[32,4096]{1,0:T(8,128)(2,1)S(1)}, bf16[2,256,128]{2,1,0:T(8,128)(2,1)S(1)}, bf16[2,128,256]{2,1,0:T(8,128)(2,1)S(1)}, bf16[2,128,256]{2,1,0:T(8,128)(2,1)S(1)}) custom-call(f32[2,128,256]{2,1,0:T(8,128)S(1)} %get-tuple-element.46.refs_0_.refs_4_, bf16[1,32,4096]{2,1,0:T(8,128)(2,1)S(1)} %copy-done.2, ...), custom_call_target="tpu_custom_call" | custom-call | tf_op jit(solution)/shard_map/first_far_rows/pallas_call | solution.py:491
  14.4 1.3 %collective-permute-start.7 = (bf16[32,4096]{1,0:T(8,128)(2,1)S(1)}, bf16[32,4096]{1,0:T(8,128)(2,1)S(1)}, u32[]{:S(2)}, u32[]{:S(2)}) collective-permute-start(bf16[32,4096]{1,0:T(8,128)(2,1)S(1)} %get-tuple-element.58.refs_5_), channel_id=1, source_target_pairs={{16,8},{17,9},{18,10},{19,11},{20,12},{21,13},{22,14},{23,15}} | collective-permute-start | bytes 786440 | tf_op jit(solution)/shard_map/ppermute | solution.py:574
  15.7 2.4 %collective-permute-start.8 = (bf16[32,4096]{1,0:T(8,128)(2,1)S(1)}, bf16[32,4096]{1,0:T(8,128)(2,1)S(1)}, u32[]{:S(2)}, u32[]{:S(2)}) collective-permute-start(bf16[32,4096]{1,0:T(8,128)(2,1)S(1)} %get-tuple-element.58.refs_5_), channel_id=1, source_target_pairs={{0,8},{8,0},{16,24},{24,16},{1,9},{9,1},{17,25},{25,17},{2,10},{10... | collective-permute-start | bytes 786440 | tf_op jit(solution)/shard_map/ppermute | solution.py:577
  18.1 0.4 %first_keys.1 = (f32[32,128]{1,0:T(8,128)S(1)}, f32[2,256,128]{2,1,0:T(8,128)S(1)}, bf16[2,256,128]{2,1,0:T(8,128)(2,1)S(1)}) custom-call(bf16[1,2,32,4096]{3,2,1,0:T(8,128)(2,1)S(1)} %copy-done.1, bf16[2,32,4096]{2,1,0:T(8,128)(2,1)S(1)} %get-tuple-element.47.refs_1_.refs_2_, f32[2,32,128]{2,1,0:T(8,128)S(1)} %get-tuple-element.45.refs_3_.refs_2_, ...), custom_call_target="tpu_custom_call" | custom-call | tf_op jit(solution)/shard_map/first_keys/pallas_call | solution.py:491
  18.5 0.0 copy-start.3
  18.5 1.3 %collective-permute-start.9 = (bf16[2,256,128]{2,1,0:T(8,128)(2,1)S(1)}, bf16[2,256,128]{2,1,0:T(8,128)(2,1)S(1)}, u32[]{:S(2)}, u32[]{:S(2)}) collective-permute-start(bf16[2,256,128]{2,1,0:T(8,128)(2,1)S(1)} %get-tuple-element.70), channel_id=1, source_target_pairs={{0,4},{4,0},{1,5},{5,1},{2,6},{6,2},{3,7},{7,3},{8,12},{12,8},{9,1... | collective-permute-start | bytes 393224 | tf_op jit(solution)/shard_map/ppermute | solution.py:507
  19.8 0.4 %second_probs.1 = (f32[4,128,256]{2,1,0:T(8,128)S(1)}, bf16[4,128,256]{2,1,0:T(8,128)(2,1)S(1)}, f32[32,4096]{1,0:T(8,128)S(1)}) custom-call(f32[2,128,256]{2,1,0:T(8,128)S(1)} %get-tuple-element.46.refs_0_.refs_4_, bf16[2,32,4096]{2,1,0:T(8,128)(2,1)S(1)} %get-tuple-element.47.refs_1_.refs_2_, bf16[1,2,32,4096]{3,2,1,0:T(8,128)(2,1)S(1)} %copy-done.1, ...), custom_call_target="tpu_custom_call" | custom-call | tf_op jit(solution)/shard_map/second_probs/pallas_call | solution.py:491
  20.2 3.8 %collective-permute-done.7.refs_4_ = bf16[32,4096]{1,0:T(8,128)(2,1)S(1)} collective-permute-done((bf16[32,4096]{1,0:T(8,128)(2,1)S(1)}, bf16[32,4096]{1,0:T(8,128)(2,1)S(1)}, u32[]{:S(2)}, u32[]{:S(2)}) %collective-permute-start.7) | collective-permute-done | bytes 262176 | tf_op jit(solution)/shard_map/ppermute | solution.py:574
  24.1 0.0 collective-permute-done.8.refs_5_
  24.1 0.0 copy-done.3
  24.1 0.6 %second_keys.1 = (bf16[4,256,128]{2,1,0:T(8,128)(2,1)S(1)}, f32[32,128]{1,0:T(8,128)S(1)}, f32[256,128]{1,0:T(8,128)S(1)}, bf16[32,4096]{1,0:T(8,128)(2,1)S(1)},...) custom-call(f32[32,4096]{1,0:T(8,128)S(1)} %get-tuple-element.50.refs_0_, ...), custom_call_target="tpu_custom_call" | custom-call | tf_op jit(solution)/shard_map/second_keys/pallas_call | solution.py:491
  24.6 1.3 %collective-permute-start.11 = (bf16[288,128]{1,0:T(8,128)(2,1)S(1)}, bf16[288,128]{1,0:T(8,128)(2,1)S(1)}, u32[]{:S(2)}, u32[]{:S(2)}) collective-permute-start(bf16[288,128]{1,0:T(8,128)(2,1)S(1)} %get-tuple-element.76), channel_id=1, source_target_pairs={{0,5},{1,4},{2,7},{3,6},{4,1},{5,0},{6,3},{7,2},{8,13},{9,12},{10,... | collective-permute-start | bytes 221192 | tf_op jit(solution)/shard_map/ppermute | solution.py:513
  25.9 0.6 %collective-permute-start.12 = (bf16[288,128]{1,0:T(8,128)(2,1)S(1)}, bf16[288,128]{1,0:T(8,128)(2,1)S(1)}, u32[]{:S(2)}, u32[]{:S(2)}) collective-permute-start(bf16[288,128]{1,0:T(8,128)(2,1)S(1)} %get-tuple-element.77), channel_id=1, source_target_pairs={{0,4},{4,0},{1,5},{5,1},{2,6},{6,2},{3,7},{7,3},{8,12},{12,8},{9,1... | collective-permute-start | bytes 221192 | tf_op jit(solution)/shard_map/ppermute | solution.py:507
  26.5 0.8 %collective-permute-start.13 = (bf16[288,128]{1,0:T(8,128)(2,1)S(1)}, bf16[288,128]{1,0:T(8,128)(2,1)S(1)}, u32[]{:S(2)}, u32[]{:S(2)}) collective-permute-start(bf16[288,128]{1,0:T(8,128)(2,1)S(1)} %get-tuple-element.78), channel_id=1, source_target_pairs={{0,1},{1,0},{2,3},{3,2},{4,5},{5,4},{6,7},{7,6},{8,9},{9,8},{10,11... | collective-permute-start | bytes 221192 | tf_op jit(solution)/shard_map/ppermute | solution.py:505
  27.4 0.0 collective-permute-done.9.refs_1_
  27.4 0.7 %collective-permute-start.10 = (bf16[256,128]{1,0:T(8,128)(2,1)S(1)}, bf16[256,128]{1,0:T(8,128)(2,1)S(1)}, u32[]{:S(2)}, u32[]{:S(2)}) collective-permute-start(bf16[256,128]{1,0:T(8,128)(2,1)S(1)} %get-tuple-element.72), channel_id=1, source_target_pairs={{0,1},{1,0},{2,3},{3,2},{4,5},{5,4},{6,7},{7,6},{8,9},{9,8},{10,11... | collective-permute-start | bytes 196616 | tf_op jit(solution)/shard_map/ppermute | solution.py:505
  28.1 1.2 %collective-permute-done.11.refs_2_ = bf16[288,128]{1,0:T(8,128)(2,1)S(1)} collective-permute-done((bf16[288,128]{1,0:T(8,128)(2,1)S(1)}, bf16[288,128]{1,0:T(8,128)(2,1)S(1)}, u32[]{:S(2)}, u32[]{:S(2)}) %collective-permute-start.11) | collective-permute-done | bytes 73760 | tf_op jit(solution)/shard_map/ppermute | solution.py:513
  29.3 0.3 collective-permute-done.12.refs_3_
  29.6 0.4 %collective-permute-done.13.refs_4_ = bf16[288,128]{1,0:T(8,128)(2,1)S(1)} collective-permute-done((bf16[288,128]{1,0:T(8,128)(2,1)S(1)}, bf16[288,128]{1,0:T(8,128)(2,1)S(1)}, u32[]{:S(2)}, u32[]{:S(2)}) %collective-permute-start.13) | collective-permute-done | bytes 73760 | tf_op jit(solution)/shard_map/ppermute | solution.py:505
  30.0 0.1 second_near.1
  30.0 2.3 %collective-permute-start.15 = (bf16[160,128]{1,0:T(8,128)(2,1)S(1)}, bf16[160,128]{1,0:T(8,128)(2,1)S(1)}, u32[]{:S(2)}, u32[]{:S(2)}) collective-permute-start(bf16[160,128]{1,0:T(8,128)(2,1)S(1)} %get-tuple-element.81), channel_id=1, source_target_pairs={{0,2},{1,3},{2,0},{3,1},{4,6},{5,7},{6,4},{7,5},{8,10},{9,11},{10,... | collective-permute-start | bytes 122888 | tf_op jit(solution)/shard_map/ppermute | solution.py:516
  32.4 0.0 collective-permute-done.10.refs_0_
  32.4 0.8 %collective-permute-start.14 = (bf16[128,128]{1,0:T(8,128)(2,1)S(1)}, bf16[128,128]{1,0:T(8,128)(2,1)S(1)}, u32[]{:S(2)}, u32[]{:S(2)}) collective-permute-start(bf16[128,128]{1,0:T(8,128)(2,1)S(1)} %get-tuple-element.80), channel_id=1, source_target_pairs={{0,2},{1,3},{2,0},{3,1},{4,6},{5,7},{6,4},{7,5},{8,10},{9,11},{10,... | collective-permute-start | bytes 98312 | tf_op jit(solution)/shard_map/ppermute | solution.py:516
  33.2 1.2 %second_rows.1 = bf16[1,2,32,4096]{3,2,1,0:T(8,128)(2,1)} custom-call(bf16[1,2,32,4096]{3,2,1,0:T(8,128)(2,1)S(1)} %copy-done.1, f32[1,4096]{1,0:T(1,128)S(1)} %copy-done.4, f32[2,32,128]{2,1,0:T(8,128)S(1)} %get-tuple-element.45.refs_3_.refs_2_, bf16[32,4096]{1,0:T(8,128)(2,1)S(1)} %get-tuple-element.67.refs_3_, ...), custom_call_target="tpu_custom_call" | custom-call | tf_op jit(solution)/shard_map/second_rows/pallas_call | solution.py:491
  34.4 1.7 %collective-permute-done.14.refs_2_ = bf16[128,128]{1,0:T(8,128)(2,1)S(1)} collective-permute-done((bf16[128,128]{1,0:T(8,128)(2,1)S(1)}, bf16[128,128]{1,0:T(8,128)(2,1)S(1)}, u32[]{:S(2)}, u32[]{:S(2)}) %collective-permute-start.14) | collective-permute-done | bytes 32800 | tf_op jit(solution)/shard_map/ppermute | solution.py:516
  36.1 0.0 collective-permute-done.15.refs_3_
  36.1 0.7 %finish.1 = (f32[1,2,128,128]{3,2,1,0:T(8,128)}, f32[1,2,128,128]{3,2,1,0:T(8,128)}, f32[32,128]{1,0:T(8,128)}) custom-call(f32[128,128]{1,0:T(8,128)S(1)} %get-tuple-element.73.refs_0_, f32[128,128]{1,0:T(8,128)S(1)} %get-tuple-element.79.refs_1_, bf16[128,128]{1,0:T(8,128)(2,1)S(1)} %collective-permute-done.14.refs_2_, ...), custom_call_target="tpu_custom_call" | custom-call | tf_op jit(solution)/shard_map/finish/pallas_call | solution.py:491
  (3 shorter events, 0.1 us)
Async XLA Ops:
  0.6 12.2 %copy-start.2 = (bf16[1,32,4096]{2,1,0:T(8,128)(2,1)S(1)}, bf16[1,32,4096]{2,1,0:T(8,128)(2,1)}, u32[]{:S(2)}) copy-start(bf16[1,32,4096]{2,1,0:T(8,128)(2,1)} %refs_3_.2) | copy-start | bytes 786436
  1.6 9.3 %copy-start.4 = (f32[1,4096]{1,0:T(1,128)S(1)}, f32[1,4096]{1,0:T(1,128)}, u32[]{:S(2)}) copy-start(f32[1,4096]{1,0:T(1,128)} %refs_1_.5) | copy-start | bytes 49156
  1.6 9.3 %copy-start.5 = (s32[5,8]{1,0:T(8,128)S(1)}, s32[5,8]{1,0:T(8,128)}, u32[]{:S(2)}) copy-start(s32[5,8]{1,0:T(8,128)} %doc_ref.1) | copy-start | bytes 484
  1.6 5.9 %collective-permute-start.3 = (bf16[2,2,64,128]{3,2,1,0:T(8,128)(2,1)S(1)}, bf16[2,2,64,128]{3,2,1,0:T(8,128)(2,1)S(1)}, u32[]{:S(2)}, u32[]{:S(2)}) collective-permute-start(bf16[2,2,64,128]{3,2,1,0:T(8,128)(2,1)S(1)} %get-tuple-element.49), channel_id=1, source_target_pairs={{0,2},{1,3},{2,0},{3,1},{4,6},{5,7},{6,4},{7,5},{8,10},{9,11},{10,... | collective-permute-start | bytes 196616 | tf_op jit(solution)/shard_map/ppermute | solution.py:516
  4.8 5.1 %collective-permute-start = (bf16[2,2,64,128]{3,2,1,0:T(8,128)(2,1)S(1)}, bf16[2,2,64,128]{3,2,1,0:T(8,128)(2,1)S(1)}, u32[]{:S(2)}, u32[]{:S(2)}) collective-permute-start(bf16[2,2,64,128]{3,2,1,0:T(8,128)(2,1)S(1)} %get-tuple-element.48.refs_4_.refs_6_.refs_8_), channel_id=1, source_target_pairs={{0,5},{1,4},{2,7},{3,6},{4,1},{5,0},{6,3},{7,2},{8,13},{9,12},{10,... | collective-permute-start | bytes 196616 | tf_op jit(solution)/shard_map/ppermute | solution.py:513
  7.1 5.7 %collective-permute-start.1 = (bf16[2,2,64,128]{3,2,1,0:T(8,128)(2,1)S(1)}, bf16[2,2,64,128]{3,2,1,0:T(8,128)(2,1)S(1)}, u32[]{:S(2)}, u32[]{:S(2)}) collective-permute-start(bf16[2,2,64,128]{3,2,1,0:T(8,128)(2,1)S(1)} %get-tuple-element.48.refs_4_.refs_6_.refs_8_), channel_id=1, source_target_pairs={{0,4},{4,0},{1,5},{5,1},{2,6},{6,2},{3,7},{7,3},{8,12},{12,8},{9,1... | collective-permute-start | bytes 196616 | tf_op jit(solution)/shard_map/ppermute | solution.py:507
  7.3 5.5 %collective-permute-start.2 = (bf16[2,2,64,128]{3,2,1,0:T(8,128)(2,1)S(1)}, bf16[2,2,64,128]{3,2,1,0:T(8,128)(2,1)S(1)}, u32[]{:S(2)}, u32[]{:S(2)}) collective-permute-start(bf16[2,2,64,128]{3,2,1,0:T(8,128)(2,1)S(1)} %get-tuple-element.48.refs_4_.refs_6_.refs_8_), channel_id=1, source_target_pairs={{0,1},{1,0},{2,3},{3,2},{4,5},{5,4},{6,7},{7,6},{8,9},{9,8},{10,11... | collective-permute-start | bytes 196616 | tf_op jit(solution)/shard_map/ppermute | solution.py:505
  7.5 6.1 %collective-permute-start.4 = (bf16[2,2,64,128]{3,2,1,0:T(8,128)(2,1)S(1)}, bf16[2,2,64,128]{3,2,1,0:T(8,128)(2,1)S(1)}, u32[]{:S(2)}, u32[]{:S(2)}) collective-permute-start(bf16[2,2,64,128]{3,2,1,0:T(8,128)(2,1)S(1)} %collective-permute-done.3.refs_8_.refs_2_.refs_12_), channel_id=1, source_target_pairs={{0,5},{1,4},{2,7},{3,6},{4,1},{5,0},{6,3},{7,2},{8,13},{9,12},{10,... | collective-permute-start | bytes 196616 | tf_op jit(solution)/shard_map/ppermute | solution.py:513
  9.7 3.9 %collective-permute-start.5 = (bf16[2,2,64,128]{3,2,1,0:T(8,128)(2,1)S(1)}, bf16[2,2,64,128]{3,2,1,0:T(8,128)(2,1)S(1)}, u32[]{:S(2)}, u32[]{:S(2)}) collective-permute-start(bf16[2,2,64,128]{3,2,1,0:T(8,128)(2,1)S(1)} %collective-permute-done.3.refs_8_.refs_2_.refs_12_), channel_id=1, source_target_pairs={{0,4},{4,0},{1,5},{5,1},{2,6},{6,2},{3,7},{7,3},{8,12},{12,8},{9,1... | collective-permute-start | bytes 196616 | tf_op jit(solution)/shard_map/ppermute | solution.py:507
  10.0 3.6 %collective-permute-start.6 = (bf16[2,2,64,128]{3,2,1,0:T(8,128)(2,1)S(1)}, bf16[2,2,64,128]{3,2,1,0:T(8,128)(2,1)S(1)}, u32[]{:S(2)}, u32[]{:S(2)}) collective-permute-start(bf16[2,2,64,128]{3,2,1,0:T(8,128)(2,1)S(1)} %collective-permute-done.3.refs_8_.refs_2_.refs_12_), channel_id=1, source_target_pairs={{0,1},{1,0},{2,3},{3,2},{4,5},{5,4},{6,7},{7,6},{8,9},{9,8},{10,11... | collective-permute-start | bytes 196616 | tf_op jit(solution)/shard_map/ppermute | solution.py:505
  10.9 1.0 %copy-start = (bf16[1,2,32,4096]{3,2,1,0:T(8,128)(2,1)S(1)}, bf16[1,2,32,4096]{3,2,1,0:T(8,128)(2,1)}, u32[]{:S(2)}) copy-start(bf16[1,2,32,4096]{3,2,1,0:T(8,128)(2,1)} %refs_0_.5) | copy-start | bytes 1572868
  11.9 1.0 %copy-start.1 = (bf16[1,2,32,4096]{3,2,1,0:T(8,128)(2,1)S(1)}, bf16[1,2,32,4096]{3,2,1,0:T(8,128)(2,1)}, u32[]{:S(2)}) copy-start(bf16[1,2,32,4096]{3,2,1,0:T(8,128)(2,1)} %refs_0_.5) | copy-start | bytes 1572868
  14.4 9.7 %collective-permute-start.7 = (bf16[32,4096]{1,0:T(8,128)(2,1)S(1)}, bf16[32,4096]{1,0:T(8,128)(2,1)S(1)}, u32[]{:S(2)}, u32[]{:S(2)}) collective-permute-start(bf16[32,4096]{1,0:T(8,128)(2,1)S(1)} %get-tuple-element.58.refs_5_), channel_id=1, source_target_pairs={{16,8},{17,9},{18,10},{19,11},{20,12},{21,13},{22,14},{23,15}} | collective-permute-start | bytes 786440 | tf_op jit(solution)/shard_map/ppermute | solution.py:574
  15.7 8.4 %collective-permute-start.8 = (bf16[32,4096]{1,0:T(8,128)(2,1)S(1)}, bf16[32,4096]{1,0:T(8,128)(2,1)S(1)}, u32[]{:S(2)}, u32[]{:S(2)}) collective-permute-start(bf16[32,4096]{1,0:T(8,128)(2,1)S(1)} %get-tuple-element.58.refs_5_), channel_id=1, source_target_pairs={{0,8},{8,0},{16,24},{24,16},{1,9},{9,1},{17,25},{25,17},{2,10},{10... | collective-permute-start | bytes 786440 | tf_op jit(solution)/shard_map/ppermute | solution.py:577
  18.5 5.6 %copy-start.3 = (bf16[1,32,4096]{2,1,0:T(8,128)(2,1)S(1)}, bf16[1,32,4096]{2,1,0:T(8,128)(2,1)}, u32[]{:S(2)}) copy-start(bf16[1,32,4096]{2,1,0:T(8,128)(2,1)} %refs_3_.3) | copy-start | bytes 786436
  18.5 8.8 %collective-permute-start.9 = (bf16[2,256,128]{2,1,0:T(8,128)(2,1)S(1)}, bf16[2,256,128]{2,1,0:T(8,128)(2,1)S(1)}, u32[]{:S(2)}, u32[]{:S(2)}) collective-permute-start(bf16[2,256,128]{2,1,0:T(8,128)(2,1)S(1)} %get-tuple-element.70), channel_id=1, source_target_pairs={{0,4},{4,0},{1,5},{5,1},{2,6},{6,2},{3,7},{7,3},{8,12},{12,8},{9,1... | collective-permute-start | bytes 393224 | tf_op jit(solution)/shard_map/ppermute | solution.py:507
  24.6 4.6 %collective-permute-start.11 = (bf16[288,128]{1,0:T(8,128)(2,1)S(1)}, bf16[288,128]{1,0:T(8,128)(2,1)S(1)}, u32[]{:S(2)}, u32[]{:S(2)}) collective-permute-start(bf16[288,128]{1,0:T(8,128)(2,1)S(1)} %get-tuple-element.76), channel_id=1, source_target_pairs={{0,5},{1,4},{2,7},{3,6},{4,1},{5,0},{6,3},{7,2},{8,13},{9,12},{10,... | collective-permute-start | bytes 221192 | tf_op jit(solution)/shard_map/ppermute | solution.py:513
  25.9 3.7 %collective-permute-start.12 = (bf16[288,128]{1,0:T(8,128)(2,1)S(1)}, bf16[288,128]{1,0:T(8,128)(2,1)S(1)}, u32[]{:S(2)}, u32[]{:S(2)}) collective-permute-start(bf16[288,128]{1,0:T(8,128)(2,1)S(1)} %get-tuple-element.77), channel_id=1, source_target_pairs={{0,4},{4,0},{1,5},{5,1},{2,6},{6,2},{3,7},{7,3},{8,12},{12,8},{9,1... | collective-permute-start | bytes 221192 | tf_op jit(solution)/shard_map/ppermute | solution.py:507
  26.5 3.5 %collective-permute-start.13 = (bf16[288,128]{1,0:T(8,128)(2,1)S(1)}, bf16[288,128]{1,0:T(8,128)(2,1)S(1)}, u32[]{:S(2)}, u32[]{:S(2)}) collective-permute-start(bf16[288,128]{1,0:T(8,128)(2,1)S(1)} %get-tuple-element.78), channel_id=1, source_target_pairs={{0,1},{1,0},{2,3},{3,2},{4,5},{5,4},{6,7},{7,6},{8,9},{9,8},{10,11... | collective-permute-start | bytes 221192 | tf_op jit(solution)/shard_map/ppermute | solution.py:505
  27.4 5.0 %collective-permute-start.10 = (bf16[256,128]{1,0:T(8,128)(2,1)S(1)}, bf16[256,128]{1,0:T(8,128)(2,1)S(1)}, u32[]{:S(2)}, u32[]{:S(2)}) collective-permute-start(bf16[256,128]{1,0:T(8,128)(2,1)S(1)} %get-tuple-element.72), channel_id=1, source_target_pairs={{0,1},{1,0},{2,3},{3,2},{4,5},{5,4},{6,7},{7,6},{8,9},{9,8},{10,11... | collective-permute-start | bytes 196616 | tf_op jit(solution)/shard_map/ppermute | solution.py:505
  30.0 6.1 %collective-permute-start.15 = (bf16[160,128]{1,0:T(8,128)(2,1)S(1)}, bf16[160,128]{1,0:T(8,128)(2,1)S(1)}, u32[]{:S(2)}, u32[]{:S(2)}) collective-permute-start(bf16[160,128]{1,0:T(8,128)(2,1)S(1)} %get-tuple-element.81), channel_id=1, source_target_pairs={{0,2},{1,3},{2,0},{3,1},{4,6},{5,7},{6,4},{7,5},{8,10},{9,11},{10,... | collective-permute-start | bytes 122888 | tf_op jit(solution)/shard_map/ppermute | solution.py:516
  32.4 3.7 %collective-permute-start.14 = (bf16[128,128]{1,0:T(8,128)(2,1)S(1)}, bf16[128,128]{1,0:T(8,128)(2,1)S(1)}, u32[]{:S(2)}, u32[]{:S(2)}) collective-permute-start(bf16[128,128]{1,0:T(8,128)(2,1)S(1)} %get-tuple-element.80), channel_id=1, source_target_pairs={{0,2},{1,3},{2,0},{3,1},{4,6},{5,7},{6,4},{7,5},{8,10},{9,11},{10,... | collective-permute-start | bytes 98312 | tf_op jit(solution)/shard_map/ppermute | solution.py:516
